TPU v7x, 32 devices: a whole 2x2x4 slice. The times are simulated.
32 devices in a mesh: src: 2 (over y), tgt: 16 (over z, x, core).
Axes of the slice: x: 2, y: 2, z: 4, core: 2. Of those that a mesh axis runs over, the one named last changes fastest.
Arguments:
- source_points: bfloat16 [4096, 128], P(('src', 'tgt')), may hold values from -1 to 1
- target_points: bfloat16 [16384, 128], P(('tgt', 'src')), may hold values from -1 to 1
- source_mass: float32 [4096], P('src'), may hold values from 0.1 to 10
- target_mass: float32 [16384], P('tgt'), may hold values from 0.1 to 10
Outputs:
- source_potential: float32 [4096], P('src')
- target_potential: float32 [16384], P('tgt')
All inputs are finite; a program needn't handle non-finite values.
Results may differ from a plain program's by a relative error of at most 0.0003.
Values may be sent and summed in bfloat16 or wider, within the bound.
No kernel may reach another device: no remote copies, remote signals or barrier semaphores. Data moves between devices by JAX's collectives and lax.ppermute only.
A program may use at most 64 MiB of HBM per device.

v0:
```python
import math

import jax
import jax.numpy as jnp
from jax import lax
from jax.sharding import PartitionSpec as P

ITERS = 3


EPS = 0.05


def half_norm(points):
    values = points.astype(jnp.float32)
    return 0.5 * jnp.sum(values * values, axis=1)


def tile_cost(rows, rows_half, cols, cols_half):
    return (
        rows_half[:, None]
        + cols_half[None, :]
        - jnp.dot(rows, cols.T, preferred_element_type=jnp.float32)
    )


def combine(first, second):
    peak = jnp.maximum(first[0], second[0])
    return (peak, first[1] * jnp.exp(first[0] - peak) + second[1] * jnp.exp(second[0] - peak))


def finish_rows(peak, total):
    widest = lax.pmax(peak, "tgt")
    total = lax.psum(total * jnp.exp(peak - widest), "tgt")
    peak = widest
    return -EPS * (peak + jnp.log(total))


def finish_cols(peak, total):
    widest = lax.pmax(peak, "src")
    total = lax.psum(total * jnp.exp(peak - widest), "src")
    peak = widest
    return -EPS * (peak + jnp.log(total))


def row_stats(scores):
    peak = jnp.max(scores, axis=1)
    return (peak, jnp.sum(jnp.exp(scores - peak[:, None]), axis=1))


def col_stats(scores):
    peak = jnp.max(scores, axis=0)
    return (peak, jnp.sum(jnp.exp(scores - peak[None, :]), axis=0))


def local(source_points, target_points, source_mass, target_mass):
    sources = lax.all_gather(source_points, "tgt", axis=0, tiled=True)
    targets = lax.all_gather(target_points, "src", axis=0, tiled=True)
    source_half = half_norm(sources)
    target_half = half_norm(targets)
    log_a = jnp.log(source_mass)
    log_b = jnp.log(target_mass)
    count = sources.shape[0]
    width = targets.shape[0]
    block = math.gcd(512, count)
    steps_count = count // block
    source_blocks = sources.reshape(steps_count, block, sources.shape[1])
    half_blocks = source_half.reshape(steps_count, block)
    target_potential = jnp.zeros((width,), jnp.float32)
    source_potential = jnp.zeros((count,), jnp.float32)
    for step in range(ITERS):
        shift_cols = target_potential + EPS * log_b

        def block_rows(pair):
            chosen, chosen_half = pair
            cost = tile_cost(chosen, chosen_half, targets, target_half)
            return row_stats((shift_cols[None, :] - cost) / EPS)

        peak, total = lax.map(block_rows, (source_blocks, half_blocks))
        peak = peak.reshape(count)
        total = total.reshape(count)
        source_potential = finish_rows(peak, total)
        shift_rows = source_potential + EPS * log_a
        shift_blocks = shift_rows.reshape(steps_count, block)

        def block_cols(carry, pieces):
            chosen, chosen_half, chosen_shift = pieces
            cost = tile_cost(chosen, chosen_half, targets, target_half)
            return (combine(carry, col_stats((chosen_shift[:, None] - cost) / EPS)), None)

        start = (jnp.full((width,), -1e30, jnp.float32), jnp.zeros((width,), jnp.float32))
        (peak, total), unused = lax.scan(
            block_cols, start, (source_blocks, half_blocks, shift_blocks)
        )
        target_potential = finish_cols(peak, total)
    return (source_potential, target_potential)


def solution(mesh):
    placed = (P(("src", "tgt"), None), P(("tgt", "src"), None), P("src"), P("tgt"))
    return jax.shard_map(
        local, mesh=mesh, in_specs=placed, out_specs=(P("src"), P("tgt")), check_vma=False
    )
```

profile of v0, /device:TPU:0, one launch (start us, length us, event | category | flops | bytes accessed | tf_op | source)
XLA Modules:
  0.0 270.6 jit_solution(16403232946352505461)
XLA Ops:
  0.6 7.4 %all_gather.7 = bf16[1024,128]{1,0:T(8,128)(2,1)S(1)} all-gather(bf16[512,128]{1,0:T(8,128)(2,1)} %param.17), channel_id=1, replica_groups=mesh['src'=2,'tgt'=16] {'src'}, dimensions={0}, use_global_device_ids=true | all-gather | bytes 393216 | tf_op jit(solution)/shard_map/all_gather | solution.py:58
  8.2 23.6 %all_gather.6 = bf16[2048,128]{1,0:T(8,128)(2,1)S(1)} all-gather(bf16[128,128]{1,0:T(8,128)(2,1)} %param.16), channel_id=1, replica_groups=mesh['src'=2,'tgt'=16] {'tgt'}, dimensions={0}, use_global_device_ids=true | all-gather | bytes 557056 | tf_op jit(solution)/shard_map/all_gather | solution.py:57
  32.3 0.7 log_multiply_fusion.1
  33.0 5.0 %while.75 = (s32[]{:T(128)}, f32[4,512]{1,0:T(4,128)S(1)}, f32[4,512]{1,0:T(4,128)S(1)}, f32[1024]{0:T(1024)S(1)}, f32[4,512]{1,0:T(4,128)S(1)}, /*index=5*/f32[...) while((s32[]{:T(128)}, f32[4,512]{1,0:T(4,128)S(1)}, ...), condition=%wide.region_5.6_spmd, body=%wide.region_2.5_spmd.sunk | while | flops 137886720 | bytes 4616309 | solution.py:79
  38.0 30.3 %pmax.42 = f32[2048]{0:T(1024)S(1)} all-reduce(f32[2048]{0:T(1024)S(1)} %bitcast.125), channel_id=1, replica_groups=mesh['src'=2,'tgt'=16] {'tgt'}, use_global_device_ids=true, to_apply=%region_6.7 | all-reduce | flops 2048 | bytes 16384 | tf_op jit(solution)/shard_map/pmax | solution.py:33
  68.3 30.0 %psum.42 = f32[2048]{0:T(1024)S(1)} all-reduce(f32[2048]{0:T(1024)S(1)} %exponential_multiply_fusion.2), channel_id=1, replica_groups=mesh['src'=2,'tgt'=16] {'tgt'}, use_global_device_ids=true, to_apply=%region_7.8 | all-reduce | flops 2048 | bytes 16384 | tf_op jit(solution)/shard_map/psum | solution.py:34
  98.4 3.7 %while.78 = (s32[]{:T(128)}, f32[1024]{0:T(1024)S(1)}, f32[1024]{0:T(1024)S(1)}, f32[4,512]{1,0:T(4,128)S(1)}, f32[4,512]{1,0:T(4,128)S(1)}, /*index=5*/f32[1024...) while((s32[]{:T(128)}, f32[1024]{0:T(1024)S(1)}, ...), condition=%wide.region_11.12_spmd.clone, body=%wide.region_8.11_spmd.clone.sunk | while | flops 137893888 | bytes 4640887 | solution.py:92
  102.1 4.9 %pmax.43 = f32[1024]{0:T(1024)S(1)} all-reduce(f32[1024]{0:T(1024)S(1)} %get-tuple-element.262), channel_id=1, replica_groups=mesh['src'=2,'tgt'=16] {'src'}, use_global_device_ids=true, to_apply=%region_12.13 | all-reduce | flops 1024 | bytes 8192 | tf_op jit(solution)/shard_map/pmax | solution.py:40
  107.1 4.9 %psum.43 = f32[1024]{0:T(1024)S(1)} all-reduce(f32[1024]{0:T(1024)S(1)} %exponential_multiply_fusion.5), channel_id=1, replica_groups=mesh['src'=2,'tgt'=16] {'src'}, use_global_device_ids=true, to_apply=%region_13.14 | all-reduce | flops 1024 | bytes 8192 | tf_op jit(solution)/shard_map/psum | solution.py:41
  112.0 5.0 %while.76 = (s32[]{:T(128)}, f32[4,512]{1,0:T(4,128)S(1)}, f32[4,512]{1,0:T(4,128)S(1)}, f32[1024]{0:T(1024)S(1)}, f32[4,512]{1,0:T(4,128)S(1)}, /*index=5*/f32[...) while((s32[]{:T(128)}, f32[4,512]{1,0:T(4,128)S(1)}, ...), condition=%wide.region_17.18_spmd, body=%wide.region_14.17_spmd.sunk | while | flops 137886720 | bytes 4616309 | solution.py:79
  117.0 30.0 %pmax.44 = f32[2048]{0:T(1024)S(1)} all-reduce(f32[2048]{0:T(1024)S(1)} %bitcast.127), channel_id=1, replica_groups=mesh['src'=2,'tgt'=16] {'tgt'}, use_global_device_ids=true, to_apply=%region_18.19 | all-reduce | flops 2048 | bytes 16384 | tf_op jit(solution)/shard_map/pmax | solution.py:33
  147.0 30.0 %psum.44 = f32[2048]{0:T(1024)S(1)} all-reduce(f32[2048]{0:T(1024)S(1)} %exponential_multiply_fusion.1), channel_id=1, replica_groups=mesh['src'=2,'tgt'=16] {'tgt'}, use_global_device_ids=true, to_apply=%region_19.20 | all-reduce | flops 2048 | bytes 16384 | tf_op jit(solution)/shard_map/psum | solution.py:34
  177.1 3.7 %while.79 = (s32[]{:T(128)}, f32[1024]{0:T(1024)S(1)}, f32[1024]{0:T(1024)S(1)}, f32[4,512]{1,0:T(4,128)S(1)}, f32[4,512]{1,0:T(4,128)S(1)}, /*index=5*/f32[1024...) while((s32[]{:T(128)}, f32[1024]{0:T(1024)S(1)}, ...), condition=%wide.region_23.24_spmd.clone, body=%wide.region_20.23_spmd.clone.sunk | while | flops 137893888 | bytes 4640887 | solution.py:92
  180.8 4.9 %pmax.45 = f32[1024]{0:T(1024)S(1)} all-reduce(f32[1024]{0:T(1024)S(1)} %get-tuple-element.266), channel_id=1, replica_groups=mesh['src'=2,'tgt'=16] {'src'}, use_global_device_ids=true, to_apply=%region_24.25 | all-reduce | flops 1024 | bytes 8192 | tf_op jit(solution)/shard_map/pmax | solution.py:40
  185.8 4.9 %psum.45 = f32[1024]{0:T(1024)S(1)} all-reduce(f32[1024]{0:T(1024)S(1)} %exponential_multiply_fusion.4), channel_id=1, replica_groups=mesh['src'=2,'tgt'=16] {'src'}, use_global_device_ids=true, to_apply=%region_25.26 | all-reduce | flops 1024 | bytes 8192 | tf_op jit(solution)/shard_map/psum | solution.py:41
  190.7 5.0 %while.77 = (s32[]{:T(128)}, f32[4,512]{1,0:T(4,128)S(1)}, f32[4,512]{1,0:T(4,128)S(1)}, f32[1024]{0:T(1024)S(1)}, f32[4,512]{1,0:T(4,128)S(1)}, /*index=5*/f32[...) while((s32[]{:T(128)}, f32[4,512]{1,0:T(4,128)S(1)}, ...), condition=%wide.region_29.30_spmd, body=%wide.region_26.29_spmd.sunk | while | flops 137886720 | bytes 4616309 | solution.py:79
  190.8 0.6 fusion.54
  195.7 30.0 %pmax.46 = f32[2048]{0:T(1024)S(1)} all-reduce(f32[2048]{0:T(1024)S(1)} %bitcast.129), channel_id=1, replica_groups=mesh['src'=2,'tgt'=16] {'tgt'}, use_global_device_ids=true, to_apply=%region_30.31 | all-reduce | flops 2048 | bytes 16384 | tf_op jit(solution)/shard_map/pmax | solution.py:33
  225.8 30.0 %psum.46 = f32[2048]{0:T(1024)S(1)} all-reduce(f32[2048]{0:T(1024)S(1)} %exponential_multiply_fusion), channel_id=1, replica_groups=mesh['src'=2,'tgt'=16] {'tgt'}, use_global_device_ids=true, to_apply=%region_31.32 | all-reduce | flops 2048 | bytes 16384 | tf_op jit(solution)/shard_map/psum | solution.py:34
  255.8 0.6 fusion.21
  256.4 3.7 %while.80 = (s32[]{:T(128)}, f32[1024]{0:T(1024)S(1)}, f32[1024]{0:T(1024)S(1)}, f32[4,512]{1,0:T(4,128)S(1)}, f32[4,512]{1,0:T(4,128)S(1)}, /*index=5*/f32[1024...) while((s32[]{:T(128)}, f32[1024]{0:T(1024)S(1)}, ...), condition=%wide.region_35.36_spmd.clone, body=%wide.region_32.35_spmd.clone.sunk | while | flops 137893888 | bytes 4640887 | solution.py:92
  260.1 4.9 %pmax.47 = f32[1024]{0:T(1024)S(1)} all-reduce(f32[1024]{0:T(1024)S(1)} %get-tuple-element.270), channel_id=1, replica_groups=mesh['src'=2,'tgt'=16] {'src'}, use_global_device_ids=true, to_apply=%region_36.37 | all-reduce | flops 1024 | bytes 8192 | tf_op jit(solution)/shard_map/pmax | solution.py:40
  265.1 4.9 %psum.47 = f32[1024]{0:T(1024)S(1)} all-reduce(f32[1024]{0:T(1024)S(1)} %exponential_multiply_fusion.3), channel_id=1, replica_groups=mesh['src'=2,'tgt'=16] {'src'}, use_global_device_ids=true, to_apply=%region_37.38 | all-reduce | flops 1024 | bytes 8192 | tf_op jit(solution)/shard_map/psum | solution.py:41
  270.0 0.6 add_multiply_fusion.1
  (147 shorter events, 25.4 us)
Async XLA Ops:
  33.0 65.4 %copy-start = (f32[2048]{0:T(1024)S(1)}, f32[2048]{0:T(1024)}, u32[]{:S(2)}) copy-start(f32[2048]{0:T(1024)} %param.18) | copy-start | bytes 24580
  98.4 13.6 %copy-start.1 = (f32[1024]{0:T(1024)S(1)}, f32[1024]{0:T(1024)}, u32[]{:S(2)}) copy-start(f32[1024]{0:T(1024)} %param.19) | copy-start | bytes 12292
where the time goes:
time: 271 us
  blocking collectives  241 us (89%)
  matrix products  13.5 us (5%)
  other arithmetic  13 us (5%)
    pmax x3, blocking collectives, finish_rows(): widest = lax.pmax(peak, 'tgt')  90.3 us
    psum x3, blocking collectives, finish_rows(): total = lax.psum(total * jnp.exp(peak - widest), 'tgt')  90 us
    all_gather x1, blocking collectives, local(): sources = lax.all_gather(source_points, 'tgt', axis=0, tiled=True)  23.6 us
    pmax x3, blocking collectives, finish_cols(): widest = lax.pmax(peak, 'src')  14.8 us
    psum x3, blocking collectives, finish_cols(): total = lax.psum(total * jnp.exp(peak - widest), 'src')  14.8 us
    dot_general x24, matrix products, tile_cost(): jnp.dot(rows, cols.T, preferred_element_type=jnp.float32)  13.5 us
    all_gather x1, blocking collectives, local(): targets = lax.all_gather(target_points, 'src', axis=0, tiled=True)  7.39 us
    reduce_sum x12, other arithmetic, row_stats(): return (peak, jnp.sum(jnp.exp(scores - peak[:, None]), axis=1))  6.18 us

commit v1 on v0

v1 whole, which is shorter than its diff:
```python
import math

import jax
import jax.numpy as jnp
from jax import lax
from jax.experimental import pallas as pl
from jax.experimental.pallas import tpu as pltpu
from jax.sharding import Mesh, PartitionSpec as P

ITERS = 3
EPS = 0.05
SCALE = 1.0 / (EPS * math.log(2.0))
UNIT = EPS * math.log(2.0)
LANES = 128
CORES = 2
F32 = jnp.float32
VMEM = pl.BlockSpec(memory_space=pltpu.VMEM)
SMEM = pl.BlockSpec(memory_space=pltpu.SMEM)


def params(limit=24):
    return pltpu.CompilerParams(vmem_limit_bytes=limit * 1024 * 1024)


def pin(value):
    return pltpu.with_memory_space_constraint(value, pltpu.VMEM)


def rows_of(count):
    return jax.ShapeDtypeStruct((count // LANES, LANES), F32)


def diagonal():
    shape = (LANES, LANES)
    return lax.broadcasted_iota(jnp.int32, shape, 0) == lax.broadcasted_iota(jnp.int32, shape, 1)


def to_column(row, mask):
    return jnp.sum(jnp.where(mask, jnp.broadcast_to(row, mask.shape), 0.0), axis=1, keepdims=True)


def to_row(column, mask):
    return jnp.sum(jnp.where(mask, jnp.broadcast_to(column, mask.shape), 0.0), axis=0, keepdims=True)


def unfold(value):
    return jnp.concatenate([value[i : i + 1, :] for i in range(value.shape[0])], axis=1)


def fold_into(ref, value):
    for row in range(ref.shape[0]):
        ref[row : row + 1, :] = value[:, row * LANES : (row + 1) * LANES]


def tree(values, join):
    while len(values) > 1:
        values = [join(values[i], values[i + 1]) for i in range(0, len(values), 2)]
    return values[0]


def log_sum(values):
    peak = tree(values, jnp.maximum)
    return peak + jnp.log2(tree([jnp.exp2(value - peak) for value in values], jnp.add))


def product(rows, cols):
    return lax.dot_general(rows, cols, (((1,), (1,)), ((), ())), preferred_element_type=F32)


def first_rows(place, masses, sources, blocks):
    count, part = sources.shape[0], blocks[0].shape[0]
    n_blocks, n_masses = len(blocks), len(masses)
    width, chunk = n_blocks * part, masses[0].shape[0]

    def kernel(place_ref, *refs):
        mass_refs, (sources_ref, *block_refs) = refs[:n_masses], refs[n_masses : n_masses + 1 + n_blocks]
        targets_ref, mass_ref, out_ref, half_ref, scores_ref = refs[n_masses + 1 + n_blocks :]
        for step in range(n_masses):
            start = pl.multiple_of(jnp.bitwise_xor(place_ref[1], step) * chunk, chunk)
            mass_ref[pl.ds(start, chunk), :] = mass_refs[step][...]
        for step in range(n_blocks):
            src = jnp.bitwise_xor(place_ref[0], step // CORES)
            core = jnp.bitwise_xor(place_ref[1], step % CORES)
            start = pl.multiple_of((core * (n_blocks // CORES) + src) * part, part)
            targets_ref[pl.ds(start, part), :] = block_refs[step][...]
        mask = diagonal()
        peak = jnp.full((8, count), -jnp.inf, F32)
        total = jnp.zeros((8, count), F32)
        for block in range(width // LANES):
            rows = targets_ref[block * LANES : (block + 1) * LANES, :]
            scores_ref[...] = product(rows, sources_ref[...])
            values = rows.astype(F32)
            half = 0.5 * jnp.sum(values * values, axis=1, keepdims=True)
            half_ref[block : block + 1, :] = to_row(half, mask)
            offset = to_column(jnp.log2(mass_ref[block : block + 1, :]), mask) - SCALE * half
            tops = peak
            for row in range(0, LANES, 8):
                scores = scores_ref[row : row + 8, :] * SCALE + offset[row : row + 8, :]
                scores_ref[row : row + 8, :] = scores
                tops = jnp.maximum(tops, scores)
            total = total * jnp.exp2(peak - tops)
            peak = tops
            for row in range(0, LANES, 8):
                total = total + jnp.exp2(scores_ref[row : row + 8, :] - peak)
        widest = jnp.max(peak, axis=0, keepdims=True)
        fold_into(out_ref, widest + jnp.log2(jnp.sum(total * jnp.exp2(peak - widest), axis=0, keepdims=True)))

    return pl.pallas_call(
        kernel,
        out_shape=(pltpu.VMEM((width, LANES), jnp.bfloat16), rows_of(width), rows_of(count), rows_of(width)),
        in_specs=[SMEM] + [VMEM] * (n_masses + 1 + n_blocks),
        out_specs=(VMEM,) * 4,
        scratch_shapes=[pltpu.VMEM((LANES, count), F32)],
        compiler_params=params(),
        name="first_rows",
    )(place, *masses, sources, *blocks)


def first_columns(sources, targets, parts, mass):
    count, width = sources.shape[0], targets.shape[0]

    def kernel(sources_ref, targets_ref, parts_ref, mass_ref, plan_ref, peak_ref, out_ref, lse_ref):
        lse = log_sum([parts_ref[i] for i in range(parts.shape[0])])
        lse_ref[...] = lse
        shift = unfold(jnp.log2(mass_ref[...]) - lse)
        mask = diagonal()
        for block in range(width // LANES):
            at = block * LANES
            plan_ref[at : at + LANES, :] = product(targets_ref[at : at + LANES, :], sources_ref[...])
            peaks, totals = [], []
            for row in range(at, at + LANES, 8):
                scores = plan_ref[row : row + 8, :] * SCALE + shift
                peak = jnp.max(scores, axis=1, keepdims=True)
                plan = jnp.exp2(scores - peak)
                plan_ref[row : row + 8, :] = plan
                peaks.append(peak)
                totals.append(jnp.sum(plan, axis=1, keepdims=True))
            peak = jnp.concatenate(peaks, axis=0)
            total = jnp.concatenate(totals, axis=0)
            peak_ref[block : block + 1, :] = to_row(peak, mask)
            out_ref[block : block + 1, :] = to_row(peak + jnp.log2(total), mask)

    return pl.pallas_call(
        kernel,
        out_shape=(pltpu.VMEM((width, count), F32), rows_of(width), rows_of(width), rows_of(count)),
        in_specs=[VMEM] * 4,
        out_specs=(VMEM,) * 4,
        compiler_params=params(),
        name="first_columns",
    )(pin(sources), pin(targets), parts, mass)


def weighted_rows(weight, plan_ref, out_ref):
    mask = diagonal()
    total = jnp.zeros((8, plan_ref.shape[1]), F32)
    for block in range(plan_ref.shape[0] // LANES):
        column = to_column(weight[block : block + 1, :], mask)
        for row in range(0, LANES, 8):
            at = block * LANES + row
            total = total + plan_ref[at : at + 8, :] * column[row : row + 8, :]
    fold_into(out_ref, jnp.sum(total, axis=0, keepdims=True))


def second_rows(plan, peak, mass, parts):
    width, count = plan.shape

    def kernel(plan_ref, peak_ref, mass_ref, *refs):
        part_refs, (lse_ref, reach_ref, out_ref) = refs[:-3], refs[-3:]
        lse = log_sum([ref[...] for ref in part_refs])
        lse_ref[...] = lse
        reach = jnp.exp2(peak_ref[...] - lse)
        reach_ref[...] = reach
        weighted_rows(reach * mass_ref[...], plan_ref, out_ref)

    return pl.pallas_call(
        kernel,
        out_shape=(rows_of(width), rows_of(width), rows_of(count)),
        in_specs=[VMEM] * (3 + len(parts)),
        out_specs=(VMEM,) * 3,
        compiler_params=params(),
        name="second_rows",
    )(pin(plan), peak, mass, *parts)


def later_rows(plan, reach, mass, parts):
    width, count = plan.shape

    def kernel(plan_ref, reach_ref, mass_ref, *refs):
        part_refs, out_ref = refs[:-1], refs[-1]
        weighted_rows(reach_ref[...] * mass_ref[...] / tree([ref[...] for ref in part_refs], jnp.add), plan_ref, out_ref)

    return pl.pallas_call(
        kernel,
        out_shape=rows_of(count),
        in_specs=[VMEM] * (3 + len(parts)),
        out_specs=VMEM,
        compiler_params=params(),
        name="later_rows",
    )(pin(plan), reach, mass, *parts)


def later_columns(plan, reach, parts, mass, lse, half):
    width, count = plan.shape

    def kernel(plan_ref, reach_ref, parts_ref, mass_ref, lse_ref, half_ref, out_ref, potential_ref):
        mask = diagonal()
        factor = mass_ref[...] / tree([parts_ref[i] for i in range(parts.shape[0])], jnp.add)
        potential_ref[...] = half_ref[...] + UNIT * (jnp.log2(factor) - lse_ref[...])
        factor = unfold(factor)
        for block in range(width // LANES):
            totals = []
            for row in range(0, LANES, 8):
                at = block * LANES + row
                totals.append(jnp.sum(plan_ref[at : at + 8, :] * factor, axis=1, keepdims=True))
            total = to_row(jnp.concatenate(totals, axis=0), mask)
            out_ref[block : block + 1, :] = total * reach_ref[block : block + 1, :]

    return pl.pallas_call(
        kernel,
        out_shape=(rows_of(width), rows_of(count)),
        in_specs=[VMEM] * 6,
        out_specs=(VMEM,) * 2,
        compiler_params=params(),
        name="later_columns",
    )(pin(plan), reach, parts, mass, lse, half)


def levels_of(size):
    bits = size.bit_length() - 1
    out = []
    while bits > 0:
        take = 2 if bits % 2 == 0 else 1
        bits -= take
        out.append([step << bits for step in range(1, 1 << take)])
    return out


def swap(value, axes, size, distance):
    return lax.ppermute(value, axes, [(i, i ^ distance) for i in range(size)])


def swap_all(value, axes, size):
    values = [value]
    for distances in levels_of(size):
        got = {d: [swap(value, axes, size, d) for value in values] for d in reversed(distances)}
        values = [part for i in range(len(values)) for part in [values[i]] + [got[d][i] for d in distances]]
    return values


def share(value, size):
    copies = jnp.broadcast_to(value[None], (size,) + value.shape)
    return lax.all_to_all(copies, "far", 0, 0, tiled=True)


def half_norm(points):
    values = points.astype(F32)
    return 0.5 * jnp.sum(values * values, axis=1)


def make_local(n_src, n_far):
    near, n_near = ("src", "core"), n_src * CORES

    def local(source_points, target_points, source_mass, target_mass):
        core = lax.axis_index("core")
        place = jnp.stack([lax.axis_index("src"), core]).astype(jnp.int32)
        part = source_points.shape[0]
        a = source_mass.reshape(n_far, CORES, part)
        a = lax.dynamic_index_in_dim(a, core, axis=1, keepdims=False).reshape(-1, LANES)
        b = target_mass.reshape(-1, LANES)
        blocks = swap_all(target_points, near, n_near)
        masses = swap_all(b, "core", CORES)
        sources = share(source_points, n_far).reshape(-1, LANES)
        targets, b, own, half_y = first_rows(place, masses, sources, blocks)
        plan, peak, own, row_lse = first_columns(sources, targets, share(own, n_far), a)
        early, own = lax.optimization_barrier((sources, own))
        half_x = half_norm(early).reshape(-1, LANES)
        parts = swap_all(own, near, n_near)
        half_x, *parts = lax.optimization_barrier((half_x, *parts))
        col_lse, reach, rows = second_rows(plan, peak, b, parts)
        for step in range(1, ITERS):
            if step > 1:
                rows = later_rows(plan, reach, b, parts)
            own, potential = later_columns(plan, reach, share(rows, n_far), a, row_lse, half_x)
            parts = swap_all(own, near, n_near)
        mine, other = swap_all(potential.reshape(n_far, part), "core", CORES)
        low, high = jnp.where(core == 0, mine, other), jnp.where(core == 0, other, mine)
        source_potential = jnp.stack([low, high], axis=1).reshape(-1)
        target_potential = half_y - UNIT * (col_lse + jnp.log2(tree(parts, jnp.add)))
        target_potential = target_potential.reshape(CORES, -1)
        target_potential = lax.dynamic_index_in_dim(target_potential, core, axis=0, keepdims=False)
        return source_potential, target_potential

    return local


def solution(mesh):
    n_src, n_tgt = mesh.shape["src"], mesh.shape["tgt"]
    n_far = n_tgt // CORES
    split = Mesh(mesh.devices.reshape(n_src, n_far, CORES), ("src", "far", "core"))
    placed = (P(("src", "far", "core"), None), P(("far", "core", "src"), None), P("src"), P(("far", "core")))
    return jax.shard_map(
        make_local(n_src, n_far),
        mesh=split,
        in_specs=placed,
        out_specs=(P("src"), P(("far", "core"))),
        check_vma=False,
    )
```

time: 271 us -> 74.9 us (0.28)
  blocking collectives: 241 us -> 18.1 us
  starting transfers between devices: 0 us -> 20 us
  waiting for transfers between devices: 0 us -> 18.6 us
  matrix products: 13.5 us -> 0 us
  other arithmetic: 13 us -> 0.31 us
  Pallas kernels: 0 us -> 11.7 us
  local copies, waits for them, and re-layouts: 1.43 us -> 4.98 us
    pmax x6 -> x0, blocking collectives: 105 us -> none  [the longest x3 90.3 us: finish_rows(): widest = lax.pmax(peak, 'tgt')]
    psum x6 -> x0, blocking collectives: 105 us -> none  [the longest x3 90 us: finish_rows(): total = lax.psum(total * jnp.exp(peak - widest), 'tgt')]
    all_gather x2 -> x0, blocking collectives: 31 us -> none  [the longest x1 23.6 us: local(): sources = lax.all_gather(source_points, 'tgt', axis=0, tiled=True)]
    all_to_all x0 -> x2, blocking collectives: none -> 18.1 us  [share(): return lax.all_to_all(copies, 'far', 0, 0, tiled=True)]
    dot_general x24 -> x0, matrix products: 13.5 us -> none  [tile_cost(): jnp.dot(rows, cols.T, preferred_element_type=jnp.float32)]
    all_to_all x0 -> x2, starting transfers between devices: none -> 11.8 us  [share(): return lax.all_to_all(copies, 'far', 0, 0, tiled=True)]
    pallas_call x0 -> x6, Pallas kernels: none -> 11.7 us  [the longest x1 4.52 us: first_columns(): pl.pallas_call(kernel, out_shape=(pltpu.VMEM((width, count), F32), rows_o...]
    ppermute x0 -> x14, waiting for transfers between devices: none -> 10.5 us  [swap(): return lax.ppermute(value, axes, [(i, i ^ distance) for i in range(size)])]
  transfers between devices with their start and end apart: 0 -> 16, of which waited for: 0 -> 11; matrix products, arithmetic and copies ran while one was open for 0% -> 1% of each run, Pallas kernels for 0% -> 0%
where the time goes in v1:
time: 74.9 us; the launch traced here: 74.4 us
  starting transfers between devices  20 us (27%)
  waiting for transfers between devices  18.6 us (25%)
  blocking collectives  18.1 us (24%)
  Pallas kernels  11.7 us (16%)
  local copies, waits for them, and re-layouts  4.98 us (7%)
  between operations  0.76 us (1%)
    all_to_all x2, blocking collectives, share(): return lax.all_to_all(copies, 'far', 0, 0, tiled=True)  18.1 us
    all_to_all x2, starting transfers between devices, share(): return lax.all_to_all(copies, 'far', 0, 0, tiled=True)  11.8 us
    ppermute x14, waiting for transfers between devices, swap(): return lax.ppermute(value, axes, [(i, i ^ distance) for i in range(size)])  10.5 us
    ppermute x14, starting transfers between devices, swap(): return lax.ppermute(value, axes, [(i, i ^ distance) for i in range(size)])  8.14 us
    all_to_all x2, waiting for transfers between devices, share(): return lax.all_to_all(copies, 'far', 0, 0, tiled=True)  8.06 us
    pallas_call x1, Pallas kernels, first_columns(): pl.pallas_call(kernel, out_shape=(pltpu.VMEM((width, count), F32), rows_o...  4.52 us
    pallas_call x1, Pallas kernels, first_rows(): pl.pallas_call(kernel, out_shape=(pltpu.VMEM((width, LANES), jnp.bfloat16...  3.49 us
    pallas_call x2, Pallas kernels, later_columns(): pl.pallas_call(kernel, out_shape=(rows_of(width), rows_of(count)), in_spe...  2.33 us
  transfers between devices with their start and end apart: 16, of which 11 were waited for; matrix products, arithmetic and copies ran while one was open for 1% of the time, Pallas kernels for 0%

profile of v1, /device:TPU:0, one launch (start us, length us, event | category | flops | bytes accessed | tf_op | source)
XLA Modules:
  0.0 74.4 jit_solution(18267339979577826721)
XLA Ops:
  0.6 1.5 %broadcast_in_dim.8 = bf16[8,128,128]{2,1,0:T(8,128)(2,1)} broadcast(bf16[128,128]{1,0:T(8,128)(2,1)} %param.4), dimensions={1,2} | broadcast | bytes 294912 | tf_op jit(solution)/shard_map/broadcast_in_dim | solution.py:251
  2.2 7.3 %all-to-all-start = ((bf16[8,128,128]{2,1,0:T(8,128)(2,1)}), bf16[8,128,128]{2,1,0:T(8,128)(2,1)S(1)}, u32[]{:S(2)}, u32[]{:S(2)}) async-start(bf16[8,128,128]{2,1,0:T(8,128)(2,1)} %broadcast_in_dim.8), calls=%async_computation | async-start | bytes 524288 | tf_op jit(solution)/shard_map/all_to_all | solution.py:252
  9.4 1.5 %collective-permute-start.2 = (bf16[512,128]{1,0:T(8,128)(2,1)}, bf16[512,128]{1,0:T(8,128)(2,1)S(1)}, u32[]{:S(2)}, u32[]{:S(2)}) collective-permute-start(bf16[512,128]{1,0:T(8,128)(2,1)} %refs_3_.1), channel_id=1, source_target_pairs={{0,16},{1,17},{16,0},{17,1},{2,18},{3,19},{18,2},{19,3},{4,20},{5,... | collective-permute-start | bytes 393224 | tf_op jit(solution)/shard_map/ppermute | solution.py:239
  11.6 1.3 %collective-permute-done.refs_1_ = f32[8,128]{1,0:T(8,128)S(1)} collective-permute-done((f32[8,128]{1,0:T(8,128)}, f32[8,128]{1,0:T(8,128)S(1)}, u32[]{:S(2)}, u32[]{:S(2)}) %collective-permute-start) | collective-permute-done | bytes 4128 | tf_op jit(solution)/shard_map/ppermute | solution.py:239
  12.9 2.2 %collective-permute-done.2.refs_5_ = bf16[512,128]{1,0:T(8,128)(2,1)S(1)} collective-permute-done((bf16[512,128]{1,0:T(8,128)(2,1)}, bf16[512,128]{1,0:T(8,128)(2,1)S(1)}, u32[]{:S(2)}, u32[]{:S(2)}) %collective-permute-start.2) | collective-permute-done | bytes 131104 | tf_op jit(solution)/shard_map/ppermute | solution.py:239
  15.1 1.8 %collective-permute-done.3.refs_6_ = bf16[512,128]{1,0:T(8,128)(2,1)S(1)} collective-permute-done((bf16[512,128]{1,0:T(8,128)(2,1)}, bf16[512,128]{1,0:T(8,128)(2,1)S(1)}, u32[]{:S(2)}, u32[]{:S(2)}) %collective-permute-start.3) | collective-permute-done | bytes 131104 | tf_op jit(solution)/shard_map/ppermute | solution.py:239
  16.9 1.4 %all-to-all-done = bf16[8,128,128]{2,1,0:T(8,128)(2,1)S(1)} async-done(((bf16[8,128,128]{2,1,0:T(8,128)(2,1)}), bf16[8,128,128]{2,1,0:T(8,128)(2,1)S(1)}, u32[]{:S(2)}, u32[]{:S(2)}) %all-to-all-start) | async-done | bytes 262176 | tf_op jit(solution)/shard_map/all_to_all | solution.py:252
  18.3 0.9 %copy-done.1 = bf16[512,128]{1,0:T(8,128)(2,1)S(1)} copy-done((bf16[512,128]{1,0:T(8,128)(2,1)S(1)}, bf16[512,128]{1,0:T(8,128)(2,1)}, u32[]{:S(2)}) %copy-start.1) | copy-done | bytes 131096
  19.2 0.7 copy-done.2
  19.9 3.5 %first_rows.1 = (bf16[2048,128]{1,0:T(8,128)(2,1)S(1)}, f32[16,128]{1,0:T(8,128)S(1)}, f32[8,128]{1,0:T(8,128)S(1)}, f32[16,128]{1,0:T(8,128)S(1)}) custom-call(s32[2]{0:T(128)S(1)} %pad_add_fusion.place_ref, f32[8,128]{1,0:T(8,128)S(1)} %bitcast.22, f32[8,128]{1,0:T(8,128)S(1)} %collective-permute-done.refs_1_, bf16[1024,128]{1,0:T(8,128)(2,1)S(1)} %bitcast.15, ...), custom_call_target="tpu_custom_call" | custom-call | tf_op jit(solution)/shard_map/first_rows/pallas_call | solution.py:108
  24.0 4.6 %all-to-all-start.1 = ((f32[8,8,128]{2,1,0:T(8,128)}), f32[8,8,128]{2,1,0:T(8,128)S(1)}, u32[]{:S(2)}, u32[]{:S(2)}) async-start(f32[8,8,128]{2,1,0:T(8,128)} %broadcast_in_dim.9), calls=%async_computation.1 | async-start | bytes 65536 | tf_op jit(solution)/shard_map/all_to_all | solution.py:252
  28.7 6.7 %all-to-all-done.1.parts_ref = f32[8,8,128]{2,1,0:T(8,128)S(1)} async-done(((f32[8,8,128]{2,1,0:T(8,128)}), f32[8,8,128]{2,1,0:T(8,128)S(1)}, u32[]{:S(2)}, u32[]{:S(2)}) %all-to-all-start.1) | async-done | bytes 32800 | tf_op jit(solution)/shard_map/all_to_all | solution.py:252
  35.3 4.5 %first_columns.1 = (f32[2048,1024]{1,0:T(8,128)S(1)}, f32[16,128]{1,0:T(8,128)S(1)}, f32[16,128]{1,0:T(8,128)S(1)}, f32[8,128]{1,0:T(8,128)S(1)}) custom-call(bf16[1024,128]{1,0:T(8,128)(2,1)S(1)} %bitcast.16, bf16[2048,128]{1,0:T(8,128)(2,1)S(1)} %get-tuple-element.23.targets_ref, f32[8,8,128]{2,1,0:T(8,128)S(1)} %all-to-all-done.1.parts_ref, ...), custom_call_target="tpu_custom_call" | custom-call | tf_op jit(solution)/shard_map/first_columns/pallas_call | solution.py:143
  40.7 1.0 %collective-permute-start.4 = (f32[16,128]{1,0:T(8,128)S(1)}, f32[16,128]{1,0:T(8,128)S(1)}, u32[]{:S(2)}, u32[]{:S(2)}) collective-permute-start(f32[16,128]{1,0:T(8,128)S(1)} %get-tuple-element.31.refs_0_), channel_id=1, source_target_pairs={{0,1},{1,0},{16,17},{17,16},{2,3},{3,2},{18,19},{19,18},{4,5},{5,4... | collective-permute-start | bytes 24584 | tf_op jit(solution)/shard_map/ppermute | solution.py:239
  42.0 1.0 %collective-permute-done.6.refs_3_ = f32[16,128]{1,0:T(8,128)S(1)} collective-permute-done((f32[16,128]{1,0:T(8,128)S(1)}, f32[16,128]{1,0:T(8,128)S(1)}, u32[]{:S(2)}, u32[]{:S(2)}) %collective-permute-start.6) | collective-permute-done | bytes 8224 | tf_op jit(solution)/shard_map/ppermute | solution.py:239
  43.0 1.0 %collective-permute-done.5.refs_2_ = f32[16,128]{1,0:T(8,128)S(1)} collective-permute-done((f32[16,128]{1,0:T(8,128)S(1)}, f32[16,128]{1,0:T(8,128)S(1)}, u32[]{:S(2)}, u32[]{:S(2)}) %collective-permute-start.5) | collective-permute-done | bytes 8224 | tf_op jit(solution)/shard_map/ppermute | solution.py:239
  44.7 9.1 %all_to_all.20.parts_ref = f32[8,8,128]{2,1,0:T(8,128)S(1)} all-to-all(f32[8,8,128]{2,1,0:T(8,128)S(1)} %broadcast_in_dim.10), channel_id=1, replica_groups=mesh['src'=2,'far'=8,'core'=2] {'far'}, dimensions={0} | all-to-all | bytes 65536 | tf_op jit(solution)/shard_map/all_to_all | solution.py:252
  53.8 1.4 %later_columns.2 = (f32[16,128]{1,0:T(8,128)S(1)}, f32[8,128]{1,0:T(8,128)}) custom-call(f32[2048,1024]{1,0:T(8,128)S(1)} %get-tuple-element.25.plan_ref, f32[16,128]{1,0:T(8,128)S(1)} %get-tuple-element.35.reach_ref, f32[8,8,128]{2,1,0:T(8,128)S(1)} %all_to_all.20.parts_ref, f32[8,128]{1,0:T(8,128)S(1)} %bitcast.19, ...), custom_call_target="tpu_custom_call" | custom-call | tf_op jit(solution)/shard_map/later_columns/pallas_call | solution.py:218
  55.6 1.4 %collective-permute-start.7 = (f32[16,128]{1,0:T(8,128)S(1)}, f32[16,128]{1,0:T(8,128)S(1)}, u32[]{:S(2)}, u32[]{:S(2)}) collective-permute-start(f32[16,128]{1,0:T(8,128)S(1)} %get-tuple-element.39.refs_0_), channel_id=1, source_target_pairs={{0,1},{1,0},{16,17},{17,16},{2,3},{3,2},{18,19},{19,18},{4,5},{5,4... | collective-permute-start | bytes 24584 | tf_op jit(solution)/shard_map/ppermute | solution.py:239
  57.0 1.2 %collective-permute-done.9.refs_3_ = f32[16,128]{1,0:T(8,128)S(1)} collective-permute-done((f32[16,128]{1,0:T(8,128)S(1)}, f32[16,128]{1,0:T(8,128)S(1)}, u32[]{:S(2)}, u32[]{:S(2)}) %collective-permute-start.9) | collective-permute-done | bytes 8224 | tf_op jit(solution)/shard_map/ppermute | solution.py:239
  59.6 9.1 %all_to_all.21.parts_ref = f32[8,8,128]{2,1,0:T(8,128)S(1)} all-to-all(f32[8,8,128]{2,1,0:T(8,128)S(1)} %broadcast_in_dim.11), channel_id=1, replica_groups=mesh['src'=2,'far'=8,'core'=2] {'far'}, dimensions={0} | all-to-all | bytes 65536 | tf_op jit(solution)/shard_map/all_to_all | solution.py:252
  68.6 0.9 %later_columns.3 = (f32[16,128]{1,0:T(8,128)S(1)}, f32[8,128]{1,0:T(8,128)S(1)}) custom-call(f32[2048,1024]{1,0:T(8,128)S(1)} %get-tuple-element.25.plan_ref, f32[16,128]{1,0:T(8,128)S(1)} %get-tuple-element.35.reach_ref, f32[8,8,128]{2,1,0:T(8,128)S(1)} %all_to_all.21.parts_ref, f32[8,128]{1,0:T(8,128)S(1)} %bitcast.20, ...), custom_call_target="tpu_custom_call" | custom-call | tf_op jit(solution)/shard_map/later_columns/pallas_call | solution.py:218
  70.1 1.6 %collective-permute-start.12 = (f32[16,128]{1,0:T(8,128)S(1)}, f32[16,128]{1,0:T(8,128)S(1)}, u32[]{:S(2)}, u32[]{:S(2)}) collective-permute-start(f32[16,128]{1,0:T(8,128)S(1)} %get-tuple-element.43), channel_id=1, source_target_pairs={{0,16},{1,17},{16,0},{17,1},{2,18},{3,19},{18,2},{19,3},{4,20},{5,... | collective-permute-start | bytes 24584 | tf_op jit(solution)/shard_map/ppermute | solution.py:239
  72.7 1.0 %collective-permute-done.12 = f32[16,128]{1,0:T(8,128)S(1)} collective-permute-done((f32[16,128]{1,0:T(8,128)S(1)}, f32[16,128]{1,0:T(8,128)S(1)}, u32[]{:S(2)}, u32[]{:S(2)}) %collective-permute-start.12) | collective-permute-done | bytes 8224 | tf_op jit(solution)/shard_map/ppermute | solution.py:239
  (36 shorter events, 7.0 us)
Async XLA Ops:
  0.6 28.0 %copy-start = (f32[2048]{0:T(1024)S(1)}, f32[2048]{0:T(1024)}, u32[]{:S(2)}) copy-start(f32[2048]{0:T(1024)} %param.6) | copy-start | bytes 24580
  2.2 16.2 %all-to-all-start = ((bf16[8,128,128]{2,1,0:T(8,128)(2,1)}), bf16[8,128,128]{2,1,0:T(8,128)(2,1)S(1)}, u32[]{:S(2)}, u32[]{:S(2)}) async-start(bf16[8,128,128]{2,1,0:T(8,128)(2,1)} %broadcast_in_dim.8), calls=%async_computation | async-start | bytes 524288 | tf_op jit(solution)/shard_map/all_to_all | solution.py:252
  9.4 5.7 %collective-permute-start.2 = (bf16[512,128]{1,0:T(8,128)(2,1)}, bf16[512,128]{1,0:T(8,128)(2,1)S(1)}, u32[]{:S(2)}, u32[]{:S(2)}) collective-permute-start(bf16[512,128]{1,0:T(8,128)(2,1)} %refs_3_.1), channel_id=1, source_target_pairs={{0,16},{1,17},{16,0},{17,1},{2,18},{3,19},{18,2},{19,3},{4,20},{5,... | collective-permute-start | bytes 393224 | tf_op jit(solution)/shard_map/ppermute | solution.py:239
  10.9 4.2 %collective-permute-start.1 = (bf16[512,128]{1,0:T(8,128)(2,1)}, bf16[512,128]{1,0:T(8,128)(2,1)S(1)}, u32[]{:S(2)}, u32[]{:S(2)}) collective-permute-start(bf16[512,128]{1,0:T(8,128)(2,1)} %refs_3_.1), channel_id=1, source_target_pairs={{0,1},{1,0},{16,17},{17,16},{2,3},{3,2},{18,19},{19,18},{4,5},{5,4... | collective-permute-start | bytes 393224 | tf_op jit(solution)/shard_map/ppermute | solution.py:239
  10.9 6.0 %collective-permute-start.3 = (bf16[512,128]{1,0:T(8,128)(2,1)}, bf16[512,128]{1,0:T(8,128)(2,1)S(1)}, u32[]{:S(2)}, u32[]{:S(2)}) collective-permute-start(bf16[512,128]{1,0:T(8,128)(2,1)} %refs_3_.1), channel_id=1, source_target_pairs={{0,17},{1,16},{16,1},{17,0},{2,19},{3,18},{18,3},{19,2},{4,21},{5,... | collective-permute-start | bytes 393224 | tf_op jit(solution)/shard_map/ppermute | solution.py:239
  11.6 1.4 %collective-permute-start = (f32[8,128]{1,0:T(8,128)}, f32[8,128]{1,0:T(8,128)S(1)}, u32[]{:S(2)}, u32[]{:S(2)}) collective-permute-start(f32[8,128]{1,0:T(8,128)} %bitcast.21), channel_id=1, source_target_pairs={{0,1},{1,0},{2,3},{3,2},{4,5},{5,4},{6,7},{7,6},{8,9},{9,8},{10,11... | collective-permute-start | bytes 12296 | tf_op jit(solution)/shard_map/ppermute | solution.py:239
  18.3 0.9 %copy-start.1 = (bf16[512,128]{1,0:T(8,128)(2,1)S(1)}, bf16[512,128]{1,0:T(8,128)(2,1)}, u32[]{:S(2)}) copy-start(bf16[512,128]{1,0:T(8,128)(2,1)} %refs_3_.1) | copy-start | bytes 393220
  19.2 0.7 copy-start.2
  24.0 11.3 %all-to-all-start.1 = ((f32[8,8,128]{2,1,0:T(8,128)}), f32[8,8,128]{2,1,0:T(8,128)S(1)}, u32[]{:S(2)}, u32[]{:S(2)}) async-start(f32[8,8,128]{2,1,0:T(8,128)} %broadcast_in_dim.9), calls=%async_computation.1 | async-start | bytes 65536 | tf_op jit(solution)/shard_map/all_to_all | solution.py:252
  39.8 3.1 %collective-permute-start.6 = (f32[16,128]{1,0:T(8,128)S(1)}, f32[16,128]{1,0:T(8,128)S(1)}, u32[]{:S(2)}, u32[]{:S(2)}) collective-permute-start(f32[16,128]{1,0:T(8,128)S(1)} %get-tuple-element.31.refs_0_), channel_id=1, source_target_pairs={{0,17},{1,16},{16,1},{17,0},{2,19},{3,18},{18,3},{19,2},{4,21},{5,... | collective-permute-start | bytes 24584 | tf_op jit(solution)/shard_map/ppermute | solution.py:239
  40.3 3.7 %collective-permute-start.5 = (f32[16,128]{1,0:T(8,128)S(1)}, f32[16,128]{1,0:T(8,128)S(1)}, u32[]{:S(2)}, u32[]{:S(2)}) collective-permute-start(f32[16,128]{1,0:T(8,128)S(1)} %get-tuple-element.31.refs_0_), channel_id=1, source_target_pairs={{0,16},{1,17},{16,0},{17,1},{2,18},{3,19},{18,2},{19,3},{4,20},{5,... | collective-permute-start | bytes 24584 | tf_op jit(solution)/shard_map/ppermute | solution.py:239
  40.7 3.3 %collective-permute-start.4 = (f32[16,128]{1,0:T(8,128)S(1)}, f32[16,128]{1,0:T(8,128)S(1)}, u32[]{:S(2)}, u32[]{:S(2)}) collective-permute-start(f32[16,128]{1,0:T(8,128)S(1)} %get-tuple-element.31.refs_0_), channel_id=1, source_target_pairs={{0,1},{1,0},{16,17},{17,16},{2,3},{3,2},{18,19},{19,18},{4,5},{5,4... | collective-permute-start | bytes 24584 | tf_op jit(solution)/shard_map/ppermute | solution.py:239
  55.2 3.1 %collective-permute-start.9 = (f32[16,128]{1,0:T(8,128)S(1)}, f32[16,128]{1,0:T(8,128)S(1)}, u32[]{:S(2)}, u32[]{:S(2)}) collective-permute-start(f32[16,128]{1,0:T(8,128)S(1)} %get-tuple-element.39.refs_0_), channel_id=1, source_target_pairs={{0,17},{1,16},{16,1},{17,0},{2,19},{3,18},{18,3},{19,2},{4,21},{5,... | collective-permute-start | bytes 24584 | tf_op jit(solution)/shard_map/ppermute | solution.py:239
  55.2 3.7 %collective-permute-start.8 = (f32[16,128]{1,0:T(8,128)S(1)}, f32[16,128]{1,0:T(8,128)S(1)}, u32[]{:S(2)}, u32[]{:S(2)}) collective-permute-start(f32[16,128]{1,0:T(8,128)S(1)} %get-tuple-element.39.refs_0_), channel_id=1, source_target_pairs={{0,16},{1,17},{16,0},{17,1},{2,18},{3,19},{18,2},{19,3},{4,20},{5,... | collective-permute-start | bytes 24584 | tf_op jit(solution)/shard_map/ppermute | solution.py:239
  55.6 3.3 %collective-permute-start.7 = (f32[16,128]{1,0:T(8,128)S(1)}, f32[16,128]{1,0:T(8,128)S(1)}, u32[]{:S(2)}, u32[]{:S(2)}) collective-permute-start(f32[16,128]{1,0:T(8,128)S(1)} %get-tuple-element.39.refs_0_), channel_id=1, source_target_pairs={{0,1},{1,0},{16,17},{17,16},{2,3},{3,2},{18,19},{19,18},{4,5},{5,4... | collective-permute-start | bytes 24584 | tf_op jit(solution)/shard_map/ppermute | solution.py:239
  69.5 2.2 %collective-permute-start.10 = (f32[8,128]{1,0:T(8,128)S(1)}, f32[8,128]{1,0:T(8,128)S(1)}, u32[]{:S(2)}, u32[]{:S(2)}) collective-permute-start(f32[8,128]{1,0:T(8,128)S(1)} %get-tuple-element.40), channel_id=1, source_target_pairs={{0,1},{1,0},{2,3},{3,2},{4,5},{5,4},{6,7},{7,6},{8,9},{9,8},{10,11... | collective-permute-start | bytes 12296 | tf_op jit(solution)/shard_map/ppermute | solution.py:239
  69.6 3.1 %collective-permute-start.13 = (f32[16,128]{1,0:T(8,128)S(1)}, f32[16,128]{1,0:T(8,128)S(1)}, u32[]{:S(2)}, u32[]{:S(2)}) collective-permute-start(f32[16,128]{1,0:T(8,128)S(1)} %get-tuple-element.43), channel_id=1, source_target_pairs={{0,17},{1,16},{16,1},{17,0},{2,19},{3,18},{18,3},{19,2},{4,21},{5,... | collective-permute-start | bytes 24584 | tf_op jit(solution)/shard_map/ppermute | solution.py:239
  70.1 3.7 %collective-permute-start.12 = (f32[16,128]{1,0:T(8,128)S(1)}, f32[16,128]{1,0:T(8,128)S(1)}, u32[]{:S(2)}, u32[]{:S(2)}) collective-permute-start(f32[16,128]{1,0:T(8,128)S(1)} %get-tuple-element.43), channel_id=1, source_target_pairs={{0,16},{1,17},{16,0},{17,1},{2,18},{3,19},{18,2},{19,3},{4,20},{5,... | collective-permute-start | bytes 24584 | tf_op jit(solution)/shard_map/ppermute | solution.py:239
  71.7 2.0 %collective-permute-start.11 = (f32[16,128]{1,0:T(8,128)S(1)}, f32[16,128]{1,0:T(8,128)S(1)}, u32[]{:S(2)}, u32[]{:S(2)}) collective-permute-start(f32[16,128]{1,0:T(8,128)S(1)} %get-tuple-element.43), channel_id=1, source_target_pairs={{0,1},{1,0},{16,17},{17,16},{2,3},{3,2},{18,19},{19,18},{4,5},{5,4... | collective-permute-start | bytes 24584 | tf_op jit(solution)/shard_map/ppermute | solution.py:239

commit v2 on v1

--- a/solution.py
+++ b/solution.py
@@ -68,20 +68,25 @@
 
 
 def first_rows(place, masses, sources, blocks):
-    count, part = sources.shape[0], blocks[0].shape[0]
-    n_blocks, n_masses = len(blocks), len(masses)
-    width, chunk = n_blocks * part, masses[0].shape[0]
+    n_masses, n_sources, n_blocks = len(masses), len(sources), len(blocks)
+    group, part, chunk = sources[0].shape[0], blocks[0].shape[0], masses[0].shape[0]
+    count, width = n_sources * group, n_blocks * part
+    n_in = n_masses + n_sources + n_blocks
 
     def kernel(place_ref, *refs):
-        mass_refs, (sources_ref, *block_refs) = refs[:n_masses], refs[n_masses : n_masses + 1 + n_blocks]
-        targets_ref, mass_ref, out_ref, half_ref, scores_ref = refs[n_masses + 1 + n_blocks :]
+        mass_refs, source_refs = refs[:n_masses], refs[n_masses : n_masses + n_sources]
+        block_refs = refs[n_masses + n_sources : n_in]
+        sources_ref, targets_ref, mass_ref, out_ref, half_ref, scores_ref = refs[n_in:]
+        for step in range(n_sources):
+            start = pl.multiple_of(jnp.bitwise_xor(place_ref[2], step) * group, group)
+            sources_ref[pl.ds(start, group), :] = source_refs[step][...]
         for step in range(n_masses):
             start = pl.multiple_of(jnp.bitwise_xor(place_ref[1], step) * chunk, chunk)
             mass_ref[pl.ds(start, chunk), :] = mass_refs[step][...]
         for step in range(n_blocks):
             src = jnp.bitwise_xor(place_ref[0], step // CORES)
-            core = jnp.bitwise_xor(place_ref[1], step % CORES)
-            start = pl.multiple_of((core * (n_blocks // CORES) + src) * part, part)
+            low = jnp.bitwise_xor(place_ref[1], step % 2)
+            start = pl.multiple_of((low * (n_blocks // 2) + src) * part, part)
             targets_ref[pl.ds(start, part), :] = block_refs[step][...]
         mask = diagonal()
         peak = jnp.full((8, count), -jnp.inf, F32)
@@ -107,20 +112,27 @@
 
     return pl.pallas_call(
         kernel,
-        out_shape=(pltpu.VMEM((width, LANES), jnp.bfloat16), rows_of(width), rows_of(count), rows_of(width)),
-        in_specs=[SMEM] + [VMEM] * (n_masses + 1 + n_blocks),
-        out_specs=(VMEM,) * 4,
+        out_shape=(
+            pltpu.VMEM((count, LANES), jnp.bfloat16),
+            pltpu.VMEM((width, LANES), jnp.bfloat16),
+            rows_of(width),
+            rows_of(count),
+            rows_of(width),
+        ),
+        in_specs=[SMEM] + [VMEM] * n_in,
+        out_specs=(VMEM,) * 5,
         scratch_shapes=[pltpu.VMEM((LANES, count), F32)],
         compiler_params=params(),
         name="first_rows",
-    )(place, *masses, sources, *blocks)
+    )(place, *masses, *sources, *blocks)
 
 
 def first_columns(sources, targets, parts, mass):
     count, width = sources.shape[0], targets.shape[0]
 
-    def kernel(sources_ref, targets_ref, parts_ref, mass_ref, plan_ref, peak_ref, out_ref, lse_ref):
-        lse = log_sum([parts_ref[i] for i in range(parts.shape[0])])
+    def kernel(sources_ref, targets_ref, mass_ref, *refs):
+        part_refs, (plan_ref, peak_ref, out_ref, lse_ref) = refs[:-4], refs[-4:]
+        lse = log_sum([ref[...] for ref in part_refs])
         lse_ref[...] = lse
         shift = unfold(jnp.log2(mass_ref[...]) - lse)
         mask = diagonal()
@@ -143,11 +155,11 @@
     return pl.pallas_call(
         kernel,
         out_shape=(pltpu.VMEM((width, count), F32), rows_of(width), rows_of(width), rows_of(count)),
-        in_specs=[VMEM] * 4,
+        in_specs=[VMEM] * (3 + len(parts)),
         out_specs=(VMEM,) * 4,
         compiler_params=params(),
         name="first_columns",
-    )(pin(sources), pin(targets), parts, mass)
+    )(pin(sources), pin(targets), mass, *parts)
 
 
 def weighted_rows(weight, plan_ref, out_ref):
@@ -184,10 +196,12 @@
 
 def later_rows(plan, reach, mass, parts):
     width, count = plan.shape
+    rows = width // LANES
 
     def kernel(plan_ref, reach_ref, mass_ref, *refs):
         part_refs, out_ref = refs[:-1], refs[-1]
-        weighted_rows(reach_ref[...] * mass_ref[...] / tree([ref[...] for ref in part_refs], jnp.add), plan_ref, out_ref)
+        total = tree([ref[:rows, :] for ref in part_refs], jnp.add)
+        weighted_rows(reach_ref[...] * mass_ref[...] / total, plan_ref, out_ref)
 
     return pl.pallas_call(
         kernel,
@@ -202,10 +216,11 @@
 def later_columns(plan, reach, parts, mass, lse, half):
     width, count = plan.shape
 
-    def kernel(plan_ref, reach_ref, parts_ref, mass_ref, lse_ref, half_ref, out_ref, potential_ref):
+    def kernel(plan_ref, reach_ref, mass_ref, lse_ref, half_ref, *refs):
+        part_refs, out_ref = refs[:-1], refs[-1]
         mask = diagonal()
-        factor = mass_ref[...] / tree([parts_ref[i] for i in range(parts.shape[0])], jnp.add)
-        potential_ref[...] = half_ref[...] + UNIT * (jnp.log2(factor) - lse_ref[...])
+        factor = mass_ref[...] / tree([ref[...] for ref in part_refs], jnp.add)
+        out_ref[width // LANES :, :] = half_ref[...] + UNIT * (jnp.log2(factor) - lse_ref[...])
         factor = unfold(factor)
         for block in range(width // LANES):
             totals = []
@@ -217,12 +232,12 @@
 
     return pl.pallas_call(
         kernel,
-        out_shape=(rows_of(width), rows_of(count)),
-        in_specs=[VMEM] * 6,
-        out_specs=(VMEM,) * 2,
+        out_shape=rows_of(width + count),
+        in_specs=[VMEM] * (5 + len(parts)),
+        out_specs=VMEM,
         compiler_params=params(),
         name="later_columns",
-    )(pin(plan), reach, parts, mass, lse, half)
+    )(pin(plan), reach, mass, lse, half, *parts)
 
 
 def levels_of(size):
@@ -247,31 +262,33 @@
     return values
 
 
-def share(value, size):
-    copies = jnp.broadcast_to(value[None], (size,) + value.shape)
-    return lax.all_to_all(copies, "far", 0, 0, tiled=True)
-
-
 def half_norm(points):
     values = points.astype(F32)
     return 0.5 * jnp.sum(values * values, axis=1)
 
 
-def make_local(n_src, n_far):
-    near, n_near = ("src", "core"), n_src * CORES
+def make_local(n_src, n_high, n_x):
+    near, n_near = ("src", "low"), n_src * 2
+    far, n_far = ("high", "x"), n_high * n_x
+
+    def swap_rows(rows, join):
+        mine, other = swap_all(rows, "core", CORES)
+        return swap_all(join(mine, other), far, n_far)
 
     def local(source_points, target_points, source_mass, target_mass):
-        core = lax.axis_index("core")
-        place = jnp.stack([lax.axis_index("src"), core]).astype(jnp.int32)
+        low, core = lax.axis_index("low"), lax.axis_index("core")
+        index = lax.axis_index(far) * CORES + core
+        place = jnp.stack([lax.axis_index("src"), low, index]).astype(jnp.int32)
         part = source_points.shape[0]
-        a = source_mass.reshape(n_far, CORES, part)
-        a = lax.dynamic_index_in_dim(a, core, axis=1, keepdims=False).reshape(-1, LANES)
-        b = target_mass.reshape(-1, LANES)
+        a = source_mass.reshape(n_high, 2, -1)
+        a = lax.dynamic_index_in_dim(a, low, axis=1, keepdims=False).reshape(-1, LANES)
         blocks = swap_all(target_points, near, n_near)
-        masses = swap_all(b, "core", CORES)
-        sources = share(source_points, n_far).reshape(-1, LANES)
-        targets, b, own, half_y = first_rows(place, masses, sources, blocks)
-        plan, peak, own, row_lse = first_columns(sources, targets, share(own, n_far), a)
+        sources = swap_all(source_points, far, n_far)
+        masses = swap_all(target_mass.reshape(-1, LANES), "low", 2)
+        sources = [block for pair in [swap_all(block, "core", CORES) for block in sources] for block in pair]
+        sources, targets, b, own, half_y = first_rows(place, masses, sources, blocks)
+        parts = swap_rows(own, lambda *pair: log_sum(list(pair)))
+        plan, peak, own, row_lse = first_columns(sources, targets, parts, a)
         early, own = lax.optimization_barrier((sources, own))
         half_x = half_norm(early).reshape(-1, LANES)
         parts = swap_all(own, near, n_near)
@@ -280,14 +297,15 @@
         for step in range(1, ITERS):
             if step > 1:
                 rows = later_rows(plan, reach, b, parts)
-            own, potential = later_columns(plan, reach, share(rows, n_far), a, row_lse, half_x)
+            own = later_columns(plan, reach, swap_rows(rows, jnp.add), a, row_lse, half_x)
             parts = swap_all(own, near, n_near)
-        mine, other = swap_all(potential.reshape(n_far, part), "core", CORES)
-        low, high = jnp.where(core == 0, mine, other), jnp.where(core == 0, other, mine)
-        source_potential = jnp.stack([low, high], axis=1).reshape(-1)
-        target_potential = half_y - UNIT * (col_lse + jnp.log2(tree(parts, jnp.add)))
-        target_potential = target_potential.reshape(CORES, -1)
-        target_potential = lax.dynamic_index_in_dim(target_potential, core, axis=0, keepdims=False)
+        rows = col_lse.shape[0]
+        mine, other = [value[rows:].reshape(n_high, -1) for value in parts[:2]]
+        first, second = jnp.where(low == 0, mine, other), jnp.where(low == 0, other, mine)
+        source_potential = jnp.stack([first, second], axis=1).reshape(-1)
+        total = tree([value[:rows] for value in parts], jnp.add)
+        target_potential = (half_y - UNIT * (col_lse + jnp.log2(total))).reshape(2, -1)
+        target_potential = lax.dynamic_index_in_dim(target_potential, low, axis=0, keepdims=False)
         return source_potential, target_potential
 
     return local
@@ -295,13 +313,14 @@
 
 def solution(mesh):
     n_src, n_tgt = mesh.shape["src"], mesh.shape["tgt"]
-    n_far = n_tgt // CORES
-    split = Mesh(mesh.devices.reshape(n_src, n_far, CORES), ("src", "far", "core"))
-    placed = (P(("src", "far", "core"), None), P(("far", "core", "src"), None), P("src"), P(("far", "core")))
+    n_high, n_x = 2, n_tgt // (4 * CORES)
+    split = Mesh(mesh.devices.reshape(n_src, n_high, 2, n_x, CORES), ("src", "high", "low", "x", "core"))
+    tgt = ("high", "low", "x", "core")
+    placed = (P(("src", *tgt), None), P((*tgt, "src"), None), P("src"), P(tgt))
     return jax.shard_map(
-        make_local(n_src, n_far),
+        make_local(n_src, n_high, n_x),
         mesh=split,
         in_specs=placed,
-        out_specs=(P("src"), P(("far", "core"))),
+        out_specs=(P("src"), P(tgt)),
         check_vma=False,
     )

time: 74.9 us -> 79.4 us (1.060)
  blocking collectives: 18.1 us -> 0 us
  starting transfers between devices: 20 us -> 35.3 us
  waiting for transfers between devices: 18.6 us -> 27.3 us
    ppermute x14 -> x32, starting transfers between devices: 8.14 us -> 35.3 us  [swap(): return lax.ppermute(value, axes, [(i, i ^ distance) for i in range(size)])]
    all_to_all x2 -> x0, blocking collectives: 18.1 us -> none  [share(): return lax.all_to_all(copies, 'far', 0, 0, tiled=True)]
    ppermute x14 -> x32, waiting for transfers between devices: 10.5 us -> 27.3 us  [swap(): return lax.ppermute(value, axes, [(i, i ^ distance) for i in range(size)])]
    all_to_all x2 -> x0, starting transfers between devices: 11.8 us -> none  [share(): return lax.all_to_all(copies, 'far', 0, 0, tiled=True)]
    all_to_all x2 -> x0, waiting for transfers between devices: 8.06 us -> none  [share(): return lax.all_to_all(copies, 'far', 0, 0, tiled=True)]
    broadcast_in_dim x4 -> x0, local copies, waits for them, and re-layouts: 2.15 us -> none  [share(): copies = jnp.broadcast_to(value[None], (size,) + value.shape)]
    unnamed x6 -> x7, local copies, waits for them, and re-layouts: 1.6 us -> 2.95 us
  transfers between devices with their start and end apart: 16 -> 32, of which waited for: 11 -> 25; matrix products, arithmetic and copies ran while one was open for 1% -> 2% of each run, Pallas kernels for 0% -> 0%
where the time goes in v2:
time: 79.4 us; the launch traced here: 79.1 us
  starting transfers between devices  35.3 us (44%)
  waiting for transfers between devices  27.3 us (34%)
  Pallas kernels  11.1 us (14%)
  local copies, waits for them, and re-layouts  4.28 us (5%)
    ppermute x32, starting transfers between devices, swap(): return lax.ppermute(value, axes, [(i, i ^ distance) for i in range(size)])  35.3 us
    ppermute x32, waiting for transfers between devices, swap(): return lax.ppermute(value, axes, [(i, i ^ distance) for i in range(size)])  27.3 us
    pallas_call x1, Pallas kernels, first_columns(): pl.pallas_call(kernel, out_shape=(pltpu.VMEM((width, count), F32), rows_o...  4.51 us
    pallas_call x1, Pallas kernels, first_rows(): pl.pallas_call(kernel, out_shape=(pltpu.VMEM((count, LANES), jnp.bfloat16...  3.43 us
    unnamed x7, local copies, waits for them, and re-layouts  2.95 us
    pallas_call x2, Pallas kernels, later_columns(): pl.pallas_call(kernel, out_shape=rows_of(width + count), in_specs=[VMEM]...  1.8 us
  transfers between devices with their start and end apart: 32, of which 25 were waited for; matrix products, arithmetic and copies ran while one was open for 2% of the time, Pallas kernels for 0%

profile of v2, /device:TPU:0, one launch (start us, length us, event | category | flops | bytes accessed | tf_op | source)
XLA Modules:
  0.0 79.1 jit_solution(3898480367147487952)
XLA Ops:
  0.6 4.1 %collective-permute-start.4 = (bf16[128,128]{1,0:T(8,128)(2,1)}, bf16[128,128]{1,0:T(8,128)(2,1)S(1)}, u32[]{:S(2)}, u32[]{:S(2)}) collective-permute-start(bf16[128,128]{1,0:T(8,128)(2,1)} %refs_2_.1), channel_id=1, source_target_pairs={{0,8},{2,10},{8,0},{10,2},{1,9},{3,11},{9,1},{11,3},{4,12},{6,14},... | collective-permute-start | bytes 98312 | tf_op jit(solution)/shard_map/ppermute | solution.py:254
  4.7 1.5 %collective-permute-start.2 = (bf16[128,128]{1,0:T(8,128)(2,1)}, bf16[128,128]{1,0:T(8,128)(2,1)S(1)}, u32[]{:S(2)}, u32[]{:S(2)}) collective-permute-start(bf16[128,128]{1,0:T(8,128)(2,1)} %refs_2_.1), channel_id=1, source_target_pairs={{0,2},{2,0},{8,10},{10,8},{1,3},{3,1},{9,11},{11,9},{4,6},{6,4},{1... | collective-permute-start | bytes 98312 | tf_op jit(solution)/shard_map/ppermute | solution.py:254
  7.2 1.6 %collective-permute-start = (f32[8,128]{1,0:T(8,128)}, f32[8,128]{1,0:T(8,128)S(1)}, u32[]{:S(2)}, u32[]{:S(2)}) collective-permute-start(f32[8,128]{1,0:T(8,128)} %bitcast.16), channel_id=1, source_target_pairs={{0,4},{4,0},{1,5},{5,1},{2,6},{6,2},{3,7},{7,3},{8,12},{12,8},{9,1... | collective-permute-start | bytes 12296 | tf_op jit(solution)/shard_map/ppermute | solution.py:254
  8.7 2.5 %collective-permute-done.refs_1_ = f32[8,128]{1,0:T(8,128)S(1)} collective-permute-done((f32[8,128]{1,0:T(8,128)}, f32[8,128]{1,0:T(8,128)S(1)}, u32[]{:S(2)}, u32[]{:S(2)}) %collective-permute-start) | collective-permute-done | bytes 4128 | tf_op jit(solution)/shard_map/ppermute | solution.py:254
  11.3 1.5 %collective-permute-start.9 = (bf16[512,128]{1,0:T(8,128)(2,1)}, bf16[512,128]{1,0:T(8,128)(2,1)S(1)}, u32[]{:S(2)}, u32[]{:S(2)}) collective-permute-start(bf16[512,128]{1,0:T(8,128)(2,1)} %refs_10_.1), channel_id=1, source_target_pairs={{0,16},{4,20},{16,0},{20,4},{1,17},{5,21},{17,1},{21,5},{2,18},{6,... | collective-permute-start | bytes 393224 | tf_op jit(solution)/shard_map/ppermute | solution.py:254
  12.8 1.3 %collective-permute-start.8 = (bf16[512,128]{1,0:T(8,128)(2,1)}, bf16[512,128]{1,0:T(8,128)(2,1)S(1)}, u32[]{:S(2)}, u32[]{:S(2)}) collective-permute-start(bf16[512,128]{1,0:T(8,128)(2,1)} %refs_10_.1), channel_id=1, source_target_pairs={{0,4},{4,0},{16,20},{20,16},{1,5},{5,1},{17,21},{21,17},{2,6},{6,2... | collective-permute-start | bytes 393224 | tf_op jit(solution)/shard_map/ppermute | solution.py:254
  16.4 2.4 %collective-permute-done.8.refs_11_ = bf16[512,128]{1,0:T(8,128)(2,1)S(1)} collective-permute-done((bf16[512,128]{1,0:T(8,128)(2,1)}, bf16[512,128]{1,0:T(8,128)(2,1)S(1)}, u32[]{:S(2)}, u32[]{:S(2)}) %collective-permute-start.8) | collective-permute-done | bytes 131104 | tf_op jit(solution)/shard_map/ppermute | solution.py:254
  18.9 1.8 %collective-permute-done.10.refs_13_ = bf16[512,128]{1,0:T(8,128)(2,1)S(1)} collective-permute-done((bf16[512,128]{1,0:T(8,128)(2,1)}, bf16[512,128]{1,0:T(8,128)(2,1)S(1)}, u32[]{:S(2)}, u32[]{:S(2)}) %collective-permute-start.10) | collective-permute-done | bytes 131104 | tf_op jit(solution)/shard_map/ppermute | solution.py:254
  23.1 3.4 %first_rows.1 = (bf16[1024,128]{1,0:T(8,128)(2,1)S(1)}, bf16[2048,128]{1,0:T(8,128)(2,1)S(1)}, f32[16,128]{1,0:T(8,128)S(1)}, f32[8,128]{1,0:T(8,128)S(1)}, f32[16,128]{1,0:T(8,128)S(1)}) custom-call(s32[3]{0:T(128)S(1)} %pad_add_fusion.place_ref, f32[8,128]{1,0:T(8,128)S(1)} %bitcast.17, f32[8,128]{1,0:T(8,128)S(1)} %collective-permute-done.refs_1_, ...), custom_call_target="tpu_custom_call" | custom-call | tf_op jit(solution)/shard_map/first_rows/pallas_call | solution.py:113
  27.8 3.3 %collective-permute-start.14 = (f32[8,128]{1,0:T(8,128)S(1)}, f32[8,128]{1,0:T(8,128)S(1)}, u32[]{:S(2)}, u32[]{:S(2)}) collective-permute-start(f32[8,128]{1,0:T(8,128)S(1)} %multiply_add_fusion.refs_0_), channel_id=1, source_target_pairs={{0,10},{2,8},{8,2},{10,0},{1,11},{3,9},{9,3},{11,1},{4,14},{6,12},... | collective-permute-start | bytes 12296 | tf_op jit(solution)/shard_map/ppermute | solution.py:254
  33.2 2.4 %collective-permute-done.13.refs_2_ = f32[8,128]{1,0:T(8,128)S(1)} collective-permute-done((f32[8,128]{1,0:T(8,128)S(1)}, f32[8,128]{1,0:T(8,128)S(1)}, u32[]{:S(2)}, u32[]{:S(2)}) %collective-permute-start.13) | collective-permute-done | bytes 4128 | tf_op jit(solution)/shard_map/ppermute | solution.py:254
  35.6 4.5 %first_columns.1 = (f32[2048,1024]{1,0:T(8,128)S(1)}, f32[16,128]{1,0:T(8,128)S(1)}, f32[16,128]{1,0:T(8,128)S(1)}, f32[8,128]{1,0:T(8,128)S(1)}) custom-call(bf16[1024,128]{1,0:T(8,128)(2,1)S(1)} %get-tuple-element.28.sources_ref, bf16[2048,128]{1,0:T(8,128)(2,1)S(1)} %get-tuple-element.22.targets_ref, f32[8,128]{1,0:T(8,128)S(1)} %bitcast.13, ...), custom_call_target="tpu_custom_call" | custom-call | tf_op jit(solution)/shard_map/first_columns/pallas_call | solution.py:155
  40.1 2.3 %collective-permute-start.17 = (f32[16,128]{1,0:T(8,128)S(1)}, f32[16,128]{1,0:T(8,128)S(1)}, u32[]{:S(2)}, u32[]{:S(2)}) collective-permute-start(f32[16,128]{1,0:T(8,128)S(1)} %get-tuple-element.30.refs_0_), channel_id=1, source_target_pairs={{0,20},{4,16},{16,4},{20,0},{1,21},{5,17},{17,5},{21,1},{2,22},{6,... | collective-permute-start | bytes 24584 | tf_op jit(solution)/shard_map/ppermute | solution.py:254
  44.8 1.3 %collective-permute-done.16.refs_2_ = f32[16,128]{1,0:T(8,128)S(1)} collective-permute-done((f32[16,128]{1,0:T(8,128)S(1)}, f32[16,128]{1,0:T(8,128)S(1)}, u32[]{:S(2)}, u32[]{:S(2)}) %collective-permute-start.16) | collective-permute-done | bytes 8224 | tf_op jit(solution)/shard_map/ppermute | solution.py:254
  48.5 2.0 %collective-permute-start.21 = (f32[8,128]{1,0:T(8,128)S(1)}, f32[8,128]{1,0:T(8,128)S(1)}, u32[]{:S(2)}, u32[]{:S(2)}) collective-permute-start(f32[8,128]{1,0:T(8,128)S(1)} %add.41.refs_0_), channel_id=1, source_target_pairs={{0,10},{2,8},{8,2},{10,0},{1,11},{3,9},{9,3},{11,1},{4,14},{6,12},... | collective-permute-start | bytes 12296 | tf_op jit(solution)/shard_map/ppermute | solution.py:254
  51.4 1.5 %collective-permute-start.19 = (f32[8,128]{1,0:T(8,128)S(1)}, f32[8,128]{1,0:T(8,128)S(1)}, u32[]{:S(2)}, u32[]{:S(2)}) collective-permute-start(f32[8,128]{1,0:T(8,128)S(1)} %add.41.refs_0_), channel_id=1, source_target_pairs={{0,2},{2,0},{8,10},{10,8},{1,3},{3,1},{9,11},{11,9},{4,6},{6,4},{1... | collective-permute-start | bytes 12296 | tf_op jit(solution)/shard_map/ppermute | solution.py:254
  55.9 1.3 %collective-permute-start.24 = (f32[24,128]{1,0:T(8,128)S(1)}, f32[24,128]{1,0:T(8,128)S(1)}, u32[]{:S(2)}, u32[]{:S(2)}) collective-permute-start(f32[24,128]{1,0:T(8,128)S(1)} %later_columns.2.refs_0_), channel_id=1, source_target_pairs={{0,20},{4,16},{16,4},{20,0},{1,21},{5,17},{17,5},{21,1},{2,22},{6,... | collective-permute-start | bytes 36872 | tf_op jit(solution)/shard_map/ppermute | solution.py:254
  58.2 1.3 %collective-permute-start.22 = (f32[24,128]{1,0:T(8,128)S(1)}, f32[24,128]{1,0:T(8,128)S(1)}, u32[]{:S(2)}, u32[]{:S(2)}) collective-permute-start(f32[24,128]{1,0:T(8,128)S(1)} %later_columns.2.refs_0_), channel_id=1, source_target_pairs={{0,4},{4,0},{16,20},{20,16},{1,5},{5,1},{17,21},{21,17},{2,6},{6,2... | collective-permute-start | bytes 36872 | tf_op jit(solution)/shard_map/ppermute | solution.py:254
  62.6 1.2 %collective-permute-done.25 = f32[8,128]{1,0:T(8,128)S(1)} collective-permute-done((f32[8,128]{1,0:T(8,128)S(1)}, f32[8,128]{1,0:T(8,128)S(1)}, u32[]{:S(2)}, u32[]{:S(2)}) %collective-permute-start.25) | collective-permute-done | bytes 4128 | tf_op jit(solution)/shard_map/ppermute | solution.py:254
  63.8 2.9 %collective-permute-start.28 = (f32[8,128]{1,0:T(8,128)S(1)}, f32[8,128]{1,0:T(8,128)S(1)}, u32[]{:S(2)}, u32[]{:S(2)}) collective-permute-start(f32[8,128]{1,0:T(8,128)S(1)} %add.42.refs_0_), channel_id=1, source_target_pairs={{0,10},{2,8},{8,2},{10,0},{1,11},{3,9},{9,3},{11,1},{4,14},{6,12},... | collective-permute-start | bytes 12296 | tf_op jit(solution)/shard_map/ppermute | solution.py:254
  69.2 2.0 %collective-permute-done.27.refs_2_ = f32[8,128]{1,0:T(8,128)S(1)} collective-permute-done((f32[8,128]{1,0:T(8,128)S(1)}, f32[8,128]{1,0:T(8,128)S(1)}, u32[]{:S(2)}, u32[]{:S(2)}) %collective-permute-start.27) | collective-permute-done | bytes 4128 | tf_op jit(solution)/shard_map/ppermute | solution.py:254
  72.1 1.4 %collective-permute-start.29 = (f32[24,128]{1,0:T(8,128)S(1)}, f32[24,128]{1,0:T(8,128)S(1)}, u32[]{:S(2)}, u32[]{:S(2)}) collective-permute-start(f32[24,128]{1,0:T(8,128)S(1)} %later_columns.3), channel_id=1, source_target_pairs={{0,4},{4,0},{16,20},{20,16},{1,5},{5,1},{17,21},{21,17},{2,6},{6,2... | collective-permute-start | bytes 36872 | tf_op jit(solution)/shard_map/ppermute | solution.py:254
  73.5 1.3 %collective-permute-start.31 = (f32[24,128]{1,0:T(8,128)S(1)}, f32[24,128]{1,0:T(8,128)S(1)}, u32[]{:S(2)}, u32[]{:S(2)}) collective-permute-start(f32[24,128]{1,0:T(8,128)S(1)} %later_columns.3), channel_id=1, source_target_pairs={{0,20},{4,16},{16,4},{20,0},{1,21},{5,17},{17,5},{21,1},{2,22},{6,... | collective-permute-start | bytes 36872 | tf_op jit(solution)/shard_map/ppermute | solution.py:254
  76.5 1.6 %collective-permute-done.31 = f32[24,128]{1,0:T(8,128)S(1)} collective-permute-done((f32[24,128]{1,0:T(8,128)S(1)}, f32[24,128]{1,0:T(8,128)S(1)}, u32[]{:S(2)}, u32[]{:S(2)}) %collective-permute-start.31) | collective-permute-done | bytes 12320 | tf_op jit(solution)/shard_map/ppermute | solution.py:254
  (66 shorter events, 27.8 us)
Async XLA Ops:
  0.6 6.6 %collective-permute-start.4 = (bf16[128,128]{1,0:T(8,128)(2,1)}, bf16[128,128]{1,0:T(8,128)(2,1)S(1)}, u32[]{:S(2)}, u32[]{:S(2)}) collective-permute-start(bf16[128,128]{1,0:T(8,128)(2,1)} %refs_2_.1), channel_id=1, source_target_pairs={{0,8},{2,10},{8,0},{10,2},{1,9},{3,11},{9,1},{11,3},{4,12},{6,14},... | collective-permute-start | bytes 98312 | tf_op jit(solution)/shard_map/ppermute | solution.py:254
  4.7 8.1 %collective-permute-start.2 = (bf16[128,128]{1,0:T(8,128)(2,1)}, bf16[128,128]{1,0:T(8,128)(2,1)S(1)}, u32[]{:S(2)}, u32[]{:S(2)}) collective-permute-start(bf16[128,128]{1,0:T(8,128)(2,1)} %refs_2_.1), channel_id=1, source_target_pairs={{0,2},{2,0},{8,10},{10,8},{1,3},{3,1},{9,11},{11,9},{4,6},{6,4},{1... | collective-permute-start | bytes 98312 | tf_op jit(solution)/shard_map/ppermute | solution.py:254
  6.2 7.9 %collective-permute-start.1 = (bf16[128,128]{1,0:T(8,128)(2,1)}, bf16[128,128]{1,0:T(8,128)(2,1)S(1)}, u32[]{:S(2)}, u32[]{:S(2)}) collective-permute-start(bf16[128,128]{1,0:T(8,128)(2,1)} %refs_2_.1), channel_id=1, source_target_pairs={{0,1},{1,0},{2,3},{3,2},{4,5},{5,4},{6,7},{7,6},{8,9},{9,8},{10,11... | collective-permute-start | bytes 98312 | tf_op jit(solution)/shard_map/ppermute | solution.py:254
  6.2 8.5 %collective-permute-start.6 = (bf16[128,128]{1,0:T(8,128)(2,1)}, bf16[128,128]{1,0:T(8,128)(2,1)S(1)}, u32[]{:S(2)}, u32[]{:S(2)}) collective-permute-start(bf16[128,128]{1,0:T(8,128)(2,1)} %refs_2_.1), channel_id=1, source_target_pairs={{0,10},{2,8},{8,2},{10,0},{1,11},{3,9},{9,3},{11,1},{4,14},{6,12},... | collective-permute-start | bytes 98312 | tf_op jit(solution)/shard_map/ppermute | solution.py:254
  7.2 7.6 %collective-permute-start.5 = (bf16[128,128]{1,0:T(8,128)(2,1)S(1)}, bf16[128,128]{1,0:T(8,128)(2,1)S(1)}, u32[]{:S(2)}, u32[]{:S(2)}) collective-permute-start(bf16[128,128]{1,0:T(8,128)(2,1)S(1)} %collective-permute-done.4.refs_6_), channel_id=1, source_target_pairs={{0,1},{1,0},{2,3},{3,2},{4,5},{5,4},{6,7},{7,6},{8,9},{9,8},{10,11... | collective-permute-start | bytes 98312 | tf_op jit(solution)/shard_map/ppermute | solution.py:254
  7.2 4.1 %collective-permute-start = (f32[8,128]{1,0:T(8,128)}, f32[8,128]{1,0:T(8,128)S(1)}, u32[]{:S(2)}, u32[]{:S(2)}) collective-permute-start(f32[8,128]{1,0:T(8,128)} %bitcast.16), channel_id=1, source_target_pairs={{0,4},{4,0},{1,5},{5,1},{2,6},{6,2},{3,7},{7,3},{8,12},{12,8},{9,1... | collective-permute-start | bytes 12296 | tf_op jit(solution)/shard_map/ppermute | solution.py:254
  11.3 5.2 %collective-permute-start.9 = (bf16[512,128]{1,0:T(8,128)(2,1)}, bf16[512,128]{1,0:T(8,128)(2,1)S(1)}, u32[]{:S(2)}, u32[]{:S(2)}) collective-permute-start(bf16[512,128]{1,0:T(8,128)(2,1)} %refs_10_.1), channel_id=1, source_target_pairs={{0,16},{4,20},{16,0},{20,4},{1,17},{5,21},{17,1},{21,5},{2,18},{6,... | collective-permute-start | bytes 393224 | tf_op jit(solution)/shard_map/ppermute | solution.py:254
  12.8 6.1 %collective-permute-start.8 = (bf16[512,128]{1,0:T(8,128)(2,1)}, bf16[512,128]{1,0:T(8,128)(2,1)S(1)}, u32[]{:S(2)}, u32[]{:S(2)}) collective-permute-start(bf16[512,128]{1,0:T(8,128)(2,1)} %refs_10_.1), channel_id=1, source_target_pairs={{0,4},{4,0},{16,20},{20,16},{1,5},{5,1},{17,21},{21,17},{2,6},{6,2... | collective-permute-start | bytes 393224 | tf_op jit(solution)/shard_map/ppermute | solution.py:254
  14.1 6.6 %collective-permute-start.10 = (bf16[512,128]{1,0:T(8,128)(2,1)}, bf16[512,128]{1,0:T(8,128)(2,1)S(1)}, u32[]{:S(2)}, u32[]{:S(2)}) collective-permute-start(bf16[512,128]{1,0:T(8,128)(2,1)} %refs_10_.1), channel_id=1, source_target_pairs={{0,20},{4,16},{16,4},{20,0},{1,21},{5,17},{17,5},{21,1},{2,22},{6,... | collective-permute-start | bytes 393224 | tf_op jit(solution)/shard_map/ppermute | solution.py:254
  27.8 5.5 %collective-permute-start.14 = (f32[8,128]{1,0:T(8,128)S(1)}, f32[8,128]{1,0:T(8,128)S(1)}, u32[]{:S(2)}, u32[]{:S(2)}) collective-permute-start(f32[8,128]{1,0:T(8,128)S(1)} %multiply_add_fusion.refs_0_), channel_id=1, source_target_pairs={{0,10},{2,8},{8,2},{10,0},{1,11},{3,9},{9,3},{11,1},{4,14},{6,12},... | collective-permute-start | bytes 12296 | tf_op jit(solution)/shard_map/ppermute | solution.py:254
  31.1 4.5 %collective-permute-start.13 = (f32[8,128]{1,0:T(8,128)S(1)}, f32[8,128]{1,0:T(8,128)S(1)}, u32[]{:S(2)}, u32[]{:S(2)}) collective-permute-start(f32[8,128]{1,0:T(8,128)S(1)} %multiply_add_fusion.refs_0_), channel_id=1, source_target_pairs={{0,8},{2,10},{8,0},{10,2},{1,9},{3,11},{9,1},{11,3},{4,12},{6,14},... | collective-permute-start | bytes 12296 | tf_op jit(solution)/shard_map/ppermute | solution.py:254
  31.7 3.9 %collective-permute-start.12 = (f32[8,128]{1,0:T(8,128)S(1)}, f32[8,128]{1,0:T(8,128)S(1)}, u32[]{:S(2)}, u32[]{:S(2)}) collective-permute-start(f32[8,128]{1,0:T(8,128)S(1)} %multiply_add_fusion.refs_0_), channel_id=1, source_target_pairs={{0,2},{2,0},{8,10},{10,8},{1,3},{3,1},{9,11},{11,9},{4,6},{6,4},{1... | collective-permute-start | bytes 12296 | tf_op jit(solution)/shard_map/ppermute | solution.py:254
  40.1 4.7 %collective-permute-start.17 = (f32[16,128]{1,0:T(8,128)S(1)}, f32[16,128]{1,0:T(8,128)S(1)}, u32[]{:S(2)}, u32[]{:S(2)}) collective-permute-start(f32[16,128]{1,0:T(8,128)S(1)} %get-tuple-element.30.refs_0_), channel_id=1, source_target_pairs={{0,20},{4,16},{16,4},{20,0},{1,21},{5,17},{17,5},{21,1},{2,22},{6,... | collective-permute-start | bytes 24584 | tf_op jit(solution)/shard_map/ppermute | solution.py:254
  42.4 3.7 %collective-permute-start.16 = (f32[16,128]{1,0:T(8,128)S(1)}, f32[16,128]{1,0:T(8,128)S(1)}, u32[]{:S(2)}, u32[]{:S(2)}) collective-permute-start(f32[16,128]{1,0:T(8,128)S(1)} %get-tuple-element.30.refs_0_), channel_id=1, source_target_pairs={{0,16},{4,20},{16,0},{20,4},{1,17},{5,21},{17,1},{21,5},{2,18},{6,... | collective-permute-start | bytes 24584 | tf_op jit(solution)/shard_map/ppermute | solution.py:254
  48.5 5.4 %collective-permute-start.21 = (f32[8,128]{1,0:T(8,128)S(1)}, f32[8,128]{1,0:T(8,128)S(1)}, u32[]{:S(2)}, u32[]{:S(2)}) collective-permute-start(f32[8,128]{1,0:T(8,128)S(1)} %add.41.refs_0_), channel_id=1, source_target_pairs={{0,10},{2,8},{8,2},{10,0},{1,11},{3,9},{9,3},{11,1},{4,14},{6,12},... | collective-permute-start | bytes 12296 | tf_op jit(solution)/shard_map/ppermute | solution.py:254
  50.5 4.5 %collective-permute-start.20 = (f32[8,128]{1,0:T(8,128)S(1)}, f32[8,128]{1,0:T(8,128)S(1)}, u32[]{:S(2)}, u32[]{:S(2)}) collective-permute-start(f32[8,128]{1,0:T(8,128)S(1)} %add.41.refs_0_), channel_id=1, source_target_pairs={{0,8},{2,10},{8,0},{10,2},{1,9},{3,11},{9,1},{11,3},{4,12},{6,14},... | collective-permute-start | bytes 12296 | tf_op jit(solution)/shard_map/ppermute | solution.py:254
  55.9 4.7 %collective-permute-start.24 = (f32[24,128]{1,0:T(8,128)S(1)}, f32[24,128]{1,0:T(8,128)S(1)}, u32[]{:S(2)}, u32[]{:S(2)}) collective-permute-start(f32[24,128]{1,0:T(8,128)S(1)} %later_columns.2.refs_0_), channel_id=1, source_target_pairs={{0,20},{4,16},{16,4},{20,0},{1,21},{5,17},{17,5},{21,1},{2,22},{6,... | collective-permute-start | bytes 36872 | tf_op jit(solution)/shard_map/ppermute | solution.py:254
  57.2 3.7 %collective-permute-start.23 = (f32[24,128]{1,0:T(8,128)S(1)}, f32[24,128]{1,0:T(8,128)S(1)}, u32[]{:S(2)}, u32[]{:S(2)}) collective-permute-start(f32[24,128]{1,0:T(8,128)S(1)} %later_columns.2.refs_0_), channel_id=1, source_target_pairs={{0,16},{4,20},{16,0},{20,4},{1,17},{5,21},{17,1},{21,5},{2,18},{6,... | collective-permute-start | bytes 36872 | tf_op jit(solution)/shard_map/ppermute | solution.py:254
  58.2 3.7 %collective-permute-start.22 = (f32[24,128]{1,0:T(8,128)S(1)}, f32[24,128]{1,0:T(8,128)S(1)}, u32[]{:S(2)}, u32[]{:S(2)}) collective-permute-start(f32[24,128]{1,0:T(8,128)S(1)} %later_columns.2.refs_0_), channel_id=1, source_target_pairs={{0,4},{4,0},{16,20},{20,16},{1,5},{5,1},{17,21},{21,17},{2,6},{6,2... | collective-permute-start | bytes 36872 | tf_op jit(solution)/shard_map/ppermute | solution.py:254
  63.8 5.4 %collective-permute-start.28 = (f32[8,128]{1,0:T(8,128)S(1)}, f32[8,128]{1,0:T(8,128)S(1)}, u32[]{:S(2)}, u32[]{:S(2)}) collective-permute-start(f32[8,128]{1,0:T(8,128)S(1)} %add.42.refs_0_), channel_id=1, source_target_pairs={{0,10},{2,8},{8,2},{10,0},{1,11},{3,9},{9,3},{11,1},{4,14},{6,12},... | collective-permute-start | bytes 12296 | tf_op jit(solution)/shard_map/ppermute | solution.py:254
  66.7 4.5 %collective-permute-start.27 = (f32[8,128]{1,0:T(8,128)S(1)}, f32[8,128]{1,0:T(8,128)S(1)}, u32[]{:S(2)}, u32[]{:S(2)}) collective-permute-start(f32[8,128]{1,0:T(8,128)S(1)} %add.42.refs_0_), channel_id=1, source_target_pairs={{0,8},{2,10},{8,0},{10,2},{1,9},{3,11},{9,1},{11,3},{4,12},{6,14},... | collective-permute-start | bytes 12296 | tf_op jit(solution)/shard_map/ppermute | solution.py:254
  72.1 3.8 %collective-permute-start.29 = (f32[24,128]{1,0:T(8,128)S(1)}, f32[24,128]{1,0:T(8,128)S(1)}, u32[]{:S(2)}, u32[]{:S(2)}) collective-permute-start(f32[24,128]{1,0:T(8,128)S(1)} %later_columns.3), channel_id=1, source_target_pairs={{0,4},{4,0},{16,20},{20,16},{1,5},{5,1},{17,21},{21,17},{2,6},{6,2... | collective-permute-start | bytes 36872 | tf_op jit(solution)/shard_map/ppermute | solution.py:254
  73.5 4.6 %collective-permute-start.31 = (f32[24,128]{1,0:T(8,128)S(1)}, f32[24,128]{1,0:T(8,128)S(1)}, u32[]{:S(2)}, u32[]{:S(2)}) collective-permute-start(f32[24,128]{1,0:T(8,128)S(1)} %later_columns.3), channel_id=1, source_target_pairs={{0,20},{4,16},{16,4},{20,0},{1,21},{5,17},{17,5},{21,1},{2,22},{6,... | collective-permute-start | bytes 36872 | tf_op jit(solution)/shard_map/ppermute | solution.py:254
  74.8 3.7 %collective-permute-start.30 = (f32[24,128]{1,0:T(8,128)S(1)}, f32[24,128]{1,0:T(8,128)S(1)}, u32[]{:S(2)}, u32[]{:S(2)}) collective-permute-start(f32[24,128]{1,0:T(8,128)S(1)} %later_columns.3), channel_id=1, source_target_pairs={{0,16},{4,20},{16,0},{20,4},{1,17},{5,21},{17,1},{21,5},{2,18},{6,... | collective-permute-start | bytes 36872 | tf_op jit(solution)/shard_map/ppermute | solution.py:254
  (11 other events, 19.5 us)

commit v3 on v1

v3 whole, which is shorter than its diff:
```python
import math

import jax
import jax.numpy as jnp
from jax import lax
from jax.experimental import pallas as pl
from jax.experimental.pallas import tpu as pltpu
from jax.sharding import Mesh, PartitionSpec as P

ITERS = 3
EPS = 0.05
SCALE = 1.0 / (EPS * math.log(2.0))
UNIT = EPS * math.log(2.0)
LANES = 128
CORES = 2
PIECES = 3
ROWS = 256
F32 = jnp.float32
VMEM = pl.BlockSpec(memory_space=pltpu.VMEM)
SMEM = pl.BlockSpec(memory_space=pltpu.SMEM)


def params(limit=24):
    return pltpu.CompilerParams(vmem_limit_bytes=limit * 1024 * 1024)


def pin(value):
    return pltpu.with_memory_space_constraint(value, pltpu.VMEM)


def rows_of(count):
    return jax.ShapeDtypeStruct((count // LANES, LANES), F32)


def diagonal():
    shape = (LANES, LANES)
    return lax.broadcasted_iota(jnp.int32, shape, 0) == lax.broadcasted_iota(jnp.int32, shape, 1)


def to_column(row, mask):
    return jnp.sum(jnp.where(mask, jnp.broadcast_to(row, mask.shape), 0.0), axis=1, keepdims=True)


def to_row(column, mask):
    return jnp.sum(jnp.where(mask, jnp.broadcast_to(column, mask.shape), 0.0), axis=0, keepdims=True)


def unfold(value):
    return jnp.concatenate([value[i : i + 1, :] for i in range(value.shape[0])], axis=1)


def fold_into(ref, value):
    for row in range(ref.shape[0]):
        ref[row : row + 1, :] = value[:, row * LANES : (row + 1) * LANES]


def tree(values, join):
    while len(values) > 1:
        values = [join(values[i], values[i + 1]) for i in range(0, len(values), 2)]
    return values[0]


def log_sum(values):
    peak = tree(values, jnp.maximum)
    return peak + jnp.log2(tree([jnp.exp2(value - peak) for value in values], jnp.add))


def product(rows, cols):
    return lax.dot_general(rows, cols, (((1,), (1,)), ((), ())), preferred_element_type=F32)


def ready(targets, mass, source_mass):
    def kernel(targets_ref, mass_ref, source_ref, targets_out, mass_out, source_out):
        targets_out[...] = targets_ref[...]
        mass_out[...] = mass_ref[...]
        source_out[...] = jnp.log2(source_ref[...])

    return pl.pallas_call(
        kernel,
        out_shape=(
            pltpu.VMEM(targets.shape, targets.dtype),
            pltpu.VMEM(mass.shape, F32),
            pltpu.VMEM(source_mass.shape, F32),
        ),
        in_specs=[VMEM] * 3,
        out_specs=(VMEM,) * 3,
        compiler_params=params(),
        cost_estimate=pl.CostEstimate(flops=1 << 20, bytes_accessed=1 << 20, transcendentals=0),
        name="ready",
    )(targets, mass, source_mass)


def pieces_of(value):
    lane = lax.broadcasted_iota(jnp.int32, (value.shape[0], LANES), 1)
    tile = jnp.zeros((value.shape[0], LANES), F32)
    for step in range(PIECES):
        piece = value.astype(jnp.bfloat16).astype(F32)
        tile = jnp.where(lane == step, piece, tile)
        value = value - piece
    return tile.astype(jnp.bfloat16)


def ones_for(rows):
    lane = lax.broadcasted_iota(jnp.int32, (rows, LANES), 1)
    return jnp.where(lane < PIECES, 1.0, 0.0).astype(jnp.bfloat16)


def first_rows(place, masses, sources, blocks):
    count, part = sources.shape[0], blocks[0].shape[0]
    n_blocks, n_masses = len(blocks), len(masses)
    width, chunk = n_blocks * part, masses[0].shape[0]

    def kernel(place_ref, *refs):
        mass_refs, (sources_ref, *block_refs) = refs[:n_masses], refs[n_masses : n_masses + 1 + n_blocks]
        targets_ref, mass_ref, out_ref, *score_refs = refs[n_masses + 1 + n_blocks :]
        for step in range(n_masses):
            start = pl.multiple_of(jnp.bitwise_xor(place_ref[1], step) * chunk, chunk)
            mass_ref[pl.ds(start, chunk), :] = mass_refs[step][...]
        for step in range(n_blocks):
            src = jnp.bitwise_xor(place_ref[0], step // CORES)
            core = jnp.bitwise_xor(place_ref[1], step % CORES)
            start = pl.multiple_of((core * (n_blocks // CORES) + src) * part, part)
            targets_ref[pl.ds(start, part), :] = block_refs[step][...]
        mask = diagonal()
        log_mass = jnp.log2(mass_ref[...]) * (1.0 / SCALE)
        cols = jnp.concatenate([sources_ref[...], ones_for(count)], axis=1)
        peak = jnp.full((8, count), -1e30, F32)
        total = jnp.zeros((8, count), F32)
        for at in range(0, width, ROWS):
            scores_ref = score_refs[at // ROWS % len(score_refs)]
            offsets = []
            for row in range(at, at + ROWS, LANES):
                values = targets_ref[row : row + LANES, :].astype(F32)
                half = 0.5 * jnp.sum(values * values, axis=1, keepdims=True)
                block = row // LANES
                offsets.append(pieces_of(to_column(log_mass[block : block + 1, :], mask) - half))
            rows = jnp.concatenate([targets_ref[at : at + ROWS, :], jnp.concatenate(offsets, axis=0)], axis=1)
            scores_ref[...] = product(rows, cols)
            tops = peak
            for row in range(0, ROWS, 8):
                tops = jnp.maximum(tops, scores_ref[row : row + 8, :])
            total = total * jnp.exp2((peak - tops) * SCALE)
            peak = tops
            for row in range(0, ROWS, 8):
                total = total + jnp.exp2((scores_ref[row : row + 8, :] - peak) * SCALE)
        widest = jnp.max(peak, axis=0, keepdims=True)
        total = jnp.sum(total * jnp.exp2((peak - widest) * SCALE), axis=0, keepdims=True)
        fold_into(out_ref, widest * SCALE + jnp.log2(total))

    return pl.pallas_call(
        kernel,
        out_shape=(pltpu.VMEM((width, LANES), jnp.bfloat16), rows_of(width), rows_of(count)),
        in_specs=[SMEM] + [VMEM] * (n_masses + 1 + n_blocks),
        out_specs=(VMEM,) * 3,
        scratch_shapes=[pltpu.VMEM((ROWS, count), F32)] * 2,
        compiler_params=params(),
        name="first_rows",
    )(place, *masses, sources, *blocks)


def first_columns(sources, targets, parts, log_mass):
    count, width = sources.shape[0], targets.shape[0]

    def kernel(sources_ref, targets_ref, parts_ref, log_ref, plan_ref, peak_ref, out_ref, lse_ref, *score_refs):
        lse = log_sum([parts_ref[i] for i in range(parts.shape[0])])
        lse_ref[...] = lse
        mask = diagonal()
        shift = (log_ref[...] - lse) * (1.0 / SCALE)
        shift = [pieces_of(to_column(shift[i : i + 1, :], mask)) for i in range(count // LANES)]
        cols = jnp.concatenate([sources_ref[...], jnp.concatenate(shift, axis=0)], axis=1)
        ones = ones_for(ROWS)
        for at in range(0, width, ROWS):
            scores_ref = score_refs[at // ROWS % len(score_refs)]
            scores_ref[...] = product(jnp.concatenate([targets_ref[at : at + ROWS, :], ones], axis=1), cols)
            for block in range(0, ROWS, LANES):
                peaks, totals = [], []
                for row in range(block, block + LANES, 8):
                    scores = scores_ref[row : row + 8, :]
                    pieces = [scores[:, lane : lane + LANES] for lane in range(0, count, LANES)]
                    peak = tree(pieces, jnp.maximum)
                    pieces = [jnp.exp2((piece - peak) * SCALE) for piece in pieces]
                    plan_ref[at + row : at + row + 8, :] = jnp.concatenate(pieces, axis=1)
                    peaks.append(peak * SCALE)
                    totals.append(tree(pieces, jnp.add))
                peak = jnp.concatenate(peaks, axis=0)
                peak_ref[at + block : at + block + LANES, :] = peak
                peak, total = peak.T, jnp.concatenate(totals, axis=0).T
                top = jnp.max(peak, axis=0, keepdims=True)
                total = jnp.sum(total * jnp.exp2(peak - top), axis=0, keepdims=True)
                index = (at + block) // LANES
                out_ref[index : index + 1, :] = top + jnp.log2(total)

    return pl.pallas_call(
        kernel,
        out_shape=(pltpu.VMEM((width, count), F32), pltpu.VMEM((width, LANES), F32), rows_of(width), rows_of(count)),
        in_specs=[VMEM] * 4,
        out_specs=(VMEM,) * 4,
        scratch_shapes=[pltpu.VMEM((ROWS, count), F32)] * 2,
        compiler_params=params(),
        name="first_columns",
    )(pin(sources), pin(targets), parts, log_mass)


def weighted_rows(reach_of, weight, plan_ref, out_ref):
    count = plan_ref.shape[1]
    mask = diagonal()
    total = jnp.zeros((8, count), F32)
    for block in range(plan_ref.shape[0] // LANES):
        at = block * LANES
        reach = reach_of(at, block, mask) * to_column(weight[block : block + 1, :], mask)
        for row in range(0, LANES, 8):
            factor = jnp.concatenate([reach[row : row + 8, :]] * (count // LANES), axis=1)
            total = total + plan_ref[at + row : at + row + 8, :] * factor
    fold_into(out_ref, jnp.sum(total, axis=0, keepdims=True))


def second_rows(plan, peak, mass, parts):
    width, count = plan.shape

    def kernel(plan_ref, peak_ref, mass_ref, *refs):
        part_refs, (lse_ref, reach_ref, out_ref) = refs[:-3], refs[-3:]
        lse = log_sum([ref[...] for ref in part_refs])
        lse_ref[...] = lse

        def reach_of(at, block, mask):
            reach = jnp.exp2(peak_ref[at : at + LANES, :] - to_column(lse[block : block + 1, :], mask))
            reach_ref[at : at + LANES, :] = reach
            return reach

        weighted_rows(reach_of, mass_ref[...], plan_ref, out_ref)

    return pl.pallas_call(
        kernel,
        out_shape=(rows_of(width), pltpu.VMEM((width, LANES), F32), rows_of(count)),
        in_specs=[VMEM] * (3 + len(parts)),
        out_specs=(VMEM,) * 3,
        compiler_params=params(),
        name="second_rows",
    )(pin(plan), pin(peak), mass, *parts)


def later_rows(plan, reach, mass, parts):
    width, count = plan.shape

    def kernel(plan_ref, reach_ref, mass_ref, *refs):
        part_refs, out_ref = refs[:-1], refs[-1]
        weight = mass_ref[...] / tree([ref[...] for ref in part_refs], jnp.add)
        weighted_rows(lambda at, block, mask: reach_ref[at : at + LANES, :], weight, plan_ref, out_ref)

    return pl.pallas_call(
        kernel,
        out_shape=rows_of(count),
        in_specs=[VMEM] * (3 + len(parts)),
        out_specs=VMEM,
        compiler_params=params(),
        name="later_rows",
    )(pin(plan), pin(reach), mass, *parts)


def later_columns(plan, reach, parts, log_mass, lse, half):
    width, count = plan.shape

    def kernel(plan_ref, reach_ref, parts_ref, log_ref, lse_ref, half_ref, out_ref, potential_ref):
        factor = log_ref[...] - jnp.log2(tree([parts_ref[i] for i in range(parts.shape[0])], jnp.add))
        potential_ref[...] = half_ref[...] + UNIT * (factor - lse_ref[...])
        factor = unfold(jnp.exp2(factor))
        factors = [factor[:, lane : lane + LANES] for lane in range(0, count, LANES)]
        for at in range(0, width, LANES):
            totals = []
            for row in range(at, at + LANES, 8):
                plan = plan_ref[row : row + 8, :]
                totals.append(tree([plan[:, i * LANES : (i + 1) * LANES] * factors[i] for i in range(count // LANES)], jnp.add))
            total = jnp.concatenate(totals, axis=0) * reach_ref[at : at + LANES, :]
            out_ref[at // LANES : at // LANES + 1, :] = jnp.sum(total.T, axis=0, keepdims=True)

    return pl.pallas_call(
        kernel,
        out_shape=(rows_of(width), rows_of(count)),
        in_specs=[VMEM] * 6,
        out_specs=(VMEM,) * 2,
        compiler_params=params(),
        name="later_columns",
    )(pin(plan), pin(reach), parts, log_mass, lse, half)


def levels_of(size):
    bits = size.bit_length() - 1
    out = []
    while bits > 0:
        take = 2 if bits % 2 == 0 else 1
        bits -= take
        out.append([step << bits for step in range(1, 1 << take)])
    return out


def swap(value, axes, size, distance):
    return lax.ppermute(value, axes, [(i, i ^ distance) for i in range(size)])


def swap_all(value, axes, size):
    values = [value]
    for distances in levels_of(size):
        got = {d: [swap(value, axes, size, d) for value in values] for d in reversed(distances)}
        values = [part for i in range(len(values)) for part in [values[i]] + [got[d][i] for d in distances]]
    return values


def share(value, size):
    copies = jnp.broadcast_to(value[None], (size,) + value.shape)
    return lax.all_to_all(copies, "far", 0, 0, tiled=True)


def half_norm(points):
    values = points.astype(F32)
    return 0.5 * jnp.sum(values * values, axis=1)


def make_local(n_src, n_far):
    near, n_near = ("src", "core"), n_src * CORES

    def local(source_points, target_points, source_mass, target_mass):
        core = lax.axis_index("core")
        place = jnp.stack([lax.axis_index("src"), core]).astype(jnp.int32)
        part = source_points.shape[0]
        a = source_mass.reshape(n_far, CORES, part)
        a = lax.dynamic_index_in_dim(a, core, axis=1, keepdims=False).reshape(-1, LANES)
        b = target_mass.reshape(-1, LANES)
        blocks = swap_all(target_points, near, n_near)
        masses = swap_all(b, "core", CORES)
        sources = lax.all_gather(source_points, "far", axis=0, tiled=True)
        blocks[0], masses[0], a = ready(target_points, b, a)
        place, a = lax.optimization_barrier((place, a))
        targets, b, own = first_rows(place, masses, sources, blocks)
        plan, peak, own, row_lse = first_columns(sources, targets, share(own, n_far), a)
        early_x, early_y, own = lax.optimization_barrier((sources, targets, own))
        half_x, half_y = half_norm(early_x).reshape(-1, LANES), half_norm(early_y).reshape(-1, LANES)
        parts = swap_all(own, near, n_near)
        half_x, half_y, *parts = lax.optimization_barrier((half_x, half_y, *parts))
        col_lse, reach, rows = second_rows(plan, peak, b, parts)
        for step in range(1, ITERS):
            if step > 1:
                rows = later_rows(plan, reach, b, parts)
            own, potential = later_columns(plan, reach, share(rows, n_far), a, row_lse, half_x)
            parts = swap_all(own, near, n_near)
        mine, other = swap_all(potential.reshape(n_far, part), "core", CORES)
        low, high = jnp.where(core == 0, mine, other), jnp.where(core == 0, other, mine)
        source_potential = jnp.stack([low, high], axis=1).reshape(-1)
        target_potential = half_y - UNIT * (col_lse + jnp.log2(tree(parts, jnp.add)))
        target_potential = target_potential.reshape(CORES, -1)
        target_potential = lax.dynamic_index_in_dim(target_potential, core, axis=0, keepdims=False)
        return source_potential, target_potential

    return local


def solution(mesh):
    n_src, n_tgt = mesh.shape["src"], mesh.shape["tgt"]
    n_far = n_tgt // CORES
    split = Mesh(mesh.devices.reshape(n_src, n_far, CORES), ("src", "far", "core"))
    placed = (P(("src", "far", "core"), None), P(("far", "core", "src"), None), P("src"), P(("far", "core")))
    return jax.shard_map(
        make_local(n_src, n_far),
        mesh=split,
        in_specs=placed,
        out_specs=(P("src"), P(("far", "core"))),
        check_vma=False,
    )
```

time: 74.9 us -> 90.6 us (1.21)
  blocking collectives: 18.1 us -> 61.8 us
  waiting for transfers between devices: 18.6 us -> 5.64 us
  starting transfers between devices: 20 us -> 9.29 us
  Pallas kernels: 11.7 us -> 9.27 us
  local copies, waits for them, and re-layouts: 4.98 us -> 2.84 us
    all_gather x0 -> x1, blocking collectives: none -> 31.7 us  [local(): sources = lax.all_gather(source_points, 'far', axis=0, tiled=True)]
    all_to_all x2 -> x3, blocking collectives: 18.1 us -> 30.1 us  [share(): return lax.all_to_all(copies, 'far', 0, 0, tiled=True)]
    all_to_all x2 -> x0, starting transfers between devices: 11.8 us -> none  [share(): return lax.all_to_all(copies, 'far', 0, 0, tiled=True)]
    all_to_all x2 -> x0, waiting for transfers between devices: 8.06 us -> none  [share(): return lax.all_to_all(copies, 'far', 0, 0, tiled=True)]
    ppermute x14, waiting for transfers between devices: 10.5 us -> 5.64 us  [swap(): return lax.ppermute(value, axes, [(i, i ^ distance) for i in range(size)])]
    broadcast_in_dim x4 -> x3, local copies, waits for them, and re-layouts: 2.15 us -> 0.01 us  [share(): copies = jnp.broadcast_to(value[None], (size,) + value.shape)]
    pallas_call x2 -> x3, Pallas kernels: 5.19 us -> 3.45 us  [the longest x1 2.53 us: first_columns(): pl.pallas_call(kernel, out_shape=(pltpu.VMEM((width, count), F32), pltpu....]
    ppermute x14, starting transfers between devices: 8.14 us -> 9.29 us  [swap(): return lax.ppermute(value, axes, [(i, i ^ distance) for i in range(size)])]
  transfers between devices with their start and end apart: 16 -> 14, of which waited for: 11 -> 6; matrix products, arithmetic and copies ran while one was open for 1% -> 1% of each run, Pallas kernels for 0% -> 0%
where the time goes in v3:
time: 90.6 us; the launch traced here: 90.3 us
  blocking collectives  61.8 us (68%)
  starting transfers between devices  9.29 us (10%)
  Pallas kernels  9.27 us (10%)
  waiting for transfers between devices  5.64 us (6%)
  local copies, waits for them, and re-layouts  2.84 us (3%)
    all_gather x1, blocking collectives, local(): sources = lax.all_gather(source_points, 'far', axis=0, tiled=True)  31.7 us
    all_to_all x3, blocking collectives, share(): return lax.all_to_all(copies, 'far', 0, 0, tiled=True)  30.1 us
    ppermute x14, starting transfers between devices, swap(): return lax.ppermute(value, axes, [(i, i ^ distance) for i in range(size)])  9.29 us
    ppermute x14, waiting for transfers between devices, swap(): return lax.ppermute(value, axes, [(i, i ^ distance) for i in range(size)])  5.64 us
    pallas_call x1, Pallas kernels, first_rows(): pl.pallas_call(kernel, out_shape=(pltpu.VMEM((width, LANES), jnp.bfloat16...  3.1 us
    pallas_call x1, Pallas kernels, first_columns(): pl.pallas_call(kernel, out_shape=(pltpu.VMEM((width, count), F32), pltpu....  2.53 us
    pallas_call x2, Pallas kernels, later_columns(): pl.pallas_call(kernel, out_shape=(rows_of(width), rows_of(count)), in_spe...  1.99 us
  transfers between devices with their start and end apart: 14, of which 6 were waited for; matrix products, arithmetic and copies ran while one was open for 1% of the time, Pallas kernels for 0%

profile of v3, /device:TPU:0, one launch (start us, length us, event | category | flops | bytes accessed | tf_op | source)
XLA Modules:
  0.0 90.3 jit_solution(9526547692862079950)
XLA Ops:
  0.6 0.5 collective-permute-start.1
  1.2 2.6 %collective-permute-start.3 = (bf16[512,128]{1,0:T(8,128)(2,1)}, bf16[512,128]{1,0:T(8,128)(2,1)S(1)}, u32[]{:S(2)}, u32[]{:S(2)}) collective-permute-start(bf16[512,128]{1,0:T(8,128)(2,1)} %targets_ref.1), channel_id=1, source_target_pairs={{0,17},{1,16},{16,1},{17,0},{2,19},{3,18},{18,3},{19,2},{4,21},{5,... | collective-permute-start | bytes 393224 | tf_op jit(solution)/shard_map/ppermute | solution.py:297
  3.9 31.7 %all_gather.3.refs_2_.sources_ref = bf16[1024,128]{1,0:T(8,128)(2,1)S(1)} all-gather(bf16[128,128]{1,0:T(8,128)(2,1)} %param.4), channel_id=1, replica_groups=mesh['src'=2,'far'=8,'core'=2] {'far'}, dimensions={0}, use_global_device_ids=true | all-gather | bytes 294912 | tf_op jit(solution)/shard_map/all_gather | solution.py:330
  35.8 0.9 copy-done.1
  36.7 0.7 copy-done.2
  37.4 3.1 %first_rows.1 = (bf16[2048,128]{1,0:T(8,128)(2,1)S(1)}, f32[16,128]{1,0:T(8,128)S(1)}, f32[8,128]{1,0:T(8,128)S(1)}) custom-call(s32[2]{0:T(128)S(1)} %pad_add_fusion.place_ref, f32[8,128]{1,0:T(8,128)S(1)} %get-tuple-element.31.refs_0_, f32[8,128]{1,0:T(8,128)S(1)} %collective-permute-done.refs_1_, bf16[1024,128]{1,0:T(8,128)(2,1)S(1)} %all_gather.3.refs_2_.sources_ref, ...), custom_call_target="tpu_custom_call" | custom-call | tf_op jit(solution)/shard_map/first_rows/pallas_call | solution.py:150
  40.5 12.0 %all_to_all.15.parts_ref = f32[8,8,128]{2,1,0:T(8,128)S(1)} all-to-all(f32[8,8,128]{2,1,0:T(8,128)S(1)} %broadcast_in_dim.6), channel_id=1, replica_groups=mesh['src'=2,'far'=8,'core'=2] {'far'}, dimensions={0} | all-to-all | bytes 65536 | tf_op jit(solution)/shard_map/all_to_all | solution.py:310
  52.5 2.5 %first_columns.1 = (f32[2048,1024]{1,0:T(8,128)S(1)}, f32[2048,128]{1,0:T(8,128)S(1)}, f32[16,128]{1,0:T(8,128)S(1)}, f32[8,128]{1,0:T(8,128)S(1)}) custom-call(bf16[1024,128]{1,0:T(8,128)(2,1)S(1)} %all_gather.3.refs_2_.sources_ref, bf16[2048,128]{1,0:T(8,128)(2,1)S(1)} %get-tuple-element.41.targets_ref, f32[8,8,128]{2,1,0:T(8,128)S(1)} %all_to_all.15.parts_ref, ...), custom_call_target="tpu_custom_call" | custom-call | tf_op jit(solution)/shard_map/first_columns/pallas_call | solution.py:193
  55.1 1.6 %collective-permute-start.5 = (f32[16,128]{1,0:T(8,128)S(1)}, f32[16,128]{1,0:T(8,128)S(1)}, u32[]{:S(2)}, u32[]{:S(2)}) collective-permute-start(f32[16,128]{1,0:T(8,128)S(1)} %get-tuple-element.43.refs_0_), channel_id=1, source_target_pairs={{0,16},{1,17},{16,0},{17,1},{2,18},{3,19},{18,2},{19,3},{4,20},{5,... | collective-permute-start | bytes 24584 | tf_op jit(solution)/shard_map/ppermute | solution.py:297
  57.5 0.6 collective-permute-done.6.refs_3_
  58.2 0.6 collective-permute-done.5.refs_2_
  58.8 0.9 second_rows.1
  59.7 9.1 %all_to_all.16.parts_ref = f32[8,8,128]{2,1,0:T(8,128)S(1)} all-to-all(f32[8,8,128]{2,1,0:T(8,128)S(1)} %broadcast_in_dim.7), channel_id=1, replica_groups=mesh['src'=2,'far'=8,'core'=2] {'far'}, dimensions={0} | all-to-all | bytes 65536 | tf_op jit(solution)/shard_map/all_to_all | solution.py:310
  68.8 1.3 %later_columns.2 = (f32[16,128]{1,0:T(8,128)S(1)}, f32[8,128]{1,0:T(8,128)}) custom-call(f32[2048,1024]{1,0:T(8,128)S(1)} %get-tuple-element.36.plan_ref, f32[2048,128]{1,0:T(8,128)S(1)} %get-tuple-element.47.reach_ref, f32[8,8,128]{2,1,0:T(8,128)S(1)} %all_to_all.16.parts_ref, f32[8,128]{1,0:T(8,128)S(1)} %get-tuple-element.35.log_ref, ...), custom_call_target="tpu_custom_call" | custom-call | tf_op jit(solution)/shard_map/later_columns/pallas_call | solution.py:276
  70.1 1.5 %collective-permute-start.8 = (f32[16,128]{1,0:T(8,128)S(1)}, f32[16,128]{1,0:T(8,128)S(1)}, u32[]{:S(2)}, u32[]{:S(2)}) collective-permute-start(f32[16,128]{1,0:T(8,128)S(1)} %get-tuple-element.51.refs_0_), channel_id=1, source_target_pairs={{0,16},{1,17},{16,0},{17,1},{2,18},{3,19},{18,2},{19,3},{4,20},{5,... | collective-permute-start | bytes 24584 | tf_op jit(solution)/shard_map/ppermute | solution.py:297
  71.9 1.2 %collective-permute-done.9.refs_3_ = f32[16,128]{1,0:T(8,128)S(1)} collective-permute-done((f32[16,128]{1,0:T(8,128)S(1)}, f32[16,128]{1,0:T(8,128)S(1)}, u32[]{:S(2)}, u32[]{:S(2)}) %collective-permute-start.9) | collective-permute-done | bytes 8224 | tf_op jit(solution)/shard_map/ppermute | solution.py:297
  73.2 0.6 collective-permute-done.8.refs_2_
  73.8 0.7 later_rows.1
  74.5 9.1 %all_to_all.17.parts_ref = f32[8,8,128]{2,1,0:T(8,128)S(1)} all-to-all(f32[8,8,128]{2,1,0:T(8,128)S(1)} %broadcast_in_dim.8), channel_id=1, replica_groups=mesh['src'=2,'far'=8,'core'=2] {'far'}, dimensions={0} | all-to-all | bytes 65536 | tf_op jit(solution)/shard_map/all_to_all | solution.py:310
  83.6 0.7 later_columns.3
  84.4 1.6 %collective-permute-start.13 = (f32[16,128]{1,0:T(8,128)S(1)}, f32[16,128]{1,0:T(8,128)S(1)}, u32[]{:S(2)}, u32[]{:S(2)}) collective-permute-start(f32[16,128]{1,0:T(8,128)S(1)} %get-tuple-element.55), channel_id=1, source_target_pairs={{0,17},{1,16},{16,1},{17,0},{2,19},{3,18},{18,3},{19,2},{4,21},{5,... | collective-permute-start | bytes 24584 | tf_op jit(solution)/shard_map/ppermute | solution.py:297
  86.6 0.6 copy.6
  87.5 2.1 %collective-permute-done.12 = f32[16,128]{1,0:T(8,128)S(1)} collective-permute-done((f32[16,128]{1,0:T(8,128)S(1)}, f32[16,128]{1,0:T(8,128)S(1)}, u32[]{:S(2)}, u32[]{:S(2)}) %collective-permute-start.12) | collective-permute-done | bytes 8224 | tf_op jit(solution)/shard_map/ppermute | solution.py:297
  89.7 0.6 constant_dynamic-slice_fusion
  (36 shorter events, 2.5 us)
Async XLA Ops:
  0.6 35.1 %copy-start = (f32[2048]{0:T(1024)S(1)}, f32[2048]{0:T(1024)}, u32[]{:S(2)}) copy-start(f32[2048]{0:T(1024)} %param.6) | copy-start | bytes 24580
  0.6 36.8 %collective-permute-start.1 = (bf16[512,128]{1,0:T(8,128)(2,1)}, bf16[512,128]{1,0:T(8,128)(2,1)S(1)}, u32[]{:S(2)}, u32[]{:S(2)}) collective-permute-start(bf16[512,128]{1,0:T(8,128)(2,1)} %targets_ref.1), channel_id=1, source_target_pairs={{0,1},{1,0},{16,17},{17,16},{2,3},{3,2},{18,19},{19,18},{4,5},{5,4... | collective-permute-start | bytes 393224 | tf_op jit(solution)/shard_map/ppermute | solution.py:297
  1.2 36.2 %collective-permute-start.3 = (bf16[512,128]{1,0:T(8,128)(2,1)}, bf16[512,128]{1,0:T(8,128)(2,1)S(1)}, u32[]{:S(2)}, u32[]{:S(2)}) collective-permute-start(bf16[512,128]{1,0:T(8,128)(2,1)} %targets_ref.1), channel_id=1, source_target_pairs={{0,17},{1,16},{16,1},{17,0},{2,19},{3,18},{18,3},{19,2},{4,21},{5,... | collective-permute-start | bytes 393224 | tf_op jit(solution)/shard_map/ppermute | solution.py:297
  3.8 33.6 %collective-permute-start.2 = (bf16[512,128]{1,0:T(8,128)(2,1)}, bf16[512,128]{1,0:T(8,128)(2,1)S(1)}, u32[]{:S(2)}, u32[]{:S(2)}) collective-permute-start(bf16[512,128]{1,0:T(8,128)(2,1)} %targets_ref.1), channel_id=1, source_target_pairs={{0,16},{1,17},{16,0},{17,1},{2,18},{3,19},{18,2},{19,3},{4,20},{5,... | collective-permute-start | bytes 393224 | tf_op jit(solution)/shard_map/ppermute | solution.py:297
  3.9 33.5 %collective-permute-start = (f32[8,128]{1,0:T(8,128)}, f32[8,128]{1,0:T(8,128)S(1)}, u32[]{:S(2)}, u32[]{:S(2)}) collective-permute-start(f32[8,128]{1,0:T(8,128)} %bitcast.17), channel_id=1, source_target_pairs={{0,1},{1,0},{2,3},{3,2},{4,5},{5,4},{6,7},{7,6},{8,9},{9,8},{10,11... | collective-permute-start | bytes 12296 | tf_op jit(solution)/shard_map/ppermute | solution.py:297
  35.8 0.9 %copy-start.1 = (bf16[512,128]{1,0:T(8,128)(2,1)S(1)}, bf16[512,128]{1,0:T(8,128)(2,1)}, u32[]{:S(2)}) copy-start(bf16[512,128]{1,0:T(8,128)(2,1)} %targets_ref.1) | copy-start | bytes 393220
  36.7 0.7 copy-start.2
  55.0 3.2 %collective-permute-start.6 = (f32[16,128]{1,0:T(8,128)S(1)}, f32[16,128]{1,0:T(8,128)S(1)}, u32[]{:S(2)}, u32[]{:S(2)}) collective-permute-start(f32[16,128]{1,0:T(8,128)S(1)} %get-tuple-element.43.refs_0_), channel_id=1, source_target_pairs={{0,17},{1,16},{16,1},{17,0},{2,19},{3,18},{18,3},{19,2},{4,21},{5,... | collective-permute-start | bytes 24584 | tf_op jit(solution)/shard_map/ppermute | solution.py:297
  55.1 3.7 %collective-permute-start.5 = (f32[16,128]{1,0:T(8,128)S(1)}, f32[16,128]{1,0:T(8,128)S(1)}, u32[]{:S(2)}, u32[]{:S(2)}) collective-permute-start(f32[16,128]{1,0:T(8,128)S(1)} %get-tuple-element.43.refs_0_), channel_id=1, source_target_pairs={{0,16},{1,17},{16,0},{17,1},{2,18},{3,19},{18,2},{19,3},{4,20},{5,... | collective-permute-start | bytes 24584 | tf_op jit(solution)/shard_map/ppermute | solution.py:297
  56.7 2.1 %collective-permute-start.4 = (f32[16,128]{1,0:T(8,128)S(1)}, f32[16,128]{1,0:T(8,128)S(1)}, u32[]{:S(2)}, u32[]{:S(2)}) collective-permute-start(f32[16,128]{1,0:T(8,128)S(1)} %get-tuple-element.43.refs_0_), channel_id=1, source_target_pairs={{0,1},{1,0},{16,17},{17,16},{2,3},{3,2},{18,19},{19,18},{4,5},{5,4... | collective-permute-start | bytes 24584 | tf_op jit(solution)/shard_map/ppermute | solution.py:297
  70.1 3.1 %collective-permute-start.9 = (f32[16,128]{1,0:T(8,128)S(1)}, f32[16,128]{1,0:T(8,128)S(1)}, u32[]{:S(2)}, u32[]{:S(2)}) collective-permute-start(f32[16,128]{1,0:T(8,128)S(1)} %get-tuple-element.51.refs_0_), channel_id=1, source_target_pairs={{0,17},{1,16},{16,1},{17,0},{2,19},{3,18},{18,3},{19,2},{4,21},{5,... | collective-permute-start | bytes 24584 | tf_op jit(solution)/shard_map/ppermute | solution.py:297
  70.1 3.7 %collective-permute-start.8 = (f32[16,128]{1,0:T(8,128)S(1)}, f32[16,128]{1,0:T(8,128)S(1)}, u32[]{:S(2)}, u32[]{:S(2)}) collective-permute-start(f32[16,128]{1,0:T(8,128)S(1)} %get-tuple-element.51.refs_0_), channel_id=1, source_target_pairs={{0,16},{1,17},{16,0},{17,1},{2,18},{3,19},{18,2},{19,3},{4,20},{5,... | collective-permute-start | bytes 24584 | tf_op jit(solution)/shard_map/ppermute | solution.py:297
  71.6 2.1 %collective-permute-start.7 = (f32[16,128]{1,0:T(8,128)S(1)}, f32[16,128]{1,0:T(8,128)S(1)}, u32[]{:S(2)}, u32[]{:S(2)}) collective-permute-start(f32[16,128]{1,0:T(8,128)S(1)} %get-tuple-element.51.refs_0_), channel_id=1, source_target_pairs={{0,1},{1,0},{16,17},{17,16},{2,3},{3,2},{18,19},{19,18},{4,5},{5,4... | collective-permute-start | bytes 24584 | tf_op jit(solution)/shard_map/ppermute | solution.py:297
  84.3 2.2 %collective-permute-start.10 = (f32[8,128]{1,0:T(8,128)S(1)}, f32[8,128]{1,0:T(8,128)S(1)}, u32[]{:S(2)}, u32[]{:S(2)}) collective-permute-start(f32[8,128]{1,0:T(8,128)S(1)} %get-tuple-element.52), channel_id=1, source_target_pairs={{0,1},{1,0},{2,3},{3,2},{4,5},{5,4},{6,7},{7,6},{8,9},{9,8},{10,11... | collective-permute-start | bytes 12296 | tf_op jit(solution)/shard_map/ppermute | solution.py:297
  84.4 3.1 %collective-permute-start.13 = (f32[16,128]{1,0:T(8,128)S(1)}, f32[16,128]{1,0:T(8,128)S(1)}, u32[]{:S(2)}, u32[]{:S(2)}) collective-permute-start(f32[16,128]{1,0:T(8,128)S(1)} %get-tuple-element.55), channel_id=1, source_target_pairs={{0,17},{1,16},{16,1},{17,0},{2,19},{3,18},{18,3},{19,2},{4,21},{5,... | collective-permute-start | bytes 24584 | tf_op jit(solution)/shard_map/ppermute | solution.py:297
  86.0 3.7 %collective-permute-start.12 = (f32[16,128]{1,0:T(8,128)S(1)}, f32[16,128]{1,0:T(8,128)S(1)}, u32[]{:S(2)}, u32[]{:S(2)}) collective-permute-start(f32[16,128]{1,0:T(8,128)S(1)} %get-tuple-element.55), channel_id=1, source_target_pairs={{0,16},{1,17},{16,0},{17,1},{2,18},{3,19},{18,2},{19,3},{4,20},{5,... | collective-permute-start | bytes 24584 | tf_op jit(solution)/shard_map/ppermute | solution.py:297
  86.5 3.1 %collective-permute-start.11 = (f32[16,128]{1,0:T(8,128)S(1)}, f32[16,128]{1,0:T(8,128)S(1)}, u32[]{:S(2)}, u32[]{:S(2)}) collective-permute-start(f32[16,128]{1,0:T(8,128)S(1)} %get-tuple-element.55), channel_id=1, source_target_pairs={{0,1},{1,0},{16,17},{17,16},{2,3},{3,2},{18,19},{19,18},{4,5},{5,4... | collective-permute-start | bytes 24584 | tf_op jit(solution)/shard_map/ppermute | solution.py:297

commit v4 on v3

--- a/solution.py
+++ b/solution.py
@@ -70,15 +70,23 @@
 
 
 def ready(targets, mass, source_mass):
-    def kernel(targets_ref, mass_ref, source_ref, targets_out, mass_out, source_out):
-        targets_out[...] = targets_ref[...]
+    part, chunk = targets.shape[0], mass.shape[0]
+
+    def kernel(targets_ref, mass_ref, source_ref, packed_ref, mass_out, source_out):
+        packed_ref[:part, :] = targets_ref[...]
         mass_out[...] = mass_ref[...]
         source_out[...] = jnp.log2(source_ref[...])
+        value, pieces = mass_ref[...], []
+        for step in range(PIECES):
+            pieces.append(value.astype(jnp.bfloat16).astype(F32))
+            value = value - pieces[-1]
+        pieces.append(jnp.zeros_like(value))
+        packed_ref[part:, :] = jnp.concatenate(pieces, axis=0).astype(jnp.bfloat16)
 
     return pl.pallas_call(
         kernel,
         out_shape=(
-            pltpu.VMEM(targets.shape, targets.dtype),
+            pltpu.VMEM((part + (PIECES + 1) * chunk, LANES), jnp.bfloat16),
             pltpu.VMEM(mass.shape, F32),
             pltpu.VMEM(source_mass.shape, F32),
         ),
@@ -88,6 +96,26 @@
         cost_estimate=pl.CostEstimate(flops=1 << 20, bytes_accessed=1 << 20, transcendentals=0),
         name="ready",
     )(targets, mass, source_mass)
+
+
+def pack(place, blocks):
+    part = blocks[0].shape[0]
+
+    def kernel(place_ref, *refs):
+        out_ref = refs[-1]
+        for step in range(len(blocks)):
+            start = pl.multiple_of(jnp.bitwise_xor(place_ref[0], step) * part, part)
+            out_ref[pl.ds(start, part), :] = refs[step][...]
+
+    return pl.pallas_call(
+        kernel,
+        out_shape=pltpu.VMEM((len(blocks) * part, LANES), jnp.bfloat16),
+        in_specs=[SMEM] + [VMEM] * len(blocks),
+        out_specs=VMEM,
+        compiler_params=params(),
+        cost_estimate=pl.CostEstimate(flops=1 << 20, bytes_accessed=1 << 18, transcendentals=0),
+        name="pack",
+    )(place, *blocks)
 
 
 def pieces_of(value):
@@ -105,63 +133,117 @@
     return jnp.where(lane < PIECES, 1.0, 0.0).astype(jnp.bfloat16)
 
 
-def first_rows(place, masses, sources, blocks):
-    count, part = sources.shape[0], blocks[0].shape[0]
-    n_blocks, n_masses = len(blocks), len(masses)
-    width, chunk = n_blocks * part, masses[0].shape[0]
-
-    def kernel(place_ref, *refs):
-        mass_refs, (sources_ref, *block_refs) = refs[:n_masses], refs[n_masses : n_masses + 1 + n_blocks]
-        targets_ref, mass_ref, out_ref, *score_refs = refs[n_masses + 1 + n_blocks :]
-        for step in range(n_masses):
-            start = pl.multiple_of(jnp.bitwise_xor(place_ref[1], step) * chunk, chunk)
-            mass_ref[pl.ds(start, chunk), :] = mass_refs[step][...]
-        for step in range(n_blocks):
-            src = jnp.bitwise_xor(place_ref[0], step // CORES)
-            core = jnp.bitwise_xor(place_ref[1], step % CORES)
-            start = pl.multiple_of((core * (n_blocks // CORES) + src) * part, part)
-            targets_ref[pl.ds(start, part), :] = block_refs[step][...]
+class Rows:
+    def __init__(self, count):
+        self.peak = jnp.full((8, count), -1e30, F32)
+        self.total = jnp.zeros((8, count), F32)
+
+    def add(self, scores_ref):
+        tops = self.peak
+        for row in range(0, ROWS, 8):
+            tops = jnp.maximum(tops, scores_ref[row : row + 8, :])
+        self.total = self.total * jnp.exp2((self.peak - tops) * SCALE)
+        self.peak = tops
+        for row in range(0, ROWS, 8):
+            self.total = self.total + jnp.exp2((scores_ref[row : row + 8, :] - tops) * SCALE)
+
+    def lse(self):
+        widest = jnp.max(self.peak, axis=0, keepdims=True)
+        total = jnp.sum(self.total * jnp.exp2((self.peak - widest) * SCALE), axis=0, keepdims=True)
+        return widest * SCALE + jnp.log2(total)
+
+
+def first_rows(place, mass, packed, blocks, sources):
+    count, chunk = sources.shape[0], mass.shape[0]
+    n_src = len(blocks) // CORES + 1
+    part = blocks[0].shape[0]
+    width = CORES * n_src * part
+
+    def kernel(place_ref, mass_ref, sources_ref, *refs):
+        own_ref, other_ref, block_refs = refs[0], refs[1], refs[2 : 2 + len(blocks)]
+        targets_ref, offset_ref, full_ref, out_ref, *score_refs = refs[2 + len(blocks) :]
+        src, core = place_ref[0], place_ref[1]
+        full_ref[pl.ds(pl.multiple_of(core * chunk, chunk), chunk), :] = mass_ref[...]
+        parts = [other_ref[part + i * chunk : part + (i + 1) * chunk, :].astype(F32) for i in range(PIECES)]
+        start = pl.multiple_of(jnp.bitwise_xor(core, 1) * chunk, chunk)
+        full_ref[pl.ds(start, chunk), :] = parts[0] + (parts[1] + parts[2])
+        for dc in range(CORES):
+            for ds in range(n_src):
+                index = jnp.bitwise_xor(core, dc) * n_src + jnp.bitwise_xor(src, ds)
+                start = pl.multiple_of(index * part, part)
+                ref = refs[dc] if ds == 0 else block_refs[dc * (n_src - 1) + ds - 1]
+                targets_ref[pl.ds(start, part), :] = ref[:part, :]
         mask = diagonal()
-        log_mass = jnp.log2(mass_ref[...]) * (1.0 / SCALE)
+        log_mass = jnp.log2(full_ref[...]) * (1.0 / SCALE)
         cols = jnp.concatenate([sources_ref[...], ones_for(count)], axis=1)
-        peak = jnp.full((8, count), -1e30, F32)
-        total = jnp.zeros((8, count), F32)
+        rows = Rows(count)
         for at in range(0, width, ROWS):
             scores_ref = score_refs[at // ROWS % len(score_refs)]
-            offsets = []
             for row in range(at, at + ROWS, LANES):
                 values = targets_ref[row : row + LANES, :].astype(F32)
                 half = 0.5 * jnp.sum(values * values, axis=1, keepdims=True)
                 block = row // LANES
-                offsets.append(pieces_of(to_column(log_mass[block : block + 1, :], mask) - half))
-            rows = jnp.concatenate([targets_ref[at : at + ROWS, :], jnp.concatenate(offsets, axis=0)], axis=1)
-            scores_ref[...] = product(rows, cols)
-            tops = peak
-            for row in range(0, ROWS, 8):
-                tops = jnp.maximum(tops, scores_ref[row : row + 8, :])
-            total = total * jnp.exp2((peak - tops) * SCALE)
-            peak = tops
-            for row in range(0, ROWS, 8):
-                total = total + jnp.exp2((scores_ref[row : row + 8, :] - peak) * SCALE)
-        widest = jnp.max(peak, axis=0, keepdims=True)
-        total = jnp.sum(total * jnp.exp2((peak - widest) * SCALE), axis=0, keepdims=True)
-        fold_into(out_ref, widest * SCALE + jnp.log2(total))
-
-    return pl.pallas_call(
-        kernel,
-        out_shape=(pltpu.VMEM((width, LANES), jnp.bfloat16), rows_of(width), rows_of(count)),
-        in_specs=[SMEM] + [VMEM] * (n_masses + 1 + n_blocks),
-        out_specs=(VMEM,) * 3,
+                offset_ref[row : row + LANES, :] = pieces_of(to_column(log_mass[block : block + 1, :], mask) - half)
+            scores_ref[...] = product(jnp.concatenate([targets_ref[at : at + ROWS, :], offset_ref[at : at + ROWS, :]], axis=1), cols)
+            rows.add(scores_ref)
+        fold_into(out_ref, rows.lse())
+
+    return pl.pallas_call(
+        kernel,
+        out_shape=(
+            pltpu.VMEM((width, LANES), jnp.bfloat16),
+            pltpu.VMEM((width, LANES), jnp.bfloat16),
+            rows_of(width),
+            rows_of(count),
+        ),
+        in_specs=[SMEM] + [VMEM] * (4 + len(blocks)),
+        out_specs=(VMEM,) * 4,
         scratch_shapes=[pltpu.VMEM((ROWS, count), F32)] * 2,
         compiler_params=params(),
+        cost_estimate=pl.CostEstimate(flops=1 << 29, bytes_accessed=1 << 20, transcendentals=1 << 20),
         name="first_rows",
-    )(place, *masses, sources, *blocks)
-
-
-def first_columns(sources, targets, parts, log_mass):
-    count, width = sources.shape[0], targets.shape[0]
-
-    def kernel(sources_ref, targets_ref, parts_ref, log_ref, plan_ref, peak_ref, out_ref, lse_ref, *score_refs):
+    )(place, mass, pin(sources), *[pin(value) for value in packed], *[pin(value) for value in blocks])
+
+
+def other_rows(place, targets, offsets, first, groups):
+    width, count, each = targets.shape[0], sum(group.shape[0] for group in groups), groups[0].shape[0] // LANES
+
+    def kernel(place_ref, targets_ref, offset_ref, first_ref, *refs):
+        group_refs, (out_ref, *score_refs) = refs[: len(groups)], refs[len(groups) :]
+        cols = jnp.concatenate([ref[...] for ref in group_refs], axis=0)
+        cols = jnp.concatenate([cols, ones_for(count)], axis=1)
+        rows = Rows(count)
+        for at in range(0, width, ROWS):
+            scores_ref = score_refs[at // ROWS % len(score_refs)]
+            scores_ref[...] = product(jnp.concatenate([targets_ref[at : at + ROWS, :], offset_ref[at : at + ROWS, :]], axis=1), cols)
+            rows.add(scores_ref)
+        lse = rows.lse()
+        for step in range(len(groups) + 1):
+            start = jnp.bitwise_xor(place_ref[2], step) * each
+            for row in range(each):
+                at = ((step - 1) * each + row) * LANES
+                out_ref[pl.ds(start + row, 1), :] = first_ref[row : row + 1, :] if step == 0 else lse[:, at : at + LANES]
+
+    return pl.pallas_call(
+        kernel,
+        out_shape=rows_of(count + each * LANES),
+        in_specs=[SMEM] + [VMEM] * (3 + len(groups)),
+        out_specs=VMEM,
+        scratch_shapes=[pltpu.VMEM((ROWS, count), F32)] * 2,
+        compiler_params=params(),
+        name="other_rows",
+    )(place, pin(targets), pin(offsets), first, *groups)
+
+
+def first_columns(place, groups, targets, parts, log_mass):
+    each, width = groups[0].shape[0], targets.shape[0]
+    count = each * len(groups)
+
+    def kernel(place_ref, targets_ref, parts_ref, log_ref, *refs):
+        group_refs, (plan_ref, peak_ref, out_ref, lse_ref, sources_ref, *score_refs) = refs[: len(groups)], refs[len(groups) :]
+        for step in range(len(groups)):
+            start = pl.multiple_of(jnp.bitwise_xor(place_ref[2], step) * each, each)
+            sources_ref[pl.ds(start, each), :] = group_refs[step][...]
         lse = log_sum([parts_ref[i] for i in range(parts.shape[0])])
         lse_ref[...] = lse
         mask = diagonal()
@@ -192,13 +274,19 @@
 
     return pl.pallas_call(
         kernel,
-        out_shape=(pltpu.VMEM((width, count), F32), pltpu.VMEM((width, LANES), F32), rows_of(width), rows_of(count)),
-        in_specs=[VMEM] * 4,
-        out_specs=(VMEM,) * 4,
+        out_shape=(
+            pltpu.VMEM((width, count), F32),
+            pltpu.VMEM((width, LANES), F32),
+            rows_of(width),
+            rows_of(count),
+            pltpu.VMEM((count, LANES), jnp.bfloat16),
+        ),
+        in_specs=[SMEM] + [VMEM] * (3 + len(groups)),
+        out_specs=(VMEM,) * 5,
         scratch_shapes=[pltpu.VMEM((ROWS, count), F32)] * 2,
         compiler_params=params(),
         name="first_columns",
-    )(pin(sources), pin(targets), parts, log_mass)
+    )(place, pin(targets), parts, log_mass, *[pin(group) for group in groups])
 
 
 def weighted_rows(reach_of, weight, plan_ref, out_ref):
@@ -307,7 +395,7 @@
 
 def share(value, size):
     copies = jnp.broadcast_to(value[None], (size,) + value.shape)
-    return lax.all_to_all(copies, "far", 0, 0, tiled=True)
+    return lax.all_to_all(copies, ("z", "x"), 0, 0, tiled=True)
 
 
 def half_norm(points):
@@ -315,25 +403,29 @@
     return 0.5 * jnp.sum(values * values, axis=1)
 
 
-def make_local(n_src, n_far):
+def make_local(n_src, n_z, n_x):
     near, n_near = ("src", "core"), n_src * CORES
+    n_far = n_z * n_x
 
     def local(source_points, target_points, source_mass, target_mass):
-        core = lax.axis_index("core")
-        place = jnp.stack([lax.axis_index("src"), core]).astype(jnp.int32)
+        core, x = lax.axis_index("core"), lax.axis_index("x")
+        place = jnp.stack([lax.axis_index("src"), core, x]).astype(jnp.int32)
+        along = lax.axis_index("z").astype(jnp.int32).reshape(1)
         part = source_points.shape[0]
-        a = source_mass.reshape(n_far, CORES, part)
-        a = lax.dynamic_index_in_dim(a, core, axis=1, keepdims=False).reshape(-1, LANES)
-        b = target_mass.reshape(-1, LANES)
-        blocks = swap_all(target_points, near, n_near)
-        masses = swap_all(b, "core", CORES)
-        sources = lax.all_gather(source_points, "far", axis=0, tiled=True)
-        blocks[0], masses[0], a = ready(target_points, b, a)
+        a = source_mass.reshape(n_z, n_x, CORES, part)
+        a = lax.dynamic_index_in_dim(a, core, axis=2, keepdims=False).swapaxes(0, 1).reshape(-1, LANES)
+        blocks = swap_all(target_points, "src", n_src)[1:]
+        sources = swap_all(source_points, "z", n_z)
+        packed, b, a = ready(target_points, target_mass.reshape(-1, LANES), a)
+        packed = swap_all(packed, "core", CORES)
+        blocks = blocks + [swap(block, "core", CORES, 1) for block in blocks]
+        groups = swap_all(pack(along, sources), "x", n_x)
         place, a = lax.optimization_barrier((place, a))
-        targets, b, own = first_rows(place, masses, sources, blocks)
-        plan, peak, own, row_lse = first_columns(sources, targets, share(own, n_far), a)
-        early_x, early_y, own = lax.optimization_barrier((sources, targets, own))
-        half_x, half_y = half_norm(early_x).reshape(-1, LANES), half_norm(early_y).reshape(-1, LANES)
+        targets, offsets, b, first = first_rows(place, b, packed, blocks, groups[0])
+        own = other_rows(place, targets, offsets, first, groups[1:])
+        plan, peak, own, row_lse, sources = first_columns(place, groups, targets, share(own, n_far), a)
+        early_y, own = lax.optimization_barrier((targets, own))
+        half_x, half_y = half_norm(sources).reshape(-1, LANES), half_norm(early_y).reshape(-1, LANES)
         parts = swap_all(own, near, n_near)
         half_x, half_y, *parts = lax.optimization_barrier((half_x, half_y, *parts))
         col_lse, reach, rows = second_rows(plan, peak, b, parts)
@@ -342,9 +434,9 @@
                 rows = later_rows(plan, reach, b, parts)
             own, potential = later_columns(plan, reach, share(rows, n_far), a, row_lse, half_x)
             parts = swap_all(own, near, n_near)
-        mine, other = swap_all(potential.reshape(n_far, part), "core", CORES)
+        mine, other = swap_all(potential.reshape(n_x, n_z, part), "core", CORES)
         low, high = jnp.where(core == 0, mine, other), jnp.where(core == 0, other, mine)
-        source_potential = jnp.stack([low, high], axis=1).reshape(-1)
+        source_potential = jnp.stack([low, high], axis=2).swapaxes(0, 1).reshape(-1)
         target_potential = half_y - UNIT * (col_lse + jnp.log2(tree(parts, jnp.add)))
         target_potential = target_potential.reshape(CORES, -1)
         target_potential = lax.dynamic_index_in_dim(target_potential, core, axis=0, keepdims=False)
@@ -355,13 +447,15 @@
 
 def solution(mesh):
     n_src, n_tgt = mesh.shape["src"], mesh.shape["tgt"]
-    n_far = n_tgt // CORES
-    split = Mesh(mesh.devices.reshape(n_src, n_far, CORES), ("src", "far", "core"))
-    placed = (P(("src", "far", "core"), None), P(("far", "core", "src"), None), P("src"), P(("far", "core")))
+    n_z = 4
+    n_x = n_tgt // (n_z * CORES)
+    split = Mesh(mesh.devices.reshape(n_src, n_z, n_x, CORES), ("src", "z", "x", "core"))
+    tgt = ("z", "x", "core")
+    placed = (P(("src", *tgt), None), P((*tgt, "src"), None), P("src"), P(tgt))
     return jax.shard_map(
-        make_local(n_src, n_far),
+        make_local(n_src, n_z, n_x),
         mesh=split,
         in_specs=placed,
-        out_specs=(P("src"), P(("far", "core"))),
+        out_specs=(P("src"), P(tgt)),
         check_vma=False,
     )

time: 90.6 us -> 68.4 us (0.75)
  blocking collectives: 61.8 us -> 27.5 us
  starting transfers between devices: 9.29 us -> 15.5 us
  waiting for transfers between devices: 5.64 us -> 9.31 us
  Pallas kernels: 9.27 us -> 10.7 us
    all_gather x1 -> x0, blocking collectives: 31.7 us -> none  [local(): sources = lax.all_gather(source_points, 'far', axis=0, tiled=True)]
    ppermute x14 -> x17, starting transfers between devices: 9.29 us -> 15.5 us  [swap(): return lax.ppermute(value, axes, [(i, i ^ distance) for i in range(size)])]
    ppermute x14 -> x17, waiting for transfers between devices: 5.64 us -> 9.31 us  [swap(): return lax.ppermute(value, axes, [(i, i ^ distance) for i in range(size)])]
    all_to_all x3, blocking collectives: 30.1 us -> 27.5 us  [share(): return lax.all_to_all(copies, ('z', 'x'), 0, 0, tiled=True)]
    pallas_call x1 -> x3, Pallas kernels: 0.01 us -> 1.79 us  [the longest x1 1.77 us: other_rows(): pl.pallas_call(kernel, out_shape=rows_of(count + each * LANES), in_specs=...]
    pallas_call x1, Pallas kernels: 3.1 us -> 2.18 us  [first_rows(): pl.pallas_call(kernel, out_shape=(pltpu.VMEM((width, LANES), jnp.bfloat16...]
    unnamed x6 -> x8, local copies, waits for them, and re-layouts: 1.6 us -> 2.35 us
  transfers between devices with their start and end apart: 14 -> 17, of which waited for: 6 -> 9; matrix products, arithmetic and copies ran while one was open for 1% -> 2% of each run, Pallas kernels for 0% -> 3%
where the time goes in v4:
time: 68.4 us; the launch traced here: 68 us
  blocking collectives  27.5 us (40%)
  starting transfers between devices  15.5 us (23%)
  Pallas kernels  10.7 us (16%)
  waiting for transfers between devices  9.31 us (14%)
  local copies, waits for them, and re-layouts  3 us (4%)
  other arithmetic  1.26 us (2%)
  between operations  0.82 us (1%)
    all_to_all x3, blocking collectives, share(): return lax.all_to_all(copies, ('z', 'x'), 0, 0, tiled=True)  27.5 us
    ppermute x17, starting transfers between devices, swap(): return lax.ppermute(value, axes, [(i, i ^ distance) for i in range(size)])  15.5 us
    ppermute x17, waiting for transfers between devices, swap(): return lax.ppermute(value, axes, [(i, i ^ distance) for i in range(size)])  9.31 us
    pallas_call x1, Pallas kernels, first_columns(): pl.pallas_call(kernel, out_shape=(pltpu.VMEM((width, count), F32), pltpu....  3.07 us
    unnamed x8, local copies, waits for them, and re-layouts  2.35 us
    pallas_call x1, Pallas kernels, first_rows(): pl.pallas_call(kernel, out_shape=(pltpu.VMEM((width, LANES), jnp.bfloat16...  2.18 us
    pallas_call x2, Pallas kernels, later_columns(): pl.pallas_call(kernel, out_shape=(rows_of(width), rows_of(count)), in_spe...  1.99 us
    pallas_call x1, Pallas kernels, other_rows(): pl.pallas_call(kernel, out_shape=rows_of(count + each * LANES), in_specs=...  1.77 us
  transfers between devices with their start and end apart: 17, of which 9 were waited for; matrix products, arithmetic and copies ran while one was open for 2% of the time, Pallas kernels for 3%

profile of v4, /device:TPU:0, one launch (start us, length us, event | category | flops | bytes accessed | tf_op | source)
XLA Modules:
  0.0 68.0 jit_solution(6187836490843618024)
XLA Ops:
  0.6 3.0 %collective-permute-start.4 = (bf16[512,128]{1,0:T(8,128)(2,1)}, bf16[512,128]{1,0:T(8,128)(2,1)S(1)}, u32[]{:S(2)}, u32[]{:S(2)}) collective-permute-start(bf16[512,128]{1,0:T(8,128)(2,1)} %targets_ref.1), channel_id=1, source_target_pairs={{0,16},{16,0},{1,17},{17,1},{2,18},{18,2},{3,19},{19,3},{4,20},{20... | collective-permute-start | bytes 393224 | tf_op jit(solution)/shard_map/ppermute | solution.py:385
  3.7 2.6 %collective-permute-start.1 = (bf16[128,128]{1,0:T(8,128)(2,1)}, bf16[128,128]{1,0:T(8,128)(2,1)S(1)}, u32[]{:S(2)}, u32[]{:S(2)}) collective-permute-start(bf16[128,128]{1,0:T(8,128)(2,1)} %refs_0_.1), channel_id=1, source_target_pairs={{0,8},{4,12},{8,0},{12,4},{1,9},{5,13},{9,1},{13,5},{2,10},{6,14},... | collective-permute-start | bytes 98312 | tf_op jit(solution)/shard_map/ppermute | solution.py:385
  6.3 1.6 %collective-permute-start = (bf16[128,128]{1,0:T(8,128)(2,1)}, bf16[128,128]{1,0:T(8,128)(2,1)S(1)}, u32[]{:S(2)}, u32[]{:S(2)}) collective-permute-start(bf16[128,128]{1,0:T(8,128)(2,1)} %refs_0_.1), channel_id=1, source_target_pairs={{0,4},{4,0},{8,12},{12,8},{1,5},{5,1},{9,13},{13,9},{2,6},{6,2},{1... | collective-permute-start | bytes 98312 | tf_op jit(solution)/shard_map/ppermute | solution.py:385
  8.1 0.9 %copy-done.1 = bf16[512,128]{1,0:T(8,128)(2,1)S(1)} copy-done((bf16[512,128]{1,0:T(8,128)(2,1)S(1)}, bf16[512,128]{1,0:T(8,128)(2,1)}, u32[]{:S(2)}) %copy-start.1) | copy-done | bytes 131096
  9.0 0.7 %copy-done.3 = f32[1024]{0:T(1024)S(1)} copy-done((f32[1024]{0:T(1024)S(1)}, f32[1024]{0:T(1024)}, u32[]{:S(2)}) %copy-start.3) | copy-done | bytes 4120
  10.4 3.4 %collective-permute-done.2.refs_3_ = bf16[128,128]{1,0:T(8,128)(2,1)S(1)} collective-permute-done((bf16[128,128]{1,0:T(8,128)(2,1)}, bf16[128,128]{1,0:T(8,128)(2,1)S(1)}, u32[]{:S(2)}, u32[]{:S(2)}) %collective-permute-start.2) | collective-permute-done | bytes 32800 | tf_op jit(solution)/shard_map/ppermute | solution.py:385
  13.8 0.8 %copy-done.2 = bf16[128,128]{1,0:T(8,128)(2,1)S(1)} copy-done((bf16[128,128]{1,0:T(8,128)(2,1)S(1)}, bf16[128,128]{1,0:T(8,128)(2,1)}, u32[]{:S(2)}) %copy-start.2) | copy-done | bytes 32792
  14.5 1.6 %collective-permute-start.6 = (bf16[512,128]{1,0:T(8,128)(2,1)S(1)}, bf16[512,128]{1,0:T(8,128)(2,1)S(1)}, u32[]{:S(2)}, u32[]{:S(2)}) collective-permute-start(bf16[512,128]{1,0:T(8,128)(2,1)S(1)} %pack.1.sources_ref.refs_0_), channel_id=1, source_target_pairs={{0,2},{2,0},{1,3},{3,1},{4,6},{6,4},{5,7},{7,5},{8,10},{10,8},{9,1... | collective-permute-start | bytes 393224 | tf_op jit(solution)/shard_map/ppermute | solution.py:385
  16.2 2.2 %first_rows.1 = (bf16[2048,128]{1,0:T(8,128)(2,1)S(1)}, bf16[2048,128]{1,0:T(8,128)(2,1)S(1)}, f32[16,128]{1,0:T(8,128)S(1)}, f32[4,128]{1,0:T(4,128)S(1)}) custom-call(s32[3]{0:T(128)S(1)} %pad_add_fusion.place_ref, f32[8,128]{1,0:T(8,128)S(1)} %get-tuple-element.32.mass_ref, bf16[512,128]{1,0:T(8,128)(2,1)S(1)} %pack.1.sources_ref.refs_0_, ...), custom_call_target="tpu_custom_call" | custom-call | flops 536870912 | bytes 1048576 | tf_op jit(solution)/shard_map/first_rows/pallas_call | solution.py:191
  18.4 1.2 %collective-permute-done.6.refs_0_.refs_1_ = bf16[512,128]{1,0:T(8,128)(2,1)S(1)} collective-permute-done((bf16[512,128]{1,0:T(8,128)(2,1)S(1)}, bf16[512,128]{1,0:T(8,128)(2,1)S(1)}, u32[]{:S(2)}, u32[]{:S(2)}) %collective-permute-start.6) | collective-permute-done | bytes 131104 | tf_op jit(solution)/shard_map/ppermute | solution.py:385
  19.6 1.8 %other_rows.1 = f32[8,128]{1,0:T(8,128)S(1)} custom-call(s32[3]{0:T(128)S(1)} %pad_add_fusion.place_ref, bf16[2048,128]{1,0:T(8,128)(2,1)S(1)} %get-tuple-element.43.targets_ref, bf16[2048,128]{1,0:T(8,128)(2,1)S(1)} %get-tuple-element.35.offset_ref, f32[4,128]{1,0:T(4,128)S(1)} %get-tuple-element.36.first_ref, ...), custom_call_target="tpu_custom_call" | custom-call | tf_op jit(solution)/shard_map/other_rows/pallas_call | solution.py:227
  21.4 9.3 %all_to_all.15.parts_ref = f32[8,8,128]{2,1,0:T(8,128)S(1)} all-to-all(f32[8,8,128]{2,1,0:T(8,128)S(1)} %broadcast_in_dim.6), channel_id=1, replica_groups=mesh['src'=2,'z'=4,'x'=2,'core'=2] {'z','x'}, dimensions={0} | all-to-all | bytes 65536 | tf_op jit(solution)/shard_map/all_to_all | solution.py:398
  30.7 3.1 %first_columns.1 = (f32[2048,1024]{1,0:T(8,128)S(1)}, f32[2048,128]{1,0:T(8,128)S(1)}, f32[16,128]{1,0:T(8,128)S(1)}, f32[8,128]{1,0:T(8,128)S(1)}, bf16[1024,128]{1,0:T(8,128)(2,1)S(1)}) custom-call(s32[3]{0:T(128)S(1)} %pad_add_fusion.place_ref, bf16[2048,128]{1,0:T(8,128)(2,1)S(1)} %get-tuple-element.43.targets_ref, ...), custom_call_target="tpu_custom_call" | custom-call | tf_op jit(solution)/shard_map/first_columns/pallas_call | solution.py:275
  34.4 1.3 %collective-permute-start.7 = (f32[16,128]{1,0:T(8,128)S(1)}, f32[16,128]{1,0:T(8,128)S(1)}, u32[]{:S(2)}, u32[]{:S(2)}) collective-permute-start(f32[16,128]{1,0:T(8,128)S(1)} %get-tuple-element.45.refs_0_), channel_id=1, source_target_pairs={{0,1},{1,0},{16,17},{17,16},{2,3},{3,2},{18,19},{19,18},{4,5},{5,4... | collective-permute-start | bytes 24584 | tf_op jit(solution)/shard_map/ppermute | solution.py:385
  37.6 0.9 %second_rows.1 = (f32[16,128]{1,0:T(8,128)S(1)}, f32[2048,128]{1,0:T(8,128)S(1)}, f32[8,128]{1,0:T(8,128)S(1)}) custom-call(f32[2048,1024]{1,0:T(8,128)S(1)} %get-tuple-element.38.plan_ref, f32[2048,128]{1,0:T(8,128)S(1)} %get-tuple-element.39.peak_ref, f32[16,128]{1,0:T(8,128)S(1)} %get-tuple-element.40.mass_ref, f32[16,128]{1,0:T(8,128)S(1)} %get-tuple-element.45.refs_0_, ...), custom_call_target="tpu_custom_call" | custom-call | tf_op jit(solution)/shard_map/second_rows/pallas_call | solution.py:320
  38.5 9.1 %all_to_all.16.parts_ref = f32[8,8,128]{2,1,0:T(8,128)S(1)} all-to-all(f32[8,8,128]{2,1,0:T(8,128)S(1)} %broadcast_in_dim.7), channel_id=1, replica_groups=mesh['src'=2,'z'=4,'x'=2,'core'=2] {'z','x'}, dimensions={0} | all-to-all | bytes 65536 | tf_op jit(solution)/shard_map/all_to_all | solution.py:398
  47.5 1.3 %later_columns.2 = (f32[16,128]{1,0:T(8,128)S(1)}, f32[8,128]{1,0:T(8,128)}) custom-call(f32[2048,1024]{1,0:T(8,128)S(1)} %get-tuple-element.38.plan_ref, f32[2048,128]{1,0:T(8,128)S(1)} %get-tuple-element.49.reach_ref, f32[8,8,128]{2,1,0:T(8,128)S(1)} %all_to_all.16.parts_ref, f32[8,128]{1,0:T(8,128)S(1)} %get-tuple-element.37.log_ref, ...), custom_call_target="tpu_custom_call" | custom-call | tf_op jit(solution)/shard_map/later_columns/pallas_call | solution.py:364
  49.3 1.3 %collective-permute-start.10 = (f32[16,128]{1,0:T(8,128)S(1)}, f32[16,128]{1,0:T(8,128)S(1)}, u32[]{:S(2)}, u32[]{:S(2)}) collective-permute-start(f32[16,128]{1,0:T(8,128)S(1)} %get-tuple-element.53.refs_0_), channel_id=1, source_target_pairs={{0,1},{1,0},{16,17},{17,16},{2,3},{3,2},{18,19},{19,18},{4,5},{5,4... | collective-permute-start | bytes 24584 | tf_op jit(solution)/shard_map/ppermute | solution.py:385
  50.6 1.2 %collective-permute-done.12.refs_3_ = f32[16,128]{1,0:T(8,128)S(1)} collective-permute-done((f32[16,128]{1,0:T(8,128)S(1)}, f32[16,128]{1,0:T(8,128)S(1)}, u32[]{:S(2)}, u32[]{:S(2)}) %collective-permute-start.12) | collective-permute-done | bytes 8224 | tf_op jit(solution)/shard_map/ppermute | solution.py:385
  52.5 0.7 %later_rows.1 = f32[8,128]{1,0:T(8,128)S(1)} custom-call(f32[2048,1024]{1,0:T(8,128)S(1)} %get-tuple-element.38.plan_ref, f32[2048,128]{1,0:T(8,128)S(1)} %get-tuple-element.49.reach_ref, f32[16,128]{1,0:T(8,128)S(1)} %get-tuple-element.40.mass_ref, f32[16,128]{1,0:T(8,128)S(1)} %get-tuple-element.53.refs_0_, f32[16,128]{1,0:T(8,128)S(1)} %collective-permute-done.10.refs_1_, ...), custom_call_target="tpu_custom_call" | custom-call | tf_op jit(solution)/shard_map/later_rows/pallas_call | solution.py:338
  53.2 9.1 %all_to_all.17.parts_ref = f32[8,8,128]{2,1,0:T(8,128)S(1)} all-to-all(f32[8,8,128]{2,1,0:T(8,128)S(1)} %broadcast_in_dim.8), channel_id=1, replica_groups=mesh['src'=2,'z'=4,'x'=2,'core'=2] {'z','x'}, dimensions={0} | all-to-all | bytes 65536 | tf_op jit(solution)/shard_map/all_to_all | solution.py:398
  62.3 0.7 %later_columns.3 = (f32[16,128]{1,0:T(8,128)S(1)}, f32[8,128]{1,0:T(8,128)S(1)}) custom-call(f32[2048,1024]{1,0:T(8,128)S(1)} %get-tuple-element.38.plan_ref, f32[2048,128]{1,0:T(8,128)S(1)} %get-tuple-element.49.reach_ref, f32[8,8,128]{2,1,0:T(8,128)S(1)} %all_to_all.17.parts_ref, f32[8,128]{1,0:T(8,128)S(1)} %get-tuple-element.37.log_ref, ...), custom_call_target="tpu_custom_call" | custom-call | tf_op jit(solution)/shard_map/later_columns/pallas_call | solution.py:364
  63.7 1.5 %collective-permute-start.15 = (f32[16,128]{1,0:T(8,128)S(1)}, f32[16,128]{1,0:T(8,128)S(1)}, u32[]{:S(2)}, u32[]{:S(2)}) collective-permute-start(f32[16,128]{1,0:T(8,128)S(1)} %get-tuple-element.57), channel_id=1, source_target_pairs={{0,16},{1,17},{16,0},{17,1},{2,18},{3,19},{18,2},{19,3},{4,20},{5,... | collective-permute-start | bytes 24584 | tf_op jit(solution)/shard_map/ppermute | solution.py:385
  66.3 1.1 %collective-permute-done.15 = f32[16,128]{1,0:T(8,128)S(1)} collective-permute-done((f32[16,128]{1,0:T(8,128)S(1)}, f32[16,128]{1,0:T(8,128)S(1)}, u32[]{:S(2)}, u32[]{:S(2)}) %collective-permute-start.15) | collective-permute-done | bytes 8224 | tf_op jit(solution)/shard_map/ppermute | solution.py:385
  (46 shorter events, 7.0 us)
Async XLA Ops:
  0.6 7.4 %copy-start = (f32[2048]{0:T(1024)S(1)}, f32[2048]{0:T(1024)}, u32[]{:S(2)}) copy-start(f32[2048]{0:T(1024)} %param.6) | copy-start | bytes 24580
  0.6 9.1 %collective-permute-start.4 = (bf16[512,128]{1,0:T(8,128)(2,1)}, bf16[512,128]{1,0:T(8,128)(2,1)S(1)}, u32[]{:S(2)}, u32[]{:S(2)}) collective-permute-start(bf16[512,128]{1,0:T(8,128)(2,1)} %targets_ref.1), channel_id=1, source_target_pairs={{0,16},{16,0},{1,17},{17,1},{2,18},{18,2},{3,19},{19,3},{4,20},{20... | collective-permute-start | bytes 393224 | tf_op jit(solution)/shard_map/ppermute | solution.py:385
  3.7 6.6 %collective-permute-start.1 = (bf16[128,128]{1,0:T(8,128)(2,1)}, bf16[128,128]{1,0:T(8,128)(2,1)S(1)}, u32[]{:S(2)}, u32[]{:S(2)}) collective-permute-start(bf16[128,128]{1,0:T(8,128)(2,1)} %refs_0_.1), channel_id=1, source_target_pairs={{0,8},{4,12},{8,0},{12,4},{1,9},{5,13},{9,1},{13,5},{2,10},{6,14},... | collective-permute-start | bytes 98312 | tf_op jit(solution)/shard_map/ppermute | solution.py:385
  6.3 4.1 %collective-permute-start = (bf16[128,128]{1,0:T(8,128)(2,1)}, bf16[128,128]{1,0:T(8,128)(2,1)S(1)}, u32[]{:S(2)}, u32[]{:S(2)}) collective-permute-start(bf16[128,128]{1,0:T(8,128)(2,1)} %refs_0_.1), channel_id=1, source_target_pairs={{0,4},{4,0},{8,12},{12,8},{1,5},{5,1},{9,13},{13,9},{2,6},{6,2},{1... | collective-permute-start | bytes 98312 | tf_op jit(solution)/shard_map/ppermute | solution.py:385
  7.8 5.9 %collective-permute-start.2 = (bf16[128,128]{1,0:T(8,128)(2,1)}, bf16[128,128]{1,0:T(8,128)(2,1)S(1)}, u32[]{:S(2)}, u32[]{:S(2)}) collective-permute-start(bf16[128,128]{1,0:T(8,128)(2,1)} %refs_0_.1), channel_id=1, source_target_pairs={{0,12},{4,8},{8,4},{12,0},{1,13},{5,9},{9,5},{13,1},{2,14},{6,10},... | collective-permute-start | bytes 98312 | tf_op jit(solution)/shard_map/ppermute | solution.py:385
  8.1 0.9 %copy-start.1 = (bf16[512,128]{1,0:T(8,128)(2,1)S(1)}, bf16[512,128]{1,0:T(8,128)(2,1)}, u32[]{:S(2)}) copy-start(bf16[512,128]{1,0:T(8,128)(2,1)} %targets_ref.1) | copy-start | bytes 393220
  9.0 0.7 %copy-start.3 = (f32[1024]{0:T(1024)S(1)}, f32[1024]{0:T(1024)}, u32[]{:S(2)}) copy-start(f32[1024]{0:T(1024)} %param.7) | copy-start | bytes 12292
  9.7 6.5 %collective-permute-start.3 = (bf16[544,128]{1,0:T(8,128)(2,1)S(1)}, bf16[544,128]{1,0:T(8,128)(2,1)S(1)}, u32[]{:S(2)}, u32[]{:S(2)}) collective-permute-start(bf16[544,128]{1,0:T(8,128)(2,1)S(1)} %get-tuple-element.33.refs_0_), channel_id=1, source_target_pairs={{0,1},{1,0},{2,3},{3,2},{4,5},{5,4},{6,7},{7,6},{8,9},{9,8},{10,11... | collective-permute-start | bytes 417800 | tf_op jit(solution)/shard_map/ppermute | solution.py:385
  9.8 6.4 %collective-permute-start.5 = (bf16[512,128]{1,0:T(8,128)(2,1)S(1)}, bf16[512,128]{1,0:T(8,128)(2,1)S(1)}, u32[]{:S(2)}, u32[]{:S(2)}) collective-permute-start(bf16[512,128]{1,0:T(8,128)(2,1)S(1)} %collective-permute-done.4.refs_2_), channel_id=1, source_target_pairs={{0,1},{1,0},{2,3},{3,2},{4,5},{5,4},{6,7},{7,6},{8,9},{9,8},{10,11... | collective-permute-start | bytes 393224 | tf_op jit(solution)/shard_map/ppermute | solution.py:385
  13.8 0.8 %copy-start.2 = (bf16[128,128]{1,0:T(8,128)(2,1)S(1)}, bf16[128,128]{1,0:T(8,128)(2,1)}, u32[]{:S(2)}) copy-start(bf16[128,128]{1,0:T(8,128)(2,1)} %refs_0_.1) | copy-start | bytes 98308
  14.5 5.0 %collective-permute-start.6 = (bf16[512,128]{1,0:T(8,128)(2,1)S(1)}, bf16[512,128]{1,0:T(8,128)(2,1)S(1)}, u32[]{:S(2)}, u32[]{:S(2)}) collective-permute-start(bf16[512,128]{1,0:T(8,128)(2,1)S(1)} %pack.1.sources_ref.refs_0_), channel_id=1, source_target_pairs={{0,2},{2,0},{1,3},{3,1},{4,6},{6,4},{5,7},{7,5},{8,10},{10,8},{9,1... | collective-permute-start | bytes 393224 | tf_op jit(solution)/shard_map/ppermute | solution.py:385
  33.8 3.1 %collective-permute-start.9 = (f32[16,128]{1,0:T(8,128)S(1)}, f32[16,128]{1,0:T(8,128)S(1)}, u32[]{:S(2)}, u32[]{:S(2)}) collective-permute-start(f32[16,128]{1,0:T(8,128)S(1)} %get-tuple-element.45.refs_0_), channel_id=1, source_target_pairs={{0,17},{1,16},{16,1},{17,0},{2,19},{3,18},{18,3},{19,2},{4,21},{5,... | collective-permute-start | bytes 24584 | tf_op jit(solution)/shard_map/ppermute | solution.py:385
  33.8 3.7 %collective-permute-start.8 = (f32[16,128]{1,0:T(8,128)S(1)}, f32[16,128]{1,0:T(8,128)S(1)}, u32[]{:S(2)}, u32[]{:S(2)}) collective-permute-start(f32[16,128]{1,0:T(8,128)S(1)} %get-tuple-element.45.refs_0_), channel_id=1, source_target_pairs={{0,16},{1,17},{16,0},{17,1},{2,18},{3,19},{18,2},{19,3},{4,20},{5,... | collective-permute-start | bytes 24584 | tf_op jit(solution)/shard_map/ppermute | solution.py:385
  34.4 3.2 %collective-permute-start.7 = (f32[16,128]{1,0:T(8,128)S(1)}, f32[16,128]{1,0:T(8,128)S(1)}, u32[]{:S(2)}, u32[]{:S(2)}) collective-permute-start(f32[16,128]{1,0:T(8,128)S(1)} %get-tuple-element.45.refs_0_), channel_id=1, source_target_pairs={{0,1},{1,0},{16,17},{17,16},{2,3},{3,2},{18,19},{19,18},{4,5},{5,4... | collective-permute-start | bytes 24584 | tf_op jit(solution)/shard_map/ppermute | solution.py:385
  48.8 3.1 %collective-permute-start.12 = (f32[16,128]{1,0:T(8,128)S(1)}, f32[16,128]{1,0:T(8,128)S(1)}, u32[]{:S(2)}, u32[]{:S(2)}) collective-permute-start(f32[16,128]{1,0:T(8,128)S(1)} %get-tuple-element.53.refs_0_), channel_id=1, source_target_pairs={{0,17},{1,16},{16,1},{17,0},{2,19},{3,18},{18,3},{19,2},{4,21},{5,... | collective-permute-start | bytes 24584 | tf_op jit(solution)/shard_map/ppermute | solution.py:385
  48.8 3.7 %collective-permute-start.11 = (f32[16,128]{1,0:T(8,128)S(1)}, f32[16,128]{1,0:T(8,128)S(1)}, u32[]{:S(2)}, u32[]{:S(2)}) collective-permute-start(f32[16,128]{1,0:T(8,128)S(1)} %get-tuple-element.53.refs_0_), channel_id=1, source_target_pairs={{0,16},{1,17},{16,0},{17,1},{2,18},{3,19},{18,2},{19,3},{4,20},{5,... | collective-permute-start | bytes 24584 | tf_op jit(solution)/shard_map/ppermute | solution.py:385
  49.3 3.2 %collective-permute-start.10 = (f32[16,128]{1,0:T(8,128)S(1)}, f32[16,128]{1,0:T(8,128)S(1)}, u32[]{:S(2)}, u32[]{:S(2)}) collective-permute-start(f32[16,128]{1,0:T(8,128)S(1)} %get-tuple-element.53.refs_0_), channel_id=1, source_target_pairs={{0,1},{1,0},{16,17},{17,16},{2,3},{3,2},{18,19},{19,18},{4,5},{5,4... | collective-permute-start | bytes 24584 | tf_op jit(solution)/shard_map/ppermute | solution.py:385
  63.0 2.2 %collective-permute-start.13 = (f32[2,4,128]{2,0,1:T(2,128)S(1)}, f32[2,4,128]{2,0,1:T(2,128)S(1)}, u32[]{:S(2)}, u32[]{:S(2)}) collective-permute-start(f32[2,4,128]{2,0,1:T(2,128)S(1)} %copy.12), channel_id=1, source_target_pairs={{0,1},{1,0},{2,3},{3,2},{4,5},{5,4},{6,7},{7,6},{8,9},{9,8},{10,11... | collective-permute-start | bytes 12296 | tf_op jit(solution)/shard_map/ppermute | solution.py:385
  63.1 3.1 %collective-permute-start.16 = (f32[16,128]{1,0:T(8,128)S(1)}, f32[16,128]{1,0:T(8,128)S(1)}, u32[]{:S(2)}, u32[]{:S(2)}) collective-permute-start(f32[16,128]{1,0:T(8,128)S(1)} %get-tuple-element.57), channel_id=1, source_target_pairs={{0,17},{1,16},{16,1},{17,0},{2,19},{3,18},{18,3},{19,2},{4,21},{5,... | collective-permute-start | bytes 24584 | tf_op jit(solution)/shard_map/ppermute | solution.py:385
  63.7 3.7 %collective-permute-start.15 = (f32[16,128]{1,0:T(8,128)S(1)}, f32[16,128]{1,0:T(8,128)S(1)}, u32[]{:S(2)}, u32[]{:S(2)}) collective-permute-start(f32[16,128]{1,0:T(8,128)S(1)} %get-tuple-element.57), channel_id=1, source_target_pairs={{0,16},{1,17},{16,0},{17,1},{2,18},{3,19},{18,2},{19,3},{4,20},{5,... | collective-permute-start | bytes 24584 | tf_op jit(solution)/shard_map/ppermute | solution.py:385
  65.3 2.1 %collective-permute-start.14 = (f32[16,128]{1,0:T(8,128)S(1)}, f32[16,128]{1,0:T(8,128)S(1)}, u32[]{:S(2)}, u32[]{:S(2)}) collective-permute-start(f32[16,128]{1,0:T(8,128)S(1)} %get-tuple-element.57), channel_id=1, source_target_pairs={{0,1},{1,0},{16,17},{17,16},{2,3},{3,2},{18,19},{19,18},{4,5},{5,4... | collective-permute-start | bytes 24584 | tf_op jit(solution)/shard_map/ppermute | solution.py:385

commit v5 on v4

--- a/solution.py
+++ b/solution.py
@@ -69,53 +69,44 @@
     return lax.dot_general(rows, cols, (((1,), (1,)), ((), ())), preferred_element_type=F32)
 
 
-def ready(targets, mass, source_mass):
+def ready(sources, targets, mass, source_mass):
     part, chunk = targets.shape[0], mass.shape[0]
-
-    def kernel(targets_ref, mass_ref, source_ref, packed_ref, mass_out, source_out):
-        packed_ref[:part, :] = targets_ref[...]
-        mass_out[...] = mass_ref[...]
+    anywhere = pl.BlockSpec(memory_space=pl.ANY)
+
+    def kernel(sources_ref, targets_ref, mass_ref, source_ref, sources_out, packed_ref, mass_out, source_out, *sems):
+        copies = [
+            pltpu.make_async_copy(mass_ref, mass_out, sems[0]),
+            pltpu.make_async_copy(targets_ref, packed_ref.at[:part], sems[1]),
+            pltpu.make_async_copy(sources_ref, sources_out, sems[2]),
+        ]
+        for copy in copies:
+            copy.start()
         source_out[...] = jnp.log2(source_ref[...])
-        value, pieces = mass_ref[...], []
+        copies[0].wait()
+        value, pieces = mass_out[...], []
         for step in range(PIECES):
             pieces.append(value.astype(jnp.bfloat16).astype(F32))
             value = value - pieces[-1]
         pieces.append(jnp.zeros_like(value))
         packed_ref[part:, :] = jnp.concatenate(pieces, axis=0).astype(jnp.bfloat16)
+        copies[1].wait()
+        copies[2].wait()
 
     return pl.pallas_call(
         kernel,
         out_shape=(
+            pltpu.VMEM(sources.shape, jnp.bfloat16),
             pltpu.VMEM((part + (PIECES + 1) * chunk, LANES), jnp.bfloat16),
             pltpu.VMEM(mass.shape, F32),
             pltpu.VMEM(source_mass.shape, F32),
         ),
-        in_specs=[VMEM] * 3,
-        out_specs=(VMEM,) * 3,
+        in_specs=[anywhere, anywhere, anywhere, VMEM],
+        out_specs=(VMEM,) * 4,
+        scratch_shapes=[pltpu.SemaphoreType.DMA] * 3,
         compiler_params=params(),
         cost_estimate=pl.CostEstimate(flops=1 << 20, bytes_accessed=1 << 20, transcendentals=0),
         name="ready",
-    )(targets, mass, source_mass)
-
-
-def pack(place, blocks):
-    part = blocks[0].shape[0]
-
-    def kernel(place_ref, *refs):
-        out_ref = refs[-1]
-        for step in range(len(blocks)):
-            start = pl.multiple_of(jnp.bitwise_xor(place_ref[0], step) * part, part)
-            out_ref[pl.ds(start, part), :] = refs[step][...]
-
-    return pl.pallas_call(
-        kernel,
-        out_shape=pltpu.VMEM((len(blocks) * part, LANES), jnp.bfloat16),
-        in_specs=[SMEM] + [VMEM] * len(blocks),
-        out_specs=VMEM,
-        compiler_params=params(),
-        cost_estimate=pl.CostEstimate(flops=1 << 20, bytes_accessed=1 << 18, transcendentals=0),
-        name="pack",
-    )(place, *blocks)
+    )(*[pltpu.with_memory_space_constraint(value, pltpu.HBM) for value in (sources, targets, mass)], source_mass)
 
 
 def pieces_of(value):
@@ -153,15 +144,75 @@
         return widest * SCALE + jnp.log2(total)
 
 
-def first_rows(place, mass, packed, blocks, sources):
-    count, chunk = sources.shape[0], mass.shape[0]
-    n_src = len(blocks) // CORES + 1
-    part = blocks[0].shape[0]
+class Units:
+    def __init__(self, blocks, low, high):
+        self.part = blocks[0][0].shape[0]
+        self.each = max(1, LANES // self.part)
+        self.n_z = len(blocks[0]) // self.each
+        self.steps = [(dx, dz) for dz in range(low // self.each, high // self.each) for dx in range(len(blocks))]
+        self.arrays = [blocks[dx][dz * self.each + inner] for dx, dz in self.steps for inner in range(self.each)]
+        self.size = self.part * self.each
+        self.count = self.size * len(self.steps)
+
+    def place(self, place_ref, refs, out_ref, starts):
+        for step, start in enumerate(starts):
+            for inner in range(self.each):
+                at = start
+                if self.each > 1:
+                    low = jnp.bitwise_and(place_ref[3], self.each - 1)
+                    at = pl.multiple_of(start + jnp.bitwise_xor(low, inner) * self.part, self.part)
+                out_ref[pl.ds(at, self.part), :] = refs[step * self.each + inner][...]
+
+    def columns(self, place_ref, refs, scratch_ref):
+        if self.each == 1:
+            return jnp.concatenate([ref[...] for ref in refs], axis=0)
+        self.place(place_ref, refs, scratch_ref, range(0, self.count, self.size))
+        return scratch_ref[...]
+
+    def starts(self, place_ref):
+        high = place_ref[3] // self.each
+        return [
+            pl.multiple_of((jnp.bitwise_xor(place_ref[2], dx) * self.n_z + jnp.bitwise_xor(high, dz)) * self.size, self.size)
+            for dx, dz in self.steps
+        ]
+
+    def write(self, place_ref, lse, out_ref):
+        rows = self.size // LANES
+        for step, start in enumerate(self.starts(place_ref)):
+            for row in range(rows):
+                at = (step * rows + row) * LANES
+                out_ref[pl.ds(start // LANES + row, 1), :] = lse[:, at : at + LANES]
+
+
+class Rows:
+    def __init__(self, count):
+        self.peak = jnp.full((8, count), -1e30, F32)
+        self.total = jnp.zeros((8, count), F32)
+
+    def add(self, scores_ref):
+        tops = self.peak
+        for row in range(0, ROWS, 8):
+            tops = jnp.maximum(tops, scores_ref[row : row + 8, :])
+        self.total = self.total * jnp.exp2((self.peak - tops) * SCALE)
+        self.peak = tops
+        for row in range(0, ROWS, 8):
+            self.total = self.total + jnp.exp2((scores_ref[row : row + 8, :] - tops) * SCALE)
+
+    def lse(self):
+        widest = jnp.max(self.peak, axis=0, keepdims=True)
+        total = jnp.sum(self.total * jnp.exp2((self.peak - widest) * SCALE), axis=0, keepdims=True)
+        return widest * SCALE + jnp.log2(total)
+
+
+def first_rows(place, mass, packed, blocks, units, total_rows):
+    chunk, part = mass.shape[0], packed[0].shape[0] - (PIECES + 1) * mass.shape[0]
+    n_src, n_units = len(blocks) // CORES + 1, len(units.arrays)
     width = CORES * n_src * part
 
-    def kernel(place_ref, mass_ref, sources_ref, *refs):
-        own_ref, other_ref, block_refs = refs[0], refs[1], refs[2 : 2 + len(blocks)]
-        targets_ref, offset_ref, full_ref, out_ref, *score_refs = refs[2 + len(blocks) :]
+    def kernel(place_ref, mass_ref, *refs):
+        unit_refs, refs = refs[:n_units], refs[n_units:]
+        other_ref, block_refs = refs[1], refs[2 : 2 + len(blocks)]
+        targets_ref, offset_ref, full_ref, out_ref, scratch_ref, *score_refs = refs[2 + len(blocks) :]
         src, core = place_ref[0], place_ref[1]
         full_ref[pl.ds(pl.multiple_of(core * chunk, chunk), chunk), :] = mass_ref[...]
         parts = [other_ref[part + i * chunk : part + (i + 1) * chunk, :].astype(F32) for i in range(PIECES)]
@@ -175,8 +226,8 @@
                 targets_ref[pl.ds(start, part), :] = ref[:part, :]
         mask = diagonal()
         log_mass = jnp.log2(full_ref[...]) * (1.0 / SCALE)
-        cols = jnp.concatenate([sources_ref[...], ones_for(count)], axis=1)
-        rows = Rows(count)
+        cols = jnp.concatenate([units.columns(place_ref, unit_refs, scratch_ref), ones_for(units.count)], axis=1)
+        rows = Rows(units.count)
         for at in range(0, width, ROWS):
             scores_ref = score_refs[at // ROWS % len(score_refs)]
             for row in range(at, at + ROWS, LANES):
@@ -186,7 +237,8 @@
                 offset_ref[row : row + LANES, :] = pieces_of(to_column(log_mass[block : block + 1, :], mask) - half)
             scores_ref[...] = product(jnp.concatenate([targets_ref[at : at + ROWS, :], offset_ref[at : at + ROWS, :]], axis=1), cols)
             rows.add(scores_ref)
-        fold_into(out_ref, rows.lse())
+        out_ref[...] = jnp.zeros_like(out_ref)
+        units.write(place_ref, rows.lse(), out_ref)
 
     return pl.pallas_call(
         kernel,
@@ -194,56 +246,50 @@
             pltpu.VMEM((width, LANES), jnp.bfloat16),
             pltpu.VMEM((width, LANES), jnp.bfloat16),
             rows_of(width),
-            rows_of(count),
+            pltpu.VMEM((total_rows, LANES), F32),
         ),
-        in_specs=[SMEM] + [VMEM] * (4 + len(blocks)),
+        in_specs=[SMEM] + [VMEM] * (3 + len(blocks) + n_units),
         out_specs=(VMEM,) * 4,
-        scratch_shapes=[pltpu.VMEM((ROWS, count), F32)] * 2,
+        scratch_shapes=[pltpu.VMEM((units.count, LANES), jnp.bfloat16)] + [pltpu.VMEM((ROWS, units.count), F32)] * 2,
         compiler_params=params(),
         cost_estimate=pl.CostEstimate(flops=1 << 29, bytes_accessed=1 << 20, transcendentals=1 << 20),
         name="first_rows",
-    )(place, mass, pin(sources), *[pin(value) for value in packed], *[pin(value) for value in blocks])
-
-
-def other_rows(place, targets, offsets, first, groups):
-    width, count, each = targets.shape[0], sum(group.shape[0] for group in groups), groups[0].shape[0] // LANES
+    )(place, mass, *[pin(value) for value in units.arrays], *[pin(value) for value in packed], *[pin(value) for value in blocks])
+
+
+def other_rows(place, targets, offsets, first, early, late):
+    width, n_early = targets.shape[0], len(early.arrays)
+    total = early.count + late.count
 
     def kernel(place_ref, targets_ref, offset_ref, first_ref, *refs):
-        group_refs, (out_ref, *score_refs) = refs[: len(groups)], refs[len(groups) :]
-        cols = jnp.concatenate([ref[...] for ref in group_refs], axis=0)
-        cols = jnp.concatenate([cols, ones_for(count)], axis=1)
-        rows = Rows(count)
+        early_refs, late_refs = refs[:n_early], refs[n_early : n_early + len(late.arrays)]
+        out_ref, sources_ref, scratch_ref, *score_refs = refs[n_early + len(late.arrays) :]
+        cols = jnp.concatenate([late.columns(place_ref, late_refs, scratch_ref), ones_for(late.count)], axis=1)
+        rows = Rows(late.count)
         for at in range(0, width, ROWS):
             scores_ref = score_refs[at // ROWS % len(score_refs)]
             scores_ref[...] = product(jnp.concatenate([targets_ref[at : at + ROWS, :], offset_ref[at : at + ROWS, :]], axis=1), cols)
             rows.add(scores_ref)
-        lse = rows.lse()
-        for step in range(len(groups) + 1):
-            start = jnp.bitwise_xor(place_ref[2], step) * each
-            for row in range(each):
-                at = ((step - 1) * each + row) * LANES
-                out_ref[pl.ds(start + row, 1), :] = first_ref[row : row + 1, :] if step == 0 else lse[:, at : at + LANES]
-
-    return pl.pallas_call(
-        kernel,
-        out_shape=rows_of(count + each * LANES),
-        in_specs=[SMEM] + [VMEM] * (3 + len(groups)),
-        out_specs=VMEM,
-        scratch_shapes=[pltpu.VMEM((ROWS, count), F32)] * 2,
+        early.place(place_ref, early_refs, sources_ref, early.starts(place_ref))
+        late.place(place_ref, late_refs, sources_ref, late.starts(place_ref))
+        out_ref[...] = first_ref[...]
+        late.write(place_ref, rows.lse(), out_ref)
+
+    return pl.pallas_call(
+        kernel,
+        out_shape=(rows_of(total), pltpu.VMEM((total, LANES), jnp.bfloat16)),
+        in_specs=[SMEM] + [VMEM] * (3 + n_early + len(late.arrays)),
+        out_specs=(VMEM,) * 2,
+        scratch_shapes=[pltpu.VMEM((late.count, LANES), jnp.bfloat16)] + [pltpu.VMEM((ROWS, late.count), F32)] * 2,
         compiler_params=params(),
         name="other_rows",
-    )(place, pin(targets), pin(offsets), first, *groups)
-
-
-def first_columns(place, groups, targets, parts, log_mass):
-    each, width = groups[0].shape[0], targets.shape[0]
-    count = each * len(groups)
-
-    def kernel(place_ref, targets_ref, parts_ref, log_ref, *refs):
-        group_refs, (plan_ref, peak_ref, out_ref, lse_ref, sources_ref, *score_refs) = refs[: len(groups)], refs[len(groups) :]
-        for step in range(len(groups)):
-            start = pl.multiple_of(jnp.bitwise_xor(place_ref[2], step) * each, each)
-            sources_ref[pl.ds(start, each), :] = group_refs[step][...]
+    )(place, pin(targets), pin(offsets), pin(first), *[pin(value) for value in early.arrays], *[pin(value) for value in late.arrays])
+
+
+def first_columns(sources, targets, parts, log_mass):
+    count, width = sources.shape[0], targets.shape[0]
+
+    def kernel(sources_ref, targets_ref, parts_ref, log_ref, plan_ref, peak_ref, out_ref, lse_ref, *score_refs):
         lse = log_sum([parts_ref[i] for i in range(parts.shape[0])])
         lse_ref[...] = lse
         mask = diagonal()
@@ -279,14 +325,13 @@
             pltpu.VMEM((width, LANES), F32),
             rows_of(width),
             rows_of(count),
-            pltpu.VMEM((count, LANES), jnp.bfloat16),
         ),
-        in_specs=[SMEM] + [VMEM] * (3 + len(groups)),
-        out_specs=(VMEM,) * 5,
+        in_specs=[VMEM] * 4,
+        out_specs=(VMEM,) * 4,
         scratch_shapes=[pltpu.VMEM((ROWS, count), F32)] * 2,
         compiler_params=params(),
         name="first_columns",
-    )(place, pin(targets), parts, log_mass, *[pin(group) for group in groups])
+    )(pin(sources), pin(targets), parts, log_mass)
 
 
 def weighted_rows(reach_of, weight, plan_ref, out_ref):
@@ -408,24 +453,28 @@
     n_far = n_z * n_x
 
     def local(source_points, target_points, source_mass, target_mass):
-        core, x = lax.axis_index("core"), lax.axis_index("x")
-        place = jnp.stack([lax.axis_index("src"), core, x]).astype(jnp.int32)
-        along = lax.axis_index("z").astype(jnp.int32).reshape(1)
+        core = lax.axis_index("core")
+        place = jnp.stack([lax.axis_index(axis) for axis in ("src", "core", "x", "z")]).astype(jnp.int32)
         part = source_points.shape[0]
         a = source_mass.reshape(n_z, n_x, CORES, part)
         a = lax.dynamic_index_in_dim(a, core, axis=2, keepdims=False).swapaxes(0, 1).reshape(-1, LANES)
+        two = swap(source_points, "z", n_z, 2)
         blocks = swap_all(target_points, "src", n_src)[1:]
-        sources = swap_all(source_points, "z", n_z)
-        packed, b, a = ready(target_points, target_mass.reshape(-1, LANES), a)
+        one = swap(source_points, "z", n_z, 1)
+        sources = [source_points, one, two, swap(two, "z", n_z, 1)]
+        across = [[swap(block, "x", n_x, dx) for block in sources] for dx in range(1, n_x)]
+        mine, packed, b, a = ready(source_points, target_points, target_mass.reshape(-1, LANES), a)
+        sources = [[mine, *sources[1:]], *across]
         packed = swap_all(packed, "core", CORES)
         blocks = blocks + [swap(block, "core", CORES, 1) for block in blocks]
-        groups = swap_all(pack(along, sources), "x", n_x)
         place, a = lax.optimization_barrier((place, a))
-        targets, offsets, b, first = first_rows(place, b, packed, blocks, groups[0])
-        own = other_rows(place, targets, offsets, first, groups[1:])
-        plan, peak, own, row_lse, sources = first_columns(place, groups, targets, share(own, n_far), a)
-        early_y, own = lax.optimization_barrier((targets, own))
-        half_x, half_y = half_norm(sources).reshape(-1, LANES), half_norm(early_y).reshape(-1, LANES)
+        last = n_z - max(1, LANES // part)
+        early, late = Units(sources, 0, last), Units(sources, last, n_z)
+        targets, offsets, b, first = first_rows(place, b, packed, blocks, early, a.shape[0])
+        own, sources = other_rows(place, targets, offsets, first, early, late)
+        plan, peak, own, row_lse = first_columns(sources, targets, share(own, n_far), a)
+        early_x, early_y, own = lax.optimization_barrier((sources, targets, own))
+        half_x, half_y = half_norm(early_x).reshape(-1, LANES), half_norm(early_y).reshape(-1, LANES)
         parts = swap_all(own, near, n_near)
         half_x, half_y, *parts = lax.optimization_barrier((half_x, half_y, *parts))
         col_lse, reach, rows = second_rows(plan, peak, b, parts)

time: 68.4 us -> 68.7 us (level)
  starting transfers between devices: 15.5 us -> 18.7 us
  waiting for transfers between devices: 9.31 us -> 6.44 us
  local copies, waits for them, and re-layouts: 3 us -> 0.65 us
  blocking collectives: 27.5 us -> 29.6 us
    ppermute x17 -> x20, starting transfers between devices: 15.5 us -> 18.7 us  [swap(): return lax.ppermute(value, axes, [(i, i ^ distance) for i in range(size)])]
    ppermute x17 -> x20, waiting for transfers between devices: 9.31 us -> 6.44 us  [swap(): return lax.ppermute(value, axes, [(i, i ^ distance) for i in range(size)])]
    unnamed x8 -> x2, local copies, waits for them, and re-layouts: 2.35 us -> 0.01 us
    all_to_all x3, blocking collectives: 27.5 us -> 29.6 us  [share(): return lax.all_to_all(copies, ('z', 'x'), 0, 0, tiled=True)]
    pallas_call x3 -> x2, Pallas kernels: 1.79 us -> 2.19 us  [the longest x1 1.24 us: other_rows(): pl.pallas_call(kernel, out_shape=(rows_of(total), pltpu.VMEM((total, LANE...]
  transfers between devices with their start and end apart: 17 -> 20, of which waited for: 9 -> 9; matrix products, arithmetic and copies ran while one was open for 2% -> 2% of each run, Pallas kernels for 3% -> 5%
where the time goes in v5:
time: 68.7 us; the launch traced here: 68.4 us
  blocking collectives  29.6 us (43%)
  starting transfers between devices  18.7 us (27%)
  Pallas kernels  10.9 us (16%)
  waiting for transfers between devices  6.44 us (9%)
  other arithmetic  1.26 us (2%)
  between operations  0.83 us (1%)
    all_to_all x3, blocking collectives, share(): return lax.all_to_all(copies, ('z', 'x'), 0, 0, tiled=True)  29.6 us
    ppermute x20, starting transfers between devices, swap(): return lax.ppermute(value, axes, [(i, i ^ distance) for i in range(size)])  18.7 us
    ppermute x20, waiting for transfers between devices, swap(): return lax.ppermute(value, axes, [(i, i ^ distance) for i in range(size)])  6.44 us
    pallas_call x1, Pallas kernels, first_rows(): pl.pallas_call(kernel, out_shape=(pltpu.VMEM((width, LANES), jnp.bfloat16...  2.66 us
    pallas_call x1, Pallas kernels, first_columns(): pl.pallas_call(kernel, out_shape=(pltpu.VMEM((width, count), F32), pltpu....  2.47 us
    pallas_call x2, Pallas kernels, later_columns(): pl.pallas_call(kernel, out_shape=(rows_of(width), rows_of(count)), in_spe...  1.99 us
  transfers between devices with their start and end apart: 20, of which 9 were waited for; matrix products, arithmetic and copies ran while one was open for 2% of the time, Pallas kernels for 5%

profile of v5, /device:TPU:0, one launch (start us, length us, event | category | flops | bytes accessed | tf_op | source)
XLA Modules:
  0.0 68.4 jit_solution(6132972548566064097)
XLA Ops:
  0.6 3.0 %collective-permute-start.6 = (bf16[512,128]{1,0:T(8,128)(2,1)}, bf16[512,128]{1,0:T(8,128)(2,1)S(1)}, u32[]{:S(2)}, u32[]{:S(2)}) collective-permute-start(bf16[512,128]{1,0:T(8,128)(2,1)} %targets_ref.1), channel_id=1, source_target_pairs={{0,16},{16,0},{1,17},{17,1},{2,18},{18,2},{3,19},{19,3},{4,20},{20... | collective-permute-start | bytes 393224 | tf_op jit(solution)/shard_map/ppermute | solution.py:430
  3.7 1.5 %collective-permute-start = (bf16[128,128]{1,0:T(8,128)(2,1)}, bf16[128,128]{1,0:T(8,128)(2,1)S(1)}, u32[]{:S(2)}, u32[]{:S(2)}) collective-permute-start(bf16[128,128]{1,0:T(8,128)(2,1)} %sources_ref.1), channel_id=1, source_target_pairs={{0,2},{2,0},{1,3},{3,1},{4,6},{6,4},{5,7},{7,5},{8,10},{10,8},{9,1... | collective-permute-start | bytes 98312 | tf_op jit(solution)/shard_map/ppermute | solution.py:430
  5.2 2.6 %collective-permute-start.3 = (bf16[128,128]{1,0:T(8,128)(2,1)}, bf16[128,128]{1,0:T(8,128)(2,1)S(1)}, u32[]{:S(2)}, u32[]{:S(2)}) collective-permute-start(bf16[128,128]{1,0:T(8,128)(2,1)} %sources_ref.1), channel_id=1, source_target_pairs={{0,8},{4,12},{8,0},{12,4},{1,9},{5,13},{9,1},{13,5},{2,10},{6,14},... | collective-permute-start | bytes 98312 | tf_op jit(solution)/shard_map/ppermute | solution.py:430
  7.8 1.6 %collective-permute-start.1 = (bf16[128,128]{1,0:T(8,128)(2,1)}, bf16[128,128]{1,0:T(8,128)(2,1)S(1)}, u32[]{:S(2)}, u32[]{:S(2)}) collective-permute-start(bf16[128,128]{1,0:T(8,128)(2,1)} %sources_ref.1), channel_id=1, source_target_pairs={{0,4},{4,0},{8,12},{12,8},{1,5},{5,1},{9,13},{13,9},{2,6},{6,2},{1... | collective-permute-start | bytes 98312 | tf_op jit(solution)/shard_map/ppermute | solution.py:430
  9.4 1.0 %ready.1 = (bf16[128,128]{1,0:T(8,128)(2,1)S(1)}, bf16[544,128]{1,0:T(8,128)(2,1)S(1)}, f32[8,128]{1,0:T(8,128)S(1)}, f32[8,128]{1,0:T(8,128)S(1)}) custom-call(bf16[128,128]{1,0:T(8,128)(2,1)} %sources_ref.1, bf16[512,128]{1,0:T(8,128)(2,1)} %targets_ref.1, f32[8,128]{1,0:T(8,128)} %bitcast.31, f32[8,128]{1,0:T(8,128)S(1)} %bitcast.24), custom_call_target="tpu_custom_call" | custom-call | flops 1048576 | bytes 1048576 | tf_op jit(solution)/shard_map/ready/pallas_call | solution.py:95
  10.9 0.9 %collective-permute-start.8 = (bf16[128,128]{1,0:T(8,128)(2,1)S(1)}, bf16[128,128]{1,0:T(8,128)(2,1)S(1)}, u32[]{:S(2)}, u32[]{:S(2)}) collective-permute-start(bf16[128,128]{1,0:T(8,128)(2,1)S(1)} %collective-permute-done.3.refs_4_), channel_id=1, source_target_pairs={{0,4},{4,0},{8,12},{12,8},{1,5},{5,1},{9,13},{13,9},{2,6},{6,2},{1... | collective-permute-start | bytes 98312 | tf_op jit(solution)/shard_map/ppermute | solution.py:430
  12.3 1.5 %collective-permute-start.2 = (bf16[128,128]{1,0:T(8,128)(2,1)S(1)}, bf16[128,128]{1,0:T(8,128)(2,1)S(1)}, u32[]{:S(2)}, u32[]{:S(2)}) collective-permute-start(bf16[128,128]{1,0:T(8,128)(2,1)S(1)} %collective-permute-done.1.refs_2_), channel_id=1, source_target_pairs={{0,2},{2,0},{1,3},{3,1},{4,6},{6,4},{5,7},{7,5},{8,10},{10,8},{9,1... | collective-permute-start | bytes 98312 | tf_op jit(solution)/shard_map/ppermute | solution.py:430
  13.9 0.9 %collective-permute-done.8.refs_6_ = bf16[128,128]{1,0:T(8,128)(2,1)S(1)} collective-permute-done((bf16[128,128]{1,0:T(8,128)(2,1)S(1)}, bf16[128,128]{1,0:T(8,128)(2,1)S(1)}, u32[]{:S(2)}, u32[]{:S(2)}) %collective-permute-start.8) | collective-permute-done | bytes 32800 | tf_op jit(solution)/shard_map/ppermute | solution.py:430
  16.2 2.7 %first_rows.1 = (bf16[2048,128]{1,0:T(8,128)(2,1)S(1)}, bf16[2048,128]{1,0:T(8,128)(2,1)S(1)}, f32[16,128]{1,0:T(8,128)S(1)}, f32[8,128]{1,0:T(8,128)S(1)}) custom-call(s32[4]{0:T(128)S(1)} %pad_add_fusion.place_ref, f32[8,128]{1,0:T(8,128)S(1)} %get-tuple-element.35.mass_ref, bf16[128,128]{1,0:T(8,128)(2,1)S(1)} %get-tuple-element.36.refs_0_, ...), custom_call_target="tpu_custom_call" | custom-call | flops 536870912 | bytes 1048576 | tf_op jit(solution)/shard_map/first_rows/pallas_call | solution.py:243
  18.9 1.2 %other_rows.1 = (f32[8,128]{1,0:T(8,128)S(1)}, bf16[1024,128]{1,0:T(8,128)(2,1)S(1)}) custom-call(s32[4]{0:T(128)S(1)} %pad_add_fusion.place_ref, bf16[2048,128]{1,0:T(8,128)(2,1)S(1)} %get-tuple-element.49.targets_ref, bf16[2048,128]{1,0:T(8,128)(2,1)S(1)} %get-tuple-element.39.offset_ref, f32[8,128]{1,0:T(8,128)S(1)} %get-tuple-element.40.first_ref, ...), custom_call_target="tpu_custom_call" | custom-call | tf_op jit(solution)/shard_map/other_rows/pallas_call | solution.py:278
  20.2 11.5 %all_to_all.15.parts_ref = f32[8,8,128]{2,1,0:T(8,128)S(1)} all-to-all(f32[8,8,128]{2,1,0:T(8,128)S(1)} %broadcast_in_dim.6), channel_id=1, replica_groups=mesh['src'=2,'z'=4,'x'=2,'core'=2] {'z','x'}, dimensions={0} | all-to-all | bytes 65536 | tf_op jit(solution)/shard_map/all_to_all | solution.py:443
  31.7 2.5 %first_columns.1 = (f32[2048,1024]{1,0:T(8,128)S(1)}, f32[2048,128]{1,0:T(8,128)S(1)}, f32[16,128]{1,0:T(8,128)S(1)}, f32[8,128]{1,0:T(8,128)S(1)}) custom-call(bf16[1024,128]{1,0:T(8,128)(2,1)S(1)} %get-tuple-element.48.sources_ref, bf16[2048,128]{1,0:T(8,128)(2,1)S(1)} %get-tuple-element.49.targets_ref, f32[8,8,128]{2,1,0:T(8,128)S(1)} %all_to_all.15.parts_ref, ...), custom_call_target="tpu_custom_call" | custom-call | tf_op jit(solution)/shard_map/first_columns/pallas_call | solution.py:321
  34.8 1.3 %collective-permute-start.10 = (f32[16,128]{1,0:T(8,128)S(1)}, f32[16,128]{1,0:T(8,128)S(1)}, u32[]{:S(2)}, u32[]{:S(2)}) collective-permute-start(f32[16,128]{1,0:T(8,128)S(1)} %get-tuple-element.51.refs_0_), channel_id=1, source_target_pairs={{0,1},{1,0},{16,17},{17,16},{2,3},{3,2},{18,19},{19,18},{4,5},{5,4... | collective-permute-start | bytes 24584 | tf_op jit(solution)/shard_map/ppermute | solution.py:430
  37.3 0.7 collective-permute-done.11.refs_2_
  38.0 0.9 %second_rows.1 = (f32[16,128]{1,0:T(8,128)S(1)}, f32[2048,128]{1,0:T(8,128)S(1)}, f32[8,128]{1,0:T(8,128)S(1)}) custom-call(f32[2048,1024]{1,0:T(8,128)S(1)} %get-tuple-element.44.plan_ref, f32[2048,128]{1,0:T(8,128)S(1)} %get-tuple-element.45.peak_ref, f32[16,128]{1,0:T(8,128)S(1)} %get-tuple-element.46.mass_ref, f32[16,128]{1,0:T(8,128)S(1)} %get-tuple-element.51.refs_0_, ...), custom_call_target="tpu_custom_call" | custom-call | tf_op jit(solution)/shard_map/second_rows/pallas_call | solution.py:365
  38.9 9.1 %all_to_all.16.parts_ref = f32[8,8,128]{2,1,0:T(8,128)S(1)} all-to-all(f32[8,8,128]{2,1,0:T(8,128)S(1)} %broadcast_in_dim.7), channel_id=1, replica_groups=mesh['src'=2,'z'=4,'x'=2,'core'=2] {'z','x'}, dimensions={0} | all-to-all | bytes 65536 | tf_op jit(solution)/shard_map/all_to_all | solution.py:443
  47.9 1.3 %later_columns.2 = (f32[16,128]{1,0:T(8,128)S(1)}, f32[8,128]{1,0:T(8,128)}) custom-call(f32[2048,1024]{1,0:T(8,128)S(1)} %get-tuple-element.44.plan_ref, f32[2048,128]{1,0:T(8,128)S(1)} %get-tuple-element.55.reach_ref, f32[8,8,128]{2,1,0:T(8,128)S(1)} %all_to_all.16.parts_ref, f32[8,128]{1,0:T(8,128)S(1)} %get-tuple-element.43.log_ref, ...), custom_call_target="tpu_custom_call" | custom-call | tf_op jit(solution)/shard_map/later_columns/pallas_call | solution.py:409
  49.7 1.3 %collective-permute-start.13 = (f32[16,128]{1,0:T(8,128)S(1)}, f32[16,128]{1,0:T(8,128)S(1)}, u32[]{:S(2)}, u32[]{:S(2)}) collective-permute-start(f32[16,128]{1,0:T(8,128)S(1)} %get-tuple-element.59.refs_0_), channel_id=1, source_target_pairs={{0,1},{1,0},{16,17},{17,16},{2,3},{3,2},{18,19},{19,18},{4,5},{5,4... | collective-permute-start | bytes 24584 | tf_op jit(solution)/shard_map/ppermute | solution.py:430
  51.0 1.2 %collective-permute-done.15.refs_3_ = f32[16,128]{1,0:T(8,128)S(1)} collective-permute-done((f32[16,128]{1,0:T(8,128)S(1)}, f32[16,128]{1,0:T(8,128)S(1)}, u32[]{:S(2)}, u32[]{:S(2)}) %collective-permute-start.15) | collective-permute-done | bytes 8224 | tf_op jit(solution)/shard_map/ppermute | solution.py:430
  52.9 0.7 %later_rows.1 = f32[8,128]{1,0:T(8,128)S(1)} custom-call(f32[2048,1024]{1,0:T(8,128)S(1)} %get-tuple-element.44.plan_ref, f32[2048,128]{1,0:T(8,128)S(1)} %get-tuple-element.55.reach_ref, f32[16,128]{1,0:T(8,128)S(1)} %get-tuple-element.46.mass_ref, f32[16,128]{1,0:T(8,128)S(1)} %get-tuple-element.59.refs_0_, f32[16,128]{1,0:T(8,128)S(1)} %collective-permute-done.13.refs_1_, ...), custom_call_target="tpu_custom_call" | custom-call | tf_op jit(solution)/shard_map/later_rows/pallas_call | solution.py:383
  53.6 9.1 %all_to_all.17.parts_ref = f32[8,8,128]{2,1,0:T(8,128)S(1)} all-to-all(f32[8,8,128]{2,1,0:T(8,128)S(1)} %broadcast_in_dim.8), channel_id=1, replica_groups=mesh['src'=2,'z'=4,'x'=2,'core'=2] {'z','x'}, dimensions={0} | all-to-all | bytes 65536 | tf_op jit(solution)/shard_map/all_to_all | solution.py:443
  62.7 0.7 %later_columns.3 = (f32[16,128]{1,0:T(8,128)S(1)}, f32[8,128]{1,0:T(8,128)S(1)}) custom-call(f32[2048,1024]{1,0:T(8,128)S(1)} %get-tuple-element.44.plan_ref, f32[2048,128]{1,0:T(8,128)S(1)} %get-tuple-element.55.reach_ref, f32[8,8,128]{2,1,0:T(8,128)S(1)} %all_to_all.17.parts_ref, f32[8,128]{1,0:T(8,128)S(1)} %get-tuple-element.43.log_ref, ...), custom_call_target="tpu_custom_call" | custom-call | tf_op jit(solution)/shard_map/later_columns/pallas_call | solution.py:409
  64.1 1.5 %collective-permute-start.18 = (f32[16,128]{1,0:T(8,128)S(1)}, f32[16,128]{1,0:T(8,128)S(1)}, u32[]{:S(2)}, u32[]{:S(2)}) collective-permute-start(f32[16,128]{1,0:T(8,128)S(1)} %get-tuple-element.63), channel_id=1, source_target_pairs={{0,16},{1,17},{16,0},{17,1},{2,18},{3,19},{18,2},{19,3},{4,20},{5,... | collective-permute-start | bytes 24584 | tf_op jit(solution)/shard_map/ppermute | solution.py:430
  66.7 1.1 %collective-permute-done.18 = f32[16,128]{1,0:T(8,128)S(1)} collective-permute-done((f32[16,128]{1,0:T(8,128)S(1)}, f32[16,128]{1,0:T(8,128)S(1)}, u32[]{:S(2)}, u32[]{:S(2)}) %collective-permute-start.18) | collective-permute-done | bytes 8224 | tf_op jit(solution)/shard_map/ppermute | solution.py:430
  (45 shorter events, 7.9 us)
Async XLA Ops:
  0.6 8.7 %copy-start = (f32[2048]{0:T(1024)S(1)}, f32[2048]{0:T(1024)}, u32[]{:S(2)}) copy-start(f32[2048]{0:T(1024)} %param.6) | copy-start | bytes 24580
  0.6 9.8 %collective-permute-start.6 = (bf16[512,128]{1,0:T(8,128)(2,1)}, bf16[512,128]{1,0:T(8,128)(2,1)S(1)}, u32[]{:S(2)}, u32[]{:S(2)}) collective-permute-start(bf16[512,128]{1,0:T(8,128)(2,1)} %targets_ref.1), channel_id=1, source_target_pairs={{0,16},{16,0},{1,17},{17,1},{2,18},{18,2},{3,19},{19,3},{4,20},{20... | collective-permute-start | bytes 393224 | tf_op jit(solution)/shard_map/ppermute | solution.py:430
  3.7 8.1 %collective-permute-start = (bf16[128,128]{1,0:T(8,128)(2,1)}, bf16[128,128]{1,0:T(8,128)(2,1)S(1)}, u32[]{:S(2)}, u32[]{:S(2)}) collective-permute-start(bf16[128,128]{1,0:T(8,128)(2,1)} %sources_ref.1), channel_id=1, source_target_pairs={{0,2},{2,0},{1,3},{3,1},{4,6},{6,4},{5,7},{7,5},{8,10},{10,8},{9,1... | collective-permute-start | bytes 98312 | tf_op jit(solution)/shard_map/ppermute | solution.py:430
  5.2 5.7 %collective-permute-start.3 = (bf16[128,128]{1,0:T(8,128)(2,1)}, bf16[128,128]{1,0:T(8,128)(2,1)S(1)}, u32[]{:S(2)}, u32[]{:S(2)}) collective-permute-start(bf16[128,128]{1,0:T(8,128)(2,1)} %sources_ref.1), channel_id=1, source_target_pairs={{0,8},{4,12},{8,0},{12,4},{1,9},{5,13},{9,1},{13,5},{2,10},{6,14},... | collective-permute-start | bytes 98312 | tf_op jit(solution)/shard_map/ppermute | solution.py:430
  7.8 4.6 %collective-permute-start.1 = (bf16[128,128]{1,0:T(8,128)(2,1)}, bf16[128,128]{1,0:T(8,128)(2,1)S(1)}, u32[]{:S(2)}, u32[]{:S(2)}) collective-permute-start(bf16[128,128]{1,0:T(8,128)(2,1)} %sources_ref.1), channel_id=1, source_target_pairs={{0,4},{4,0},{8,12},{12,8},{1,5},{5,1},{9,13},{13,9},{2,6},{6,2},{1... | collective-permute-start | bytes 98312 | tf_op jit(solution)/shard_map/ppermute | solution.py:430
  10.3 5.9 %collective-permute-start.5 = (bf16[544,128]{1,0:T(8,128)(2,1)S(1)}, bf16[544,128]{1,0:T(8,128)(2,1)S(1)}, u32[]{:S(2)}, u32[]{:S(2)}) collective-permute-start(bf16[544,128]{1,0:T(8,128)(2,1)S(1)} %get-tuple-element.37.refs_6_), channel_id=1, source_target_pairs={{0,1},{1,0},{2,3},{3,2},{4,5},{5,4},{6,7},{7,6},{8,9},{9,8},{10,11... | collective-permute-start | bytes 417800 | tf_op jit(solution)/shard_map/ppermute | solution.py:430
  10.4 5.8 %collective-permute-start.7 = (bf16[512,128]{1,0:T(8,128)(2,1)S(1)}, bf16[512,128]{1,0:T(8,128)(2,1)S(1)}, u32[]{:S(2)}, u32[]{:S(2)}) collective-permute-start(bf16[512,128]{1,0:T(8,128)(2,1)S(1)} %collective-permute-done.6.refs_8_), channel_id=1, source_target_pairs={{0,1},{1,0},{2,3},{3,2},{4,5},{5,4},{6,7},{7,6},{8,9},{9,8},{10,11... | collective-permute-start | bytes 393224 | tf_op jit(solution)/shard_map/ppermute | solution.py:430
  10.9 3.9 %collective-permute-start.8 = (bf16[128,128]{1,0:T(8,128)(2,1)S(1)}, bf16[128,128]{1,0:T(8,128)(2,1)S(1)}, u32[]{:S(2)}, u32[]{:S(2)}) collective-permute-start(bf16[128,128]{1,0:T(8,128)(2,1)S(1)} %collective-permute-done.3.refs_4_), channel_id=1, source_target_pairs={{0,4},{4,0},{8,12},{12,8},{1,5},{5,1},{9,13},{13,9},{2,6},{6,2},{1... | collective-permute-start | bytes 98312 | tf_op jit(solution)/shard_map/ppermute | solution.py:430
  11.8 3.9 %collective-permute-start.4 = (bf16[128,128]{1,0:T(8,128)(2,1)S(1)}, bf16[128,128]{1,0:T(8,128)(2,1)S(1)}, u32[]{:S(2)}, u32[]{:S(2)}) collective-permute-start(bf16[128,128]{1,0:T(8,128)(2,1)S(1)} %collective-permute-done.3.refs_4_), channel_id=1, source_target_pairs={{0,2},{2,0},{1,3},{3,1},{4,6},{6,4},{5,7},{7,5},{8,10},{10,8},{9,1... | collective-permute-start | bytes 98312 | tf_op jit(solution)/shard_map/ppermute | solution.py:430
  12.3 3.9 %collective-permute-start.2 = (bf16[128,128]{1,0:T(8,128)(2,1)S(1)}, bf16[128,128]{1,0:T(8,128)(2,1)S(1)}, u32[]{:S(2)}, u32[]{:S(2)}) collective-permute-start(bf16[128,128]{1,0:T(8,128)(2,1)S(1)} %collective-permute-done.1.refs_2_), channel_id=1, source_target_pairs={{0,2},{2,0},{1,3},{3,1},{4,6},{6,4},{5,7},{7,5},{8,10},{10,8},{9,1... | collective-permute-start | bytes 98312 | tf_op jit(solution)/shard_map/ppermute | solution.py:430
  14.8 4.1 %collective-permute-start.9 = (bf16[128,128]{1,0:T(8,128)(2,1)S(1)}, bf16[128,128]{1,0:T(8,128)(2,1)S(1)}, u32[]{:S(2)}, u32[]{:S(2)}) collective-permute-start(bf16[128,128]{1,0:T(8,128)(2,1)S(1)} %collective-permute-done.8.refs_6_), channel_id=1, source_target_pairs={{0,2},{2,0},{1,3},{3,1},{4,6},{6,4},{5,7},{7,5},{8,10},{10,8},{9,1... | collective-permute-start | bytes 98312 | tf_op jit(solution)/shard_map/ppermute | solution.py:430
  34.2 3.1 %collective-permute-start.12 = (f32[16,128]{1,0:T(8,128)S(1)}, f32[16,128]{1,0:T(8,128)S(1)}, u32[]{:S(2)}, u32[]{:S(2)}) collective-permute-start(f32[16,128]{1,0:T(8,128)S(1)} %get-tuple-element.51.refs_0_), channel_id=1, source_target_pairs={{0,17},{1,16},{16,1},{17,0},{2,19},{3,18},{18,3},{19,2},{4,21},{5,... | collective-permute-start | bytes 24584 | tf_op jit(solution)/shard_map/ppermute | solution.py:430
  34.2 3.7 %collective-permute-start.11 = (f32[16,128]{1,0:T(8,128)S(1)}, f32[16,128]{1,0:T(8,128)S(1)}, u32[]{:S(2)}, u32[]{:S(2)}) collective-permute-start(f32[16,128]{1,0:T(8,128)S(1)} %get-tuple-element.51.refs_0_), channel_id=1, source_target_pairs={{0,16},{1,17},{16,0},{17,1},{2,18},{3,19},{18,2},{19,3},{4,20},{5,... | collective-permute-start | bytes 24584 | tf_op jit(solution)/shard_map/ppermute | solution.py:430
  34.8 3.2 %collective-permute-start.10 = (f32[16,128]{1,0:T(8,128)S(1)}, f32[16,128]{1,0:T(8,128)S(1)}, u32[]{:S(2)}, u32[]{:S(2)}) collective-permute-start(f32[16,128]{1,0:T(8,128)S(1)} %get-tuple-element.51.refs_0_), channel_id=1, source_target_pairs={{0,1},{1,0},{16,17},{17,16},{2,3},{3,2},{18,19},{19,18},{4,5},{5,4... | collective-permute-start | bytes 24584 | tf_op jit(solution)/shard_map/ppermute | solution.py:430
  49.2 3.1 %collective-permute-start.15 = (f32[16,128]{1,0:T(8,128)S(1)}, f32[16,128]{1,0:T(8,128)S(1)}, u32[]{:S(2)}, u32[]{:S(2)}) collective-permute-start(f32[16,128]{1,0:T(8,128)S(1)} %get-tuple-element.59.refs_0_), channel_id=1, source_target_pairs={{0,17},{1,16},{16,1},{17,0},{2,19},{3,18},{18,3},{19,2},{4,21},{5,... | collective-permute-start | bytes 24584 | tf_op jit(solution)/shard_map/ppermute | solution.py:430
  49.2 3.7 %collective-permute-start.14 = (f32[16,128]{1,0:T(8,128)S(1)}, f32[16,128]{1,0:T(8,128)S(1)}, u32[]{:S(2)}, u32[]{:S(2)}) collective-permute-start(f32[16,128]{1,0:T(8,128)S(1)} %get-tuple-element.59.refs_0_), channel_id=1, source_target_pairs={{0,16},{1,17},{16,0},{17,1},{2,18},{3,19},{18,2},{19,3},{4,20},{5,... | collective-permute-start | bytes 24584 | tf_op jit(solution)/shard_map/ppermute | solution.py:430
  49.7 3.2 %collective-permute-start.13 = (f32[16,128]{1,0:T(8,128)S(1)}, f32[16,128]{1,0:T(8,128)S(1)}, u32[]{:S(2)}, u32[]{:S(2)}) collective-permute-start(f32[16,128]{1,0:T(8,128)S(1)} %get-tuple-element.59.refs_0_), channel_id=1, source_target_pairs={{0,1},{1,0},{16,17},{17,16},{2,3},{3,2},{18,19},{19,18},{4,5},{5,4... | collective-permute-start | bytes 24584 | tf_op jit(solution)/shard_map/ppermute | solution.py:430
  63.4 2.2 %collective-permute-start.16 = (f32[2,4,128]{2,0,1:T(2,128)S(1)}, f32[2,4,128]{2,0,1:T(2,128)S(1)}, u32[]{:S(2)}, u32[]{:S(2)}) collective-permute-start(f32[2,4,128]{2,0,1:T(2,128)S(1)} %copy.12), channel_id=1, source_target_pairs={{0,1},{1,0},{2,3},{3,2},{4,5},{5,4},{6,7},{7,6},{8,9},{9,8},{10,11... | collective-permute-start | bytes 12296 | tf_op jit(solution)/shard_map/ppermute | solution.py:430
  63.5 3.1 %collective-permute-start.19 = (f32[16,128]{1,0:T(8,128)S(1)}, f32[16,128]{1,0:T(8,128)S(1)}, u32[]{:S(2)}, u32[]{:S(2)}) collective-permute-start(f32[16,128]{1,0:T(8,128)S(1)} %get-tuple-element.63), channel_id=1, source_target_pairs={{0,17},{1,16},{16,1},{17,0},{2,19},{3,18},{18,3},{19,2},{4,21},{5,... | collective-permute-start | bytes 24584 | tf_op jit(solution)/shard_map/ppermute | solution.py:430
  64.1 3.7 %collective-permute-start.18 = (f32[16,128]{1,0:T(8,128)S(1)}, f32[16,128]{1,0:T(8,128)S(1)}, u32[]{:S(2)}, u32[]{:S(2)}) collective-permute-start(f32[16,128]{1,0:T(8,128)S(1)} %get-tuple-element.63), channel_id=1, source_target_pairs={{0,16},{1,17},{16,0},{17,1},{2,18},{3,19},{18,2},{19,3},{4,20},{5,... | collective-permute-start | bytes 24584 | tf_op jit(solution)/shard_map/ppermute | solution.py:430
  65.7 2.1 %collective-permute-start.17 = (f32[16,128]{1,0:T(8,128)S(1)}, f32[16,128]{1,0:T(8,128)S(1)}, u32[]{:S(2)}, u32[]{:S(2)}) collective-permute-start(f32[16,128]{1,0:T(8,128)S(1)} %get-tuple-element.63), channel_id=1, source_target_pairs={{0,1},{1,0},{16,17},{17,16},{2,3},{3,2},{18,19},{19,18},{4,5},{5,4... | collective-permute-start | bytes 24584 | tf_op jit(solution)/shard_map/ppermute | solution.py:430

commit v6 on v4

--- a/solution.py
+++ b/solution.py
@@ -69,36 +69,65 @@
     return lax.dot_general(rows, cols, (((1,), (1,)), ((), ())), preferred_element_type=F32)
 
 
-def ready(targets, mass, source_mass):
+def ready(sources, targets, mass, source_mass):
     part, chunk = targets.shape[0], mass.shape[0]
-
-    def kernel(targets_ref, mass_ref, source_ref, packed_ref, mass_out, source_out):
-        packed_ref[:part, :] = targets_ref[...]
-        mass_out[...] = mass_ref[...]
+    anywhere = pl.BlockSpec(memory_space=pl.ANY)
+
+    def kernel(sources_ref, targets_ref, mass_ref, source_ref, sources_out, packed_ref, mass_out, source_out, *sems):
+        copies = [
+            pltpu.make_async_copy(mass_ref, mass_out, sems[0]),
+            pltpu.make_async_copy(targets_ref, packed_ref.at[:part], sems[1]),
+            pltpu.make_async_copy(sources_ref, sources_out, sems[2]),
+        ]
+        for copy in copies:
+            copy.start()
         source_out[...] = jnp.log2(source_ref[...])
-        value, pieces = mass_ref[...], []
+        copies[0].wait()
+        value, pieces = mass_out[...], []
         for step in range(PIECES):
             pieces.append(value.astype(jnp.bfloat16).astype(F32))
             value = value - pieces[-1]
         pieces.append(jnp.zeros_like(value))
         packed_ref[part:, :] = jnp.concatenate(pieces, axis=0).astype(jnp.bfloat16)
+        copies[1].wait()
+        copies[2].wait()
 
     return pl.pallas_call(
         kernel,
         out_shape=(
+            pltpu.VMEM(sources.shape, jnp.bfloat16),
             pltpu.VMEM((part + (PIECES + 1) * chunk, LANES), jnp.bfloat16),
             pltpu.VMEM(mass.shape, F32),
             pltpu.VMEM(source_mass.shape, F32),
         ),
-        in_specs=[VMEM] * 3,
-        out_specs=(VMEM,) * 3,
+        in_specs=[anywhere, anywhere, anywhere, VMEM],
+        out_specs=(VMEM,) * 4,
+        scratch_shapes=[pltpu.SemaphoreType.DMA] * 3,
         compiler_params=params(),
         cost_estimate=pl.CostEstimate(flops=1 << 20, bytes_accessed=1 << 20, transcendentals=0),
         name="ready",
-    )(targets, mass, source_mass)
-
-
-def pack(place, blocks):
+    )(*[pltpu.with_memory_space_constraint(value, pltpu.HBM) for value in (sources, targets, mass)], source_mass)
+
+
+def lay(place, block, step, count):
+    part = block.shape[0]
+
+    def kernel(place_ref, block_ref, out_ref):
+        start = pl.multiple_of(jnp.bitwise_xor(place_ref[0], step) * part, part)
+        out_ref[pl.ds(start, part), :] = block_ref[...]
+
+    return pl.pallas_call(
+        kernel,
+        out_shape=pltpu.VMEM((count * part, LANES), jnp.bfloat16),
+        in_specs=[SMEM, VMEM],
+        out_specs=VMEM,
+        compiler_params=params(),
+        cost_estimate=pl.CostEstimate(flops=1 << 20, bytes_accessed=1 << 20, transcendentals=0),
+        name="lay",
+    )(place, block)
+
+
+def pack(place, blocks, laid):
     part = blocks[0].shape[0]
 
     def kernel(place_ref, *refs):
@@ -109,13 +138,14 @@
 
     return pl.pallas_call(
         kernel,
-        out_shape=pltpu.VMEM((len(blocks) * part, LANES), jnp.bfloat16),
-        in_specs=[SMEM] + [VMEM] * len(blocks),
+        out_shape=pltpu.VMEM(laid.shape, jnp.bfloat16),
+        in_specs=[SMEM] + [VMEM] * (len(blocks) + 1),
         out_specs=VMEM,
+        input_output_aliases={1 + len(blocks): 0},
         compiler_params=params(),
         cost_estimate=pl.CostEstimate(flops=1 << 20, bytes_accessed=1 << 18, transcendentals=0),
         name="pack",
-    )(place, *blocks)
+    )(place, *blocks, laid)
 
 
 def pieces_of(value):
@@ -206,10 +236,11 @@
 
 
 def other_rows(place, targets, offsets, first, groups):
-    width, count, each = targets.shape[0], sum(group.shape[0] for group in groups), groups[0].shape[0] // LANES
-
-    def kernel(place_ref, targets_ref, offset_ref, first_ref, *refs):
-        group_refs, (out_ref, *score_refs) = refs[: len(groups)], refs[len(groups) :]
+    mine, groups = groups[0], groups[1:]
+    width, count, each = targets.shape[0], sum(group.shape[0] for group in groups), mine.shape[0] // LANES
+
+    def kernel(place_ref, targets_ref, offset_ref, first_ref, mine_ref, *refs):
+        group_refs, (out_ref, sources_ref, *score_refs) = refs[: len(groups)], refs[len(groups) :]
         cols = jnp.concatenate([ref[...] for ref in group_refs], axis=0)
         cols = jnp.concatenate([cols, ones_for(count)], axis=1)
         rows = Rows(count)
@@ -220,30 +251,27 @@
         lse = rows.lse()
         for step in range(len(groups) + 1):
             start = jnp.bitwise_xor(place_ref[2], step) * each
+            ref = group_refs[step - 1] if step else mine_ref
+            sources_ref[pl.ds(pl.multiple_of(start * LANES, each * LANES), each * LANES), :] = ref[...]
             for row in range(each):
                 at = ((step - 1) * each + row) * LANES
                 out_ref[pl.ds(start + row, 1), :] = first_ref[row : row + 1, :] if step == 0 else lse[:, at : at + LANES]
 
     return pl.pallas_call(
         kernel,
-        out_shape=rows_of(count + each * LANES),
-        in_specs=[SMEM] + [VMEM] * (3 + len(groups)),
-        out_specs=VMEM,
+        out_shape=(rows_of(count + each * LANES), pltpu.VMEM((count + each * LANES, LANES), jnp.bfloat16)),
+        in_specs=[SMEM] + [VMEM] * (3 + len(groups) + 1),
+        out_specs=(VMEM,) * 2,
         scratch_shapes=[pltpu.VMEM((ROWS, count), F32)] * 2,
         compiler_params=params(),
         name="other_rows",
-    )(place, pin(targets), pin(offsets), first, *groups)
-
-
-def first_columns(place, groups, targets, parts, log_mass):
-    each, width = groups[0].shape[0], targets.shape[0]
-    count = each * len(groups)
-
-    def kernel(place_ref, targets_ref, parts_ref, log_ref, *refs):
-        group_refs, (plan_ref, peak_ref, out_ref, lse_ref, sources_ref, *score_refs) = refs[: len(groups)], refs[len(groups) :]
-        for step in range(len(groups)):
-            start = pl.multiple_of(jnp.bitwise_xor(place_ref[2], step) * each, each)
-            sources_ref[pl.ds(start, each), :] = group_refs[step][...]
+    )(place, pin(targets), pin(offsets), first, pin(mine), *groups)
+
+
+def first_columns(sources, targets, parts, log_mass):
+    count, width = sources.shape[0], targets.shape[0]
+
+    def kernel(sources_ref, targets_ref, parts_ref, log_ref, plan_ref, peak_ref, out_ref, lse_ref, *score_refs):
         lse = log_sum([parts_ref[i] for i in range(parts.shape[0])])
         lse_ref[...] = lse
         mask = diagonal()
@@ -279,14 +307,13 @@
             pltpu.VMEM((width, LANES), F32),
             rows_of(width),
             rows_of(count),
-            pltpu.VMEM((count, LANES), jnp.bfloat16),
         ),
-        in_specs=[SMEM] + [VMEM] * (3 + len(groups)),
-        out_specs=(VMEM,) * 5,
+        in_specs=[VMEM] * 4,
+        out_specs=(VMEM,) * 4,
         scratch_shapes=[pltpu.VMEM((ROWS, count), F32)] * 2,
         compiler_params=params(),
         name="first_columns",
-    )(place, pin(targets), parts, log_mass, *[pin(group) for group in groups])
+    )(pin(sources), pin(targets), parts, log_mass)
 
 
 def weighted_rows(reach_of, weight, plan_ref, out_ref):
@@ -415,17 +442,18 @@
         a = source_mass.reshape(n_z, n_x, CORES, part)
         a = lax.dynamic_index_in_dim(a, core, axis=2, keepdims=False).swapaxes(0, 1).reshape(-1, LANES)
         blocks = swap_all(target_points, "src", n_src)[1:]
-        sources = swap_all(source_points, "z", n_z)
-        packed, b, a = ready(target_points, target_mass.reshape(-1, LANES), a)
+        three, two, one = [swap(source_points, "z", n_z, d) for d in (3, 2, 1)]
+        mine, packed, b, a = ready(source_points, target_points, target_mass.reshape(-1, LANES), a)
+        laid = lay(along, three, 3, n_z)
         packed = swap_all(packed, "core", CORES)
         blocks = blocks + [swap(block, "core", CORES, 1) for block in blocks]
-        groups = swap_all(pack(along, sources), "x", n_x)
+        groups = swap_all(pack(along, [mine, one, two], laid), "x", n_x)
         place, a = lax.optimization_barrier((place, a))
         targets, offsets, b, first = first_rows(place, b, packed, blocks, groups[0])
-        own = other_rows(place, targets, offsets, first, groups[1:])
-        plan, peak, own, row_lse, sources = first_columns(place, groups, targets, share(own, n_far), a)
-        early_y, own = lax.optimization_barrier((targets, own))
-        half_x, half_y = half_norm(sources).reshape(-1, LANES), half_norm(early_y).reshape(-1, LANES)
+        own, sources = other_rows(place, targets, offsets, first, groups)
+        plan, peak, own, row_lse = first_columns(sources, targets, share(own, n_far), a)
+        early_x, early_y, own = lax.optimization_barrier((sources, targets, own))
+        half_x, half_y = half_norm(early_x).reshape(-1, LANES), half_norm(early_y).reshape(-1, LANES)
         parts = swap_all(own, near, n_near)
         half_x, half_y, *parts = lax.optimization_barrier((half_x, half_y, *parts))
         col_lse, reach, rows = second_rows(plan, peak, b, parts)

time: 68.4 us -> 66.9 us (0.978)
  local copies, waits for them, and re-layouts: 3 us -> 0.65 us
    unnamed x8 -> x2, local copies, waits for them, and re-layouts: 2.35 us -> 0.01 us
    pallas_call x3 -> x4, Pallas kernels: 1.79 us -> 2.74 us  [the longest x1 1.77 us: other_rows(): pl.pallas_call(kernel, out_shape=(rows_of(count + each * LANES), pltpu.VM...]
  transfers between devices with their start and end apart: 17 -> 17, of which waited for: 9 -> 9; matrix products, arithmetic and copies ran while one was open for 2% -> 2% of each run, Pallas kernels for 3% -> 5%
where the time goes in v6:
time: 66.9 us; the launch traced here: 66.6 us
  blocking collectives  28.1 us (42%)
  starting transfers between devices  15.3 us (23%)
  Pallas kernels  11 us (16%)
  waiting for transfers between devices  9.52 us (14%)
  other arithmetic  1.26 us (2%)
  between operations  0.82 us (1%)
    all_to_all x3, blocking collectives, share(): return lax.all_to_all(copies, ('z', 'x'), 0, 0, tiled=True)  28.1 us
    ppermute x17, starting transfers between devices, swap(): return lax.ppermute(value, axes, [(i, i ^ distance) for i in range(size)])  15.3 us
    ppermute x17, waiting for transfers between devices, swap(): return lax.ppermute(value, axes, [(i, i ^ distance) for i in range(size)])  9.52 us
    pallas_call x1, Pallas kernels, first_columns(): pl.pallas_call(kernel, out_shape=(pltpu.VMEM((width, count), F32), pltpu....  2.47 us
    pallas_call x1, Pallas kernels, first_rows(): pl.pallas_call(kernel, out_shape=(pltpu.VMEM((width, LANES), jnp.bfloat16...  2.19 us
    pallas_call x2, Pallas kernels, later_columns(): pl.pallas_call(kernel, out_shape=(rows_of(width), rows_of(count)), in_spe...  1.99 us
    pallas_call x1, Pallas kernels, other_rows(): pl.pallas_call(kernel, out_shape=(rows_of(count + each * LANES), pltpu.VM...  1.77 us
  transfers between devices with their start and end apart: 17, of which 9 were waited for; matrix products, arithmetic and copies ran while one was open for 2% of the time, Pallas kernels for 5%

profile of v6, /device:TPU:0, one launch (start us, length us, event | category | flops | bytes accessed | tf_op | source)
XLA Modules:
  0.0 66.6 jit_solution(10423945385174803180)
XLA Ops:
  0.6 3.0 %collective-permute-start.4 = (bf16[512,128]{1,0:T(8,128)(2,1)}, bf16[512,128]{1,0:T(8,128)(2,1)S(1)}, u32[]{:S(2)}, u32[]{:S(2)}) collective-permute-start(bf16[512,128]{1,0:T(8,128)(2,1)} %targets_ref.1), channel_id=1, source_target_pairs={{0,16},{16,0},{1,17},{17,1},{2,18},{18,2},{3,19},{19,3},{4,20},{20... | collective-permute-start | bytes 393224 | tf_op jit(solution)/shard_map/ppermute | solution.py:412
  3.7 1.6 %collective-permute-start = (bf16[128,128]{1,0:T(8,128)(2,1)}, bf16[128,128]{1,0:T(8,128)(2,1)S(1)}, u32[]{:S(2)}, u32[]{:S(2)}) collective-permute-start(bf16[128,128]{1,0:T(8,128)(2,1)} %sources_ref.1), channel_id=1, source_target_pairs={{0,4},{4,0},{8,12},{12,8},{1,5},{5,1},{9,13},{13,9},{2,6},{6,2},{1... | collective-permute-start | bytes 98312 | tf_op jit(solution)/shard_map/ppermute | solution.py:412
  5.3 2.5 %collective-permute-start.2 = (bf16[128,128]{1,0:T(8,128)(2,1)}, bf16[128,128]{1,0:T(8,128)(2,1)S(1)}, u32[]{:S(2)}, u32[]{:S(2)}) collective-permute-start(bf16[128,128]{1,0:T(8,128)(2,1)} %sources_ref.1), channel_id=1, source_target_pairs={{0,12},{4,8},{8,4},{12,0},{1,13},{5,9},{9,5},{13,1},{2,14},{6,10},... | collective-permute-start | bytes 98312 | tf_op jit(solution)/shard_map/ppermute | solution.py:412
  7.9 1.0 %ready.1 = (bf16[128,128]{1,0:T(8,128)(2,1)S(1)}, bf16[544,128]{1,0:T(8,128)(2,1)S(1)}, f32[8,128]{1,0:T(8,128)S(1)}, f32[8,128]{1,0:T(8,128)S(1)}) custom-call(bf16[128,128]{1,0:T(8,128)(2,1)} %sources_ref.1, bf16[512,128]{1,0:T(8,128)(2,1)} %targets_ref.1, f32[8,128]{1,0:T(8,128)} %bitcast.31, f32[8,128]{1,0:T(8,128)S(1)} %bitcast.24), custom_call_target="tpu_custom_call" | custom-call | flops 1048576 | bytes 1048576 | tf_op jit(solution)/shard_map/ready/pallas_call | solution.py:95
  9.4 1.9 %collective-permute-done.2.block_ref = bf16[128,128]{1,0:T(8,128)(2,1)S(1)} collective-permute-done((bf16[128,128]{1,0:T(8,128)(2,1)}, bf16[128,128]{1,0:T(8,128)(2,1)S(1)}, u32[]{:S(2)}, u32[]{:S(2)}) %collective-permute-start.2) | collective-permute-done | bytes 32800 | tf_op jit(solution)/shard_map/ppermute | solution.py:412
  11.4 1.8 %collective-permute-done.1.refs_2_ = bf16[128,128]{1,0:T(8,128)(2,1)S(1)} collective-permute-done((bf16[128,128]{1,0:T(8,128)(2,1)}, bf16[128,128]{1,0:T(8,128)(2,1)S(1)}, u32[]{:S(2)}, u32[]{:S(2)}) %collective-permute-start.1) | collective-permute-done | bytes 32800 | tf_op jit(solution)/shard_map/ppermute | solution.py:412
  13.1 1.6 %collective-permute-start.6 = (bf16[512,128]{1,0:T(8,128)(2,1)S(1)}, bf16[512,128]{1,0:T(8,128)(2,1)S(1)}, u32[]{:S(2)}, u32[]{:S(2)}) collective-permute-start(bf16[512,128]{1,0:T(8,128)(2,1)S(1)} %pack.1.sources_ref.mine_ref), channel_id=1, source_target_pairs={{0,2},{2,0},{1,3},{3,1},{4,6},{6,4},{5,7},{7,5},{8,10},{10,8},{9,1... | collective-permute-start | bytes 393224 | tf_op jit(solution)/shard_map/ppermute | solution.py:412
  14.8 2.2 %first_rows.1 = (bf16[2048,128]{1,0:T(8,128)(2,1)S(1)}, bf16[2048,128]{1,0:T(8,128)(2,1)S(1)}, f32[16,128]{1,0:T(8,128)S(1)}, f32[4,128]{1,0:T(4,128)S(1)}) custom-call(s32[3]{0:T(128)S(1)} %pad_add_fusion.place_ref, f32[8,128]{1,0:T(8,128)S(1)} %get-tuple-element.35.mass_ref, bf16[512,128]{1,0:T(8,128)(2,1)S(1)} %pack.1.sources_ref.mine_ref, ...), custom_call_target="tpu_custom_call" | custom-call | flops 536870912 | bytes 1048576 | tf_op jit(solution)/shard_map/first_rows/pallas_call | solution.py:221
  16.9 1.2 %collective-permute-done.6.refs_0_ = bf16[512,128]{1,0:T(8,128)(2,1)S(1)} collective-permute-done((bf16[512,128]{1,0:T(8,128)(2,1)S(1)}, bf16[512,128]{1,0:T(8,128)(2,1)S(1)}, u32[]{:S(2)}, u32[]{:S(2)}) %collective-permute-start.6) | collective-permute-done | bytes 131104 | tf_op jit(solution)/shard_map/ppermute | solution.py:412
  18.2 1.8 %other_rows.1 = (f32[8,128]{1,0:T(8,128)S(1)}, bf16[1024,128]{1,0:T(8,128)(2,1)S(1)}) custom-call(s32[3]{0:T(128)S(1)} %pad_add_fusion.place_ref, bf16[2048,128]{1,0:T(8,128)(2,1)S(1)} %get-tuple-element.49.targets_ref, bf16[2048,128]{1,0:T(8,128)(2,1)S(1)} %get-tuple-element.39.offset_ref, f32[4,128]{1,0:T(4,128)S(1)} %get-tuple-element.40.first_ref, ...), custom_call_target="tpu_custom_call" | custom-call | tf_op jit(solution)/shard_map/other_rows/pallas_call | solution.py:260
  19.9 9.9 %all_to_all.15.parts_ref = f32[8,8,128]{2,1,0:T(8,128)S(1)} all-to-all(f32[8,8,128]{2,1,0:T(8,128)S(1)} %broadcast_in_dim.6), channel_id=1, replica_groups=mesh['src'=2,'z'=4,'x'=2,'core'=2] {'z','x'}, dimensions={0} | all-to-all | bytes 65536 | tf_op jit(solution)/shard_map/all_to_all | solution.py:425
  29.9 2.5 %first_columns.1 = (f32[2048,1024]{1,0:T(8,128)S(1)}, f32[2048,128]{1,0:T(8,128)S(1)}, f32[16,128]{1,0:T(8,128)S(1)}, f32[8,128]{1,0:T(8,128)S(1)}) custom-call(bf16[1024,128]{1,0:T(8,128)(2,1)S(1)} %get-tuple-element.48.sources_ref, bf16[2048,128]{1,0:T(8,128)(2,1)S(1)} %get-tuple-element.49.targets_ref, f32[8,8,128]{2,1,0:T(8,128)S(1)} %all_to_all.15.parts_ref, ...), custom_call_target="tpu_custom_call" | custom-call | tf_op jit(solution)/shard_map/first_columns/pallas_call | solution.py:303
  33.0 1.3 %collective-permute-start.7 = (f32[16,128]{1,0:T(8,128)S(1)}, f32[16,128]{1,0:T(8,128)S(1)}, u32[]{:S(2)}, u32[]{:S(2)}) collective-permute-start(f32[16,128]{1,0:T(8,128)S(1)} %get-tuple-element.51.refs_0_), channel_id=1, source_target_pairs={{0,1},{1,0},{16,17},{17,16},{2,3},{3,2},{18,19},{19,18},{4,5},{5,4... | collective-permute-start | bytes 24584 | tf_op jit(solution)/shard_map/ppermute | solution.py:412
  35.5 0.7 collective-permute-done.8.refs_2_
  36.2 0.9 %second_rows.1 = (f32[16,128]{1,0:T(8,128)S(1)}, f32[2048,128]{1,0:T(8,128)S(1)}, f32[8,128]{1,0:T(8,128)S(1)}) custom-call(f32[2048,1024]{1,0:T(8,128)S(1)} %get-tuple-element.44.plan_ref, f32[2048,128]{1,0:T(8,128)S(1)} %get-tuple-element.45.peak_ref, f32[16,128]{1,0:T(8,128)S(1)} %get-tuple-element.46.mass_ref, f32[16,128]{1,0:T(8,128)S(1)} %get-tuple-element.51.refs_0_, ...), custom_call_target="tpu_custom_call" | custom-call | tf_op jit(solution)/shard_map/second_rows/pallas_call | solution.py:347
  37.1 9.1 %all_to_all.16.parts_ref = f32[8,8,128]{2,1,0:T(8,128)S(1)} all-to-all(f32[8,8,128]{2,1,0:T(8,128)S(1)} %broadcast_in_dim.7), channel_id=1, replica_groups=mesh['src'=2,'z'=4,'x'=2,'core'=2] {'z','x'}, dimensions={0} | all-to-all | bytes 65536 | tf_op jit(solution)/shard_map/all_to_all | solution.py:425
  46.1 1.3 %later_columns.2 = (f32[16,128]{1,0:T(8,128)S(1)}, f32[8,128]{1,0:T(8,128)}) custom-call(f32[2048,1024]{1,0:T(8,128)S(1)} %get-tuple-element.44.plan_ref, f32[2048,128]{1,0:T(8,128)S(1)} %get-tuple-element.55.reach_ref, f32[8,8,128]{2,1,0:T(8,128)S(1)} %all_to_all.16.parts_ref, f32[8,128]{1,0:T(8,128)S(1)} %get-tuple-element.43.log_ref, ...), custom_call_target="tpu_custom_call" | custom-call | tf_op jit(solution)/shard_map/later_columns/pallas_call | solution.py:391
  47.9 1.3 %collective-permute-start.10 = (f32[16,128]{1,0:T(8,128)S(1)}, f32[16,128]{1,0:T(8,128)S(1)}, u32[]{:S(2)}, u32[]{:S(2)}) collective-permute-start(f32[16,128]{1,0:T(8,128)S(1)} %get-tuple-element.59.refs_0_), channel_id=1, source_target_pairs={{0,1},{1,0},{16,17},{17,16},{2,3},{3,2},{18,19},{19,18},{4,5},{5,4... | collective-permute-start | bytes 24584 | tf_op jit(solution)/shard_map/ppermute | solution.py:412
  49.2 1.2 %collective-permute-done.12.refs_3_ = f32[16,128]{1,0:T(8,128)S(1)} collective-permute-done((f32[16,128]{1,0:T(8,128)S(1)}, f32[16,128]{1,0:T(8,128)S(1)}, u32[]{:S(2)}, u32[]{:S(2)}) %collective-permute-start.12) | collective-permute-done | bytes 8224 | tf_op jit(solution)/shard_map/ppermute | solution.py:412
  51.1 0.7 %later_rows.1 = f32[8,128]{1,0:T(8,128)S(1)} custom-call(f32[2048,1024]{1,0:T(8,128)S(1)} %get-tuple-element.44.plan_ref, f32[2048,128]{1,0:T(8,128)S(1)} %get-tuple-element.55.reach_ref, f32[16,128]{1,0:T(8,128)S(1)} %get-tuple-element.46.mass_ref, f32[16,128]{1,0:T(8,128)S(1)} %get-tuple-element.59.refs_0_, f32[16,128]{1,0:T(8,128)S(1)} %collective-permute-done.10.refs_1_, ...), custom_call_target="tpu_custom_call" | custom-call | tf_op jit(solution)/shard_map/later_rows/pallas_call | solution.py:365
  51.8 9.1 %all_to_all.17.parts_ref = f32[8,8,128]{2,1,0:T(8,128)S(1)} all-to-all(f32[8,8,128]{2,1,0:T(8,128)S(1)} %broadcast_in_dim.8), channel_id=1, replica_groups=mesh['src'=2,'z'=4,'x'=2,'core'=2] {'z','x'}, dimensions={0} | all-to-all | bytes 65536 | tf_op jit(solution)/shard_map/all_to_all | solution.py:425
  60.9 0.7 %later_columns.3 = (f32[16,128]{1,0:T(8,128)S(1)}, f32[8,128]{1,0:T(8,128)S(1)}) custom-call(f32[2048,1024]{1,0:T(8,128)S(1)} %get-tuple-element.44.plan_ref, f32[2048,128]{1,0:T(8,128)S(1)} %get-tuple-element.55.reach_ref, f32[8,8,128]{2,1,0:T(8,128)S(1)} %all_to_all.17.parts_ref, f32[8,128]{1,0:T(8,128)S(1)} %get-tuple-element.43.log_ref, ...), custom_call_target="tpu_custom_call" | custom-call | tf_op jit(solution)/shard_map/later_columns/pallas_call | solution.py:391
  62.3 1.5 %collective-permute-start.15 = (f32[16,128]{1,0:T(8,128)S(1)}, f32[16,128]{1,0:T(8,128)S(1)}, u32[]{:S(2)}, u32[]{:S(2)}) collective-permute-start(f32[16,128]{1,0:T(8,128)S(1)} %get-tuple-element.63), channel_id=1, source_target_pairs={{0,16},{1,17},{16,0},{17,1},{2,18},{3,19},{18,2},{19,3},{4,20},{5,... | collective-permute-start | bytes 24584 | tf_op jit(solution)/shard_map/ppermute | solution.py:412
  64.9 1.1 %collective-permute-done.15 = f32[16,128]{1,0:T(8,128)S(1)} collective-permute-done((f32[16,128]{1,0:T(8,128)S(1)}, f32[16,128]{1,0:T(8,128)S(1)}, u32[]{:S(2)}, u32[]{:S(2)}) %collective-permute-start.15) | collective-permute-done | bytes 8224 | tf_op jit(solution)/shard_map/ppermute | solution.py:412
  (41 shorter events, 6.1 us)
Async XLA Ops:
  0.6 7.2 %copy-start = (f32[2048]{0:T(1024)S(1)}, f32[2048]{0:T(1024)}, u32[]{:S(2)}) copy-start(f32[2048]{0:T(1024)} %param.6) | copy-start | bytes 24580
  0.6 8.3 %collective-permute-start.4 = (bf16[512,128]{1,0:T(8,128)(2,1)}, bf16[512,128]{1,0:T(8,128)(2,1)S(1)}, u32[]{:S(2)}, u32[]{:S(2)}) collective-permute-start(bf16[512,128]{1,0:T(8,128)(2,1)} %targets_ref.1), channel_id=1, source_target_pairs={{0,16},{16,0},{1,17},{17,1},{2,18},{18,2},{3,19},{19,3},{4,20},{20... | collective-permute-start | bytes 393224 | tf_op jit(solution)/shard_map/ppermute | solution.py:412
  3.7 7.7 %collective-permute-start = (bf16[128,128]{1,0:T(8,128)(2,1)}, bf16[128,128]{1,0:T(8,128)(2,1)S(1)}, u32[]{:S(2)}, u32[]{:S(2)}) collective-permute-start(bf16[128,128]{1,0:T(8,128)(2,1)} %sources_ref.1), channel_id=1, source_target_pairs={{0,4},{4,0},{8,12},{12,8},{1,5},{5,1},{9,13},{13,9},{2,6},{6,2},{1... | collective-permute-start | bytes 98312 | tf_op jit(solution)/shard_map/ppermute | solution.py:412
  5.3 6.1 %collective-permute-start.2 = (bf16[128,128]{1,0:T(8,128)(2,1)}, bf16[128,128]{1,0:T(8,128)(2,1)S(1)}, u32[]{:S(2)}, u32[]{:S(2)}) collective-permute-start(bf16[128,128]{1,0:T(8,128)(2,1)} %sources_ref.1), channel_id=1, source_target_pairs={{0,12},{4,8},{8,4},{12,0},{1,13},{5,9},{9,5},{13,1},{2,14},{6,10},... | collective-permute-start | bytes 98312 | tf_op jit(solution)/shard_map/ppermute | solution.py:412
  7.7 5.4 %collective-permute-start.1 = (bf16[128,128]{1,0:T(8,128)(2,1)}, bf16[128,128]{1,0:T(8,128)(2,1)S(1)}, u32[]{:S(2)}, u32[]{:S(2)}) collective-permute-start(bf16[128,128]{1,0:T(8,128)(2,1)} %sources_ref.1), channel_id=1, source_target_pairs={{0,8},{4,12},{8,0},{12,4},{1,9},{5,13},{9,1},{13,5},{2,10},{6,14},... | collective-permute-start | bytes 98312 | tf_op jit(solution)/shard_map/ppermute | solution.py:412
  8.8 5.9 %collective-permute-start.3 = (bf16[544,128]{1,0:T(8,128)(2,1)S(1)}, bf16[544,128]{1,0:T(8,128)(2,1)S(1)}, u32[]{:S(2)}, u32[]{:S(2)}) collective-permute-start(bf16[544,128]{1,0:T(8,128)(2,1)S(1)} %get-tuple-element.37.refs_0_), channel_id=1, source_target_pairs={{0,1},{1,0},{2,3},{3,2},{4,5},{5,4},{6,7},{7,6},{8,9},{9,8},{10,11... | collective-permute-start | bytes 417800 | tf_op jit(solution)/shard_map/ppermute | solution.py:412
  8.9 5.8 %collective-permute-start.5 = (bf16[512,128]{1,0:T(8,128)(2,1)S(1)}, bf16[512,128]{1,0:T(8,128)(2,1)S(1)}, u32[]{:S(2)}, u32[]{:S(2)}) collective-permute-start(bf16[512,128]{1,0:T(8,128)(2,1)S(1)} %collective-permute-done.4.refs_2_), channel_id=1, source_target_pairs={{0,1},{1,0},{2,3},{3,2},{4,5},{5,4},{6,7},{7,6},{8,9},{9,8},{10,11... | collective-permute-start | bytes 393224 | tf_op jit(solution)/shard_map/ppermute | solution.py:412
  13.1 5.0 %collective-permute-start.6 = (bf16[512,128]{1,0:T(8,128)(2,1)S(1)}, bf16[512,128]{1,0:T(8,128)(2,1)S(1)}, u32[]{:S(2)}, u32[]{:S(2)}) collective-permute-start(bf16[512,128]{1,0:T(8,128)(2,1)S(1)} %pack.1.sources_ref.mine_ref), channel_id=1, source_target_pairs={{0,2},{2,0},{1,3},{3,1},{4,6},{6,4},{5,7},{7,5},{8,10},{10,8},{9,1... | collective-permute-start | bytes 393224 | tf_op jit(solution)/shard_map/ppermute | solution.py:412
  32.4 3.1 %collective-permute-start.9 = (f32[16,128]{1,0:T(8,128)S(1)}, f32[16,128]{1,0:T(8,128)S(1)}, u32[]{:S(2)}, u32[]{:S(2)}) collective-permute-start(f32[16,128]{1,0:T(8,128)S(1)} %get-tuple-element.51.refs_0_), channel_id=1, source_target_pairs={{0,17},{1,16},{16,1},{17,0},{2,19},{3,18},{18,3},{19,2},{4,21},{5,... | collective-permute-start | bytes 24584 | tf_op jit(solution)/shard_map/ppermute | solution.py:412
  32.4 3.7 %collective-permute-start.8 = (f32[16,128]{1,0:T(8,128)S(1)}, f32[16,128]{1,0:T(8,128)S(1)}, u32[]{:S(2)}, u32[]{:S(2)}) collective-permute-start(f32[16,128]{1,0:T(8,128)S(1)} %get-tuple-element.51.refs_0_), channel_id=1, source_target_pairs={{0,16},{1,17},{16,0},{17,1},{2,18},{3,19},{18,2},{19,3},{4,20},{5,... | collective-permute-start | bytes 24584 | tf_op jit(solution)/shard_map/ppermute | solution.py:412
  33.0 3.1 %collective-permute-start.7 = (f32[16,128]{1,0:T(8,128)S(1)}, f32[16,128]{1,0:T(8,128)S(1)}, u32[]{:S(2)}, u32[]{:S(2)}) collective-permute-start(f32[16,128]{1,0:T(8,128)S(1)} %get-tuple-element.51.refs_0_), channel_id=1, source_target_pairs={{0,1},{1,0},{16,17},{17,16},{2,3},{3,2},{18,19},{19,18},{4,5},{5,4... | collective-permute-start | bytes 24584 | tf_op jit(solution)/shard_map/ppermute | solution.py:412
  47.4 3.1 %collective-permute-start.12 = (f32[16,128]{1,0:T(8,128)S(1)}, f32[16,128]{1,0:T(8,128)S(1)}, u32[]{:S(2)}, u32[]{:S(2)}) collective-permute-start(f32[16,128]{1,0:T(8,128)S(1)} %get-tuple-element.59.refs_0_), channel_id=1, source_target_pairs={{0,17},{1,16},{16,1},{17,0},{2,19},{3,18},{18,3},{19,2},{4,21},{5,... | collective-permute-start | bytes 24584 | tf_op jit(solution)/shard_map/ppermute | solution.py:412
  47.4 3.7 %collective-permute-start.11 = (f32[16,128]{1,0:T(8,128)S(1)}, f32[16,128]{1,0:T(8,128)S(1)}, u32[]{:S(2)}, u32[]{:S(2)}) collective-permute-start(f32[16,128]{1,0:T(8,128)S(1)} %get-tuple-element.59.refs_0_), channel_id=1, source_target_pairs={{0,16},{1,17},{16,0},{17,1},{2,18},{3,19},{18,2},{19,3},{4,20},{5,... | collective-permute-start | bytes 24584 | tf_op jit(solution)/shard_map/ppermute | solution.py:412
  47.9 3.1 %collective-permute-start.10 = (f32[16,128]{1,0:T(8,128)S(1)}, f32[16,128]{1,0:T(8,128)S(1)}, u32[]{:S(2)}, u32[]{:S(2)}) collective-permute-start(f32[16,128]{1,0:T(8,128)S(1)} %get-tuple-element.59.refs_0_), channel_id=1, source_target_pairs={{0,1},{1,0},{16,17},{17,16},{2,3},{3,2},{18,19},{19,18},{4,5},{5,4... | collective-permute-start | bytes 24584 | tf_op jit(solution)/shard_map/ppermute | solution.py:412
  61.6 2.2 %collective-permute-start.13 = (f32[2,4,128]{2,0,1:T(2,128)S(1)}, f32[2,4,128]{2,0,1:T(2,128)S(1)}, u32[]{:S(2)}, u32[]{:S(2)}) collective-permute-start(f32[2,4,128]{2,0,1:T(2,128)S(1)} %copy.13), channel_id=1, source_target_pairs={{0,1},{1,0},{2,3},{3,2},{4,5},{5,4},{6,7},{7,6},{8,9},{9,8},{10,11... | collective-permute-start | bytes 12296 | tf_op jit(solution)/shard_map/ppermute | solution.py:412
  61.7 3.1 %collective-permute-start.16 = (f32[16,128]{1,0:T(8,128)S(1)}, f32[16,128]{1,0:T(8,128)S(1)}, u32[]{:S(2)}, u32[]{:S(2)}) collective-permute-start(f32[16,128]{1,0:T(8,128)S(1)} %get-tuple-element.63), channel_id=1, source_target_pairs={{0,17},{1,16},{16,1},{17,0},{2,19},{3,18},{18,3},{19,2},{4,21},{5,... | collective-permute-start | bytes 24584 | tf_op jit(solution)/shard_map/ppermute | solution.py:412
  62.3 3.7 %collective-permute-start.15 = (f32[16,128]{1,0:T(8,128)S(1)}, f32[16,128]{1,0:T(8,128)S(1)}, u32[]{:S(2)}, u32[]{:S(2)}) collective-permute-start(f32[16,128]{1,0:T(8,128)S(1)} %get-tuple-element.63), channel_id=1, source_target_pairs={{0,16},{1,17},{16,0},{17,1},{2,18},{3,19},{18,2},{19,3},{4,20},{5,... | collective-permute-start | bytes 24584 | tf_op jit(solution)/shard_map/ppermute | solution.py:412
  63.9 2.1 %collective-permute-start.14 = (f32[16,128]{1,0:T(8,128)S(1)}, f32[16,128]{1,0:T(8,128)S(1)}, u32[]{:S(2)}, u32[]{:S(2)}) collective-permute-start(f32[16,128]{1,0:T(8,128)S(1)} %get-tuple-element.63), channel_id=1, source_target_pairs={{0,1},{1,0},{16,17},{17,16},{2,3},{3,2},{18,19},{19,18},{4,5},{5,4... | collective-permute-start | bytes 24584 | tf_op jit(solution)/shard_map/ppermute | solution.py:412

commit v7 on v6

--- a/solution.py
+++ b/solution.py
@@ -15,6 +15,7 @@
 CORES = 2
 PIECES = 3
 ROWS = 256
+TURNS = 2
 F32 = jnp.float32
 VMEM = pl.BlockSpec(memory_space=pltpu.VMEM)
 SMEM = pl.BlockSpec(memory_space=pltpu.SMEM)
@@ -164,9 +165,9 @@
 
 
 class Rows:
-    def __init__(self, count):
-        self.peak = jnp.full((8, count), -1e30, F32)
-        self.total = jnp.zeros((8, count), F32)
+    def __init__(self, count, carry=None):
+        empty = (jnp.full((8, count), -1e30, F32), jnp.zeros((8, count), F32))
+        self.peak, self.total = empty if carry is None else carry
 
     def add(self, scores_ref):
         tops = self.peak
@@ -243,12 +244,18 @@
         group_refs, (out_ref, sources_ref, *score_refs) = refs[: len(groups)], refs[len(groups) :]
         cols = jnp.concatenate([ref[...] for ref in group_refs], axis=0)
         cols = jnp.concatenate([cols, ones_for(count)], axis=1)
+
+        def turn(index, carry):
+            rows = Rows(count, carry)
+            for at in range(0, width // TURNS, ROWS):
+                scores_ref = score_refs[at // ROWS % len(score_refs)]
+                span = pl.ds(pl.multiple_of(index * (width // TURNS) + at, ROWS), ROWS)
+                scores_ref[...] = product(jnp.concatenate([targets_ref[span, :], offset_ref[span, :]], axis=1), cols)
+                rows.add(scores_ref)
+            return rows.peak, rows.total
+
         rows = Rows(count)
-        for at in range(0, width, ROWS):
-            scores_ref = score_refs[at // ROWS % len(score_refs)]
-            scores_ref[...] = product(jnp.concatenate([targets_ref[at : at + ROWS, :], offset_ref[at : at + ROWS, :]], axis=1), cols)
-            rows.add(scores_ref)
-        lse = rows.lse()
+        lse = Rows(count, lax.fori_loop(0, TURNS, turn, (rows.peak, rows.total))).lse()
         for step in range(len(groups) + 1):
             start = jnp.bitwise_xor(place_ref[2], step) * each
             ref = group_refs[step - 1] if step else mine_ref
@@ -279,26 +286,32 @@
         shift = [pieces_of(to_column(shift[i : i + 1, :], mask)) for i in range(count // LANES)]
         cols = jnp.concatenate([sources_ref[...], jnp.concatenate(shift, axis=0)], axis=1)
         ones = ones_for(ROWS)
-        for at in range(0, width, ROWS):
-            scores_ref = score_refs[at // ROWS % len(score_refs)]
-            scores_ref[...] = product(jnp.concatenate([targets_ref[at : at + ROWS, :], ones], axis=1), cols)
-            for block in range(0, ROWS, LANES):
-                peaks, totals = [], []
-                for row in range(block, block + LANES, 8):
-                    scores = scores_ref[row : row + 8, :]
-                    pieces = [scores[:, lane : lane + LANES] for lane in range(0, count, LANES)]
-                    peak = tree(pieces, jnp.maximum)
-                    pieces = [jnp.exp2((piece - peak) * SCALE) for piece in pieces]
-                    plan_ref[at + row : at + row + 8, :] = jnp.concatenate(pieces, axis=1)
-                    peaks.append(peak * SCALE)
-                    totals.append(tree(pieces, jnp.add))
-                peak = jnp.concatenate(peaks, axis=0)
-                peak_ref[at + block : at + block + LANES, :] = peak
-                peak, total = peak.T, jnp.concatenate(totals, axis=0).T
-                top = jnp.max(peak, axis=0, keepdims=True)
-                total = jnp.sum(total * jnp.exp2(peak - top), axis=0, keepdims=True)
-                index = (at + block) // LANES
-                out_ref[index : index + 1, :] = top + jnp.log2(total)
+
+        def turn(index, unused):
+            base = index * (width // TURNS)
+            for at in range(0, width // TURNS, ROWS):
+                scores_ref = score_refs[at // ROWS % len(score_refs)]
+                span = pl.ds(pl.multiple_of(base + at, ROWS), ROWS)
+                scores_ref[...] = product(jnp.concatenate([targets_ref[span, :], ones], axis=1), cols)
+                for block in range(0, ROWS, LANES):
+                    peaks, totals = [], []
+                    for row in range(block, block + LANES, 8):
+                        scores = scores_ref[row : row + 8, :]
+                        pieces = [scores[:, lane : lane + LANES] for lane in range(0, count, LANES)]
+                        peak = tree(pieces, jnp.maximum)
+                        pieces = [jnp.exp2((piece - peak) * SCALE) for piece in pieces]
+                        plan_ref[pl.ds(pl.multiple_of(base + at + row, 8), 8), :] = jnp.concatenate(pieces, axis=1)
+                        peaks.append(peak * SCALE)
+                        totals.append(tree(pieces, jnp.add))
+                    peak = jnp.concatenate(peaks, axis=0)
+                    peak_ref[pl.ds(pl.multiple_of(base + at + block, LANES), LANES), :] = peak
+                    peak, total = peak.T, jnp.concatenate(totals, axis=0).T
+                    top = jnp.max(peak, axis=0, keepdims=True)
+                    total = jnp.sum(total * jnp.exp2(peak - top), axis=0, keepdims=True)
+                    out_ref[pl.ds((base + at + block) // LANES, 1), :] = top + jnp.log2(total)
+            return unused
+
+        lax.fori_loop(0, TURNS, turn, 0)
 
     return pl.pallas_call(
         kernel,
@@ -316,16 +329,21 @@
     )(pin(sources), pin(targets), parts, log_mass)
 
 
-def weighted_rows(reach_of, weight, plan_ref, out_ref):
-    count = plan_ref.shape[1]
+def weighted_rows(reach_of, weight_ref, plan_ref, out_ref):
+    width, count = plan_ref.shape
     mask = diagonal()
-    total = jnp.zeros((8, count), F32)
-    for block in range(plan_ref.shape[0] // LANES):
-        at = block * LANES
-        reach = reach_of(at, block, mask) * to_column(weight[block : block + 1, :], mask)
-        for row in range(0, LANES, 8):
-            factor = jnp.concatenate([reach[row : row + 8, :]] * (count // LANES), axis=1)
-            total = total + plan_ref[at + row : at + row + 8, :] * factor
+
+    def turn(index, total):
+        base = index * (width // TURNS)
+        for step in range(0, width // TURNS, LANES):
+            at, block = pl.multiple_of(base + step, LANES), pl.ds((base + step) // LANES, 1)
+            reach = reach_of(at, block, mask) * to_column(weight_ref[block, :], mask)
+            for row in range(0, LANES, 8):
+                factor = jnp.concatenate([reach[row : row + 8, :]] * (count // LANES), axis=1)
+                total = total + plan_ref[pl.ds(pl.multiple_of(at + row, 8), 8), :] * factor
+        return total
+
+    total = lax.fori_loop(0, TURNS, turn, jnp.zeros((8, count), F32))
     fold_into(out_ref, jnp.sum(total, axis=0, keepdims=True))
 
 
@@ -334,15 +352,14 @@
 
     def kernel(plan_ref, peak_ref, mass_ref, *refs):
         part_refs, (lse_ref, reach_ref, out_ref) = refs[:-3], refs[-3:]
-        lse = log_sum([ref[...] for ref in part_refs])
-        lse_ref[...] = lse
+        lse_ref[...] = log_sum([ref[...] for ref in part_refs])
 
         def reach_of(at, block, mask):
-            reach = jnp.exp2(peak_ref[at : at + LANES, :] - to_column(lse[block : block + 1, :], mask))
-            reach_ref[at : at + LANES, :] = reach
+            reach = jnp.exp2(peak_ref[pl.ds(at, LANES), :] - to_column(lse_ref[block, :], mask))
+            reach_ref[pl.ds(at, LANES), :] = reach
             return reach
 
-        weighted_rows(reach_of, mass_ref[...], plan_ref, out_ref)
+        weighted_rows(reach_of, mass_ref, plan_ref, out_ref)
 
     return pl.pallas_call(
         kernel,
@@ -358,15 +375,16 @@
     width, count = plan.shape
 
     def kernel(plan_ref, reach_ref, mass_ref, *refs):
-        part_refs, out_ref = refs[:-1], refs[-1]
-        weight = mass_ref[...] / tree([ref[...] for ref in part_refs], jnp.add)
-        weighted_rows(lambda at, block, mask: reach_ref[at : at + LANES, :], weight, plan_ref, out_ref)
+        part_refs, (out_ref, weight_ref) = refs[:-2], refs[-2:]
+        weight_ref[...] = mass_ref[...] / tree([ref[...] for ref in part_refs], jnp.add)
+        weighted_rows(lambda at, block, mask: reach_ref[pl.ds(at, LANES), :], weight_ref, plan_ref, out_ref)
 
     return pl.pallas_call(
         kernel,
         out_shape=rows_of(count),
         in_specs=[VMEM] * (3 + len(parts)),
         out_specs=VMEM,
+        scratch_shapes=[pltpu.VMEM((width // LANES, LANES), F32)],
         compiler_params=params(),
         name="later_rows",
     )(pin(plan), pin(reach), mass, *parts)
@@ -380,13 +398,19 @@
         potential_ref[...] = half_ref[...] + UNIT * (factor - lse_ref[...])
         factor = unfold(jnp.exp2(factor))
         factors = [factor[:, lane : lane + LANES] for lane in range(0, count, LANES)]
-        for at in range(0, width, LANES):
-            totals = []
-            for row in range(at, at + LANES, 8):
-                plan = plan_ref[row : row + 8, :]
-                totals.append(tree([plan[:, i * LANES : (i + 1) * LANES] * factors[i] for i in range(count // LANES)], jnp.add))
-            total = jnp.concatenate(totals, axis=0) * reach_ref[at : at + LANES, :]
-            out_ref[at // LANES : at // LANES + 1, :] = jnp.sum(total.T, axis=0, keepdims=True)
+
+        def turn(index, unused):
+            for step in range(0, width // TURNS, LANES):
+                at = pl.multiple_of(index * (width // TURNS) + step, LANES)
+                totals = []
+                for row in range(0, LANES, 8):
+                    plan = plan_ref[pl.ds(pl.multiple_of(at + row, 8), 8), :]
+                    totals.append(tree([plan[:, i * LANES : (i + 1) * LANES] * factors[i] for i in range(count // LANES)], jnp.add))
+                total = jnp.concatenate(totals, axis=0) * reach_ref[pl.ds(at, LANES), :]
+                out_ref[pl.ds(at // LANES, 1), :] = jnp.sum(total.T, axis=0, keepdims=True)
+            return unused
+
+        lax.fori_loop(0, TURNS, turn, 0)
 
     return pl.pallas_call(
         kernel,

time: 66.9 us -> 67.8 us (1.013)
  Pallas kernels: 11 us -> 11.9 us
where the time goes in v7:
time: 67.8 us; the launch traced here: 67.5 us
  blocking collectives  28 us (41%)
  starting transfers between devices  15.3 us (23%)
  Pallas kernels  11.9 us (18%)
  waiting for transfers between devices  9.56 us (14%)
  other arithmetic  1.26 us (2%)
  between operations  0.83 us (1%)
    all_to_all x3, blocking collectives, share(): return lax.all_to_all(copies, ('z', 'x'), 0, 0, tiled=True)  28 us
    ppermute x17, starting transfers between devices, swap(): return lax.ppermute(value, axes, [(i, i ^ distance) for i in range(size)])  15.3 us
    ppermute x17, waiting for transfers between devices, swap(): return lax.ppermute(value, axes, [(i, i ^ distance) for i in range(size)])  9.56 us
    pallas_call x1, Pallas kernels, first_columns(): pl.pallas_call(kernel, out_shape=(pltpu.VMEM((width, count), F32), pltpu....  2.88 us
    pallas_call x1, Pallas kernels, first_rows(): pl.pallas_call(kernel, out_shape=(pltpu.VMEM((width, LANES), jnp.bfloat16...  2.19 us
    pallas_call x2, Pallas kernels, later_columns(): pl.pallas_call(kernel, out_shape=(rows_of(width), rows_of(count)), in_spe...  2.12 us
    pallas_call x1, Pallas kernels, other_rows(): pl.pallas_call(kernel, out_shape=(rows_of(count + each * LANES), pltpu.VM...  1.95 us
  transfers between devices with their start and end apart: 17, of which 9 were waited for; matrix products, arithmetic and copies ran while one was open for 2% of the time, Pallas kernels for 5%

profile of v7, /device:TPU:0, one launch (start us, length us, event | category | flops | bytes accessed | tf_op | source)
XLA Modules:
  0.0 67.5 jit_solution(15714842368275536012)
XLA Ops:
  0.6 3.0 %collective-permute-start.4 = (bf16[512,128]{1,0:T(8,128)(2,1)}, bf16[512,128]{1,0:T(8,128)(2,1)S(1)}, u32[]{:S(2)}, u32[]{:S(2)}) collective-permute-start(bf16[512,128]{1,0:T(8,128)(2,1)} %targets_ref.1), channel_id=1, source_target_pairs={{0,16},{16,0},{1,17},{17,1},{2,18},{18,2},{3,19},{19,3},{4,20},{20... | collective-permute-start | bytes 393224 | tf_op jit(solution)/shard_map/ppermute | solution.py:436
  3.7 1.6 %collective-permute-start = (bf16[128,128]{1,0:T(8,128)(2,1)}, bf16[128,128]{1,0:T(8,128)(2,1)S(1)}, u32[]{:S(2)}, u32[]{:S(2)}) collective-permute-start(bf16[128,128]{1,0:T(8,128)(2,1)} %sources_ref.1), channel_id=1, source_target_pairs={{0,4},{4,0},{8,12},{12,8},{1,5},{5,1},{9,13},{13,9},{2,6},{6,2},{1... | collective-permute-start | bytes 98312 | tf_op jit(solution)/shard_map/ppermute | solution.py:436
  5.3 2.5 %collective-permute-start.2 = (bf16[128,128]{1,0:T(8,128)(2,1)}, bf16[128,128]{1,0:T(8,128)(2,1)S(1)}, u32[]{:S(2)}, u32[]{:S(2)}) collective-permute-start(bf16[128,128]{1,0:T(8,128)(2,1)} %sources_ref.1), channel_id=1, source_target_pairs={{0,12},{4,8},{8,4},{12,0},{1,13},{5,9},{9,5},{13,1},{2,14},{6,10},... | collective-permute-start | bytes 98312 | tf_op jit(solution)/shard_map/ppermute | solution.py:436
  7.9 1.0 %ready.1 = (bf16[128,128]{1,0:T(8,128)(2,1)S(1)}, bf16[544,128]{1,0:T(8,128)(2,1)S(1)}, f32[8,128]{1,0:T(8,128)S(1)}, f32[8,128]{1,0:T(8,128)S(1)}) custom-call(bf16[128,128]{1,0:T(8,128)(2,1)} %sources_ref.1, bf16[512,128]{1,0:T(8,128)(2,1)} %targets_ref.1, f32[8,128]{1,0:T(8,128)} %bitcast.31, f32[8,128]{1,0:T(8,128)S(1)} %bitcast.24), custom_call_target="tpu_custom_call" | custom-call | flops 1048576 | bytes 1048576 | tf_op jit(solution)/shard_map/ready/pallas_call | solution.py:96
  9.4 1.9 %collective-permute-done.2.block_ref = bf16[128,128]{1,0:T(8,128)(2,1)S(1)} collective-permute-done((bf16[128,128]{1,0:T(8,128)(2,1)}, bf16[128,128]{1,0:T(8,128)(2,1)S(1)}, u32[]{:S(2)}, u32[]{:S(2)}) %collective-permute-start.2) | collective-permute-done | bytes 32800 | tf_op jit(solution)/shard_map/ppermute | solution.py:436
  11.4 1.8 %collective-permute-done.1.refs_2_ = bf16[128,128]{1,0:T(8,128)(2,1)S(1)} collective-permute-done((bf16[128,128]{1,0:T(8,128)(2,1)}, bf16[128,128]{1,0:T(8,128)(2,1)S(1)}, u32[]{:S(2)}, u32[]{:S(2)}) %collective-permute-start.1) | collective-permute-done | bytes 32800 | tf_op jit(solution)/shard_map/ppermute | solution.py:436
  13.1 1.6 %collective-permute-start.6 = (bf16[512,128]{1,0:T(8,128)(2,1)S(1)}, bf16[512,128]{1,0:T(8,128)(2,1)S(1)}, u32[]{:S(2)}, u32[]{:S(2)}) collective-permute-start(bf16[512,128]{1,0:T(8,128)(2,1)S(1)} %pack.1.sources_ref.mine_ref), channel_id=1, source_target_pairs={{0,2},{2,0},{1,3},{3,1},{4,6},{6,4},{5,7},{7,5},{8,10},{10,8},{9,1... | collective-permute-start | bytes 393224 | tf_op jit(solution)/shard_map/ppermute | solution.py:436
  14.8 2.2 %first_rows.1 = (bf16[2048,128]{1,0:T(8,128)(2,1)S(1)}, bf16[2048,128]{1,0:T(8,128)(2,1)S(1)}, f32[16,128]{1,0:T(8,128)S(1)}, f32[4,128]{1,0:T(4,128)S(1)}) custom-call(s32[3]{0:T(128)S(1)} %pad_add_fusion.place_ref, f32[8,128]{1,0:T(8,128)S(1)} %get-tuple-element.35.mass_ref, bf16[512,128]{1,0:T(8,128)(2,1)S(1)} %pack.1.sources_ref.mine_ref, ...), custom_call_target="tpu_custom_call" | custom-call | flops 536870912 | bytes 1048576 | tf_op jit(solution)/shard_map/first_rows/pallas_call | solution.py:222
  16.9 1.2 %collective-permute-done.6.refs_0_ = bf16[512,128]{1,0:T(8,128)(2,1)S(1)} collective-permute-done((bf16[512,128]{1,0:T(8,128)(2,1)S(1)}, bf16[512,128]{1,0:T(8,128)(2,1)S(1)}, u32[]{:S(2)}, u32[]{:S(2)}) %collective-permute-start.6) | collective-permute-done | bytes 131104 | tf_op jit(solution)/shard_map/ppermute | solution.py:436
  18.2 2.0 %other_rows.1 = (f32[8,128]{1,0:T(8,128)S(1)}, bf16[1024,128]{1,0:T(8,128)(2,1)S(1)}) custom-call(s32[3]{0:T(128)S(1)} %pad_add_fusion.place_ref, bf16[2048,128]{1,0:T(8,128)(2,1)S(1)} %get-tuple-element.49.targets_ref, bf16[2048,128]{1,0:T(8,128)(2,1)S(1)} %get-tuple-element.39.offset_ref, f32[4,128]{1,0:T(4,128)S(1)} %get-tuple-element.40.first_ref, ...), custom_call_target="tpu_custom_call" | custom-call | tf_op jit(solution)/shard_map/other_rows/pallas_call | solution.py:267
  20.1 9.9 %all_to_all.15.parts_ref = f32[8,8,128]{2,1,0:T(8,128)S(1)} all-to-all(f32[8,8,128]{2,1,0:T(8,128)S(1)} %broadcast_in_dim.6), channel_id=1, replica_groups=mesh['src'=2,'z'=4,'x'=2,'core'=2] {'z','x'}, dimensions={0} | all-to-all | bytes 65536 | tf_op jit(solution)/shard_map/all_to_all | solution.py:449
  30.0 2.9 %first_columns.1 = (f32[2048,1024]{1,0:T(8,128)S(1)}, f32[2048,128]{1,0:T(8,128)S(1)}, f32[16,128]{1,0:T(8,128)S(1)}, f32[8,128]{1,0:T(8,128)S(1)}) custom-call(bf16[1024,128]{1,0:T(8,128)(2,1)S(1)} %get-tuple-element.48.sources_ref, bf16[2048,128]{1,0:T(8,128)(2,1)S(1)} %get-tuple-element.49.targets_ref, f32[8,8,128]{2,1,0:T(8,128)S(1)} %all_to_all.15.parts_ref, ...), custom_call_target="tpu_custom_call" | custom-call | tf_op jit(solution)/shard_map/first_columns/pallas_call | solution.py:316
  33.6 1.3 %collective-permute-start.7 = (f32[16,128]{1,0:T(8,128)S(1)}, f32[16,128]{1,0:T(8,128)S(1)}, u32[]{:S(2)}, u32[]{:S(2)}) collective-permute-start(f32[16,128]{1,0:T(8,128)S(1)} %get-tuple-element.51.refs_0_), channel_id=1, source_target_pairs={{0,1},{1,0},{16,17},{17,16},{2,3},{3,2},{18,19},{19,18},{4,5},{5,4... | collective-permute-start | bytes 24584 | tf_op jit(solution)/shard_map/ppermute | solution.py:436
  36.7 1.0 %second_rows.1 = (f32[16,128]{1,0:T(8,128)S(1)}, f32[2048,128]{1,0:T(8,128)S(1)}, f32[8,128]{1,0:T(8,128)S(1)}) custom-call(f32[2048,1024]{1,0:T(8,128)S(1)} %get-tuple-element.44.plan_ref, f32[2048,128]{1,0:T(8,128)S(1)} %get-tuple-element.45.peak_ref, f32[16,128]{1,0:T(8,128)S(1)} %get-tuple-element.46.mass_ref, f32[16,128]{1,0:T(8,128)S(1)} %get-tuple-element.51.refs_0_, ...), custom_call_target="tpu_custom_call" | custom-call | tf_op jit(solution)/shard_map/second_rows/pallas_call | solution.py:364
  37.7 9.1 %all_to_all.16.parts_ref = f32[8,8,128]{2,1,0:T(8,128)S(1)} all-to-all(f32[8,8,128]{2,1,0:T(8,128)S(1)} %broadcast_in_dim.7), channel_id=1, replica_groups=mesh['src'=2,'z'=4,'x'=2,'core'=2] {'z','x'}, dimensions={0} | all-to-all | bytes 65536 | tf_op jit(solution)/shard_map/all_to_all | solution.py:449
  46.8 1.3 %later_columns.2 = (f32[16,128]{1,0:T(8,128)S(1)}, f32[8,128]{1,0:T(8,128)}) custom-call(f32[2048,1024]{1,0:T(8,128)S(1)} %get-tuple-element.44.plan_ref, f32[2048,128]{1,0:T(8,128)S(1)} %get-tuple-element.55.reach_ref, f32[8,8,128]{2,1,0:T(8,128)S(1)} %all_to_all.16.parts_ref, f32[8,128]{1,0:T(8,128)S(1)} %get-tuple-element.43.log_ref, ...), custom_call_target="tpu_custom_call" | custom-call | tf_op jit(solution)/shard_map/later_columns/pallas_call | solution.py:415
  48.7 1.3 %collective-permute-start.10 = (f32[16,128]{1,0:T(8,128)S(1)}, f32[16,128]{1,0:T(8,128)S(1)}, u32[]{:S(2)}, u32[]{:S(2)}) collective-permute-start(f32[16,128]{1,0:T(8,128)S(1)} %get-tuple-element.59.refs_0_), channel_id=1, source_target_pairs={{0,1},{1,0},{16,17},{17,16},{2,3},{3,2},{18,19},{19,18},{4,5},{5,4... | collective-permute-start | bytes 24584 | tf_op jit(solution)/shard_map/ppermute | solution.py:436
  50.0 1.2 %collective-permute-done.12.refs_3_ = f32[16,128]{1,0:T(8,128)S(1)} collective-permute-done((f32[16,128]{1,0:T(8,128)S(1)}, f32[16,128]{1,0:T(8,128)S(1)}, u32[]{:S(2)}, u32[]{:S(2)}) %collective-permute-start.12) | collective-permute-done | bytes 8224 | tf_op jit(solution)/shard_map/ppermute | solution.py:436
  51.8 0.8 %later_rows.1 = f32[8,128]{1,0:T(8,128)S(1)} custom-call(f32[2048,1024]{1,0:T(8,128)S(1)} %get-tuple-element.44.plan_ref, f32[2048,128]{1,0:T(8,128)S(1)} %get-tuple-element.55.reach_ref, f32[16,128]{1,0:T(8,128)S(1)} %get-tuple-element.46.mass_ref, f32[16,128]{1,0:T(8,128)S(1)} %get-tuple-element.59.refs_0_, f32[16,128]{1,0:T(8,128)S(1)} %collective-permute-done.10.refs_1_, ...), custom_call_target="tpu_custom_call" | custom-call | tf_op jit(solution)/shard_map/later_rows/pallas_call | solution.py:382
  52.6 9.1 %all_to_all.17.parts_ref = f32[8,8,128]{2,1,0:T(8,128)S(1)} all-to-all(f32[8,8,128]{2,1,0:T(8,128)S(1)} %broadcast_in_dim.8), channel_id=1, replica_groups=mesh['src'=2,'z'=4,'x'=2,'core'=2] {'z','x'}, dimensions={0} | all-to-all | bytes 65536 | tf_op jit(solution)/shard_map/all_to_all | solution.py:449
  61.7 0.8 %later_columns.3 = (f32[16,128]{1,0:T(8,128)S(1)}, f32[8,128]{1,0:T(8,128)S(1)}) custom-call(f32[2048,1024]{1,0:T(8,128)S(1)} %get-tuple-element.44.plan_ref, f32[2048,128]{1,0:T(8,128)S(1)} %get-tuple-element.55.reach_ref, f32[8,8,128]{2,1,0:T(8,128)S(1)} %all_to_all.17.parts_ref, f32[8,128]{1,0:T(8,128)S(1)} %get-tuple-element.43.log_ref, ...), custom_call_target="tpu_custom_call" | custom-call | tf_op jit(solution)/shard_map/later_columns/pallas_call | solution.py:415
  62.6 0.7 collective-permute-start.16
  63.2 1.5 %collective-permute-start.15 = (f32[16,128]{1,0:T(8,128)S(1)}, f32[16,128]{1,0:T(8,128)S(1)}, u32[]{:S(2)}, u32[]{:S(2)}) collective-permute-start(f32[16,128]{1,0:T(8,128)S(1)} %get-tuple-element.63), channel_id=1, source_target_pairs={{0,16},{1,17},{16,0},{17,1},{2,18},{3,19},{18,2},{19,3},{4,20},{5,... | collective-permute-start | bytes 24584 | tf_op jit(solution)/shard_map/ppermute | solution.py:436
  65.7 1.2 %collective-permute-done.15 = f32[16,128]{1,0:T(8,128)S(1)} collective-permute-done((f32[16,128]{1,0:T(8,128)S(1)}, f32[16,128]{1,0:T(8,128)S(1)}, u32[]{:S(2)}, u32[]{:S(2)}) %collective-permute-start.15) | collective-permute-done | bytes 8224 | tf_op jit(solution)/shard_map/ppermute | solution.py:436
  (41 shorter events, 6.2 us)
Async XLA Ops:
  0.6 7.2 %copy-start = (f32[2048]{0:T(1024)S(1)}, f32[2048]{0:T(1024)}, u32[]{:S(2)}) copy-start(f32[2048]{0:T(1024)} %param.6) | copy-start | bytes 24580
  0.6 8.3 %collective-permute-start.4 = (bf16[512,128]{1,0:T(8,128)(2,1)}, bf16[512,128]{1,0:T(8,128)(2,1)S(1)}, u32[]{:S(2)}, u32[]{:S(2)}) collective-permute-start(bf16[512,128]{1,0:T(8,128)(2,1)} %targets_ref.1), channel_id=1, source_target_pairs={{0,16},{16,0},{1,17},{17,1},{2,18},{18,2},{3,19},{19,3},{4,20},{20... | collective-permute-start | bytes 393224 | tf_op jit(solution)/shard_map/ppermute | solution.py:436
  3.7 7.7 %collective-permute-start = (bf16[128,128]{1,0:T(8,128)(2,1)}, bf16[128,128]{1,0:T(8,128)(2,1)S(1)}, u32[]{:S(2)}, u32[]{:S(2)}) collective-permute-start(bf16[128,128]{1,0:T(8,128)(2,1)} %sources_ref.1), channel_id=1, source_target_pairs={{0,4},{4,0},{8,12},{12,8},{1,5},{5,1},{9,13},{13,9},{2,6},{6,2},{1... | collective-permute-start | bytes 98312 | tf_op jit(solution)/shard_map/ppermute | solution.py:436
  5.3 6.1 %collective-permute-start.2 = (bf16[128,128]{1,0:T(8,128)(2,1)}, bf16[128,128]{1,0:T(8,128)(2,1)S(1)}, u32[]{:S(2)}, u32[]{:S(2)}) collective-permute-start(bf16[128,128]{1,0:T(8,128)(2,1)} %sources_ref.1), channel_id=1, source_target_pairs={{0,12},{4,8},{8,4},{12,0},{1,13},{5,9},{9,5},{13,1},{2,14},{6,10},... | collective-permute-start | bytes 98312 | tf_op jit(solution)/shard_map/ppermute | solution.py:436
  7.7 5.4 %collective-permute-start.1 = (bf16[128,128]{1,0:T(8,128)(2,1)}, bf16[128,128]{1,0:T(8,128)(2,1)S(1)}, u32[]{:S(2)}, u32[]{:S(2)}) collective-permute-start(bf16[128,128]{1,0:T(8,128)(2,1)} %sources_ref.1), channel_id=1, source_target_pairs={{0,8},{4,12},{8,0},{12,4},{1,9},{5,13},{9,1},{13,5},{2,10},{6,14},... | collective-permute-start | bytes 98312 | tf_op jit(solution)/shard_map/ppermute | solution.py:436
  8.8 5.9 %collective-permute-start.3 = (bf16[544,128]{1,0:T(8,128)(2,1)S(1)}, bf16[544,128]{1,0:T(8,128)(2,1)S(1)}, u32[]{:S(2)}, u32[]{:S(2)}) collective-permute-start(bf16[544,128]{1,0:T(8,128)(2,1)S(1)} %get-tuple-element.37.refs_0_), channel_id=1, source_target_pairs={{0,1},{1,0},{2,3},{3,2},{4,5},{5,4},{6,7},{7,6},{8,9},{9,8},{10,11... | collective-permute-start | bytes 417800 | tf_op jit(solution)/shard_map/ppermute | solution.py:436
  8.9 5.8 %collective-permute-start.5 = (bf16[512,128]{1,0:T(8,128)(2,1)S(1)}, bf16[512,128]{1,0:T(8,128)(2,1)S(1)}, u32[]{:S(2)}, u32[]{:S(2)}) collective-permute-start(bf16[512,128]{1,0:T(8,128)(2,1)S(1)} %collective-permute-done.4.refs_2_), channel_id=1, source_target_pairs={{0,1},{1,0},{2,3},{3,2},{4,5},{5,4},{6,7},{7,6},{8,9},{9,8},{10,11... | collective-permute-start | bytes 393224 | tf_op jit(solution)/shard_map/ppermute | solution.py:436
  13.1 5.0 %collective-permute-start.6 = (bf16[512,128]{1,0:T(8,128)(2,1)S(1)}, bf16[512,128]{1,0:T(8,128)(2,1)S(1)}, u32[]{:S(2)}, u32[]{:S(2)}) collective-permute-start(bf16[512,128]{1,0:T(8,128)(2,1)S(1)} %pack.1.sources_ref.mine_ref), channel_id=1, source_target_pairs={{0,2},{2,0},{1,3},{3,1},{4,6},{6,4},{5,7},{7,5},{8,10},{10,8},{9,1... | collective-permute-start | bytes 393224 | tf_op jit(solution)/shard_map/ppermute | solution.py:436
  32.9 3.1 %collective-permute-start.9 = (f32[16,128]{1,0:T(8,128)S(1)}, f32[16,128]{1,0:T(8,128)S(1)}, u32[]{:S(2)}, u32[]{:S(2)}) collective-permute-start(f32[16,128]{1,0:T(8,128)S(1)} %get-tuple-element.51.refs_0_), channel_id=1, source_target_pairs={{0,17},{1,16},{16,1},{17,0},{2,19},{3,18},{18,3},{19,2},{4,21},{5,... | collective-permute-start | bytes 24584 | tf_op jit(solution)/shard_map/ppermute | solution.py:436
  33.0 3.7 %collective-permute-start.8 = (f32[16,128]{1,0:T(8,128)S(1)}, f32[16,128]{1,0:T(8,128)S(1)}, u32[]{:S(2)}, u32[]{:S(2)}) collective-permute-start(f32[16,128]{1,0:T(8,128)S(1)} %get-tuple-element.51.refs_0_), channel_id=1, source_target_pairs={{0,16},{1,17},{16,0},{17,1},{2,18},{3,19},{18,2},{19,3},{4,20},{5,... | collective-permute-start | bytes 24584 | tf_op jit(solution)/shard_map/ppermute | solution.py:436
  33.6 3.1 %collective-permute-start.7 = (f32[16,128]{1,0:T(8,128)S(1)}, f32[16,128]{1,0:T(8,128)S(1)}, u32[]{:S(2)}, u32[]{:S(2)}) collective-permute-start(f32[16,128]{1,0:T(8,128)S(1)} %get-tuple-element.51.refs_0_), channel_id=1, source_target_pairs={{0,1},{1,0},{16,17},{17,16},{2,3},{3,2},{18,19},{19,18},{4,5},{5,4... | collective-permute-start | bytes 24584 | tf_op jit(solution)/shard_map/ppermute | solution.py:436
  48.1 3.1 %collective-permute-start.12 = (f32[16,128]{1,0:T(8,128)S(1)}, f32[16,128]{1,0:T(8,128)S(1)}, u32[]{:S(2)}, u32[]{:S(2)}) collective-permute-start(f32[16,128]{1,0:T(8,128)S(1)} %get-tuple-element.59.refs_0_), channel_id=1, source_target_pairs={{0,17},{1,16},{16,1},{17,0},{2,19},{3,18},{18,3},{19,2},{4,21},{5,... | collective-permute-start | bytes 24584 | tf_op jit(solution)/shard_map/ppermute | solution.py:436
  48.1 3.7 %collective-permute-start.11 = (f32[16,128]{1,0:T(8,128)S(1)}, f32[16,128]{1,0:T(8,128)S(1)}, u32[]{:S(2)}, u32[]{:S(2)}) collective-permute-start(f32[16,128]{1,0:T(8,128)S(1)} %get-tuple-element.59.refs_0_), channel_id=1, source_target_pairs={{0,16},{1,17},{16,0},{17,1},{2,18},{3,19},{18,2},{19,3},{4,20},{5,... | collective-permute-start | bytes 24584 | tf_op jit(solution)/shard_map/ppermute | solution.py:436
  48.7 3.1 %collective-permute-start.10 = (f32[16,128]{1,0:T(8,128)S(1)}, f32[16,128]{1,0:T(8,128)S(1)}, u32[]{:S(2)}, u32[]{:S(2)}) collective-permute-start(f32[16,128]{1,0:T(8,128)S(1)} %get-tuple-element.59.refs_0_), channel_id=1, source_target_pairs={{0,1},{1,0},{16,17},{17,16},{2,3},{3,2},{18,19},{19,18},{4,5},{5,4... | collective-permute-start | bytes 24584 | tf_op jit(solution)/shard_map/ppermute | solution.py:436
  62.5 2.2 %collective-permute-start.13 = (f32[2,4,128]{2,0,1:T(2,128)S(1)}, f32[2,4,128]{2,0,1:T(2,128)S(1)}, u32[]{:S(2)}, u32[]{:S(2)}) collective-permute-start(f32[2,4,128]{2,0,1:T(2,128)S(1)} %copy.13), channel_id=1, source_target_pairs={{0,1},{1,0},{2,3},{3,2},{4,5},{5,4},{6,7},{7,6},{8,9},{9,8},{10,11... | collective-permute-start | bytes 12296 | tf_op jit(solution)/shard_map/ppermute | solution.py:436
  62.6 3.1 %collective-permute-start.16 = (f32[16,128]{1,0:T(8,128)S(1)}, f32[16,128]{1,0:T(8,128)S(1)}, u32[]{:S(2)}, u32[]{:S(2)}) collective-permute-start(f32[16,128]{1,0:T(8,128)S(1)} %get-tuple-element.63), channel_id=1, source_target_pairs={{0,17},{1,16},{16,1},{17,0},{2,19},{3,18},{18,3},{19,2},{4,21},{5,... | collective-permute-start | bytes 24584 | tf_op jit(solution)/shard_map/ppermute | solution.py:436
  63.2 3.7 %collective-permute-start.15 = (f32[16,128]{1,0:T(8,128)S(1)}, f32[16,128]{1,0:T(8,128)S(1)}, u32[]{:S(2)}, u32[]{:S(2)}) collective-permute-start(f32[16,128]{1,0:T(8,128)S(1)} %get-tuple-element.63), channel_id=1, source_target_pairs={{0,16},{1,17},{16,0},{17,1},{2,18},{3,19},{18,2},{19,3},{4,20},{5,... | collective-permute-start | bytes 24584 | tf_op jit(solution)/shard_map/ppermute | solution.py:436
  64.7 2.2 %collective-permute-start.14 = (f32[16,128]{1,0:T(8,128)S(1)}, f32[16,128]{1,0:T(8,128)S(1)}, u32[]{:S(2)}, u32[]{:S(2)}) collective-permute-start(f32[16,128]{1,0:T(8,128)S(1)} %get-tuple-element.63), channel_id=1, source_target_pairs={{0,1},{1,0},{16,17},{17,16},{2,3},{3,2},{18,19},{19,18},{4,5},{5,4... | collective-permute-start | bytes 24584 | tf_op jit(solution)/shard_map/ppermute | solution.py:436

commit v8 on v6

--- a/solution.py
+++ b/solution.py
@@ -193,10 +193,10 @@
         own_ref, other_ref, block_refs = refs[0], refs[1], refs[2 : 2 + len(blocks)]
         targets_ref, offset_ref, full_ref, out_ref, *score_refs = refs[2 + len(blocks) :]
         src, core = place_ref[0], place_ref[1]
-        full_ref[pl.ds(pl.multiple_of(core * chunk, chunk), chunk), :] = mass_ref[...]
+        full_ref[pl.ds(pl.multiple_of(core * chunk, chunk), chunk), :] = jnp.log2(mass_ref[...])
         parts = [other_ref[part + i * chunk : part + (i + 1) * chunk, :].astype(F32) for i in range(PIECES)]
         start = pl.multiple_of(jnp.bitwise_xor(core, 1) * chunk, chunk)
-        full_ref[pl.ds(start, chunk), :] = parts[0] + (parts[1] + parts[2])
+        full_ref[pl.ds(start, chunk), :] = jnp.log2(parts[0] + (parts[1] + parts[2]))
         for dc in range(CORES):
             for ds in range(n_src):
                 index = jnp.bitwise_xor(core, dc) * n_src + jnp.bitwise_xor(src, ds)
@@ -204,7 +204,7 @@
                 ref = refs[dc] if ds == 0 else block_refs[dc * (n_src - 1) + ds - 1]
                 targets_ref[pl.ds(start, part), :] = ref[:part, :]
         mask = diagonal()
-        log_mass = jnp.log2(full_ref[...]) * (1.0 / SCALE)
+        log_mass = full_ref[...] * (1.0 / SCALE)
         cols = jnp.concatenate([sources_ref[...], ones_for(count)], axis=1)
         rows = Rows(count)
         for at in range(0, width, ROWS):
@@ -271,9 +271,10 @@
 def first_columns(sources, targets, parts, log_mass):
     count, width = sources.shape[0], targets.shape[0]
 
-    def kernel(sources_ref, targets_ref, parts_ref, log_ref, plan_ref, peak_ref, out_ref, lse_ref, *score_refs):
+    def kernel(sources_ref, targets_ref, parts_ref, log_ref, plan_ref, reach_ref, top_ref, out_ref, lse_ref, *score_refs):
         lse = log_sum([parts_ref[i] for i in range(parts.shape[0])])
         lse_ref[...] = lse
+        out_ref[width // LANES :, :] = jnp.zeros_like(lse)
         mask = diagonal()
         shift = (log_ref[...] - lse) * (1.0 / SCALE)
         shift = [pieces_of(to_column(shift[i : i + 1, :], mask)) for i in range(count // LANES)]
@@ -293,12 +294,13 @@
                     peaks.append(peak * SCALE)
                     totals.append(tree(pieces, jnp.add))
                 peak = jnp.concatenate(peaks, axis=0)
-                peak_ref[at + block : at + block + LANES, :] = peak
-                peak, total = peak.T, jnp.concatenate(totals, axis=0).T
-                top = jnp.max(peak, axis=0, keepdims=True)
-                total = jnp.sum(total * jnp.exp2(peak - top), axis=0, keepdims=True)
+                top = jnp.max(peak, axis=1, keepdims=True)
+                reach = jnp.exp2(peak - top)
+                reach_ref[at + block : at + block + LANES, :] = reach
+                total = jnp.sum((jnp.concatenate(totals, axis=0) * reach).T, axis=0, keepdims=True)
                 index = (at + block) // LANES
-                out_ref[index : index + 1, :] = top + jnp.log2(total)
+                top_ref[index : index + 1, :] = to_row(top, mask)
+                out_ref[index : index + 1, :] = top_ref[index : index + 1, :] + jnp.log2(total)
 
     return pl.pallas_call(
         kernel,
@@ -306,78 +308,50 @@
             pltpu.VMEM((width, count), F32),
             pltpu.VMEM((width, LANES), F32),
             rows_of(width),
+            rows_of(width + count),
             rows_of(count),
         ),
         in_specs=[VMEM] * 4,
-        out_specs=(VMEM,) * 4,
+        out_specs=(VMEM,) * 5,
         scratch_shapes=[pltpu.VMEM((ROWS, count), F32)] * 2,
         compiler_params=params(),
         name="first_columns",
     )(pin(sources), pin(targets), parts, log_mass)
 
 
-def weighted_rows(reach_of, weight, plan_ref, out_ref):
-    count = plan_ref.shape[1]
-    mask = diagonal()
-    total = jnp.zeros((8, count), F32)
-    for block in range(plan_ref.shape[0] // LANES):
-        at = block * LANES
-        reach = reach_of(at, block, mask) * to_column(weight[block : block + 1, :], mask)
-        for row in range(0, LANES, 8):
-            factor = jnp.concatenate([reach[row : row + 8, :]] * (count // LANES), axis=1)
-            total = total + plan_ref[at + row : at + row + 8, :] * factor
-    fold_into(out_ref, jnp.sum(total, axis=0, keepdims=True))
-
-
-def second_rows(plan, peak, mass, parts):
+def later_rows(plan, reach, top, log_mass, parts):
     width, count = plan.shape
-
-    def kernel(plan_ref, peak_ref, mass_ref, *refs):
-        part_refs, (lse_ref, reach_ref, out_ref) = refs[:-3], refs[-3:]
-        lse = log_sum([ref[...] for ref in part_refs])
-        lse_ref[...] = lse
-
-        def reach_of(at, block, mask):
-            reach = jnp.exp2(peak_ref[at : at + LANES, :] - to_column(lse[block : block + 1, :], mask))
-            reach_ref[at : at + LANES, :] = reach
-            return reach
-
-        weighted_rows(reach_of, mass_ref[...], plan_ref, out_ref)
-
-    return pl.pallas_call(
-        kernel,
-        out_shape=(rows_of(width), pltpu.VMEM((width, LANES), F32), rows_of(count)),
-        in_specs=[VMEM] * (3 + len(parts)),
-        out_specs=(VMEM,) * 3,
-        compiler_params=params(),
-        name="second_rows",
-    )(pin(plan), pin(peak), mass, *parts)
-
-
-def later_rows(plan, reach, mass, parts):
+    rows = width // LANES
+
+    def kernel(plan_ref, reach_ref, top_ref, log_ref, *refs):
+        part_refs, out_ref = refs[:-1], refs[-1]
+        weight = jnp.exp2(log_ref[...] + (top_ref[...] - log_sum([ref[:rows, :] for ref in part_refs])))
+        mask = diagonal()
+        total = jnp.zeros((8, count), F32)
+        for block in range(rows):
+            at = block * LANES
+            factors = reach_ref[at : at + LANES, :] * to_column(weight[block : block + 1, :], mask)
+            for row in range(0, LANES, 8):
+                factor = jnp.concatenate([factors[row : row + 8, :]] * (count // LANES), axis=1)
+                total = total + plan_ref[at + row : at + row + 8, :] * factor
+        fold_into(out_ref, jnp.sum(total, axis=0, keepdims=True))
+
+    return pl.pallas_call(
+        kernel,
+        out_shape=rows_of(count),
+        in_specs=[VMEM] * (4 + len(parts)),
+        out_specs=VMEM,
+        compiler_params=params(),
+        name="later_rows",
+    )(pin(plan), pin(reach), top, log_mass, *parts)
+
+
+def later_columns(plan, reach, top, parts, log_mass, lse, half):
     width, count = plan.shape
 
-    def kernel(plan_ref, reach_ref, mass_ref, *refs):
-        part_refs, out_ref = refs[:-1], refs[-1]
-        weight = mass_ref[...] / tree([ref[...] for ref in part_refs], jnp.add)
-        weighted_rows(lambda at, block, mask: reach_ref[at : at + LANES, :], weight, plan_ref, out_ref)
-
-    return pl.pallas_call(
-        kernel,
-        out_shape=rows_of(count),
-        in_specs=[VMEM] * (3 + len(parts)),
-        out_specs=VMEM,
-        compiler_params=params(),
-        name="later_rows",
-    )(pin(plan), pin(reach), mass, *parts)
-
-
-def later_columns(plan, reach, parts, log_mass, lse, half):
-    width, count = plan.shape
-
-    def kernel(plan_ref, reach_ref, parts_ref, log_ref, lse_ref, half_ref, out_ref, potential_ref):
+    def kernel(plan_ref, reach_ref, top_ref, parts_ref, log_ref, lse_ref, half_ref, out_ref):
         factor = log_ref[...] - jnp.log2(tree([parts_ref[i] for i in range(parts.shape[0])], jnp.add))
-        potential_ref[...] = half_ref[...] + UNIT * (factor - lse_ref[...])
+        out_ref[width // LANES :, :] = half_ref[...] + UNIT * (factor - lse_ref[...])
         factor = unfold(jnp.exp2(factor))
         factors = [factor[:, lane : lane + LANES] for lane in range(0, count, LANES)]
         for at in range(0, width, LANES):
@@ -386,16 +360,18 @@
                 plan = plan_ref[row : row + 8, :]
                 totals.append(tree([plan[:, i * LANES : (i + 1) * LANES] * factors[i] for i in range(count // LANES)], jnp.add))
             total = jnp.concatenate(totals, axis=0) * reach_ref[at : at + LANES, :]
-            out_ref[at // LANES : at // LANES + 1, :] = jnp.sum(total.T, axis=0, keepdims=True)
-
-    return pl.pallas_call(
-        kernel,
-        out_shape=(rows_of(width), rows_of(count)),
-        in_specs=[VMEM] * 6,
-        out_specs=(VMEM,) * 2,
+            index = at // LANES
+            total = jnp.log2(jnp.sum(total.T, axis=0, keepdims=True))
+            out_ref[index : index + 1, :] = top_ref[index : index + 1, :] + total
+
+    return pl.pallas_call(
+        kernel,
+        out_shape=rows_of(width + count),
+        in_specs=[VMEM] * 7,
+        out_specs=VMEM,
         compiler_params=params(),
         name="later_columns",
-    )(pin(plan), pin(reach), parts, log_mass, lse, half)
+    )(pin(plan), pin(reach), top, parts, log_mass, lse, half)
 
 
 def levels_of(size):
@@ -451,21 +427,20 @@
         place, a = lax.optimization_barrier((place, a))
         targets, offsets, b, first = first_rows(place, b, packed, blocks, groups[0])
         own, sources = other_rows(place, targets, offsets, first, groups)
-        plan, peak, own, row_lse = first_columns(sources, targets, share(own, n_far), a)
+        plan, reach, top, own, row_lse = first_columns(sources, targets, share(own, n_far), a)
         early_x, early_y, own = lax.optimization_barrier((sources, targets, own))
         half_x, half_y = half_norm(early_x).reshape(-1, LANES), half_norm(early_y).reshape(-1, LANES)
         parts = swap_all(own, near, n_near)
         half_x, half_y, *parts = lax.optimization_barrier((half_x, half_y, *parts))
-        col_lse, reach, rows = second_rows(plan, peak, b, parts)
         for step in range(1, ITERS):
-            if step > 1:
-                rows = later_rows(plan, reach, b, parts)
-            own, potential = later_columns(plan, reach, share(rows, n_far), a, row_lse, half_x)
+            rows = later_rows(plan, reach, top, b, parts)
+            own = later_columns(plan, reach, top, share(rows, n_far), a, row_lse, half_x)
             parts = swap_all(own, near, n_near)
-        mine, other = swap_all(potential.reshape(n_x, n_z, part), "core", CORES)
-        low, high = jnp.where(core == 0, mine, other), jnp.where(core == 0, other, mine)
-        source_potential = jnp.stack([low, high], axis=2).swapaxes(0, 1).reshape(-1)
-        target_potential = half_y - UNIT * (col_lse + jnp.log2(tree(parts, jnp.add)))
+        rows = half_y.shape[0]
+        mine, other = [value[rows:].reshape(n_x, n_z, part) for value in parts[:CORES]]
+        first, second = jnp.where(core == 0, mine, other), jnp.where(core == 0, other, mine)
+        source_potential = jnp.stack([first, second], axis=2).swapaxes(0, 1).reshape(-1)
+        target_potential = half_y - UNIT * log_sum([value[:rows] for value in parts])
         target_potential = target_potential.reshape(CORES, -1)
         target_potential = lax.dynamic_index_in_dim(target_potential, core, axis=0, keepdims=False)
         return source_potential, target_potential

time: 66.9 us -> 67.1 us (level)
  waiting for transfers between devices: 9.52 us -> 10.3 us
  Pallas kernels: 11 us -> 10.3 us
    ppermute x17 -> x16, waiting for transfers between devices: 9.52 us -> 10.3 us  [swap(): return lax.ppermute(value, axes, [(i, i ^ distance) for i in range(size)])]
    ppermute x17 -> x16, starting transfers between devices: 15.3 us -> 15.4 us  [swap(): return lax.ppermute(value, axes, [(i, i ^ distance) for i in range(size)])]
  transfers between devices with their start and end apart: 17 -> 16, of which waited for: 9 -> 9; matrix products, arithmetic and copies ran while one was open for 2% -> 1% of each run, Pallas kernels for 5% -> 5%
where the time goes in v8:
time: 67.1 us; the launch traced here: 66.8 us
  blocking collectives  28.1 us (42%)
  starting transfers between devices  15.4 us (23%)
  Pallas kernels  10.3 us (15%)
  waiting for transfers between devices  10.3 us (15%)
  other arithmetic  1.27 us (2%)
  between operations  0.83 us (1%)
    all_to_all x3, blocking collectives, share(): return lax.all_to_all(copies, ('z', 'x'), 0, 0, tiled=True)  28.1 us
    ppermute x16, starting transfers between devices, swap(): return lax.ppermute(value, axes, [(i, i ^ distance) for i in range(size)])  15.4 us
    ppermute x16, waiting for transfers between devices, swap(): return lax.ppermute(value, axes, [(i, i ^ distance) for i in range(size)])  10.3 us
    pallas_call x1, Pallas kernels, first_columns(): pl.pallas_call(kernel, out_shape=(pltpu.VMEM((width, count), F32), pltpu....  2.45 us
    pallas_call x1, Pallas kernels, first_rows(): pl.pallas_call(kernel, out_shape=(pltpu.VMEM((width, LANES), jnp.bfloat16...  2.18 us
    pallas_call x1, Pallas kernels, other_rows(): pl.pallas_call(kernel, out_shape=(rows_of(count + each * LANES), pltpu.VM...  1.77 us
    pallas_call x2, Pallas kernels, later_rows(): pl.pallas_call(kernel, out_shape=rows_of(count), in_specs=[VMEM] * (4 + l...  1.51 us
    pallas_call x2, Pallas kernels, later_columns(): pl.pallas_call(kernel, out_shape=rows_of(width + count), in_specs=[VMEM]...  1.46 us
  transfers between devices with their start and end apart: 16, of which 9 were waited for; matrix products, arithmetic and copies ran while one was open for 1% of the time, Pallas kernels for 5%

profile of v8, /device:TPU:0, one launch (start us, length us, event | category | flops | bytes accessed | tf_op | source)
XLA Modules:
  0.0 66.8 jit_solution(6088583272800347784)
XLA Ops:
  0.6 3.0 %collective-permute-start.4 = (bf16[512,128]{1,0:T(8,128)(2,1)}, bf16[512,128]{1,0:T(8,128)(2,1)S(1)}, u32[]{:S(2)}, u32[]{:S(2)}) collective-permute-start(bf16[512,128]{1,0:T(8,128)(2,1)} %targets_ref.1), channel_id=1, source_target_pairs={{0,16},{16,0},{1,17},{17,1},{2,18},{18,2},{3,19},{19,3},{4,20},{20... | collective-permute-start | bytes 393224 | tf_op jit(solution)/shard_map/ppermute | solution.py:388
  3.7 1.6 %collective-permute-start = (bf16[128,128]{1,0:T(8,128)(2,1)}, bf16[128,128]{1,0:T(8,128)(2,1)S(1)}, u32[]{:S(2)}, u32[]{:S(2)}) collective-permute-start(bf16[128,128]{1,0:T(8,128)(2,1)} %sources_ref.1), channel_id=1, source_target_pairs={{0,4},{4,0},{8,12},{12,8},{1,5},{5,1},{9,13},{13,9},{2,6},{6,2},{1... | collective-permute-start | bytes 98312 | tf_op jit(solution)/shard_map/ppermute | solution.py:388
  5.3 2.5 %collective-permute-start.2 = (bf16[128,128]{1,0:T(8,128)(2,1)}, bf16[128,128]{1,0:T(8,128)(2,1)S(1)}, u32[]{:S(2)}, u32[]{:S(2)}) collective-permute-start(bf16[128,128]{1,0:T(8,128)(2,1)} %sources_ref.1), channel_id=1, source_target_pairs={{0,12},{4,8},{8,4},{12,0},{1,13},{5,9},{9,5},{13,1},{2,14},{6,10},... | collective-permute-start | bytes 98312 | tf_op jit(solution)/shard_map/ppermute | solution.py:388
  7.9 1.0 %ready.1 = (bf16[128,128]{1,0:T(8,128)(2,1)S(1)}, bf16[544,128]{1,0:T(8,128)(2,1)S(1)}, f32[8,128]{1,0:T(8,128)S(1)}, f32[8,128]{1,0:T(8,128)S(1)}) custom-call(bf16[128,128]{1,0:T(8,128)(2,1)} %sources_ref.1, bf16[512,128]{1,0:T(8,128)(2,1)} %targets_ref.1, f32[8,128]{1,0:T(8,128)} %bitcast.26, f32[8,128]{1,0:T(8,128)S(1)} %bitcast.21), custom_call_target="tpu_custom_call" | custom-call | flops 1048576 | bytes 1048576 | tf_op jit(solution)/shard_map/ready/pallas_call | solution.py:95
  9.4 1.9 %collective-permute-done.2.block_ref = bf16[128,128]{1,0:T(8,128)(2,1)S(1)} collective-permute-done((bf16[128,128]{1,0:T(8,128)(2,1)}, bf16[128,128]{1,0:T(8,128)(2,1)S(1)}, u32[]{:S(2)}, u32[]{:S(2)}) %collective-permute-start.2) | collective-permute-done | bytes 32800 | tf_op jit(solution)/shard_map/ppermute | solution.py:388
  11.4 1.8 %collective-permute-done.1.refs_2_ = bf16[128,128]{1,0:T(8,128)(2,1)S(1)} collective-permute-done((bf16[128,128]{1,0:T(8,128)(2,1)}, bf16[128,128]{1,0:T(8,128)(2,1)S(1)}, u32[]{:S(2)}, u32[]{:S(2)}) %collective-permute-start.1) | collective-permute-done | bytes 32800 | tf_op jit(solution)/shard_map/ppermute | solution.py:388
  13.1 1.6 %collective-permute-start.6 = (bf16[512,128]{1,0:T(8,128)(2,1)S(1)}, bf16[512,128]{1,0:T(8,128)(2,1)S(1)}, u32[]{:S(2)}, u32[]{:S(2)}) collective-permute-start(bf16[512,128]{1,0:T(8,128)(2,1)S(1)} %pack.1.sources_ref.mine_ref), channel_id=1, source_target_pairs={{0,2},{2,0},{1,3},{3,1},{4,6},{6,4},{5,7},{7,5},{8,10},{10,8},{9,1... | collective-permute-start | bytes 393224 | tf_op jit(solution)/shard_map/ppermute | solution.py:388
  14.8 2.2 %first_rows.1 = (bf16[2048,128]{1,0:T(8,128)(2,1)S(1)}, bf16[2048,128]{1,0:T(8,128)(2,1)S(1)}, f32[16,128]{1,0:T(8,128)S(1)}, f32[4,128]{1,0:T(4,128)S(1)}) custom-call(s32[3]{0:T(128)S(1)} %pad_add_fusion.place_ref, f32[8,128]{1,0:T(8,128)S(1)} %get-tuple-element.30.mass_ref, bf16[512,128]{1,0:T(8,128)(2,1)S(1)} %pack.1.sources_ref.mine_ref, ...), custom_call_target="tpu_custom_call" | custom-call | flops 536870912 | bytes 1048576 | tf_op jit(solution)/shard_map/first_rows/pallas_call | solution.py:221
  16.9 1.2 %collective-permute-done.6.refs_0_ = bf16[512,128]{1,0:T(8,128)(2,1)S(1)} collective-permute-done((bf16[512,128]{1,0:T(8,128)(2,1)S(1)}, bf16[512,128]{1,0:T(8,128)(2,1)S(1)}, u32[]{:S(2)}, u32[]{:S(2)}) %collective-permute-start.6) | collective-permute-done | bytes 131104 | tf_op jit(solution)/shard_map/ppermute | solution.py:388
  18.2 1.8 %other_rows.1 = (f32[8,128]{1,0:T(8,128)S(1)}, bf16[1024,128]{1,0:T(8,128)(2,1)S(1)}) custom-call(s32[3]{0:T(128)S(1)} %pad_add_fusion.place_ref, bf16[2048,128]{1,0:T(8,128)(2,1)S(1)} %get-tuple-element.45.targets_ref, bf16[2048,128]{1,0:T(8,128)(2,1)S(1)} %get-tuple-element.34.offset_ref, f32[4,128]{1,0:T(4,128)S(1)} %get-tuple-element.35.first_ref, ...), custom_call_target="tpu_custom_call" | custom-call | tf_op jit(solution)/shard_map/other_rows/pallas_call | solution.py:260
  19.9 9.9 %all_to_all.15.parts_ref = f32[8,8,128]{2,1,0:T(8,128)S(1)} all-to-all(f32[8,8,128]{2,1,0:T(8,128)S(1)} %broadcast_in_dim.6), channel_id=1, replica_groups=mesh['src'=2,'z'=4,'x'=2,'core'=2] {'z','x'}, dimensions={0} | all-to-all | bytes 65536 | tf_op jit(solution)/shard_map/all_to_all | solution.py:401
  29.9 2.5 %first_columns.1 = (f32[2048,1024]{1,0:T(8,128)S(1)}, f32[2048,128]{1,0:T(8,128)S(1)}, f32[16,128]{1,0:T(8,128)S(1)}, f32[24,128]{1,0:T(8,128)S(1)}, f32[8,128]{1,0:T(8,128)S(1)}) custom-call(bf16[1024,128]{1,0:T(8,128)(2,1)S(1)} %get-tuple-element.44.sources_ref, bf16[2048,128]{1,0:T(8,128)(2,1)S(1)} %get-tuple-element.45.targets_ref, ...), custom_call_target="tpu_custom_call" | custom-call | tf_op jit(solution)/shard_map/first_columns/pallas_call | solution.py:305
  33.0 1.3 %collective-permute-start.7 = (f32[24,128]{1,0:T(8,128)S(1)}, f32[24,128]{1,0:T(8,128)S(1)}, u32[]{:S(2)}, u32[]{:S(2)}) collective-permute-start(f32[24,128]{1,0:T(8,128)S(1)} %get-tuple-element.47.refs_0_), channel_id=1, source_target_pairs={{0,1},{1,0},{16,17},{17,16},{2,3},{3,2},{18,19},{19,18},{4,5},{5,4... | collective-permute-start | bytes 36872 | tf_op jit(solution)/shard_map/ppermute | solution.py:388
  36.2 0.8 %later_rows.2 = f32[8,128]{1,0:T(8,128)S(1)} custom-call(f32[2048,1024]{1,0:T(8,128)S(1)} %get-tuple-element.39.plan_ref, f32[2048,128]{1,0:T(8,128)S(1)} %get-tuple-element.40.reach_ref, f32[16,128]{1,0:T(8,128)S(1)} %get-tuple-element.41.top_ref, f32[16,128]{1,0:T(8,128)S(1)} %get-tuple-element.42.log_ref, f32[24,128]{1,0:T(8,128)S(1)} %get-tuple-element.47.refs_0_, ...), custom_call_target="tpu_custom_call" | custom-call | tf_op jit(solution)/shard_map/later_rows/pallas_call | solution.py:339
  37.0 9.1 %all_to_all.16.parts_ref = f32[8,8,128]{2,1,0:T(8,128)S(1)} all-to-all(f32[8,8,128]{2,1,0:T(8,128)S(1)} %broadcast_in_dim.7), channel_id=1, replica_groups=mesh['src'=2,'z'=4,'x'=2,'core'=2] {'z','x'}, dimensions={0} | all-to-all | bytes 65536 | tf_op jit(solution)/shard_map/all_to_all | solution.py:401
  46.0 0.7 %later_columns.2.refs_0_ = f32[24,128]{1,0:T(8,128)S(1)} custom-call(f32[2048,1024]{1,0:T(8,128)S(1)} %get-tuple-element.39.plan_ref, f32[2048,128]{1,0:T(8,128)S(1)} %get-tuple-element.40.reach_ref, f32[16,128]{1,0:T(8,128)S(1)} %get-tuple-element.41.top_ref, f32[8,8,128]{2,1,0:T(8,128)S(1)} %all_to_all.16.parts_ref, ...), custom_call_target="tpu_custom_call" | custom-call | tf_op jit(solution)/shard_map/later_columns/pallas_call | solution.py:367
  47.4 1.3 %collective-permute-start.10 = (f32[24,128]{1,0:T(8,128)S(1)}, f32[24,128]{1,0:T(8,128)S(1)}, u32[]{:S(2)}, u32[]{:S(2)}) collective-permute-start(f32[24,128]{1,0:T(8,128)S(1)} %later_columns.2.refs_0_), channel_id=1, source_target_pairs={{0,1},{1,0},{16,17},{17,16},{2,3},{3,2},{18,19},{19,18},{4,5},{5,4... | collective-permute-start | bytes 36872 | tf_op jit(solution)/shard_map/ppermute | solution.py:388
  48.7 1.3 %collective-permute-done.12.refs_3_ = f32[24,128]{1,0:T(8,128)S(1)} collective-permute-done((f32[24,128]{1,0:T(8,128)S(1)}, f32[24,128]{1,0:T(8,128)S(1)}, u32[]{:S(2)}, u32[]{:S(2)}) %collective-permute-start.12) | collective-permute-done | bytes 12320 | tf_op jit(solution)/shard_map/ppermute | solution.py:388
  50.6 0.8 %later_rows.3 = f32[8,128]{1,0:T(8,128)S(1)} custom-call(f32[2048,1024]{1,0:T(8,128)S(1)} %get-tuple-element.39.plan_ref, f32[2048,128]{1,0:T(8,128)S(1)} %get-tuple-element.40.reach_ref, f32[16,128]{1,0:T(8,128)S(1)} %get-tuple-element.41.top_ref, f32[16,128]{1,0:T(8,128)S(1)} %get-tuple-element.42.log_ref, f32[24,128]{1,0:T(8,128)S(1)} %later_columns.2.refs_0_, ...), custom_call_target="tpu_custom_call" | custom-call | tf_op jit(solution)/shard_map/later_rows/pallas_call | solution.py:339
  51.4 9.1 %all_to_all.17.parts_ref = f32[8,8,128]{2,1,0:T(8,128)S(1)} all-to-all(f32[8,8,128]{2,1,0:T(8,128)S(1)} %broadcast_in_dim.8), channel_id=1, replica_groups=mesh['src'=2,'z'=4,'x'=2,'core'=2] {'z','x'}, dimensions={0} | all-to-all | bytes 65536 | tf_op jit(solution)/shard_map/all_to_all | solution.py:401
  60.4 0.7 %later_columns.3 = f32[24,128]{1,0:T(8,128)S(1)} custom-call(f32[2048,1024]{1,0:T(8,128)S(1)} %get-tuple-element.39.plan_ref, f32[2048,128]{1,0:T(8,128)S(1)} %get-tuple-element.40.reach_ref, f32[16,128]{1,0:T(8,128)S(1)} %get-tuple-element.41.top_ref, f32[8,8,128]{2,1,0:T(8,128)S(1)} %all_to_all.17.parts_ref, f32[8,128]{1,0:T(8,128)S(1)} %get-tuple-element.38.log_ref, ...), custom_call_target="tpu_custom_call" | custom-call | tf_op jit(solution)/shard_map/later_columns/pallas_call | solution.py:367
  61.9 1.5 %collective-permute-start.14 = (f32[24,128]{1,0:T(8,128)S(1)}, f32[24,128]{1,0:T(8,128)S(1)}, u32[]{:S(2)}, u32[]{:S(2)}) collective-permute-start(f32[24,128]{1,0:T(8,128)S(1)} %later_columns.3), channel_id=1, source_target_pairs={{0,16},{1,17},{16,0},{17,1},{2,18},{3,19},{18,2},{19,3},{4,20},{5,... | collective-permute-start | bytes 36872 | tf_op jit(solution)/shard_map/ppermute | solution.py:388
  63.4 1.0 %collective-permute-done.15 = f32[24,128]{1,0:T(8,128)S(1)} collective-permute-done((f32[24,128]{1,0:T(8,128)S(1)}, f32[24,128]{1,0:T(8,128)S(1)}, u32[]{:S(2)}, u32[]{:S(2)}) %collective-permute-start.15) | collective-permute-done | bytes 12320 | tf_op jit(solution)/shard_map/ppermute | solution.py:388
  64.4 1.1 %collective-permute-done.14 = f32[24,128]{1,0:T(8,128)S(1)} collective-permute-done((f32[24,128]{1,0:T(8,128)S(1)}, f32[24,128]{1,0:T(8,128)S(1)}, u32[]{:S(2)}, u32[]{:S(2)}) %collective-permute-start.14) | collective-permute-done | bytes 12320 | tf_op jit(solution)/shard_map/ppermute | solution.py:388
  (40 shorter events, 6.6 us)
Async XLA Ops:
  0.6 7.2 %copy-start = (f32[2048]{0:T(1024)S(1)}, f32[2048]{0:T(1024)}, u32[]{:S(2)}) copy-start(f32[2048]{0:T(1024)} %param.6) | copy-start | bytes 24580
  0.6 8.3 %collective-permute-start.4 = (bf16[512,128]{1,0:T(8,128)(2,1)}, bf16[512,128]{1,0:T(8,128)(2,1)S(1)}, u32[]{:S(2)}, u32[]{:S(2)}) collective-permute-start(bf16[512,128]{1,0:T(8,128)(2,1)} %targets_ref.1), channel_id=1, source_target_pairs={{0,16},{16,0},{1,17},{17,1},{2,18},{18,2},{3,19},{19,3},{4,20},{20... | collective-permute-start | bytes 393224 | tf_op jit(solution)/shard_map/ppermute | solution.py:388
  3.7 7.7 %collective-permute-start = (bf16[128,128]{1,0:T(8,128)(2,1)}, bf16[128,128]{1,0:T(8,128)(2,1)S(1)}, u32[]{:S(2)}, u32[]{:S(2)}) collective-permute-start(bf16[128,128]{1,0:T(8,128)(2,1)} %sources_ref.1), channel_id=1, source_target_pairs={{0,4},{4,0},{8,12},{12,8},{1,5},{5,1},{9,13},{13,9},{2,6},{6,2},{1... | collective-permute-start | bytes 98312 | tf_op jit(solution)/shard_map/ppermute | solution.py:388
  5.3 6.1 %collective-permute-start.2 = (bf16[128,128]{1,0:T(8,128)(2,1)}, bf16[128,128]{1,0:T(8,128)(2,1)S(1)}, u32[]{:S(2)}, u32[]{:S(2)}) collective-permute-start(bf16[128,128]{1,0:T(8,128)(2,1)} %sources_ref.1), channel_id=1, source_target_pairs={{0,12},{4,8},{8,4},{12,0},{1,13},{5,9},{9,5},{13,1},{2,14},{6,10},... | collective-permute-start | bytes 98312 | tf_op jit(solution)/shard_map/ppermute | solution.py:388
  7.7 5.4 %collective-permute-start.1 = (bf16[128,128]{1,0:T(8,128)(2,1)}, bf16[128,128]{1,0:T(8,128)(2,1)S(1)}, u32[]{:S(2)}, u32[]{:S(2)}) collective-permute-start(bf16[128,128]{1,0:T(8,128)(2,1)} %sources_ref.1), channel_id=1, source_target_pairs={{0,8},{4,12},{8,0},{12,4},{1,9},{5,13},{9,1},{13,5},{2,10},{6,14},... | collective-permute-start | bytes 98312 | tf_op jit(solution)/shard_map/ppermute | solution.py:388
  8.8 5.9 %collective-permute-start.3 = (bf16[544,128]{1,0:T(8,128)(2,1)S(1)}, bf16[544,128]{1,0:T(8,128)(2,1)S(1)}, u32[]{:S(2)}, u32[]{:S(2)}) collective-permute-start(bf16[544,128]{1,0:T(8,128)(2,1)S(1)} %get-tuple-element.32.refs_0_), channel_id=1, source_target_pairs={{0,1},{1,0},{2,3},{3,2},{4,5},{5,4},{6,7},{7,6},{8,9},{9,8},{10,11... | collective-permute-start | bytes 417800 | tf_op jit(solution)/shard_map/ppermute | solution.py:388
  8.9 5.8 %collective-permute-start.5 = (bf16[512,128]{1,0:T(8,128)(2,1)S(1)}, bf16[512,128]{1,0:T(8,128)(2,1)S(1)}, u32[]{:S(2)}, u32[]{:S(2)}) collective-permute-start(bf16[512,128]{1,0:T(8,128)(2,1)S(1)} %collective-permute-done.4.refs_2_), channel_id=1, source_target_pairs={{0,1},{1,0},{2,3},{3,2},{4,5},{5,4},{6,7},{7,6},{8,9},{9,8},{10,11... | collective-permute-start | bytes 393224 | tf_op jit(solution)/shard_map/ppermute | solution.py:388
  13.1 5.0 %collective-permute-start.6 = (bf16[512,128]{1,0:T(8,128)(2,1)S(1)}, bf16[512,128]{1,0:T(8,128)(2,1)S(1)}, u32[]{:S(2)}, u32[]{:S(2)}) collective-permute-start(bf16[512,128]{1,0:T(8,128)(2,1)S(1)} %pack.1.sources_ref.mine_ref), channel_id=1, source_target_pairs={{0,2},{2,0},{1,3},{3,1},{4,6},{6,4},{5,7},{7,5},{8,10},{10,8},{9,1... | collective-permute-start | bytes 393224 | tf_op jit(solution)/shard_map/ppermute | solution.py:388
  32.3 3.2 %collective-permute-start.9 = (f32[24,128]{1,0:T(8,128)S(1)}, f32[24,128]{1,0:T(8,128)S(1)}, u32[]{:S(2)}, u32[]{:S(2)}) collective-permute-start(f32[24,128]{1,0:T(8,128)S(1)} %get-tuple-element.47.refs_0_), channel_id=1, source_target_pairs={{0,17},{1,16},{16,1},{17,0},{2,19},{3,18},{18,3},{19,2},{4,21},{5,... | collective-permute-start | bytes 36872 | tf_op jit(solution)/shard_map/ppermute | solution.py:388
  32.4 3.8 %collective-permute-start.8 = (f32[24,128]{1,0:T(8,128)S(1)}, f32[24,128]{1,0:T(8,128)S(1)}, u32[]{:S(2)}, u32[]{:S(2)}) collective-permute-start(f32[24,128]{1,0:T(8,128)S(1)} %get-tuple-element.47.refs_0_), channel_id=1, source_target_pairs={{0,16},{1,17},{16,0},{17,1},{2,18},{3,19},{18,2},{19,3},{4,20},{5,... | collective-permute-start | bytes 36872 | tf_op jit(solution)/shard_map/ppermute | solution.py:388
  33.0 3.2 %collective-permute-start.7 = (f32[24,128]{1,0:T(8,128)S(1)}, f32[24,128]{1,0:T(8,128)S(1)}, u32[]{:S(2)}, u32[]{:S(2)}) collective-permute-start(f32[24,128]{1,0:T(8,128)S(1)} %get-tuple-element.47.refs_0_), channel_id=1, source_target_pairs={{0,1},{1,0},{16,17},{17,16},{2,3},{3,2},{18,19},{19,18},{4,5},{5,4... | collective-permute-start | bytes 36872 | tf_op jit(solution)/shard_map/ppermute | solution.py:388
  46.7 3.2 %collective-permute-start.12 = (f32[24,128]{1,0:T(8,128)S(1)}, f32[24,128]{1,0:T(8,128)S(1)}, u32[]{:S(2)}, u32[]{:S(2)}) collective-permute-start(f32[24,128]{1,0:T(8,128)S(1)} %later_columns.2.refs_0_), channel_id=1, source_target_pairs={{0,17},{1,16},{16,1},{17,0},{2,19},{3,18},{18,3},{19,2},{4,21},{5,... | collective-permute-start | bytes 36872 | tf_op jit(solution)/shard_map/ppermute | solution.py:388
  46.8 3.8 %collective-permute-start.11 = (f32[24,128]{1,0:T(8,128)S(1)}, f32[24,128]{1,0:T(8,128)S(1)}, u32[]{:S(2)}, u32[]{:S(2)}) collective-permute-start(f32[24,128]{1,0:T(8,128)S(1)} %later_columns.2.refs_0_), channel_id=1, source_target_pairs={{0,16},{1,17},{16,0},{17,1},{2,18},{3,19},{18,2},{19,3},{4,20},{5,... | collective-permute-start | bytes 36872 | tf_op jit(solution)/shard_map/ppermute | solution.py:388
  47.4 3.2 %collective-permute-start.10 = (f32[24,128]{1,0:T(8,128)S(1)}, f32[24,128]{1,0:T(8,128)S(1)}, u32[]{:S(2)}, u32[]{:S(2)}) collective-permute-start(f32[24,128]{1,0:T(8,128)S(1)} %later_columns.2.refs_0_), channel_id=1, source_target_pairs={{0,1},{1,0},{16,17},{17,16},{2,3},{3,2},{18,19},{19,18},{4,5},{5,4... | collective-permute-start | bytes 36872 | tf_op jit(solution)/shard_map/ppermute | solution.py:388
  61.2 2.2 %collective-permute-start.13 = (f32[24,128]{1,0:T(8,128)S(1)}, f32[24,128]{1,0:T(8,128)S(1)}, u32[]{:S(2)}, u32[]{:S(2)}) collective-permute-start(f32[24,128]{1,0:T(8,128)S(1)} %later_columns.3), channel_id=1, source_target_pairs={{0,1},{1,0},{16,17},{17,16},{2,3},{3,2},{18,19},{19,18},{4,5},{5,4... | collective-permute-start | bytes 36872 | tf_op jit(solution)/shard_map/ppermute | solution.py:388
  61.2 3.2 %collective-permute-start.15 = (f32[24,128]{1,0:T(8,128)S(1)}, f32[24,128]{1,0:T(8,128)S(1)}, u32[]{:S(2)}, u32[]{:S(2)}) collective-permute-start(f32[24,128]{1,0:T(8,128)S(1)} %later_columns.3), channel_id=1, source_target_pairs={{0,17},{1,16},{16,1},{17,0},{2,19},{3,18},{18,3},{19,2},{4,21},{5,... | collective-permute-start | bytes 36872 | tf_op jit(solution)/shard_map/ppermute | solution.py:388
  61.9 3.7 %collective-permute-start.14 = (f32[24,128]{1,0:T(8,128)S(1)}, f32[24,128]{1,0:T(8,128)S(1)}, u32[]{:S(2)}, u32[]{:S(2)}) collective-permute-start(f32[24,128]{1,0:T(8,128)S(1)} %later_columns.3), channel_id=1, source_target_pairs={{0,16},{1,17},{16,0},{17,1},{2,18},{3,19},{18,2},{19,3},{4,20},{5,... | collective-permute-start | bytes 36872 | tf_op jit(solution)/shard_map/ppermute | solution.py:388

commit v9 on v8

--- a/solution.py
+++ b/solution.py
@@ -274,7 +274,6 @@
     def kernel(sources_ref, targets_ref, parts_ref, log_ref, plan_ref, reach_ref, top_ref, out_ref, lse_ref, *score_refs):
         lse = log_sum([parts_ref[i] for i in range(parts.shape[0])])
         lse_ref[...] = lse
-        out_ref[width // LANES :, :] = jnp.zeros_like(lse)
         mask = diagonal()
         shift = (log_ref[...] - lse) * (1.0 / SCALE)
         shift = [pieces_of(to_column(shift[i : i + 1, :], mask)) for i in range(count // LANES)]
@@ -308,7 +307,7 @@
             pltpu.VMEM((width, count), F32),
             pltpu.VMEM((width, LANES), F32),
             rows_of(width),
-            rows_of(width + count),
+            rows_of(width),
             rows_of(count),
         ),
         in_specs=[VMEM] * 4,
@@ -325,7 +324,7 @@
 
     def kernel(plan_ref, reach_ref, top_ref, log_ref, *refs):
         part_refs, out_ref = refs[:-1], refs[-1]
-        weight = jnp.exp2(log_ref[...] + (top_ref[...] - log_sum([ref[:rows, :] for ref in part_refs])))
+        weight = jnp.exp2(log_ref[...] + (top_ref[...] - log_sum([ref[...] for ref in part_refs])))
         mask = diagonal()
         total = jnp.zeros((8, count), F32)
         for block in range(rows):
@@ -349,9 +348,9 @@
 def later_columns(plan, reach, top, parts, log_mass, lse, half):
     width, count = plan.shape
 
-    def kernel(plan_ref, reach_ref, top_ref, parts_ref, log_ref, lse_ref, half_ref, out_ref):
+    def kernel(plan_ref, reach_ref, top_ref, parts_ref, log_ref, lse_ref, half_ref, out_ref, potential_ref):
         factor = log_ref[...] - jnp.log2(tree([parts_ref[i] for i in range(parts.shape[0])], jnp.add))
-        out_ref[width // LANES :, :] = half_ref[...] + UNIT * (factor - lse_ref[...])
+        potential_ref[...] = half_ref[...] + UNIT * (factor - lse_ref[...])
         factor = unfold(jnp.exp2(factor))
         factors = [factor[:, lane : lane + LANES] for lane in range(0, count, LANES)]
         for at in range(0, width, LANES):
@@ -366,9 +365,9 @@
 
     return pl.pallas_call(
         kernel,
-        out_shape=rows_of(width + count),
+        out_shape=(rows_of(width), pltpu.VMEM((count // LANES, LANES), F32)),
         in_specs=[VMEM] * 7,
-        out_specs=VMEM,
+        out_specs=(VMEM,) * 2,
         compiler_params=params(),
         name="later_columns",
     )(pin(plan), pin(reach), top, parts, log_mass, lse, half)
@@ -434,13 +433,12 @@
         half_x, half_y, *parts = lax.optimization_barrier((half_x, half_y, *parts))
         for step in range(1, ITERS):
             rows = later_rows(plan, reach, top, b, parts)
-            own = later_columns(plan, reach, top, share(rows, n_far), a, row_lse, half_x)
+            own, potential = later_columns(plan, reach, top, share(rows, n_far), a, row_lse, half_x)
             parts = swap_all(own, near, n_near)
-        rows = half_y.shape[0]
-        mine, other = [value[rows:].reshape(n_x, n_z, part) for value in parts[:CORES]]
+        mine, other = swap_all(potential.reshape(n_x, n_z, part), "core", CORES)
         first, second = jnp.where(core == 0, mine, other), jnp.where(core == 0, other, mine)
         source_potential = jnp.stack([first, second], axis=2).swapaxes(0, 1).reshape(-1)
-        target_potential = half_y - UNIT * log_sum([value[:rows] for value in parts])
+        target_potential = half_y - UNIT * log_sum(parts)
         target_potential = target_potential.reshape(CORES, -1)
         target_potential = lax.dynamic_index_in_dim(target_potential, core, axis=0, keepdims=False)
         return source_potential, target_potential

time: 67.1 us -> 66.7 us (level)
  waiting for transfers between devices: 10.3 us -> 9.53 us
    ppermute x16 -> x17, waiting for transfers between devices: 10.3 us -> 9.53 us  [swap(): return lax.ppermute(value, axes, [(i, i ^ distance) for i in range(size)])]
    ppermute x16 -> x17, starting transfers between devices: 15.4 us -> 15.3 us  [swap(): return lax.ppermute(value, axes, [(i, i ^ distance) for i in range(size)])]
  transfers between devices with their start and end apart: 16 -> 17, of which waited for: 9 -> 9; matrix products, arithmetic and copies ran while one was open for 1% -> 2% of each run, Pallas kernels for 5% -> 5%
where the time goes in v9:
time: 66.7 us; the launch traced here: 66.5 us
  blocking collectives  28.1 us (42%)
  starting transfers between devices  15.3 us (23%)
  Pallas kernels  10.8 us (16%)
  waiting for transfers between devices  9.53 us (14%)
  other arithmetic  1.28 us (2%)
  between operations  0.82 us (1%)
    all_to_all x3, blocking collectives, share(): return lax.all_to_all(copies, ('z', 'x'), 0, 0, tiled=True)  28.1 us
    ppermute x17, starting transfers between devices, swap(): return lax.ppermute(value, axes, [(i, i ^ distance) for i in range(size)])  15.3 us
    ppermute x17, waiting for transfers between devices, swap(): return lax.ppermute(value, axes, [(i, i ^ distance) for i in range(size)])  9.53 us
    pallas_call x1, Pallas kernels, first_columns(): pl.pallas_call(kernel, out_shape=(pltpu.VMEM((width, count), F32), pltpu....  2.44 us
    pallas_call x1, Pallas kernels, first_rows(): pl.pallas_call(kernel, out_shape=(pltpu.VMEM((width, LANES), jnp.bfloat16...  2.18 us
    pallas_call x2, Pallas kernels, later_columns(): pl.pallas_call(kernel, out_shape=(rows_of(width), pltpu.VMEM((count // LA...  1.99 us
    pallas_call x1, Pallas kernels, other_rows(): pl.pallas_call(kernel, out_shape=(rows_of(count + each * LANES), pltpu.VM...  1.77 us
    pallas_call x2, Pallas kernels, later_rows(): pl.pallas_call(kernel, out_shape=rows_of(count), in_specs=[VMEM] * (4 + l...  1.47 us
  transfers between devices with their start and end apart: 17, of which 9 were waited for; matrix products, arithmetic and copies ran while one was open for 2% of the time, Pallas kernels for 5%

profile of v9, /device:TPU:0, one launch (start us, length us, event | category | flops | bytes accessed | tf_op | source)
XLA Modules:
  0.0 66.5 jit_solution(5084777813913767057)
XLA Ops:
  0.6 3.0 %collective-permute-start.4 = (bf16[512,128]{1,0:T(8,128)(2,1)}, bf16[512,128]{1,0:T(8,128)(2,1)S(1)}, u32[]{:S(2)}, u32[]{:S(2)}) collective-permute-start(bf16[512,128]{1,0:T(8,128)(2,1)} %targets_ref.1), channel_id=1, source_target_pairs={{0,16},{16,0},{1,17},{17,1},{2,18},{18,2},{3,19},{19,3},{4,20},{20... | collective-permute-start | bytes 393224 | tf_op jit(solution)/shard_map/ppermute | solution.py:387
  3.7 1.6 %collective-permute-start = (bf16[128,128]{1,0:T(8,128)(2,1)}, bf16[128,128]{1,0:T(8,128)(2,1)S(1)}, u32[]{:S(2)}, u32[]{:S(2)}) collective-permute-start(bf16[128,128]{1,0:T(8,128)(2,1)} %sources_ref.1), channel_id=1, source_target_pairs={{0,4},{4,0},{8,12},{12,8},{1,5},{5,1},{9,13},{13,9},{2,6},{6,2},{1... | collective-permute-start | bytes 98312 | tf_op jit(solution)/shard_map/ppermute | solution.py:387
  5.3 2.5 %collective-permute-start.2 = (bf16[128,128]{1,0:T(8,128)(2,1)}, bf16[128,128]{1,0:T(8,128)(2,1)S(1)}, u32[]{:S(2)}, u32[]{:S(2)}) collective-permute-start(bf16[128,128]{1,0:T(8,128)(2,1)} %sources_ref.1), channel_id=1, source_target_pairs={{0,12},{4,8},{8,4},{12,0},{1,13},{5,9},{9,5},{13,1},{2,14},{6,10},... | collective-permute-start | bytes 98312 | tf_op jit(solution)/shard_map/ppermute | solution.py:387
  7.9 1.0 %ready.1 = (bf16[128,128]{1,0:T(8,128)(2,1)S(1)}, bf16[544,128]{1,0:T(8,128)(2,1)S(1)}, f32[8,128]{1,0:T(8,128)S(1)}, f32[8,128]{1,0:T(8,128)S(1)}) custom-call(bf16[128,128]{1,0:T(8,128)(2,1)} %sources_ref.1, bf16[512,128]{1,0:T(8,128)(2,1)} %targets_ref.1, f32[8,128]{1,0:T(8,128)} %bitcast.31, f32[8,128]{1,0:T(8,128)S(1)} %bitcast.24), custom_call_target="tpu_custom_call" | custom-call | flops 1048576 | bytes 1048576 | tf_op jit(solution)/shard_map/ready/pallas_call | solution.py:95
  9.4 1.9 %collective-permute-done.2.block_ref = bf16[128,128]{1,0:T(8,128)(2,1)S(1)} collective-permute-done((bf16[128,128]{1,0:T(8,128)(2,1)}, bf16[128,128]{1,0:T(8,128)(2,1)S(1)}, u32[]{:S(2)}, u32[]{:S(2)}) %collective-permute-start.2) | collective-permute-done | bytes 32800 | tf_op jit(solution)/shard_map/ppermute | solution.py:387
  11.4 1.8 %collective-permute-done.1.refs_2_ = bf16[128,128]{1,0:T(8,128)(2,1)S(1)} collective-permute-done((bf16[128,128]{1,0:T(8,128)(2,1)}, bf16[128,128]{1,0:T(8,128)(2,1)S(1)}, u32[]{:S(2)}, u32[]{:S(2)}) %collective-permute-start.1) | collective-permute-done | bytes 32800 | tf_op jit(solution)/shard_map/ppermute | solution.py:387
  13.1 1.6 %collective-permute-start.6 = (bf16[512,128]{1,0:T(8,128)(2,1)S(1)}, bf16[512,128]{1,0:T(8,128)(2,1)S(1)}, u32[]{:S(2)}, u32[]{:S(2)}) collective-permute-start(bf16[512,128]{1,0:T(8,128)(2,1)S(1)} %pack.1.sources_ref.mine_ref), channel_id=1, source_target_pairs={{0,2},{2,0},{1,3},{3,1},{4,6},{6,4},{5,7},{7,5},{8,10},{10,8},{9,1... | collective-permute-start | bytes 393224 | tf_op jit(solution)/shard_map/ppermute | solution.py:387
  14.8 2.2 %first_rows.1 = (bf16[2048,128]{1,0:T(8,128)(2,1)S(1)}, bf16[2048,128]{1,0:T(8,128)(2,1)S(1)}, f32[16,128]{1,0:T(8,128)S(1)}, f32[4,128]{1,0:T(4,128)S(1)}) custom-call(s32[3]{0:T(128)S(1)} %pad_add_fusion.place_ref, f32[8,128]{1,0:T(8,128)S(1)} %get-tuple-element.33.mass_ref, bf16[512,128]{1,0:T(8,128)(2,1)S(1)} %pack.1.sources_ref.mine_ref, ...), custom_call_target="tpu_custom_call" | custom-call | flops 536870912 | bytes 1048576 | tf_op jit(solution)/shard_map/first_rows/pallas_call | solution.py:221
  16.9 1.2 %collective-permute-done.6.refs_0_ = bf16[512,128]{1,0:T(8,128)(2,1)S(1)} collective-permute-done((bf16[512,128]{1,0:T(8,128)(2,1)S(1)}, bf16[512,128]{1,0:T(8,128)(2,1)S(1)}, u32[]{:S(2)}, u32[]{:S(2)}) %collective-permute-start.6) | collective-permute-done | bytes 131104 | tf_op jit(solution)/shard_map/ppermute | solution.py:387
  18.2 1.8 %other_rows.1 = (f32[8,128]{1,0:T(8,128)S(1)}, bf16[1024,128]{1,0:T(8,128)(2,1)S(1)}) custom-call(s32[3]{0:T(128)S(1)} %pad_add_fusion.place_ref, bf16[2048,128]{1,0:T(8,128)(2,1)S(1)} %get-tuple-element.48.targets_ref, bf16[2048,128]{1,0:T(8,128)(2,1)S(1)} %get-tuple-element.37.offset_ref, f32[4,128]{1,0:T(4,128)S(1)} %get-tuple-element.38.first_ref, ...), custom_call_target="tpu_custom_call" | custom-call | tf_op jit(solution)/shard_map/other_rows/pallas_call | solution.py:260
  19.9 9.9 %all_to_all.15.parts_ref = f32[8,8,128]{2,1,0:T(8,128)S(1)} all-to-all(f32[8,8,128]{2,1,0:T(8,128)S(1)} %broadcast_in_dim.6), channel_id=1, replica_groups=mesh['src'=2,'z'=4,'x'=2,'core'=2] {'z','x'}, dimensions={0} | all-to-all | bytes 65536 | tf_op jit(solution)/shard_map/all_to_all | solution.py:400
  29.9 2.4 %first_columns.1 = (f32[2048,1024]{1,0:T(8,128)S(1)}, f32[2048,128]{1,0:T(8,128)S(1)}, f32[16,128]{1,0:T(8,128)S(1)}, f32[16,128]{1,0:T(8,128)S(1)}, f32[8,128]{1,0:T(8,128)S(1)}) custom-call(bf16[1024,128]{1,0:T(8,128)(2,1)S(1)} %get-tuple-element.47.sources_ref, bf16[2048,128]{1,0:T(8,128)(2,1)S(1)} %get-tuple-element.48.targets_ref, ...), custom_call_target="tpu_custom_call" | custom-call | tf_op jit(solution)/shard_map/first_columns/pallas_call | solution.py:304
  33.0 1.3 %collective-permute-start.7 = (f32[16,128]{1,0:T(8,128)S(1)}, f32[16,128]{1,0:T(8,128)S(1)}, u32[]{:S(2)}, u32[]{:S(2)}) collective-permute-start(f32[16,128]{1,0:T(8,128)S(1)} %get-tuple-element.50.refs_0_), channel_id=1, source_target_pairs={{0,1},{1,0},{16,17},{17,16},{2,3},{3,2},{18,19},{19,18},{4,5},{5,4... | collective-permute-start | bytes 24584 | tf_op jit(solution)/shard_map/ppermute | solution.py:387
  35.5 0.7 collective-permute-done.8.refs_2_
  36.1 0.7 %later_rows.2 = f32[8,128]{1,0:T(8,128)S(1)} custom-call(f32[2048,1024]{1,0:T(8,128)S(1)} %get-tuple-element.42.plan_ref, f32[2048,128]{1,0:T(8,128)S(1)} %get-tuple-element.43.reach_ref, f32[16,128]{1,0:T(8,128)S(1)} %get-tuple-element.44.top_ref, f32[16,128]{1,0:T(8,128)S(1)} %get-tuple-element.45.log_ref, f32[16,128]{1,0:T(8,128)S(1)} %get-tuple-element.50.refs_0_, ...), custom_call_target="tpu_custom_call" | custom-call | tf_op jit(solution)/shard_map/later_rows/pallas_call | solution.py:338
  36.9 9.1 %all_to_all.16.parts_ref = f32[8,8,128]{2,1,0:T(8,128)S(1)} all-to-all(f32[8,8,128]{2,1,0:T(8,128)S(1)} %broadcast_in_dim.7), channel_id=1, replica_groups=mesh['src'=2,'z'=4,'x'=2,'core'=2] {'z','x'}, dimensions={0} | all-to-all | bytes 65536 | tf_op jit(solution)/shard_map/all_to_all | solution.py:400
  45.9 1.2 %later_columns.2 = (f32[16,128]{1,0:T(8,128)S(1)}, f32[8,128]{1,0:T(8,128)}) custom-call(f32[2048,1024]{1,0:T(8,128)S(1)} %get-tuple-element.42.plan_ref, f32[2048,128]{1,0:T(8,128)S(1)} %get-tuple-element.43.reach_ref, f32[16,128]{1,0:T(8,128)S(1)} %get-tuple-element.44.top_ref, f32[8,8,128]{2,1,0:T(8,128)S(1)} %all_to_all.16.parts_ref, ...), custom_call_target="tpu_custom_call" | custom-call | tf_op jit(solution)/shard_map/later_columns/pallas_call | solution.py:366
  47.7 1.3 %collective-permute-start.10 = (f32[16,128]{1,0:T(8,128)S(1)}, f32[16,128]{1,0:T(8,128)S(1)}, u32[]{:S(2)}, u32[]{:S(2)}) collective-permute-start(f32[16,128]{1,0:T(8,128)S(1)} %get-tuple-element.56.refs_0_), channel_id=1, source_target_pairs={{0,1},{1,0},{16,17},{17,16},{2,3},{3,2},{18,19},{19,18},{4,5},{5,4... | collective-permute-start | bytes 24584 | tf_op jit(solution)/shard_map/ppermute | solution.py:387
  49.0 1.2 %collective-permute-done.12.refs_3_ = f32[16,128]{1,0:T(8,128)S(1)} collective-permute-done((f32[16,128]{1,0:T(8,128)S(1)}, f32[16,128]{1,0:T(8,128)S(1)}, u32[]{:S(2)}, u32[]{:S(2)}) %collective-permute-start.12) | collective-permute-done | bytes 8224 | tf_op jit(solution)/shard_map/ppermute | solution.py:387
  50.9 0.7 %later_rows.3 = f32[8,128]{1,0:T(8,128)S(1)} custom-call(f32[2048,1024]{1,0:T(8,128)S(1)} %get-tuple-element.42.plan_ref, f32[2048,128]{1,0:T(8,128)S(1)} %get-tuple-element.43.reach_ref, f32[16,128]{1,0:T(8,128)S(1)} %get-tuple-element.44.top_ref, f32[16,128]{1,0:T(8,128)S(1)} %get-tuple-element.45.log_ref, f32[16,128]{1,0:T(8,128)S(1)} %get-tuple-element.56.refs_0_, ...), custom_call_target="tpu_custom_call" | custom-call | tf_op jit(solution)/shard_map/later_rows/pallas_call | solution.py:338
  51.6 9.1 %all_to_all.17.parts_ref = f32[8,8,128]{2,1,0:T(8,128)S(1)} all-to-all(f32[8,8,128]{2,1,0:T(8,128)S(1)} %broadcast_in_dim.8), channel_id=1, replica_groups=mesh['src'=2,'z'=4,'x'=2,'core'=2] {'z','x'}, dimensions={0} | all-to-all | bytes 65536 | tf_op jit(solution)/shard_map/all_to_all | solution.py:400
  60.7 0.7 %later_columns.3 = (f32[16,128]{1,0:T(8,128)S(1)}, f32[8,128]{1,0:T(8,128)S(1)}) custom-call(f32[2048,1024]{1,0:T(8,128)S(1)} %get-tuple-element.42.plan_ref, f32[2048,128]{1,0:T(8,128)S(1)} %get-tuple-element.43.reach_ref, f32[16,128]{1,0:T(8,128)S(1)} %get-tuple-element.44.top_ref, f32[8,8,128]{2,1,0:T(8,128)S(1)} %all_to_all.17.parts_ref, ...), custom_call_target="tpu_custom_call" | custom-call | tf_op jit(solution)/shard_map/later_columns/pallas_call | solution.py:366
  62.2 1.5 %collective-permute-start.15 = (f32[16,128]{1,0:T(8,128)S(1)}, f32[16,128]{1,0:T(8,128)S(1)}, u32[]{:S(2)}, u32[]{:S(2)}) collective-permute-start(f32[16,128]{1,0:T(8,128)S(1)} %get-tuple-element.59), channel_id=1, source_target_pairs={{0,16},{1,17},{16,0},{17,1},{2,18},{3,19},{18,2},{19,3},{4,20},{5,... | collective-permute-start | bytes 24584 | tf_op jit(solution)/shard_map/ppermute | solution.py:387
  64.7 1.1 %collective-permute-done.15 = f32[16,128]{1,0:T(8,128)S(1)} collective-permute-done((f32[16,128]{1,0:T(8,128)S(1)}, f32[16,128]{1,0:T(8,128)S(1)}, u32[]{:S(2)}, u32[]{:S(2)}) %collective-permute-start.15) | collective-permute-done | bytes 8224 | tf_op jit(solution)/shard_map/ppermute | solution.py:387
  (41 shorter events, 6.1 us)
Async XLA Ops:
  0.6 7.2 %copy-start = (f32[2048]{0:T(1024)S(1)}, f32[2048]{0:T(1024)}, u32[]{:S(2)}) copy-start(f32[2048]{0:T(1024)} %param.6) | copy-start | bytes 24580
  0.6 8.3 %collective-permute-start.4 = (bf16[512,128]{1,0:T(8,128)(2,1)}, bf16[512,128]{1,0:T(8,128)(2,1)S(1)}, u32[]{:S(2)}, u32[]{:S(2)}) collective-permute-start(bf16[512,128]{1,0:T(8,128)(2,1)} %targets_ref.1), channel_id=1, source_target_pairs={{0,16},{16,0},{1,17},{17,1},{2,18},{18,2},{3,19},{19,3},{4,20},{20... | collective-permute-start | bytes 393224 | tf_op jit(solution)/shard_map/ppermute | solution.py:387
  3.7 7.7 %collective-permute-start = (bf16[128,128]{1,0:T(8,128)(2,1)}, bf16[128,128]{1,0:T(8,128)(2,1)S(1)}, u32[]{:S(2)}, u32[]{:S(2)}) collective-permute-start(bf16[128,128]{1,0:T(8,128)(2,1)} %sources_ref.1), channel_id=1, source_target_pairs={{0,4},{4,0},{8,12},{12,8},{1,5},{5,1},{9,13},{13,9},{2,6},{6,2},{1... | collective-permute-start | bytes 98312 | tf_op jit(solution)/shard_map/ppermute | solution.py:387
  5.3 6.1 %collective-permute-start.2 = (bf16[128,128]{1,0:T(8,128)(2,1)}, bf16[128,128]{1,0:T(8,128)(2,1)S(1)}, u32[]{:S(2)}, u32[]{:S(2)}) collective-permute-start(bf16[128,128]{1,0:T(8,128)(2,1)} %sources_ref.1), channel_id=1, source_target_pairs={{0,12},{4,8},{8,4},{12,0},{1,13},{5,9},{9,5},{13,1},{2,14},{6,10},... | collective-permute-start | bytes 98312 | tf_op jit(solution)/shard_map/ppermute | solution.py:387
  7.7 5.4 %collective-permute-start.1 = (bf16[128,128]{1,0:T(8,128)(2,1)}, bf16[128,128]{1,0:T(8,128)(2,1)S(1)}, u32[]{:S(2)}, u32[]{:S(2)}) collective-permute-start(bf16[128,128]{1,0:T(8,128)(2,1)} %sources_ref.1), channel_id=1, source_target_pairs={{0,8},{4,12},{8,0},{12,4},{1,9},{5,13},{9,1},{13,5},{2,10},{6,14},... | collective-permute-start | bytes 98312 | tf_op jit(solution)/shard_map/ppermute | solution.py:387
  8.8 5.9 %collective-permute-start.3 = (bf16[544,128]{1,0:T(8,128)(2,1)S(1)}, bf16[544,128]{1,0:T(8,128)(2,1)S(1)}, u32[]{:S(2)}, u32[]{:S(2)}) collective-permute-start(bf16[544,128]{1,0:T(8,128)(2,1)S(1)} %get-tuple-element.35.refs_0_), channel_id=1, source_target_pairs={{0,1},{1,0},{2,3},{3,2},{4,5},{5,4},{6,7},{7,6},{8,9},{9,8},{10,11... | collective-permute-start | bytes 417800 | tf_op jit(solution)/shard_map/ppermute | solution.py:387
  8.9 5.8 %collective-permute-start.5 = (bf16[512,128]{1,0:T(8,128)(2,1)S(1)}, bf16[512,128]{1,0:T(8,128)(2,1)S(1)}, u32[]{:S(2)}, u32[]{:S(2)}) collective-permute-start(bf16[512,128]{1,0:T(8,128)(2,1)S(1)} %collective-permute-done.4.refs_2_), channel_id=1, source_target_pairs={{0,1},{1,0},{2,3},{3,2},{4,5},{5,4},{6,7},{7,6},{8,9},{9,8},{10,11... | collective-permute-start | bytes 393224 | tf_op jit(solution)/shard_map/ppermute | solution.py:387
  13.1 5.0 %collective-permute-start.6 = (bf16[512,128]{1,0:T(8,128)(2,1)S(1)}, bf16[512,128]{1,0:T(8,128)(2,1)S(1)}, u32[]{:S(2)}, u32[]{:S(2)}) collective-permute-start(bf16[512,128]{1,0:T(8,128)(2,1)S(1)} %pack.1.sources_ref.mine_ref), channel_id=1, source_target_pairs={{0,2},{2,0},{1,3},{3,1},{4,6},{6,4},{5,7},{7,5},{8,10},{10,8},{9,1... | collective-permute-start | bytes 393224 | tf_op jit(solution)/shard_map/ppermute | solution.py:387
  32.3 3.1 %collective-permute-start.9 = (f32[16,128]{1,0:T(8,128)S(1)}, f32[16,128]{1,0:T(8,128)S(1)}, u32[]{:S(2)}, u32[]{:S(2)}) collective-permute-start(f32[16,128]{1,0:T(8,128)S(1)} %get-tuple-element.50.refs_0_), channel_id=1, source_target_pairs={{0,17},{1,16},{16,1},{17,0},{2,19},{3,18},{18,3},{19,2},{4,21},{5,... | collective-permute-start | bytes 24584 | tf_op jit(solution)/shard_map/ppermute | solution.py:387
  32.4 3.7 %collective-permute-start.8 = (f32[16,128]{1,0:T(8,128)S(1)}, f32[16,128]{1,0:T(8,128)S(1)}, u32[]{:S(2)}, u32[]{:S(2)}) collective-permute-start(f32[16,128]{1,0:T(8,128)S(1)} %get-tuple-element.50.refs_0_), channel_id=1, source_target_pairs={{0,16},{1,17},{16,0},{17,1},{2,18},{3,19},{18,2},{19,3},{4,20},{5,... | collective-permute-start | bytes 24584 | tf_op jit(solution)/shard_map/ppermute | solution.py:387
  33.0 3.1 %collective-permute-start.7 = (f32[16,128]{1,0:T(8,128)S(1)}, f32[16,128]{1,0:T(8,128)S(1)}, u32[]{:S(2)}, u32[]{:S(2)}) collective-permute-start(f32[16,128]{1,0:T(8,128)S(1)} %get-tuple-element.50.refs_0_), channel_id=1, source_target_pairs={{0,1},{1,0},{16,17},{17,16},{2,3},{3,2},{18,19},{19,18},{4,5},{5,4... | collective-permute-start | bytes 24584 | tf_op jit(solution)/shard_map/ppermute | solution.py:387
  47.2 3.1 %collective-permute-start.12 = (f32[16,128]{1,0:T(8,128)S(1)}, f32[16,128]{1,0:T(8,128)S(1)}, u32[]{:S(2)}, u32[]{:S(2)}) collective-permute-start(f32[16,128]{1,0:T(8,128)S(1)} %get-tuple-element.56.refs_0_), channel_id=1, source_target_pairs={{0,17},{1,16},{16,1},{17,0},{2,19},{3,18},{18,3},{19,2},{4,21},{5,... | collective-permute-start | bytes 24584 | tf_op jit(solution)/shard_map/ppermute | solution.py:387
  47.2 3.7 %collective-permute-start.11 = (f32[16,128]{1,0:T(8,128)S(1)}, f32[16,128]{1,0:T(8,128)S(1)}, u32[]{:S(2)}, u32[]{:S(2)}) collective-permute-start(f32[16,128]{1,0:T(8,128)S(1)} %get-tuple-element.56.refs_0_), channel_id=1, source_target_pairs={{0,16},{1,17},{16,0},{17,1},{2,18},{3,19},{18,2},{19,3},{4,20},{5,... | collective-permute-start | bytes 24584 | tf_op jit(solution)/shard_map/ppermute | solution.py:387
  47.7 3.1 %collective-permute-start.10 = (f32[16,128]{1,0:T(8,128)S(1)}, f32[16,128]{1,0:T(8,128)S(1)}, u32[]{:S(2)}, u32[]{:S(2)}) collective-permute-start(f32[16,128]{1,0:T(8,128)S(1)} %get-tuple-element.56.refs_0_), channel_id=1, source_target_pairs={{0,1},{1,0},{16,17},{17,16},{2,3},{3,2},{18,19},{19,18},{4,5},{5,4... | collective-permute-start | bytes 24584 | tf_op jit(solution)/shard_map/ppermute | solution.py:387
  61.5 2.2 %collective-permute-start.13 = (f32[2,4,128]{2,0,1:T(2,128)S(1)}, f32[2,4,128]{2,0,1:T(2,128)S(1)}, u32[]{:S(2)}, u32[]{:S(2)}) collective-permute-start(f32[2,4,128]{2,0,1:T(2,128)S(1)} %copy.13), channel_id=1, source_target_pairs={{0,1},{1,0},{2,3},{3,2},{4,5},{5,4},{6,7},{7,6},{8,9},{9,8},{10,11... | collective-permute-start | bytes 12296 | tf_op jit(solution)/shard_map/ppermute | solution.py:387
  61.5 3.1 %collective-permute-start.16 = (f32[16,128]{1,0:T(8,128)S(1)}, f32[16,128]{1,0:T(8,128)S(1)}, u32[]{:S(2)}, u32[]{:S(2)}) collective-permute-start(f32[16,128]{1,0:T(8,128)S(1)} %get-tuple-element.59), channel_id=1, source_target_pairs={{0,17},{1,16},{16,1},{17,0},{2,19},{3,18},{18,3},{19,2},{4,21},{5,... | collective-permute-start | bytes 24584 | tf_op jit(solution)/shard_map/ppermute | solution.py:387
  62.2 3.7 %collective-permute-start.15 = (f32[16,128]{1,0:T(8,128)S(1)}, f32[16,128]{1,0:T(8,128)S(1)}, u32[]{:S(2)}, u32[]{:S(2)}) collective-permute-start(f32[16,128]{1,0:T(8,128)S(1)} %get-tuple-element.59), channel_id=1, source_target_pairs={{0,16},{1,17},{16,0},{17,1},{2,18},{3,19},{18,2},{19,3},{4,20},{5,... | collective-permute-start | bytes 24584 | tf_op jit(solution)/shard_map/ppermute | solution.py:387
  63.7 2.1 %collective-permute-start.14 = (f32[16,128]{1,0:T(8,128)S(1)}, f32[16,128]{1,0:T(8,128)S(1)}, u32[]{:S(2)}, u32[]{:S(2)}) collective-permute-start(f32[16,128]{1,0:T(8,128)S(1)} %get-tuple-element.59), channel_id=1, source_target_pairs={{0,1},{1,0},{16,17},{17,16},{2,3},{3,2},{18,19},{19,18},{4,5},{5,4... | collective-permute-start | bytes 24584 | tf_op jit(solution)/shard_map/ppermute | solution.py:387

commit v10 on v9

--- a/solution.py
+++ b/solution.py
@@ -345,12 +345,13 @@
     )(pin(plan), pin(reach), top, log_mass, *parts)
 
 
-def later_columns(plan, reach, top, parts, log_mass, lse, half):
+def later_columns(plan, reach, top, parts, log_mass, lse, half, last):
     width, count = plan.shape
 
-    def kernel(plan_ref, reach_ref, top_ref, parts_ref, log_ref, lse_ref, half_ref, out_ref, potential_ref):
+    def kernel(plan_ref, reach_ref, top_ref, parts_ref, log_ref, lse_ref, half_ref, out_ref, *potential_refs):
         factor = log_ref[...] - jnp.log2(tree([parts_ref[i] for i in range(parts.shape[0])], jnp.add))
-        potential_ref[...] = half_ref[...] + UNIT * (factor - lse_ref[...])
+        for ref in potential_refs:
+            ref[...] = half_ref[...] + UNIT * (factor - lse_ref[...])
         factor = unfold(jnp.exp2(factor))
         factors = [factor[:, lane : lane + LANES] for lane in range(0, count, LANES)]
         for at in range(0, width, LANES):
@@ -365,9 +366,9 @@
 
     return pl.pallas_call(
         kernel,
-        out_shape=(rows_of(width), pltpu.VMEM((count // LANES, LANES), F32)),
+        out_shape=(rows_of(width),) + (rows_of(count),) * last,
         in_specs=[VMEM] * 7,
-        out_specs=(VMEM,) * 2,
+        out_specs=(VMEM,) * (1 + last),
         compiler_params=params(),
         name="later_columns",
     )(pin(plan), pin(reach), top, parts, log_mass, lse, half)
@@ -433,9 +434,9 @@
         half_x, half_y, *parts = lax.optimization_barrier((half_x, half_y, *parts))
         for step in range(1, ITERS):
             rows = later_rows(plan, reach, top, b, parts)
-            own, potential = later_columns(plan, reach, top, share(rows, n_far), a, row_lse, half_x)
+            own, *potential = later_columns(plan, reach, top, share(rows, n_far), a, row_lse, half_x, step == ITERS - 1)
             parts = swap_all(own, near, n_near)
-        mine, other = swap_all(potential.reshape(n_x, n_z, part), "core", CORES)
+        mine, other = swap_all(potential[0].reshape(n_x, n_z, part), "core", CORES)
         first, second = jnp.where(core == 0, mine, other), jnp.where(core == 0, other, mine)
         source_potential = jnp.stack([first, second], axis=2).swapaxes(0, 1).reshape(-1)
         target_potential = half_y - UNIT * log_sum(parts)

time: 66.7 us -> 66.3 us (level)
  no operation moved by 1% of the time
where the time goes in v10:
time: 66.3 us; the launch traced here: 66.1 us
  blocking collectives  28.1 us (42%)
  starting transfers between devices  15.4 us (23%)
  Pallas kernels  10.3 us (16%)
  waiting for transfers between devices  9.57 us (14%)
  other arithmetic  1.28 us (2%)
  between operations  0.83 us (1%)
    all_to_all x3, blocking collectives, share(): return lax.all_to_all(copies, ('z', 'x'), 0, 0, tiled=True)  28.1 us
    ppermute x17, starting transfers between devices, swap(): return lax.ppermute(value, axes, [(i, i ^ distance) for i in range(size)])  15.4 us
    ppermute x17, waiting for transfers between devices, swap(): return lax.ppermute(value, axes, [(i, i ^ distance) for i in range(size)])  9.57 us
    pallas_call x1, Pallas kernels, first_columns(): pl.pallas_call(kernel, out_shape=(pltpu.VMEM((width, count), F32), pltpu....  2.44 us
    pallas_call x1, Pallas kernels, first_rows(): pl.pallas_call(kernel, out_shape=(pltpu.VMEM((width, LANES), jnp.bfloat16...  2.18 us
    pallas_call x1, Pallas kernels, other_rows(): pl.pallas_call(kernel, out_shape=(rows_of(count + each * LANES), pltpu.VM...  1.77 us
    pallas_call x2, Pallas kernels, later_columns(): pl.pallas_call(kernel, out_shape=(rows_of(width),) + (rows_of(count),) *...  1.49 us
    pallas_call x2, Pallas kernels, later_rows(): pl.pallas_call(kernel, out_shape=rows_of(count), in_specs=[VMEM] * (4 + l...  1.47 us
  transfers between devices with their start and end apart: 17, of which 9 were waited for; matrix products, arithmetic and copies ran while one was open for 2% of the time, Pallas kernels for 5%

profile of v10, /device:TPU:0, one launch (start us, length us, event | category | flops | bytes accessed | tf_op | source)
XLA Modules:
  0.0 66.1 jit_solution(9191015396873631647)
XLA Ops:
  0.6 3.0 %collective-permute-start.4 = (bf16[512,128]{1,0:T(8,128)(2,1)}, bf16[512,128]{1,0:T(8,128)(2,1)S(1)}, u32[]{:S(2)}, u32[]{:S(2)}) collective-permute-start(bf16[512,128]{1,0:T(8,128)(2,1)} %targets_ref.1), channel_id=1, source_target_pairs={{0,16},{16,0},{1,17},{17,1},{2,18},{18,2},{3,19},{19,3},{4,20},{20... | collective-permute-start | bytes 393224 | tf_op jit(solution)/shard_map/ppermute | solution.py:388
  3.7 1.6 %collective-permute-start = (bf16[128,128]{1,0:T(8,128)(2,1)}, bf16[128,128]{1,0:T(8,128)(2,1)S(1)}, u32[]{:S(2)}, u32[]{:S(2)}) collective-permute-start(bf16[128,128]{1,0:T(8,128)(2,1)} %sources_ref.1), channel_id=1, source_target_pairs={{0,4},{4,0},{8,12},{12,8},{1,5},{5,1},{9,13},{13,9},{2,6},{6,2},{1... | collective-permute-start | bytes 98312 | tf_op jit(solution)/shard_map/ppermute | solution.py:388
  5.3 2.5 %collective-permute-start.2 = (bf16[128,128]{1,0:T(8,128)(2,1)}, bf16[128,128]{1,0:T(8,128)(2,1)S(1)}, u32[]{:S(2)}, u32[]{:S(2)}) collective-permute-start(bf16[128,128]{1,0:T(8,128)(2,1)} %sources_ref.1), channel_id=1, source_target_pairs={{0,12},{4,8},{8,4},{12,0},{1,13},{5,9},{9,5},{13,1},{2,14},{6,10},... | collective-permute-start | bytes 98312 | tf_op jit(solution)/shard_map/ppermute | solution.py:388
  7.9 1.0 %ready.1 = (bf16[128,128]{1,0:T(8,128)(2,1)S(1)}, bf16[544,128]{1,0:T(8,128)(2,1)S(1)}, f32[8,128]{1,0:T(8,128)S(1)}, f32[8,128]{1,0:T(8,128)S(1)}) custom-call(bf16[128,128]{1,0:T(8,128)(2,1)} %sources_ref.1, bf16[512,128]{1,0:T(8,128)(2,1)} %targets_ref.1, f32[8,128]{1,0:T(8,128)} %bitcast.31, f32[8,128]{1,0:T(8,128)S(1)} %bitcast.24), custom_call_target="tpu_custom_call" | custom-call | flops 1048576 | bytes 1048576 | tf_op jit(solution)/shard_map/ready/pallas_call | solution.py:95
  9.4 1.9 %collective-permute-done.2.block_ref = bf16[128,128]{1,0:T(8,128)(2,1)S(1)} collective-permute-done((bf16[128,128]{1,0:T(8,128)(2,1)}, bf16[128,128]{1,0:T(8,128)(2,1)S(1)}, u32[]{:S(2)}, u32[]{:S(2)}) %collective-permute-start.2) | collective-permute-done | bytes 32800 | tf_op jit(solution)/shard_map/ppermute | solution.py:388
  11.4 1.8 %collective-permute-done.1.refs_2_ = bf16[128,128]{1,0:T(8,128)(2,1)S(1)} collective-permute-done((bf16[128,128]{1,0:T(8,128)(2,1)}, bf16[128,128]{1,0:T(8,128)(2,1)S(1)}, u32[]{:S(2)}, u32[]{:S(2)}) %collective-permute-start.1) | collective-permute-done | bytes 32800 | tf_op jit(solution)/shard_map/ppermute | solution.py:388
  13.1 1.6 %collective-permute-start.6 = (bf16[512,128]{1,0:T(8,128)(2,1)S(1)}, bf16[512,128]{1,0:T(8,128)(2,1)S(1)}, u32[]{:S(2)}, u32[]{:S(2)}) collective-permute-start(bf16[512,128]{1,0:T(8,128)(2,1)S(1)} %pack.1.sources_ref.mine_ref), channel_id=1, source_target_pairs={{0,2},{2,0},{1,3},{3,1},{4,6},{6,4},{5,7},{7,5},{8,10},{10,8},{9,1... | collective-permute-start | bytes 393224 | tf_op jit(solution)/shard_map/ppermute | solution.py:388
  14.8 2.2 %first_rows.1 = (bf16[2048,128]{1,0:T(8,128)(2,1)S(1)}, bf16[2048,128]{1,0:T(8,128)(2,1)S(1)}, f32[16,128]{1,0:T(8,128)S(1)}, f32[4,128]{1,0:T(4,128)S(1)}) custom-call(s32[3]{0:T(128)S(1)} %pad_add_fusion.place_ref, f32[8,128]{1,0:T(8,128)S(1)} %get-tuple-element.32.mass_ref, bf16[512,128]{1,0:T(8,128)(2,1)S(1)} %pack.1.sources_ref.mine_ref, ...), custom_call_target="tpu_custom_call" | custom-call | flops 536870912 | bytes 1048576 | tf_op jit(solution)/shard_map/first_rows/pallas_call | solution.py:221
  16.9 1.2 %collective-permute-done.6.refs_0_ = bf16[512,128]{1,0:T(8,128)(2,1)S(1)} collective-permute-done((bf16[512,128]{1,0:T(8,128)(2,1)S(1)}, bf16[512,128]{1,0:T(8,128)(2,1)S(1)}, u32[]{:S(2)}, u32[]{:S(2)}) %collective-permute-start.6) | collective-permute-done | bytes 131104 | tf_op jit(solution)/shard_map/ppermute | solution.py:388
  18.2 1.8 %other_rows.1 = (f32[8,128]{1,0:T(8,128)S(1)}, bf16[1024,128]{1,0:T(8,128)(2,1)S(1)}) custom-call(s32[3]{0:T(128)S(1)} %pad_add_fusion.place_ref, bf16[2048,128]{1,0:T(8,128)(2,1)S(1)} %get-tuple-element.47.targets_ref, bf16[2048,128]{1,0:T(8,128)(2,1)S(1)} %get-tuple-element.36.offset_ref, f32[4,128]{1,0:T(4,128)S(1)} %get-tuple-element.37.first_ref, ...), custom_call_target="tpu_custom_call" | custom-call | tf_op jit(solution)/shard_map/other_rows/pallas_call | solution.py:260
  19.9 9.9 %all_to_all.15.parts_ref = f32[8,8,128]{2,1,0:T(8,128)S(1)} all-to-all(f32[8,8,128]{2,1,0:T(8,128)S(1)} %broadcast_in_dim.6), channel_id=1, replica_groups=mesh['src'=2,'z'=4,'x'=2,'core'=2] {'z','x'}, dimensions={0} | all-to-all | bytes 65536 | tf_op jit(solution)/shard_map/all_to_all | solution.py:401
  29.9 2.4 %first_columns.1 = (f32[2048,1024]{1,0:T(8,128)S(1)}, f32[2048,128]{1,0:T(8,128)S(1)}, f32[16,128]{1,0:T(8,128)S(1)}, f32[16,128]{1,0:T(8,128)S(1)}, f32[8,128]{1,0:T(8,128)S(1)}) custom-call(bf16[1024,128]{1,0:T(8,128)(2,1)S(1)} %get-tuple-element.46.sources_ref, bf16[2048,128]{1,0:T(8,128)(2,1)S(1)} %get-tuple-element.47.targets_ref, ...), custom_call_target="tpu_custom_call" | custom-call | tf_op jit(solution)/shard_map/first_columns/pallas_call | solution.py:304
  33.0 1.3 %collective-permute-start.7 = (f32[16,128]{1,0:T(8,128)S(1)}, f32[16,128]{1,0:T(8,128)S(1)}, u32[]{:S(2)}, u32[]{:S(2)}) collective-permute-start(f32[16,128]{1,0:T(8,128)S(1)} %get-tuple-element.49.refs_0_), channel_id=1, source_target_pairs={{0,1},{1,0},{16,17},{17,16},{2,3},{3,2},{18,19},{19,18},{4,5},{5,4... | collective-permute-start | bytes 24584 | tf_op jit(solution)/shard_map/ppermute | solution.py:388
  35.5 0.7 collective-permute-done.8.refs_2_
  36.1 0.7 %later_rows.2 = f32[8,128]{1,0:T(8,128)S(1)} custom-call(f32[2048,1024]{1,0:T(8,128)S(1)} %get-tuple-element.41.plan_ref, f32[2048,128]{1,0:T(8,128)S(1)} %get-tuple-element.42.reach_ref, f32[16,128]{1,0:T(8,128)S(1)} %get-tuple-element.43.top_ref, f32[16,128]{1,0:T(8,128)S(1)} %get-tuple-element.44.log_ref, f32[16,128]{1,0:T(8,128)S(1)} %get-tuple-element.49.refs_0_, ...), custom_call_target="tpu_custom_call" | custom-call | tf_op jit(solution)/shard_map/later_rows/pallas_call | solution.py:338
  36.9 9.1 %all_to_all.16.parts_ref = f32[8,8,128]{2,1,0:T(8,128)S(1)} all-to-all(f32[8,8,128]{2,1,0:T(8,128)S(1)} %broadcast_in_dim.7), channel_id=1, replica_groups=mesh['src'=2,'z'=4,'x'=2,'core'=2] {'z','x'}, dimensions={0} | all-to-all | bytes 65536 | tf_op jit(solution)/shard_map/all_to_all | solution.py:401
  45.9 0.7 %later_columns.2.refs_0_ = f32[16,128]{1,0:T(8,128)S(1)} custom-call(f32[2048,1024]{1,0:T(8,128)S(1)} %get-tuple-element.41.plan_ref, f32[2048,128]{1,0:T(8,128)S(1)} %get-tuple-element.42.reach_ref, f32[16,128]{1,0:T(8,128)S(1)} %get-tuple-element.43.top_ref, f32[8,8,128]{2,1,0:T(8,128)S(1)} %all_to_all.16.parts_ref, ...), custom_call_target="tpu_custom_call" | custom-call | tf_op jit(solution)/shard_map/later_columns/pallas_call | solution.py:367
  47.3 1.3 %collective-permute-start.10 = (f32[16,128]{1,0:T(8,128)S(1)}, f32[16,128]{1,0:T(8,128)S(1)}, u32[]{:S(2)}, u32[]{:S(2)}) collective-permute-start(f32[16,128]{1,0:T(8,128)S(1)} %later_columns.2.refs_0_), channel_id=1, source_target_pairs={{0,1},{1,0},{16,17},{17,16},{2,3},{3,2},{18,19},{19,18},{4,5},{5,4... | collective-permute-start | bytes 24584 | tf_op jit(solution)/shard_map/ppermute | solution.py:388
  48.6 1.2 %collective-permute-done.12.refs_3_ = f32[16,128]{1,0:T(8,128)S(1)} collective-permute-done((f32[16,128]{1,0:T(8,128)S(1)}, f32[16,128]{1,0:T(8,128)S(1)}, u32[]{:S(2)}, u32[]{:S(2)}) %collective-permute-start.12) | collective-permute-done | bytes 8224 | tf_op jit(solution)/shard_map/ppermute | solution.py:388
  50.5 0.7 %later_rows.3 = f32[8,128]{1,0:T(8,128)S(1)} custom-call(f32[2048,1024]{1,0:T(8,128)S(1)} %get-tuple-element.41.plan_ref, f32[2048,128]{1,0:T(8,128)S(1)} %get-tuple-element.42.reach_ref, f32[16,128]{1,0:T(8,128)S(1)} %get-tuple-element.43.top_ref, f32[16,128]{1,0:T(8,128)S(1)} %get-tuple-element.44.log_ref, f32[16,128]{1,0:T(8,128)S(1)} %later_columns.2.refs_0_, ...), custom_call_target="tpu_custom_call" | custom-call | tf_op jit(solution)/shard_map/later_rows/pallas_call | solution.py:338
  51.2 9.1 %all_to_all.17.parts_ref = f32[8,8,128]{2,1,0:T(8,128)S(1)} all-to-all(f32[8,8,128]{2,1,0:T(8,128)S(1)} %broadcast_in_dim.8), channel_id=1, replica_groups=mesh['src'=2,'z'=4,'x'=2,'core'=2] {'z','x'}, dimensions={0} | all-to-all | bytes 65536 | tf_op jit(solution)/shard_map/all_to_all | solution.py:401
  60.3 0.7 %later_columns.3 = (f32[16,128]{1,0:T(8,128)S(1)}, f32[8,128]{1,0:T(8,128)S(1)}) custom-call(f32[2048,1024]{1,0:T(8,128)S(1)} %get-tuple-element.41.plan_ref, f32[2048,128]{1,0:T(8,128)S(1)} %get-tuple-element.42.reach_ref, f32[16,128]{1,0:T(8,128)S(1)} %get-tuple-element.43.top_ref, f32[8,8,128]{2,1,0:T(8,128)S(1)} %all_to_all.17.parts_ref, ...), custom_call_target="tpu_custom_call" | custom-call | tf_op jit(solution)/shard_map/later_columns/pallas_call | solution.py:367
  61.8 1.5 %collective-permute-start.15 = (f32[16,128]{1,0:T(8,128)S(1)}, f32[16,128]{1,0:T(8,128)S(1)}, u32[]{:S(2)}, u32[]{:S(2)}) collective-permute-start(f32[16,128]{1,0:T(8,128)S(1)} %get-tuple-element.57), channel_id=1, source_target_pairs={{0,16},{1,17},{16,0},{17,1},{2,18},{3,19},{18,2},{19,3},{4,20},{5,... | collective-permute-start | bytes 24584 | tf_op jit(solution)/shard_map/ppermute | solution.py:388
  64.3 1.1 %collective-permute-done.15 = f32[16,128]{1,0:T(8,128)S(1)} collective-permute-done((f32[16,128]{1,0:T(8,128)S(1)}, f32[16,128]{1,0:T(8,128)S(1)}, u32[]{:S(2)}, u32[]{:S(2)}) %collective-permute-start.15) | collective-permute-done | bytes 8224 | tf_op jit(solution)/shard_map/ppermute | solution.py:388
  (41 shorter events, 6.3 us)
Async XLA Ops:
  0.6 7.2 %copy-start = (f32[2048]{0:T(1024)S(1)}, f32[2048]{0:T(1024)}, u32[]{:S(2)}) copy-start(f32[2048]{0:T(1024)} %param.6) | copy-start | bytes 24580
  0.6 8.3 %collective-permute-start.4 = (bf16[512,128]{1,0:T(8,128)(2,1)}, bf16[512,128]{1,0:T(8,128)(2,1)S(1)}, u32[]{:S(2)}, u32[]{:S(2)}) collective-permute-start(bf16[512,128]{1,0:T(8,128)(2,1)} %targets_ref.1), channel_id=1, source_target_pairs={{0,16},{16,0},{1,17},{17,1},{2,18},{18,2},{3,19},{19,3},{4,20},{20... | collective-permute-start | bytes 393224 | tf_op jit(solution)/shard_map/ppermute | solution.py:388
  3.7 7.7 %collective-permute-start = (bf16[128,128]{1,0:T(8,128)(2,1)}, bf16[128,128]{1,0:T(8,128)(2,1)S(1)}, u32[]{:S(2)}, u32[]{:S(2)}) collective-permute-start(bf16[128,128]{1,0:T(8,128)(2,1)} %sources_ref.1), channel_id=1, source_target_pairs={{0,4},{4,0},{8,12},{12,8},{1,5},{5,1},{9,13},{13,9},{2,6},{6,2},{1... | collective-permute-start | bytes 98312 | tf_op jit(solution)/shard_map/ppermute | solution.py:388
  5.3 6.1 %collective-permute-start.2 = (bf16[128,128]{1,0:T(8,128)(2,1)}, bf16[128,128]{1,0:T(8,128)(2,1)S(1)}, u32[]{:S(2)}, u32[]{:S(2)}) collective-permute-start(bf16[128,128]{1,0:T(8,128)(2,1)} %sources_ref.1), channel_id=1, source_target_pairs={{0,12},{4,8},{8,4},{12,0},{1,13},{5,9},{9,5},{13,1},{2,14},{6,10},... | collective-permute-start | bytes 98312 | tf_op jit(solution)/shard_map/ppermute | solution.py:388
  7.7 5.4 %collective-permute-start.1 = (bf16[128,128]{1,0:T(8,128)(2,1)}, bf16[128,128]{1,0:T(8,128)(2,1)S(1)}, u32[]{:S(2)}, u32[]{:S(2)}) collective-permute-start(bf16[128,128]{1,0:T(8,128)(2,1)} %sources_ref.1), channel_id=1, source_target_pairs={{0,8},{4,12},{8,0},{12,4},{1,9},{5,13},{9,1},{13,5},{2,10},{6,14},... | collective-permute-start | bytes 98312 | tf_op jit(solution)/shard_map/ppermute | solution.py:388
  8.8 5.9 %collective-permute-start.3 = (bf16[544,128]{1,0:T(8,128)(2,1)S(1)}, bf16[544,128]{1,0:T(8,128)(2,1)S(1)}, u32[]{:S(2)}, u32[]{:S(2)}) collective-permute-start(bf16[544,128]{1,0:T(8,128)(2,1)S(1)} %get-tuple-element.34.refs_0_), channel_id=1, source_target_pairs={{0,1},{1,0},{2,3},{3,2},{4,5},{5,4},{6,7},{7,6},{8,9},{9,8},{10,11... | collective-permute-start | bytes 417800 | tf_op jit(solution)/shard_map/ppermute | solution.py:388
  8.9 5.8 %collective-permute-start.5 = (bf16[512,128]{1,0:T(8,128)(2,1)S(1)}, bf16[512,128]{1,0:T(8,128)(2,1)S(1)}, u32[]{:S(2)}, u32[]{:S(2)}) collective-permute-start(bf16[512,128]{1,0:T(8,128)(2,1)S(1)} %collective-permute-done.4.refs_2_), channel_id=1, source_target_pairs={{0,1},{1,0},{2,3},{3,2},{4,5},{5,4},{6,7},{7,6},{8,9},{9,8},{10,11... | collective-permute-start | bytes 393224 | tf_op jit(solution)/shard_map/ppermute | solution.py:388
  13.1 5.0 %collective-permute-start.6 = (bf16[512,128]{1,0:T(8,128)(2,1)S(1)}, bf16[512,128]{1,0:T(8,128)(2,1)S(1)}, u32[]{:S(2)}, u32[]{:S(2)}) collective-permute-start(bf16[512,128]{1,0:T(8,128)(2,1)S(1)} %pack.1.sources_ref.mine_ref), channel_id=1, source_target_pairs={{0,2},{2,0},{1,3},{3,1},{4,6},{6,4},{5,7},{7,5},{8,10},{10,8},{9,1... | collective-permute-start | bytes 393224 | tf_op jit(solution)/shard_map/ppermute | solution.py:388
  32.3 3.1 %collective-permute-start.9 = (f32[16,128]{1,0:T(8,128)S(1)}, f32[16,128]{1,0:T(8,128)S(1)}, u32[]{:S(2)}, u32[]{:S(2)}) collective-permute-start(f32[16,128]{1,0:T(8,128)S(1)} %get-tuple-element.49.refs_0_), channel_id=1, source_target_pairs={{0,17},{1,16},{16,1},{17,0},{2,19},{3,18},{18,3},{19,2},{4,21},{5,... | collective-permute-start | bytes 24584 | tf_op jit(solution)/shard_map/ppermute | solution.py:388
  32.4 3.7 %collective-permute-start.8 = (f32[16,128]{1,0:T(8,128)S(1)}, f32[16,128]{1,0:T(8,128)S(1)}, u32[]{:S(2)}, u32[]{:S(2)}) collective-permute-start(f32[16,128]{1,0:T(8,128)S(1)} %get-tuple-element.49.refs_0_), channel_id=1, source_target_pairs={{0,16},{1,17},{16,0},{17,1},{2,18},{3,19},{18,2},{19,3},{4,20},{5,... | collective-permute-start | bytes 24584 | tf_op jit(solution)/shard_map/ppermute | solution.py:388
  33.0 3.1 %collective-permute-start.7 = (f32[16,128]{1,0:T(8,128)S(1)}, f32[16,128]{1,0:T(8,128)S(1)}, u32[]{:S(2)}, u32[]{:S(2)}) collective-permute-start(f32[16,128]{1,0:T(8,128)S(1)} %get-tuple-element.49.refs_0_), channel_id=1, source_target_pairs={{0,1},{1,0},{16,17},{17,16},{2,3},{3,2},{18,19},{19,18},{4,5},{5,4... | collective-permute-start | bytes 24584 | tf_op jit(solution)/shard_map/ppermute | solution.py:388
  46.7 3.1 %collective-permute-start.12 = (f32[16,128]{1,0:T(8,128)S(1)}, f32[16,128]{1,0:T(8,128)S(1)}, u32[]{:S(2)}, u32[]{:S(2)}) collective-permute-start(f32[16,128]{1,0:T(8,128)S(1)} %later_columns.2.refs_0_), channel_id=1, source_target_pairs={{0,17},{1,16},{16,1},{17,0},{2,19},{3,18},{18,3},{19,2},{4,21},{5,... | collective-permute-start | bytes 24584 | tf_op jit(solution)/shard_map/ppermute | solution.py:388
  46.8 3.7 %collective-permute-start.11 = (f32[16,128]{1,0:T(8,128)S(1)}, f32[16,128]{1,0:T(8,128)S(1)}, u32[]{:S(2)}, u32[]{:S(2)}) collective-permute-start(f32[16,128]{1,0:T(8,128)S(1)} %later_columns.2.refs_0_), channel_id=1, source_target_pairs={{0,16},{1,17},{16,0},{17,1},{2,18},{3,19},{18,2},{19,3},{4,20},{5,... | collective-permute-start | bytes 24584 | tf_op jit(solution)/shard_map/ppermute | solution.py:388
  47.3 3.1 %collective-permute-start.10 = (f32[16,128]{1,0:T(8,128)S(1)}, f32[16,128]{1,0:T(8,128)S(1)}, u32[]{:S(2)}, u32[]{:S(2)}) collective-permute-start(f32[16,128]{1,0:T(8,128)S(1)} %later_columns.2.refs_0_), channel_id=1, source_target_pairs={{0,1},{1,0},{16,17},{17,16},{2,3},{3,2},{18,19},{19,18},{4,5},{5,4... | collective-permute-start | bytes 24584 | tf_op jit(solution)/shard_map/ppermute | solution.py:388
  61.1 2.2 %collective-permute-start.13 = (f32[2,4,128]{2,0,1:T(2,128)S(1)}, f32[2,4,128]{2,0,1:T(2,128)S(1)}, u32[]{:S(2)}, u32[]{:S(2)}) collective-permute-start(f32[2,4,128]{2,0,1:T(2,128)S(1)} %copy.13), channel_id=1, source_target_pairs={{0,1},{1,0},{2,3},{3,2},{4,5},{5,4},{6,7},{7,6},{8,9},{9,8},{10,11... | collective-permute-start | bytes 12296 | tf_op jit(solution)/shard_map/ppermute | solution.py:388
  61.1 3.1 %collective-permute-start.16 = (f32[16,128]{1,0:T(8,128)S(1)}, f32[16,128]{1,0:T(8,128)S(1)}, u32[]{:S(2)}, u32[]{:S(2)}) collective-permute-start(f32[16,128]{1,0:T(8,128)S(1)} %get-tuple-element.57), channel_id=1, source_target_pairs={{0,17},{1,16},{16,1},{17,0},{2,19},{3,18},{18,3},{19,2},{4,21},{5,... | collective-permute-start | bytes 24584 | tf_op jit(solution)/shard_map/ppermute | solution.py:388
  61.8 3.7 %collective-permute-start.15 = (f32[16,128]{1,0:T(8,128)S(1)}, f32[16,128]{1,0:T(8,128)S(1)}, u32[]{:S(2)}, u32[]{:S(2)}) collective-permute-start(f32[16,128]{1,0:T(8,128)S(1)} %get-tuple-element.57), channel_id=1, source_target_pairs={{0,16},{1,17},{16,0},{17,1},{2,18},{3,19},{18,2},{19,3},{4,20},{5,... | collective-permute-start | bytes 24584 | tf_op jit(solution)/shard_map/ppermute | solution.py:388
  63.3 2.1 %collective-permute-start.14 = (f32[16,128]{1,0:T(8,128)S(1)}, f32[16,128]{1,0:T(8,128)S(1)}, u32[]{:S(2)}, u32[]{:S(2)}) collective-permute-start(f32[16,128]{1,0:T(8,128)S(1)} %get-tuple-element.57), channel_id=1, source_target_pairs={{0,1},{1,0},{16,17},{17,16},{2,3},{3,2},{18,19},{19,18},{4,5},{5,4... | collective-permute-start | bytes 24584 | tf_op jit(solution)/shard_map/ppermute | solution.py:388

commit v11 on v10

--- a/solution.py
+++ b/solution.py
@@ -122,7 +122,7 @@
         in_specs=[SMEM, VMEM],
         out_specs=VMEM,
         compiler_params=params(),
-        cost_estimate=pl.CostEstimate(flops=1 << 20, bytes_accessed=1 << 20, transcendentals=0),
+        cost_estimate=pl.CostEstimate(flops=1<<30, bytes_accessed=1 << 18, transcendentals=0),
         name="lay",
     )(place, block)
 
@@ -143,7 +143,7 @@
         out_specs=VMEM,
         input_output_aliases={1 + len(blocks): 0},
         compiler_params=params(),
-        cost_estimate=pl.CostEstimate(flops=1 << 20, bytes_accessed=1 << 18, transcendentals=0),
+        cost_estimate=pl.CostEstimate(flops=1<<20, bytes_accessed=1 << 18, transcendentals=0),
         name="pack",
     )(place, *blocks, laid)
 
@@ -230,7 +230,7 @@
         out_specs=(VMEM,) * 4,
         scratch_shapes=[pltpu.VMEM((ROWS, count), F32)] * 2,
         compiler_params=params(),
-        cost_estimate=pl.CostEstimate(flops=1 << 29, bytes_accessed=1 << 20, transcendentals=1 << 20),
+        cost_estimate=pl.CostEstimate(flops=1<<20, bytes_accessed=1 << 18, transcendentals=0),
         name="first_rows",
     )(place, mass, pin(sources), *[pin(value) for value in packed], *[pin(value) for value in blocks])
 
@@ -418,8 +418,9 @@
         a = source_mass.reshape(n_z, n_x, CORES, part)
         a = lax.dynamic_index_in_dim(a, core, axis=2, keepdims=False).swapaxes(0, 1).reshape(-1, LANES)
         blocks = swap_all(target_points, "src", n_src)[1:]
-        three, two, one = [swap(source_points, "z", n_z, d) for d in (3, 2, 1)]
+        three, two = [swap(source_points, "z", n_z, d) for d in (3, 2)]
         mine, packed, b, a = ready(source_points, target_points, target_mass.reshape(-1, LANES), a)
+        one = swap(mine, "z", n_z, 1)
         laid = lay(along, three, 3, n_z)
         packed = swap_all(packed, "core", CORES)
         blocks = blocks + [swap(block, "core", CORES, 1) for block in blocks]

time: 66.3 us -> 67.9 us (1.024)
  blocking collectives: 28.1 us -> 29.7 us
    all_to_all x3, blocking collectives: 28.1 us -> 29.7 us  [share(): return lax.all_to_all(copies, ('z', 'x'), 0, 0, tiled=True)]
where the time goes in v11:
time: 67.9 us; the launch traced here: 67.6 us
  blocking collectives  29.7 us (44%)
  starting transfers between devices  15.1 us (22%)
  Pallas kernels  10.3 us (15%)
  waiting for transfers between devices  9.67 us (14%)
  other arithmetic  1.28 us (2%)
  between operations  0.82 us (1%)
    all_to_all x3, blocking collectives, share(): return lax.all_to_all(copies, ('z', 'x'), 0, 0, tiled=True)  29.7 us
    ppermute x17, starting transfers between devices, swap(): return lax.ppermute(value, axes, [(i, i ^ distance) for i in range(size)])  15.1 us
    ppermute x17, waiting for transfers between devices, swap(): return lax.ppermute(value, axes, [(i, i ^ distance) for i in range(size)])  9.67 us
    pallas_call x1, Pallas kernels, first_columns(): pl.pallas_call(kernel, out_shape=(pltpu.VMEM((width, count), F32), pltpu....  2.44 us
    pallas_call x1, Pallas kernels, first_rows(): pl.pallas_call(kernel, out_shape=(pltpu.VMEM((width, LANES), jnp.bfloat16...  2.18 us
    pallas_call x1, Pallas kernels, other_rows(): pl.pallas_call(kernel, out_shape=(rows_of(count + each * LANES), pltpu.VM...  1.78 us
    pallas_call x2, Pallas kernels, later_columns(): pl.pallas_call(kernel, out_shape=(rows_of(width),) + (rows_of(count),) *...  1.49 us
    pallas_call x2, Pallas kernels, later_rows(): pl.pallas_call(kernel, out_shape=rows_of(count), in_specs=[VMEM] * (4 + l...  1.47 us
  transfers between devices with their start and end apart: 17, of which 9 were waited for; matrix products, arithmetic and copies ran while one was open for 2% of the time, Pallas kernels for 5%

profile of v11, /device:TPU:0, one launch (start us, length us, event | category | flops | bytes accessed | tf_op | source)
XLA Modules:
  0.0 67.6 jit_solution(6692975264509774418)
XLA Ops:
  0.6 5.1 %collective-permute-start.2 = (bf16[128,128]{1,0:T(8,128)(2,1)}, bf16[128,128]{1,0:T(8,128)(2,1)S(1)}, u32[]{:S(2)}, u32[]{:S(2)}) collective-permute-start(bf16[128,128]{1,0:T(8,128)(2,1)} %sources_ref.1), channel_id=1, source_target_pairs={{0,12},{4,8},{8,4},{12,0},{1,13},{5,9},{9,5},{13,1},{2,14},{6,10},... | collective-permute-start | bytes 98312 | tf_op jit(solution)/shard_map/ppermute | solution.py:388
  5.8 1.5 %collective-permute-start.4 = (bf16[512,128]{1,0:T(8,128)(2,1)}, bf16[512,128]{1,0:T(8,128)(2,1)S(1)}, u32[]{:S(2)}, u32[]{:S(2)}) collective-permute-start(bf16[512,128]{1,0:T(8,128)(2,1)} %targets_ref.1), channel_id=1, source_target_pairs={{0,16},{16,0},{1,17},{17,1},{2,18},{18,2},{3,19},{19,3},{4,20},{20... | collective-permute-start | bytes 393224 | tf_op jit(solution)/shard_map/ppermute | solution.py:388
  7.3 1.0 %ready.1 = (bf16[128,128]{1,0:T(8,128)(2,1)S(1)}, bf16[544,128]{1,0:T(8,128)(2,1)S(1)}, f32[8,128]{1,0:T(8,128)S(1)}, f32[8,128]{1,0:T(8,128)S(1)}) custom-call(bf16[128,128]{1,0:T(8,128)(2,1)} %sources_ref.1, bf16[512,128]{1,0:T(8,128)(2,1)} %targets_ref.1, f32[8,128]{1,0:T(8,128)} %bitcast.31, f32[8,128]{1,0:T(8,128)S(1)} %bitcast.24), custom_call_target="tpu_custom_call" | custom-call | flops 1048576 | bytes 1048576 | tf_op jit(solution)/shard_map/ready/pallas_call | solution.py:95
  8.3 0.8 %collective-permute-start = (bf16[128,128]{1,0:T(8,128)(2,1)S(1)}, bf16[128,128]{1,0:T(8,128)(2,1)S(1)}, u32[]{:S(2)}, u32[]{:S(2)}) collective-permute-start(bf16[128,128]{1,0:T(8,128)(2,1)S(1)} %get-tuple-element.33.refs_0_), channel_id=1, source_target_pairs={{0,4},{4,0},{8,12},{12,8},{1,5},{5,1},{9,13},{13,9},{2,6},{6,2},{1... | collective-permute-start | bytes 98312 | tf_op jit(solution)/shard_map/ppermute | solution.py:388
  9.2 1.8 %collective-permute-done.4.refs_2_ = bf16[512,128]{1,0:T(8,128)(2,1)S(1)} collective-permute-done((bf16[512,128]{1,0:T(8,128)(2,1)}, bf16[512,128]{1,0:T(8,128)(2,1)S(1)}, u32[]{:S(2)}, u32[]{:S(2)}) %collective-permute-start.4) | collective-permute-done | bytes 131104 | tf_op jit(solution)/shard_map/ppermute | solution.py:388
  10.9 1.3 %collective-permute-done.refs_1_ = bf16[128,128]{1,0:T(8,128)(2,1)S(1)} collective-permute-done((bf16[128,128]{1,0:T(8,128)(2,1)S(1)}, bf16[128,128]{1,0:T(8,128)(2,1)S(1)}, u32[]{:S(2)}, u32[]{:S(2)}) %collective-permute-start) | collective-permute-done | bytes 32800 | tf_op jit(solution)/shard_map/ppermute | solution.py:388
  12.3 1.6 %collective-permute-start.6 = (bf16[512,128]{1,0:T(8,128)(2,1)S(1)}, bf16[512,128]{1,0:T(8,128)(2,1)S(1)}, u32[]{:S(2)}, u32[]{:S(2)}) collective-permute-start(bf16[512,128]{1,0:T(8,128)(2,1)S(1)} %pack.1.sources_ref.mine_ref), channel_id=1, source_target_pairs={{0,2},{2,0},{1,3},{3,1},{4,6},{6,4},{5,7},{7,5},{8,10},{10,8},{9,1... | collective-permute-start | bytes 393224 | tf_op jit(solution)/shard_map/ppermute | solution.py:388
  13.9 2.2 %first_rows.1 = (bf16[2048,128]{1,0:T(8,128)(2,1)S(1)}, bf16[2048,128]{1,0:T(8,128)(2,1)S(1)}, f32[16,128]{1,0:T(8,128)S(1)}, f32[4,128]{1,0:T(4,128)S(1)}) custom-call(s32[3]{0:T(128)S(1)} %pad_add_fusion.place_ref, f32[8,128]{1,0:T(8,128)S(1)} %get-tuple-element.32.mass_ref, bf16[512,128]{1,0:T(8,128)(2,1)S(1)} %pack.1.sources_ref.mine_ref, ...), custom_call_target="tpu_custom_call" | custom-call | flops 1048576 | bytes 262144 | tf_op jit(solution)/shard_map/first_rows/pallas_call | solution.py:221
  16.1 1.2 %collective-permute-done.6.refs_0_ = bf16[512,128]{1,0:T(8,128)(2,1)S(1)} collective-permute-done((bf16[512,128]{1,0:T(8,128)(2,1)S(1)}, bf16[512,128]{1,0:T(8,128)(2,1)S(1)}, u32[]{:S(2)}, u32[]{:S(2)}) %collective-permute-start.6) | collective-permute-done | bytes 131104 | tf_op jit(solution)/shard_map/ppermute | solution.py:388
  17.3 1.8 %other_rows.1 = (f32[8,128]{1,0:T(8,128)S(1)}, bf16[1024,128]{1,0:T(8,128)(2,1)S(1)}) custom-call(s32[3]{0:T(128)S(1)} %pad_add_fusion.place_ref, bf16[2048,128]{1,0:T(8,128)(2,1)S(1)} %get-tuple-element.47.targets_ref, bf16[2048,128]{1,0:T(8,128)(2,1)S(1)} %get-tuple-element.36.offset_ref, f32[4,128]{1,0:T(4,128)S(1)} %get-tuple-element.37.first_ref, ...), custom_call_target="tpu_custom_call" | custom-call | tf_op jit(solution)/shard_map/other_rows/pallas_call | solution.py:260
  19.1 11.6 %all_to_all.15.parts_ref = f32[8,8,128]{2,1,0:T(8,128)S(1)} all-to-all(f32[8,8,128]{2,1,0:T(8,128)S(1)} %broadcast_in_dim.6), channel_id=1, replica_groups=mesh['src'=2,'z'=4,'x'=2,'core'=2] {'z','x'}, dimensions={0} | all-to-all | bytes 65536 | tf_op jit(solution)/shard_map/all_to_all | solution.py:401
  30.7 2.4 %first_columns.1 = (f32[2048,1024]{1,0:T(8,128)S(1)}, f32[2048,128]{1,0:T(8,128)S(1)}, f32[16,128]{1,0:T(8,128)S(1)}, f32[16,128]{1,0:T(8,128)S(1)}, f32[8,128]{1,0:T(8,128)S(1)}) custom-call(bf16[1024,128]{1,0:T(8,128)(2,1)S(1)} %get-tuple-element.46.sources_ref, bf16[2048,128]{1,0:T(8,128)(2,1)S(1)} %get-tuple-element.47.targets_ref, ...), custom_call_target="tpu_custom_call" | custom-call | tf_op jit(solution)/shard_map/first_columns/pallas_call | solution.py:304
  33.2 1.2 %collective-permute-start.8 = (f32[16,128]{1,0:T(8,128)S(1)}, f32[16,128]{1,0:T(8,128)S(1)}, u32[]{:S(2)}, u32[]{:S(2)}) collective-permute-start(f32[16,128]{1,0:T(8,128)S(1)} %get-tuple-element.49.refs_0_), channel_id=1, source_target_pairs={{0,16},{1,17},{16,0},{17,1},{2,18},{3,19},{18,2},{19,3},{4,20},{5,... | collective-permute-start | bytes 24584 | tf_op jit(solution)/shard_map/ppermute | solution.py:388
  37.0 0.7 %later_rows.2 = f32[8,128]{1,0:T(8,128)S(1)} custom-call(f32[2048,1024]{1,0:T(8,128)S(1)} %get-tuple-element.41.plan_ref, f32[2048,128]{1,0:T(8,128)S(1)} %get-tuple-element.42.reach_ref, f32[16,128]{1,0:T(8,128)S(1)} %get-tuple-element.43.top_ref, f32[16,128]{1,0:T(8,128)S(1)} %get-tuple-element.44.log_ref, f32[16,128]{1,0:T(8,128)S(1)} %get-tuple-element.49.refs_0_, ...), custom_call_target="tpu_custom_call" | custom-call | tf_op jit(solution)/shard_map/later_rows/pallas_call | solution.py:338
  37.7 9.1 %all_to_all.16.parts_ref = f32[8,8,128]{2,1,0:T(8,128)S(1)} all-to-all(f32[8,8,128]{2,1,0:T(8,128)S(1)} %broadcast_in_dim.7), channel_id=1, replica_groups=mesh['src'=2,'z'=4,'x'=2,'core'=2] {'z','x'}, dimensions={0} | all-to-all | bytes 65536 | tf_op jit(solution)/shard_map/all_to_all | solution.py:401
  46.8 0.7 %later_columns.2.refs_0_ = f32[16,128]{1,0:T(8,128)S(1)} custom-call(f32[2048,1024]{1,0:T(8,128)S(1)} %get-tuple-element.41.plan_ref, f32[2048,128]{1,0:T(8,128)S(1)} %get-tuple-element.42.reach_ref, f32[16,128]{1,0:T(8,128)S(1)} %get-tuple-element.43.top_ref, f32[8,8,128]{2,1,0:T(8,128)S(1)} %all_to_all.16.parts_ref, ...), custom_call_target="tpu_custom_call" | custom-call | tf_op jit(solution)/shard_map/later_columns/pallas_call | solution.py:367
  47.6 1.2 %collective-permute-start.11 = (f32[16,128]{1,0:T(8,128)S(1)}, f32[16,128]{1,0:T(8,128)S(1)}, u32[]{:S(2)}, u32[]{:S(2)}) collective-permute-start(f32[16,128]{1,0:T(8,128)S(1)} %later_columns.2.refs_0_), channel_id=1, source_target_pairs={{0,16},{1,17},{16,0},{17,1},{2,18},{3,19},{18,2},{19,3},{4,20},{5,... | collective-permute-start | bytes 24584 | tf_op jit(solution)/shard_map/ppermute | solution.py:388
  49.5 1.2 %collective-permute-done.12.refs_3_ = f32[16,128]{1,0:T(8,128)S(1)} collective-permute-done((f32[16,128]{1,0:T(8,128)S(1)}, f32[16,128]{1,0:T(8,128)S(1)}, u32[]{:S(2)}, u32[]{:S(2)}) %collective-permute-start.12) | collective-permute-done | bytes 8224 | tf_op jit(solution)/shard_map/ppermute | solution.py:388
  51.3 0.7 %later_rows.3 = f32[8,128]{1,0:T(8,128)S(1)} custom-call(f32[2048,1024]{1,0:T(8,128)S(1)} %get-tuple-element.41.plan_ref, f32[2048,128]{1,0:T(8,128)S(1)} %get-tuple-element.42.reach_ref, f32[16,128]{1,0:T(8,128)S(1)} %get-tuple-element.43.top_ref, f32[16,128]{1,0:T(8,128)S(1)} %get-tuple-element.44.log_ref, f32[16,128]{1,0:T(8,128)S(1)} %later_columns.2.refs_0_, ...), custom_call_target="tpu_custom_call" | custom-call | tf_op jit(solution)/shard_map/later_rows/pallas_call | solution.py:338
  52.1 9.1 %all_to_all.17.parts_ref = f32[8,8,128]{2,1,0:T(8,128)S(1)} all-to-all(f32[8,8,128]{2,1,0:T(8,128)S(1)} %broadcast_in_dim.8), channel_id=1, replica_groups=mesh['src'=2,'z'=4,'x'=2,'core'=2] {'z','x'}, dimensions={0} | all-to-all | bytes 65536 | tf_op jit(solution)/shard_map/all_to_all | solution.py:401
  61.1 0.7 %later_columns.3 = (f32[16,128]{1,0:T(8,128)S(1)}, f32[8,128]{1,0:T(8,128)S(1)}) custom-call(f32[2048,1024]{1,0:T(8,128)S(1)} %get-tuple-element.41.plan_ref, f32[2048,128]{1,0:T(8,128)S(1)} %get-tuple-element.42.reach_ref, f32[16,128]{1,0:T(8,128)S(1)} %get-tuple-element.43.top_ref, f32[8,8,128]{2,1,0:T(8,128)S(1)} %all_to_all.17.parts_ref, ...), custom_call_target="tpu_custom_call" | custom-call | tf_op jit(solution)/shard_map/later_columns/pallas_call | solution.py:367
  62.0 1.3 %collective-permute-start.16 = (f32[16,128]{1,0:T(8,128)S(1)}, f32[16,128]{1,0:T(8,128)S(1)}, u32[]{:S(2)}, u32[]{:S(2)}) collective-permute-start(f32[16,128]{1,0:T(8,128)S(1)} %get-tuple-element.57), channel_id=1, source_target_pairs={{0,17},{1,16},{16,1},{17,0},{2,19},{3,18},{18,3},{19,2},{4,21},{5,... | collective-permute-start | bytes 24584 | tf_op jit(solution)/shard_map/ppermute | solution.py:388
  63.3 0.8 %collective-permute-start.15 = (f32[16,128]{1,0:T(8,128)S(1)}, f32[16,128]{1,0:T(8,128)S(1)}, u32[]{:S(2)}, u32[]{:S(2)}) collective-permute-start(f32[16,128]{1,0:T(8,128)S(1)} %get-tuple-element.57), channel_id=1, source_target_pairs={{0,16},{1,17},{16,0},{17,1},{2,18},{3,19},{18,2},{19,3},{4,20},{5,... | collective-permute-start | bytes 24584 | tf_op jit(solution)/shard_map/ppermute | solution.py:388
  65.1 1.8 %collective-permute-done.15 = f32[16,128]{1,0:T(8,128)S(1)} collective-permute-done((f32[16,128]{1,0:T(8,128)S(1)}, f32[16,128]{1,0:T(8,128)S(1)}, u32[]{:S(2)}, u32[]{:S(2)}) %collective-permute-start.15) | collective-permute-done | bytes 8224 | tf_op jit(solution)/shard_map/ppermute | solution.py:388
  (41 shorter events, 5.7 us)
Async XLA Ops:
  0.6 6.7 %copy-start = (f32[2048]{0:T(1024)S(1)}, f32[2048]{0:T(1024)}, u32[]{:S(2)}) copy-start(f32[2048]{0:T(1024)} %param.6) | copy-start | bytes 24580
  0.6 8.5 %collective-permute-start.2 = (bf16[128,128]{1,0:T(8,128)(2,1)}, bf16[128,128]{1,0:T(8,128)(2,1)S(1)}, u32[]{:S(2)}, u32[]{:S(2)}) collective-permute-start(bf16[128,128]{1,0:T(8,128)(2,1)} %sources_ref.1), channel_id=1, source_target_pairs={{0,12},{4,8},{8,4},{12,0},{1,13},{5,9},{9,5},{13,1},{2,14},{6,10},... | collective-permute-start | bytes 98312 | tf_op jit(solution)/shard_map/ppermute | solution.py:388
  5.8 5.2 %collective-permute-start.1 = (bf16[128,128]{1,0:T(8,128)(2,1)}, bf16[128,128]{1,0:T(8,128)(2,1)S(1)}, u32[]{:S(2)}, u32[]{:S(2)}) collective-permute-start(bf16[128,128]{1,0:T(8,128)(2,1)} %sources_ref.1), channel_id=1, source_target_pairs={{0,8},{4,12},{8,0},{12,4},{1,9},{5,13},{9,1},{13,5},{2,10},{6,14},... | collective-permute-start | bytes 98312 | tf_op jit(solution)/shard_map/ppermute | solution.py:388
  5.8 5.2 %collective-permute-start.4 = (bf16[512,128]{1,0:T(8,128)(2,1)}, bf16[512,128]{1,0:T(8,128)(2,1)S(1)}, u32[]{:S(2)}, u32[]{:S(2)}) collective-permute-start(bf16[512,128]{1,0:T(8,128)(2,1)} %targets_ref.1), channel_id=1, source_target_pairs={{0,16},{16,0},{1,17},{17,1},{2,18},{18,2},{3,19},{19,3},{4,20},{20... | collective-permute-start | bytes 393224 | tf_op jit(solution)/shard_map/ppermute | solution.py:388
  8.3 4.0 %collective-permute-start = (bf16[128,128]{1,0:T(8,128)(2,1)S(1)}, bf16[128,128]{1,0:T(8,128)(2,1)S(1)}, u32[]{:S(2)}, u32[]{:S(2)}) collective-permute-start(bf16[128,128]{1,0:T(8,128)(2,1)S(1)} %get-tuple-element.33.refs_0_), channel_id=1, source_target_pairs={{0,4},{4,0},{8,12},{12,8},{1,5},{5,1},{9,13},{13,9},{2,6},{6,2},{1... | collective-permute-start | bytes 98312 | tf_op jit(solution)/shard_map/ppermute | solution.py:388
  9.1 4.8 %collective-permute-start.3 = (bf16[544,128]{1,0:T(8,128)(2,1)S(1)}, bf16[544,128]{1,0:T(8,128)(2,1)S(1)}, u32[]{:S(2)}, u32[]{:S(2)}) collective-permute-start(bf16[544,128]{1,0:T(8,128)(2,1)S(1)} %get-tuple-element.34.refs_0_), channel_id=1, source_target_pairs={{0,1},{1,0},{2,3},{3,2},{4,5},{5,4},{6,7},{7,6},{8,9},{9,8},{10,11... | collective-permute-start | bytes 417800 | tf_op jit(solution)/shard_map/ppermute | solution.py:388
  10.9 3.0 %collective-permute-start.5 = (bf16[512,128]{1,0:T(8,128)(2,1)S(1)}, bf16[512,128]{1,0:T(8,128)(2,1)S(1)}, u32[]{:S(2)}, u32[]{:S(2)}) collective-permute-start(bf16[512,128]{1,0:T(8,128)(2,1)S(1)} %collective-permute-done.4.refs_2_), channel_id=1, source_target_pairs={{0,1},{1,0},{2,3},{3,2},{4,5},{5,4},{6,7},{7,6},{8,9},{9,8},{10,11... | collective-permute-start | bytes 393224 | tf_op jit(solution)/shard_map/ppermute | solution.py:388
  12.3 5.0 %collective-permute-start.6 = (bf16[512,128]{1,0:T(8,128)(2,1)S(1)}, bf16[512,128]{1,0:T(8,128)(2,1)S(1)}, u32[]{:S(2)}, u32[]{:S(2)}) collective-permute-start(bf16[512,128]{1,0:T(8,128)(2,1)S(1)} %pack.1.sources_ref.mine_ref), channel_id=1, source_target_pairs={{0,2},{2,0},{1,3},{3,1},{4,6},{6,4},{5,7},{7,5},{8,10},{10,8},{9,1... | collective-permute-start | bytes 393224 | tf_op jit(solution)/shard_map/ppermute | solution.py:388
  33.2 3.1 %collective-permute-start.9 = (f32[16,128]{1,0:T(8,128)S(1)}, f32[16,128]{1,0:T(8,128)S(1)}, u32[]{:S(2)}, u32[]{:S(2)}) collective-permute-start(f32[16,128]{1,0:T(8,128)S(1)} %get-tuple-element.49.refs_0_), channel_id=1, source_target_pairs={{0,17},{1,16},{16,1},{17,0},{2,19},{3,18},{18,3},{19,2},{4,21},{5,... | collective-permute-start | bytes 24584 | tf_op jit(solution)/shard_map/ppermute | solution.py:388
  33.2 3.7 %collective-permute-start.8 = (f32[16,128]{1,0:T(8,128)S(1)}, f32[16,128]{1,0:T(8,128)S(1)}, u32[]{:S(2)}, u32[]{:S(2)}) collective-permute-start(f32[16,128]{1,0:T(8,128)S(1)} %get-tuple-element.49.refs_0_), channel_id=1, source_target_pairs={{0,16},{1,17},{16,0},{17,1},{2,18},{3,19},{18,2},{19,3},{4,20},{5,... | collective-permute-start | bytes 24584 | tf_op jit(solution)/shard_map/ppermute | solution.py:388
  34.4 2.5 %collective-permute-start.7 = (f32[16,128]{1,0:T(8,128)S(1)}, f32[16,128]{1,0:T(8,128)S(1)}, u32[]{:S(2)}, u32[]{:S(2)}) collective-permute-start(f32[16,128]{1,0:T(8,128)S(1)} %get-tuple-element.49.refs_0_), channel_id=1, source_target_pairs={{0,1},{1,0},{16,17},{17,16},{2,3},{3,2},{18,19},{19,18},{4,5},{5,4... | collective-permute-start | bytes 24584 | tf_op jit(solution)/shard_map/ppermute | solution.py:388
  47.5 3.1 %collective-permute-start.12 = (f32[16,128]{1,0:T(8,128)S(1)}, f32[16,128]{1,0:T(8,128)S(1)}, u32[]{:S(2)}, u32[]{:S(2)}) collective-permute-start(f32[16,128]{1,0:T(8,128)S(1)} %later_columns.2.refs_0_), channel_id=1, source_target_pairs={{0,17},{1,16},{16,1},{17,0},{2,19},{3,18},{18,3},{19,2},{4,21},{5,... | collective-permute-start | bytes 24584 | tf_op jit(solution)/shard_map/ppermute | solution.py:388
  47.6 3.7 %collective-permute-start.11 = (f32[16,128]{1,0:T(8,128)S(1)}, f32[16,128]{1,0:T(8,128)S(1)}, u32[]{:S(2)}, u32[]{:S(2)}) collective-permute-start(f32[16,128]{1,0:T(8,128)S(1)} %later_columns.2.refs_0_), channel_id=1, source_target_pairs={{0,16},{1,17},{16,0},{17,1},{2,18},{3,19},{18,2},{19,3},{4,20},{5,... | collective-permute-start | bytes 24584 | tf_op jit(solution)/shard_map/ppermute | solution.py:388
  48.9 2.5 %collective-permute-start.10 = (f32[16,128]{1,0:T(8,128)S(1)}, f32[16,128]{1,0:T(8,128)S(1)}, u32[]{:S(2)}, u32[]{:S(2)}) collective-permute-start(f32[16,128]{1,0:T(8,128)S(1)} %later_columns.2.refs_0_), channel_id=1, source_target_pairs={{0,1},{1,0},{16,17},{17,16},{2,3},{3,2},{18,19},{19,18},{4,5},{5,4... | collective-permute-start | bytes 24584 | tf_op jit(solution)/shard_map/ppermute | solution.py:388
  61.9 2.2 %collective-permute-start.13 = (f32[2,4,128]{2,0,1:T(2,128)S(1)}, f32[2,4,128]{2,0,1:T(2,128)S(1)}, u32[]{:S(2)}, u32[]{:S(2)}) collective-permute-start(f32[2,4,128]{2,0,1:T(2,128)S(1)} %copy.13), channel_id=1, source_target_pairs={{0,1},{1,0},{2,3},{3,2},{4,5},{5,4},{6,7},{7,6},{8,9},{9,8},{10,11... | collective-permute-start | bytes 12296 | tf_op jit(solution)/shard_map/ppermute | solution.py:388
  62.0 3.1 %collective-permute-start.16 = (f32[16,128]{1,0:T(8,128)S(1)}, f32[16,128]{1,0:T(8,128)S(1)}, u32[]{:S(2)}, u32[]{:S(2)}) collective-permute-start(f32[16,128]{1,0:T(8,128)S(1)} %get-tuple-element.57), channel_id=1, source_target_pairs={{0,17},{1,16},{16,1},{17,0},{2,19},{3,18},{18,3},{19,2},{4,21},{5,... | collective-permute-start | bytes 24584 | tf_op jit(solution)/shard_map/ppermute | solution.py:388
  63.3 3.7 %collective-permute-start.15 = (f32[16,128]{1,0:T(8,128)S(1)}, f32[16,128]{1,0:T(8,128)S(1)}, u32[]{:S(2)}, u32[]{:S(2)}) collective-permute-start(f32[16,128]{1,0:T(8,128)S(1)} %get-tuple-element.57), channel_id=1, source_target_pairs={{0,16},{1,17},{16,0},{17,1},{2,18},{3,19},{18,2},{19,3},{4,20},{5,... | collective-permute-start | bytes 24584 | tf_op jit(solution)/shard_map/ppermute | solution.py:388
  64.1 2.8 %collective-permute-start.14 = (f32[16,128]{1,0:T(8,128)S(1)}, f32[16,128]{1,0:T(8,128)S(1)}, u32[]{:S(2)}, u32[]{:S(2)}) collective-permute-start(f32[16,128]{1,0:T(8,128)S(1)} %get-tuple-element.57), channel_id=1, source_target_pairs={{0,1},{1,0},{16,17},{17,16},{2,3},{3,2},{18,19},{19,18},{4,5},{5,4... | collective-permute-start | bytes 24584 | tf_op jit(solution)/shard_map/ppermute | solution.py:388

commit v12 on v10

--- a/solution.py
+++ b/solution.py
@@ -15,6 +15,7 @@
 CORES = 2
 PIECES = 3
 ROWS = 256
+CHAINS = 4
 F32 = jnp.float32
 VMEM = pl.BlockSpec(memory_space=pltpu.VMEM)
 SMEM = pl.BlockSpec(memory_space=pltpu.SMEM)
@@ -169,13 +170,15 @@
         self.total = jnp.zeros((8, count), F32)
 
     def add(self, scores_ref):
-        tops = self.peak
-        for row in range(0, ROWS, 8):
-            tops = jnp.maximum(tops, scores_ref[row : row + 8, :])
-        self.total = self.total * jnp.exp2((self.peak - tops) * SCALE)
-        self.peak = tops
-        for row in range(0, ROWS, 8):
-            self.total = self.total + jnp.exp2((scores_ref[row : row + 8, :] - tops) * SCALE)
+        slices = [scores_ref[row : row + 8, :] for row in range(0, ROWS, 8)]
+        tops = [tree(slices[i::CHAINS], jnp.maximum) for i in range(CHAINS)]
+        tops = jnp.maximum(self.peak, tree(tops, jnp.maximum))
+        totals = [self.total * jnp.exp2((self.peak - tops) * SCALE)] + [None] * (CHAINS - 1)
+        for step in range(len(slices)):
+            part = jnp.exp2((scores_ref[step * 8 : step * 8 + 8, :] - tops) * SCALE)
+            chain = (step + 1) % CHAINS
+            totals[chain] = part if totals[chain] is None else totals[chain] + part
+        self.peak, self.total = tops, tree(totals, jnp.add)
 
     def lse(self):
         widest = jnp.max(self.peak, axis=0, keepdims=True)
@@ -326,13 +329,14 @@
         part_refs, out_ref = refs[:-1], refs[-1]
         weight = jnp.exp2(log_ref[...] + (top_ref[...] - log_sum([ref[...] for ref in part_refs])))
         mask = diagonal()
-        total = jnp.zeros((8, count), F32)
+        totals = [jnp.zeros((8, count), F32)] * 2
         for block in range(rows):
             at = block * LANES
             factors = reach_ref[at : at + LANES, :] * to_column(weight[block : block + 1, :], mask)
-            for row in range(0, LANES, 8):
+            for step, row in enumerate(range(0, LANES, 8)):
                 factor = jnp.concatenate([factors[row : row + 8, :]] * (count // LANES), axis=1)
-                total = total + plan_ref[at + row : at + row + 8, :] * factor
+                totals[step % 2] = totals[step % 2] + plan_ref[at + row : at + row + 8, :] * factor
+        total = totals[0] + totals[1]
         fold_into(out_ref, jnp.sum(total, axis=0, keepdims=True))
 
     return pl.pallas_call(

time: 66.3 us -> 66.4 us (level)
  no operation moved by 1% of the time
where the time goes in v12:
time: 66.4 us; the launch traced here: 66.1 us
  blocking collectives  28.1 us (42%)
  starting transfers between devices  15.4 us (23%)
  Pallas kernels  10.4 us (16%)
  waiting for transfers between devices  9.55 us (14%)
  other arithmetic  1.28 us (2%)
  between operations  0.83 us (1%)
    all_to_all x3, blocking collectives, share(): return lax.all_to_all(copies, ('z', 'x'), 0, 0, tiled=True)  28.1 us
    ppermute x17, starting transfers between devices, swap(): return lax.ppermute(value, axes, [(i, i ^ distance) for i in range(size)])  15.4 us
    ppermute x17, waiting for transfers between devices, swap(): return lax.ppermute(value, axes, [(i, i ^ distance) for i in range(size)])  9.55 us
    pallas_call x1, Pallas kernels, first_columns(): pl.pallas_call(kernel, out_shape=(pltpu.VMEM((width, count), F32), pltpu....  2.43 us
    pallas_call x1, Pallas kernels, first_rows(): pl.pallas_call(kernel, out_shape=(pltpu.VMEM((width, LANES), jnp.bfloat16...  2.19 us
    pallas_call x1, Pallas kernels, other_rows(): pl.pallas_call(kernel, out_shape=(rows_of(count + each * LANES), pltpu.VM...  1.77 us
    pallas_call x2, Pallas kernels, later_rows(): pl.pallas_call(kernel, out_shape=rows_of(count), in_specs=[VMEM] * (4 + l...  1.52 us
    pallas_call x2, Pallas kernels, later_columns(): pl.pallas_call(kernel, out_shape=(rows_of(width),) + (rows_of(count),) *...  1.49 us
  transfers between devices with their start and end apart: 17, of which 9 were waited for; matrix products, arithmetic and copies ran while one was open for 2% of the time, Pallas kernels for 5%

profile of v12, /device:TPU:0, one launch (start us, length us, event | category | flops | bytes accessed | tf_op | source)
XLA Modules:
  0.0 66.1 jit_solution(7120001296801278766)
XLA Ops:
  0.6 3.0 %collective-permute-start.4 = (bf16[512,128]{1,0:T(8,128)(2,1)}, bf16[512,128]{1,0:T(8,128)(2,1)S(1)}, u32[]{:S(2)}, u32[]{:S(2)}) collective-permute-start(bf16[512,128]{1,0:T(8,128)(2,1)} %targets_ref.1), channel_id=1, source_target_pairs={{0,16},{16,0},{1,17},{17,1},{2,18},{18,2},{3,19},{19,3},{4,20},{20... | collective-permute-start | bytes 393224 | tf_op jit(solution)/shard_map/ppermute | solution.py:392
  3.7 1.6 %collective-permute-start = (bf16[128,128]{1,0:T(8,128)(2,1)}, bf16[128,128]{1,0:T(8,128)(2,1)S(1)}, u32[]{:S(2)}, u32[]{:S(2)}) collective-permute-start(bf16[128,128]{1,0:T(8,128)(2,1)} %sources_ref.1), channel_id=1, source_target_pairs={{0,4},{4,0},{8,12},{12,8},{1,5},{5,1},{9,13},{13,9},{2,6},{6,2},{1... | collective-permute-start | bytes 98312 | tf_op jit(solution)/shard_map/ppermute | solution.py:392
  5.3 2.5 %collective-permute-start.2 = (bf16[128,128]{1,0:T(8,128)(2,1)}, bf16[128,128]{1,0:T(8,128)(2,1)S(1)}, u32[]{:S(2)}, u32[]{:S(2)}) collective-permute-start(bf16[128,128]{1,0:T(8,128)(2,1)} %sources_ref.1), channel_id=1, source_target_pairs={{0,12},{4,8},{8,4},{12,0},{1,13},{5,9},{9,5},{13,1},{2,14},{6,10},... | collective-permute-start | bytes 98312 | tf_op jit(solution)/shard_map/ppermute | solution.py:392
  7.9 1.0 %ready.1 = (bf16[128,128]{1,0:T(8,128)(2,1)S(1)}, bf16[544,128]{1,0:T(8,128)(2,1)S(1)}, f32[8,128]{1,0:T(8,128)S(1)}, f32[8,128]{1,0:T(8,128)S(1)}) custom-call(bf16[128,128]{1,0:T(8,128)(2,1)} %sources_ref.1, bf16[512,128]{1,0:T(8,128)(2,1)} %targets_ref.1, f32[8,128]{1,0:T(8,128)} %bitcast.31, f32[8,128]{1,0:T(8,128)S(1)} %bitcast.24), custom_call_target="tpu_custom_call" | custom-call | flops 1048576 | bytes 1048576 | tf_op jit(solution)/shard_map/ready/pallas_call | solution.py:96
  9.4 1.9 %collective-permute-done.2.block_ref = bf16[128,128]{1,0:T(8,128)(2,1)S(1)} collective-permute-done((bf16[128,128]{1,0:T(8,128)(2,1)}, bf16[128,128]{1,0:T(8,128)(2,1)S(1)}, u32[]{:S(2)}, u32[]{:S(2)}) %collective-permute-start.2) | collective-permute-done | bytes 32800 | tf_op jit(solution)/shard_map/ppermute | solution.py:392
  11.4 1.8 %collective-permute-done.1.refs_2_ = bf16[128,128]{1,0:T(8,128)(2,1)S(1)} collective-permute-done((bf16[128,128]{1,0:T(8,128)(2,1)}, bf16[128,128]{1,0:T(8,128)(2,1)S(1)}, u32[]{:S(2)}, u32[]{:S(2)}) %collective-permute-start.1) | collective-permute-done | bytes 32800 | tf_op jit(solution)/shard_map/ppermute | solution.py:392
  13.1 1.6 %collective-permute-start.6 = (bf16[512,128]{1,0:T(8,128)(2,1)S(1)}, bf16[512,128]{1,0:T(8,128)(2,1)S(1)}, u32[]{:S(2)}, u32[]{:S(2)}) collective-permute-start(bf16[512,128]{1,0:T(8,128)(2,1)S(1)} %pack.1.sources_ref.mine_ref), channel_id=1, source_target_pairs={{0,2},{2,0},{1,3},{3,1},{4,6},{6,4},{5,7},{7,5},{8,10},{10,8},{9,1... | collective-permute-start | bytes 393224 | tf_op jit(solution)/shard_map/ppermute | solution.py:392
  14.8 2.2 %first_rows.1 = (bf16[2048,128]{1,0:T(8,128)(2,1)S(1)}, bf16[2048,128]{1,0:T(8,128)(2,1)S(1)}, f32[16,128]{1,0:T(8,128)S(1)}, f32[4,128]{1,0:T(4,128)S(1)}) custom-call(s32[3]{0:T(128)S(1)} %pad_add_fusion.place_ref, f32[8,128]{1,0:T(8,128)S(1)} %get-tuple-element.32.mass_ref, bf16[512,128]{1,0:T(8,128)(2,1)S(1)} %pack.1.sources_ref.mine_ref, ...), custom_call_target="tpu_custom_call" | custom-call | flops 536870912 | bytes 1048576 | tf_op jit(solution)/shard_map/first_rows/pallas_call | solution.py:224
  16.9 1.2 %collective-permute-done.6.refs_0_ = bf16[512,128]{1,0:T(8,128)(2,1)S(1)} collective-permute-done((bf16[512,128]{1,0:T(8,128)(2,1)S(1)}, bf16[512,128]{1,0:T(8,128)(2,1)S(1)}, u32[]{:S(2)}, u32[]{:S(2)}) %collective-permute-start.6) | collective-permute-done | bytes 131104 | tf_op jit(solution)/shard_map/ppermute | solution.py:392
  18.2 1.8 %other_rows.1 = (f32[8,128]{1,0:T(8,128)S(1)}, bf16[1024,128]{1,0:T(8,128)(2,1)S(1)}) custom-call(s32[3]{0:T(128)S(1)} %pad_add_fusion.place_ref, bf16[2048,128]{1,0:T(8,128)(2,1)S(1)} %get-tuple-element.47.targets_ref, bf16[2048,128]{1,0:T(8,128)(2,1)S(1)} %get-tuple-element.36.offset_ref, f32[4,128]{1,0:T(4,128)S(1)} %get-tuple-element.37.first_ref, ...), custom_call_target="tpu_custom_call" | custom-call | tf_op jit(solution)/shard_map/other_rows/pallas_call | solution.py:263
  19.9 9.9 %all_to_all.15.parts_ref = f32[8,8,128]{2,1,0:T(8,128)S(1)} all-to-all(f32[8,8,128]{2,1,0:T(8,128)S(1)} %broadcast_in_dim.6), channel_id=1, replica_groups=mesh['src'=2,'z'=4,'x'=2,'core'=2] {'z','x'}, dimensions={0} | all-to-all | bytes 65536 | tf_op jit(solution)/shard_map/all_to_all | solution.py:405
  29.9 2.4 %first_columns.1 = (f32[2048,1024]{1,0:T(8,128)S(1)}, f32[2048,128]{1,0:T(8,128)S(1)}, f32[16,128]{1,0:T(8,128)S(1)}, f32[16,128]{1,0:T(8,128)S(1)}, f32[8,128]{1,0:T(8,128)S(1)}) custom-call(bf16[1024,128]{1,0:T(8,128)(2,1)S(1)} %get-tuple-element.46.sources_ref, bf16[2048,128]{1,0:T(8,128)(2,1)S(1)} %get-tuple-element.47.targets_ref, ...), custom_call_target="tpu_custom_call" | custom-call | tf_op jit(solution)/shard_map/first_columns/pallas_call | solution.py:307
  33.0 1.3 %collective-permute-start.7 = (f32[16,128]{1,0:T(8,128)S(1)}, f32[16,128]{1,0:T(8,128)S(1)}, u32[]{:S(2)}, u32[]{:S(2)}) collective-permute-start(f32[16,128]{1,0:T(8,128)S(1)} %get-tuple-element.49.refs_0_), channel_id=1, source_target_pairs={{0,1},{1,0},{16,17},{17,16},{2,3},{3,2},{18,19},{19,18},{4,5},{5,4... | collective-permute-start | bytes 24584 | tf_op jit(solution)/shard_map/ppermute | solution.py:392
  35.5 0.7 collective-permute-done.8.refs_2_
  36.1 0.8 %later_rows.2 = f32[8,128]{1,0:T(8,128)S(1)} custom-call(f32[2048,1024]{1,0:T(8,128)S(1)} %get-tuple-element.41.plan_ref, f32[2048,128]{1,0:T(8,128)S(1)} %get-tuple-element.42.reach_ref, f32[16,128]{1,0:T(8,128)S(1)} %get-tuple-element.43.top_ref, f32[16,128]{1,0:T(8,128)S(1)} %get-tuple-element.44.log_ref, f32[16,128]{1,0:T(8,128)S(1)} %get-tuple-element.49.refs_0_, ...), custom_call_target="tpu_custom_call" | custom-call | tf_op jit(solution)/shard_map/later_rows/pallas_call | solution.py:342
  36.9 9.1 %all_to_all.16.parts_ref = f32[8,8,128]{2,1,0:T(8,128)S(1)} all-to-all(f32[8,8,128]{2,1,0:T(8,128)S(1)} %broadcast_in_dim.7), channel_id=1, replica_groups=mesh['src'=2,'z'=4,'x'=2,'core'=2] {'z','x'}, dimensions={0} | all-to-all | bytes 65536 | tf_op jit(solution)/shard_map/all_to_all | solution.py:405
  46.0 0.7 %later_columns.2.refs_0_ = f32[16,128]{1,0:T(8,128)S(1)} custom-call(f32[2048,1024]{1,0:T(8,128)S(1)} %get-tuple-element.41.plan_ref, f32[2048,128]{1,0:T(8,128)S(1)} %get-tuple-element.42.reach_ref, f32[16,128]{1,0:T(8,128)S(1)} %get-tuple-element.43.top_ref, f32[8,8,128]{2,1,0:T(8,128)S(1)} %all_to_all.16.parts_ref, ...), custom_call_target="tpu_custom_call" | custom-call | tf_op jit(solution)/shard_map/later_columns/pallas_call | solution.py:371
  47.4 1.3 %collective-permute-start.10 = (f32[16,128]{1,0:T(8,128)S(1)}, f32[16,128]{1,0:T(8,128)S(1)}, u32[]{:S(2)}, u32[]{:S(2)}) collective-permute-start(f32[16,128]{1,0:T(8,128)S(1)} %later_columns.2.refs_0_), channel_id=1, source_target_pairs={{0,1},{1,0},{16,17},{17,16},{2,3},{3,2},{18,19},{19,18},{4,5},{5,4... | collective-permute-start | bytes 24584 | tf_op jit(solution)/shard_map/ppermute | solution.py:392
  48.6 1.2 %collective-permute-done.12.refs_3_ = f32[16,128]{1,0:T(8,128)S(1)} collective-permute-done((f32[16,128]{1,0:T(8,128)S(1)}, f32[16,128]{1,0:T(8,128)S(1)}, u32[]{:S(2)}, u32[]{:S(2)}) %collective-permute-start.12) | collective-permute-done | bytes 8224 | tf_op jit(solution)/shard_map/ppermute | solution.py:392
  50.5 0.8 %later_rows.3 = f32[8,128]{1,0:T(8,128)S(1)} custom-call(f32[2048,1024]{1,0:T(8,128)S(1)} %get-tuple-element.41.plan_ref, f32[2048,128]{1,0:T(8,128)S(1)} %get-tuple-element.42.reach_ref, f32[16,128]{1,0:T(8,128)S(1)} %get-tuple-element.43.top_ref, f32[16,128]{1,0:T(8,128)S(1)} %get-tuple-element.44.log_ref, f32[16,128]{1,0:T(8,128)S(1)} %later_columns.2.refs_0_, ...), custom_call_target="tpu_custom_call" | custom-call | tf_op jit(solution)/shard_map/later_rows/pallas_call | solution.py:342
  51.3 9.1 %all_to_all.17.parts_ref = f32[8,8,128]{2,1,0:T(8,128)S(1)} all-to-all(f32[8,8,128]{2,1,0:T(8,128)S(1)} %broadcast_in_dim.8), channel_id=1, replica_groups=mesh['src'=2,'z'=4,'x'=2,'core'=2] {'z','x'}, dimensions={0} | all-to-all | bytes 65536 | tf_op jit(solution)/shard_map/all_to_all | solution.py:405
  60.3 0.7 %later_columns.3 = (f32[16,128]{1,0:T(8,128)S(1)}, f32[8,128]{1,0:T(8,128)S(1)}) custom-call(f32[2048,1024]{1,0:T(8,128)S(1)} %get-tuple-element.41.plan_ref, f32[2048,128]{1,0:T(8,128)S(1)} %get-tuple-element.42.reach_ref, f32[16,128]{1,0:T(8,128)S(1)} %get-tuple-element.43.top_ref, f32[8,8,128]{2,1,0:T(8,128)S(1)} %all_to_all.17.parts_ref, ...), custom_call_target="tpu_custom_call" | custom-call | tf_op jit(solution)/shard_map/later_columns/pallas_call | solution.py:371
  61.8 1.5 %collective-permute-start.15 = (f32[16,128]{1,0:T(8,128)S(1)}, f32[16,128]{1,0:T(8,128)S(1)}, u32[]{:S(2)}, u32[]{:S(2)}) collective-permute-start(f32[16,128]{1,0:T(8,128)S(1)} %get-tuple-element.57), channel_id=1, source_target_pairs={{0,16},{1,17},{16,0},{17,1},{2,18},{3,19},{18,2},{19,3},{4,20},{5,... | collective-permute-start | bytes 24584 | tf_op jit(solution)/shard_map/ppermute | solution.py:392
  64.3 1.1 %collective-permute-done.15 = f32[16,128]{1,0:T(8,128)S(1)} collective-permute-done((f32[16,128]{1,0:T(8,128)S(1)}, f32[16,128]{1,0:T(8,128)S(1)}, u32[]{:S(2)}, u32[]{:S(2)}) %collective-permute-start.15) | collective-permute-done | bytes 8224 | tf_op jit(solution)/shard_map/ppermute | solution.py:392
  (41 shorter events, 6.3 us)
Async XLA Ops:
  0.6 7.2 %copy-start = (f32[2048]{0:T(1024)S(1)}, f32[2048]{0:T(1024)}, u32[]{:S(2)}) copy-start(f32[2048]{0:T(1024)} %param.6) | copy-start | bytes 24580
  0.6 8.3 %collective-permute-start.4 = (bf16[512,128]{1,0:T(8,128)(2,1)}, bf16[512,128]{1,0:T(8,128)(2,1)S(1)}, u32[]{:S(2)}, u32[]{:S(2)}) collective-permute-start(bf16[512,128]{1,0:T(8,128)(2,1)} %targets_ref.1), channel_id=1, source_target_pairs={{0,16},{16,0},{1,17},{17,1},{2,18},{18,2},{3,19},{19,3},{4,20},{20... | collective-permute-start | bytes 393224 | tf_op jit(solution)/shard_map/ppermute | solution.py:392
  3.7 7.7 %collective-permute-start = (bf16[128,128]{1,0:T(8,128)(2,1)}, bf16[128,128]{1,0:T(8,128)(2,1)S(1)}, u32[]{:S(2)}, u32[]{:S(2)}) collective-permute-start(bf16[128,128]{1,0:T(8,128)(2,1)} %sources_ref.1), channel_id=1, source_target_pairs={{0,4},{4,0},{8,12},{12,8},{1,5},{5,1},{9,13},{13,9},{2,6},{6,2},{1... | collective-permute-start | bytes 98312 | tf_op jit(solution)/shard_map/ppermute | solution.py:392
  5.3 6.1 %collective-permute-start.2 = (bf16[128,128]{1,0:T(8,128)(2,1)}, bf16[128,128]{1,0:T(8,128)(2,1)S(1)}, u32[]{:S(2)}, u32[]{:S(2)}) collective-permute-start(bf16[128,128]{1,0:T(8,128)(2,1)} %sources_ref.1), channel_id=1, source_target_pairs={{0,12},{4,8},{8,4},{12,0},{1,13},{5,9},{9,5},{13,1},{2,14},{6,10},... | collective-permute-start | bytes 98312 | tf_op jit(solution)/shard_map/ppermute | solution.py:392
  7.7 5.4 %collective-permute-start.1 = (bf16[128,128]{1,0:T(8,128)(2,1)}, bf16[128,128]{1,0:T(8,128)(2,1)S(1)}, u32[]{:S(2)}, u32[]{:S(2)}) collective-permute-start(bf16[128,128]{1,0:T(8,128)(2,1)} %sources_ref.1), channel_id=1, source_target_pairs={{0,8},{4,12},{8,0},{12,4},{1,9},{5,13},{9,1},{13,5},{2,10},{6,14},... | collective-permute-start | bytes 98312 | tf_op jit(solution)/shard_map/ppermute | solution.py:392
  8.8 5.9 %collective-permute-start.3 = (bf16[544,128]{1,0:T(8,128)(2,1)S(1)}, bf16[544,128]{1,0:T(8,128)(2,1)S(1)}, u32[]{:S(2)}, u32[]{:S(2)}) collective-permute-start(bf16[544,128]{1,0:T(8,128)(2,1)S(1)} %get-tuple-element.34.refs_0_), channel_id=1, source_target_pairs={{0,1},{1,0},{2,3},{3,2},{4,5},{5,4},{6,7},{7,6},{8,9},{9,8},{10,11... | collective-permute-start | bytes 417800 | tf_op jit(solution)/shard_map/ppermute | solution.py:392
  8.9 5.8 %collective-permute-start.5 = (bf16[512,128]{1,0:T(8,128)(2,1)S(1)}, bf16[512,128]{1,0:T(8,128)(2,1)S(1)}, u32[]{:S(2)}, u32[]{:S(2)}) collective-permute-start(bf16[512,128]{1,0:T(8,128)(2,1)S(1)} %collective-permute-done.4.refs_2_), channel_id=1, source_target_pairs={{0,1},{1,0},{2,3},{3,2},{4,5},{5,4},{6,7},{7,6},{8,9},{9,8},{10,11... | collective-permute-start | bytes 393224 | tf_op jit(solution)/shard_map/ppermute | solution.py:392
  13.1 5.0 %collective-permute-start.6 = (bf16[512,128]{1,0:T(8,128)(2,1)S(1)}, bf16[512,128]{1,0:T(8,128)(2,1)S(1)}, u32[]{:S(2)}, u32[]{:S(2)}) collective-permute-start(bf16[512,128]{1,0:T(8,128)(2,1)S(1)} %pack.1.sources_ref.mine_ref), channel_id=1, source_target_pairs={{0,2},{2,0},{1,3},{3,1},{4,6},{6,4},{5,7},{7,5},{8,10},{10,8},{9,1... | collective-permute-start | bytes 393224 | tf_op jit(solution)/shard_map/ppermute | solution.py:392
  32.3 3.1 %collective-permute-start.9 = (f32[16,128]{1,0:T(8,128)S(1)}, f32[16,128]{1,0:T(8,128)S(1)}, u32[]{:S(2)}, u32[]{:S(2)}) collective-permute-start(f32[16,128]{1,0:T(8,128)S(1)} %get-tuple-element.49.refs_0_), channel_id=1, source_target_pairs={{0,17},{1,16},{16,1},{17,0},{2,19},{3,18},{18,3},{19,2},{4,21},{5,... | collective-permute-start | bytes 24584 | tf_op jit(solution)/shard_map/ppermute | solution.py:392
  32.4 3.7 %collective-permute-start.8 = (f32[16,128]{1,0:T(8,128)S(1)}, f32[16,128]{1,0:T(8,128)S(1)}, u32[]{:S(2)}, u32[]{:S(2)}) collective-permute-start(f32[16,128]{1,0:T(8,128)S(1)} %get-tuple-element.49.refs_0_), channel_id=1, source_target_pairs={{0,16},{1,17},{16,0},{17,1},{2,18},{3,19},{18,2},{19,3},{4,20},{5,... | collective-permute-start | bytes 24584 | tf_op jit(solution)/shard_map/ppermute | solution.py:392
  33.0 3.2 %collective-permute-start.7 = (f32[16,128]{1,0:T(8,128)S(1)}, f32[16,128]{1,0:T(8,128)S(1)}, u32[]{:S(2)}, u32[]{:S(2)}) collective-permute-start(f32[16,128]{1,0:T(8,128)S(1)} %get-tuple-element.49.refs_0_), channel_id=1, source_target_pairs={{0,1},{1,0},{16,17},{17,16},{2,3},{3,2},{18,19},{19,18},{4,5},{5,4... | collective-permute-start | bytes 24584 | tf_op jit(solution)/shard_map/ppermute | solution.py:392
  46.7 3.1 %collective-permute-start.12 = (f32[16,128]{1,0:T(8,128)S(1)}, f32[16,128]{1,0:T(8,128)S(1)}, u32[]{:S(2)}, u32[]{:S(2)}) collective-permute-start(f32[16,128]{1,0:T(8,128)S(1)} %later_columns.2.refs_0_), channel_id=1, source_target_pairs={{0,17},{1,16},{16,1},{17,0},{2,19},{3,18},{18,3},{19,2},{4,21},{5,... | collective-permute-start | bytes 24584 | tf_op jit(solution)/shard_map/ppermute | solution.py:392
  46.8 3.7 %collective-permute-start.11 = (f32[16,128]{1,0:T(8,128)S(1)}, f32[16,128]{1,0:T(8,128)S(1)}, u32[]{:S(2)}, u32[]{:S(2)}) collective-permute-start(f32[16,128]{1,0:T(8,128)S(1)} %later_columns.2.refs_0_), channel_id=1, source_target_pairs={{0,16},{1,17},{16,0},{17,1},{2,18},{3,19},{18,2},{19,3},{4,20},{5,... | collective-permute-start | bytes 24584 | tf_op jit(solution)/shard_map/ppermute | solution.py:392
  47.4 3.2 %collective-permute-start.10 = (f32[16,128]{1,0:T(8,128)S(1)}, f32[16,128]{1,0:T(8,128)S(1)}, u32[]{:S(2)}, u32[]{:S(2)}) collective-permute-start(f32[16,128]{1,0:T(8,128)S(1)} %later_columns.2.refs_0_), channel_id=1, source_target_pairs={{0,1},{1,0},{16,17},{17,16},{2,3},{3,2},{18,19},{19,18},{4,5},{5,4... | collective-permute-start | bytes 24584 | tf_op jit(solution)/shard_map/ppermute | solution.py:392
  61.1 2.2 %collective-permute-start.13 = (f32[2,4,128]{2,0,1:T(2,128)S(1)}, f32[2,4,128]{2,0,1:T(2,128)S(1)}, u32[]{:S(2)}, u32[]{:S(2)}) collective-permute-start(f32[2,4,128]{2,0,1:T(2,128)S(1)} %copy.13), channel_id=1, source_target_pairs={{0,1},{1,0},{2,3},{3,2},{4,5},{5,4},{6,7},{7,6},{8,9},{9,8},{10,11... | collective-permute-start | bytes 12296 | tf_op jit(solution)/shard_map/ppermute | solution.py:392
  61.2 3.1 %collective-permute-start.16 = (f32[16,128]{1,0:T(8,128)S(1)}, f32[16,128]{1,0:T(8,128)S(1)}, u32[]{:S(2)}, u32[]{:S(2)}) collective-permute-start(f32[16,128]{1,0:T(8,128)S(1)} %get-tuple-element.57), channel_id=1, source_target_pairs={{0,17},{1,16},{16,1},{17,0},{2,19},{3,18},{18,3},{19,2},{4,21},{5,... | collective-permute-start | bytes 24584 | tf_op jit(solution)/shard_map/ppermute | solution.py:392
  61.8 3.7 %collective-permute-start.15 = (f32[16,128]{1,0:T(8,128)S(1)}, f32[16,128]{1,0:T(8,128)S(1)}, u32[]{:S(2)}, u32[]{:S(2)}) collective-permute-start(f32[16,128]{1,0:T(8,128)S(1)} %get-tuple-element.57), channel_id=1, source_target_pairs={{0,16},{1,17},{16,0},{17,1},{2,18},{3,19},{18,2},{19,3},{4,20},{5,... | collective-permute-start | bytes 24584 | tf_op jit(solution)/shard_map/ppermute | solution.py:392
  63.3 2.1 %collective-permute-start.14 = (f32[16,128]{1,0:T(8,128)S(1)}, f32[16,128]{1,0:T(8,128)S(1)}, u32[]{:S(2)}, u32[]{:S(2)}) collective-permute-start(f32[16,128]{1,0:T(8,128)S(1)} %get-tuple-element.57), channel_id=1, source_target_pairs={{0,1},{1,0},{16,17},{17,16},{2,3},{3,2},{18,19},{19,18},{4,5},{5,4... | collective-permute-start | bytes 24584 | tf_op jit(solution)/shard_map/ppermute | solution.py:392

commit v13 on v10

--- a/solution.py
+++ b/solution.py
@@ -14,7 +14,7 @@
 LANES = 128
 CORES = 2
 PIECES = 3
-ROWS = 256
+ROWS = 512
 F32 = jnp.float32
 VMEM = pl.BlockSpec(memory_space=pltpu.VMEM)
 SMEM = pl.BlockSpec(memory_space=pltpu.SMEM)

time: 66.3 us -> 66.3 us (level)
  no operation moved by 1% of the time
where the time goes in v13:
time: 66.3 us; the launch traced here: 66.1 us
  blocking collectives  28.1 us (42%)
  starting transfers between devices  15.4 us (23%)
  Pallas kernels  10.4 us (16%)
  waiting for transfers between devices  9.49 us (14%)
  other arithmetic  1.28 us (2%)
  between operations  0.83 us (1%)
    all_to_all x3, blocking collectives, share(): return lax.all_to_all(copies, ('z', 'x'), 0, 0, tiled=True)  28.1 us
    ppermute x17, starting transfers between devices, swap(): return lax.ppermute(value, axes, [(i, i ^ distance) for i in range(size)])  15.4 us
    ppermute x17, waiting for transfers between devices, swap(): return lax.ppermute(value, axes, [(i, i ^ distance) for i in range(size)])  9.49 us
    pallas_call x1, Pallas kernels, first_columns(): pl.pallas_call(kernel, out_shape=(pltpu.VMEM((width, count), F32), pltpu....  2.41 us
    pallas_call x1, Pallas kernels, first_rows(): pl.pallas_call(kernel, out_shape=(pltpu.VMEM((width, LANES), jnp.bfloat16...  2.26 us
    pallas_call x1, Pallas kernels, other_rows(): pl.pallas_call(kernel, out_shape=(rows_of(count + each * LANES), pltpu.VM...  1.8 us
    pallas_call x2, Pallas kernels, later_columns(): pl.pallas_call(kernel, out_shape=(rows_of(width),) + (rows_of(count),) *...  1.49 us
    pallas_call x2, Pallas kernels, later_rows(): pl.pallas_call(kernel, out_shape=rows_of(count), in_specs=[VMEM] * (4 + l...  1.47 us
  transfers between devices with their start and end apart: 17, of which 9 were waited for; matrix products, arithmetic and copies ran while one was open for 2% of the time, Pallas kernels for 5%

profile of v13, /device:TPU:0, one launch (start us, length us, event | category | flops | bytes accessed | tf_op | source)
XLA Modules:
  0.0 66.1 jit_solution(13566531337848055871)
XLA Ops:
  0.6 3.0 %collective-permute-start.4 = (bf16[512,128]{1,0:T(8,128)(2,1)}, bf16[512,128]{1,0:T(8,128)(2,1)S(1)}, u32[]{:S(2)}, u32[]{:S(2)}) collective-permute-start(bf16[512,128]{1,0:T(8,128)(2,1)} %targets_ref.1), channel_id=1, source_target_pairs={{0,16},{16,0},{1,17},{17,1},{2,18},{18,2},{3,19},{19,3},{4,20},{20... | collective-permute-start | bytes 393224 | tf_op jit(solution)/shard_map/ppermute | solution.py:388
  3.7 1.6 %collective-permute-start = (bf16[128,128]{1,0:T(8,128)(2,1)}, bf16[128,128]{1,0:T(8,128)(2,1)S(1)}, u32[]{:S(2)}, u32[]{:S(2)}) collective-permute-start(bf16[128,128]{1,0:T(8,128)(2,1)} %sources_ref.1), channel_id=1, source_target_pairs={{0,4},{4,0},{8,12},{12,8},{1,5},{5,1},{9,13},{13,9},{2,6},{6,2},{1... | collective-permute-start | bytes 98312 | tf_op jit(solution)/shard_map/ppermute | solution.py:388
  5.3 2.5 %collective-permute-start.2 = (bf16[128,128]{1,0:T(8,128)(2,1)}, bf16[128,128]{1,0:T(8,128)(2,1)S(1)}, u32[]{:S(2)}, u32[]{:S(2)}) collective-permute-start(bf16[128,128]{1,0:T(8,128)(2,1)} %sources_ref.1), channel_id=1, source_target_pairs={{0,12},{4,8},{8,4},{12,0},{1,13},{5,9},{9,5},{13,1},{2,14},{6,10},... | collective-permute-start | bytes 98312 | tf_op jit(solution)/shard_map/ppermute | solution.py:388
  7.9 1.0 %ready.1 = (bf16[128,128]{1,0:T(8,128)(2,1)S(1)}, bf16[544,128]{1,0:T(8,128)(2,1)S(1)}, f32[8,128]{1,0:T(8,128)S(1)}, f32[8,128]{1,0:T(8,128)S(1)}) custom-call(bf16[128,128]{1,0:T(8,128)(2,1)} %sources_ref.1, bf16[512,128]{1,0:T(8,128)(2,1)} %targets_ref.1, f32[8,128]{1,0:T(8,128)} %bitcast.31, f32[8,128]{1,0:T(8,128)S(1)} %bitcast.24), custom_call_target="tpu_custom_call" | custom-call | flops 1048576 | bytes 1048576 | tf_op jit(solution)/shard_map/ready/pallas_call | solution.py:95
  9.4 1.9 %collective-permute-done.2.block_ref = bf16[128,128]{1,0:T(8,128)(2,1)S(1)} collective-permute-done((bf16[128,128]{1,0:T(8,128)(2,1)}, bf16[128,128]{1,0:T(8,128)(2,1)S(1)}, u32[]{:S(2)}, u32[]{:S(2)}) %collective-permute-start.2) | collective-permute-done | bytes 32800 | tf_op jit(solution)/shard_map/ppermute | solution.py:388
  11.4 1.8 %collective-permute-done.1.refs_2_ = bf16[128,128]{1,0:T(8,128)(2,1)S(1)} collective-permute-done((bf16[128,128]{1,0:T(8,128)(2,1)}, bf16[128,128]{1,0:T(8,128)(2,1)S(1)}, u32[]{:S(2)}, u32[]{:S(2)}) %collective-permute-start.1) | collective-permute-done | bytes 32800 | tf_op jit(solution)/shard_map/ppermute | solution.py:388
  13.1 1.6 %collective-permute-start.6 = (bf16[512,128]{1,0:T(8,128)(2,1)S(1)}, bf16[512,128]{1,0:T(8,128)(2,1)S(1)}, u32[]{:S(2)}, u32[]{:S(2)}) collective-permute-start(bf16[512,128]{1,0:T(8,128)(2,1)S(1)} %pack.1.sources_ref.mine_ref), channel_id=1, source_target_pairs={{0,2},{2,0},{1,3},{3,1},{4,6},{6,4},{5,7},{7,5},{8,10},{10,8},{9,1... | collective-permute-start | bytes 393224 | tf_op jit(solution)/shard_map/ppermute | solution.py:388
  14.8 2.3 %first_rows.1 = (bf16[2048,128]{1,0:T(8,128)(2,1)S(1)}, bf16[2048,128]{1,0:T(8,128)(2,1)S(1)}, f32[16,128]{1,0:T(8,128)S(1)}, f32[4,128]{1,0:T(4,128)S(1)}) custom-call(s32[3]{0:T(128)S(1)} %pad_add_fusion.place_ref, f32[8,128]{1,0:T(8,128)S(1)} %get-tuple-element.32.mass_ref, bf16[512,128]{1,0:T(8,128)(2,1)S(1)} %pack.1.sources_ref.mine_ref, ...), custom_call_target="tpu_custom_call" | custom-call | flops 536870912 | bytes 1048576 | tf_op jit(solution)/shard_map/first_rows/pallas_call | solution.py:221
  17.0 1.1 %collective-permute-done.6.refs_0_ = bf16[512,128]{1,0:T(8,128)(2,1)S(1)} collective-permute-done((bf16[512,128]{1,0:T(8,128)(2,1)S(1)}, bf16[512,128]{1,0:T(8,128)(2,1)S(1)}, u32[]{:S(2)}, u32[]{:S(2)}) %collective-permute-start.6) | collective-permute-done | bytes 131104 | tf_op jit(solution)/shard_map/ppermute | solution.py:388
  18.2 1.8 %other_rows.1 = (f32[8,128]{1,0:T(8,128)S(1)}, bf16[1024,128]{1,0:T(8,128)(2,1)S(1)}) custom-call(s32[3]{0:T(128)S(1)} %pad_add_fusion.place_ref, bf16[2048,128]{1,0:T(8,128)(2,1)S(1)} %get-tuple-element.47.targets_ref, bf16[2048,128]{1,0:T(8,128)(2,1)S(1)} %get-tuple-element.36.offset_ref, f32[4,128]{1,0:T(4,128)S(1)} %get-tuple-element.37.first_ref, ...), custom_call_target="tpu_custom_call" | custom-call | tf_op jit(solution)/shard_map/other_rows/pallas_call | solution.py:260
  20.0 9.9 %all_to_all.15.parts_ref = f32[8,8,128]{2,1,0:T(8,128)S(1)} all-to-all(f32[8,8,128]{2,1,0:T(8,128)S(1)} %broadcast_in_dim.6), channel_id=1, replica_groups=mesh['src'=2,'z'=4,'x'=2,'core'=2] {'z','x'}, dimensions={0} | all-to-all | bytes 65536 | tf_op jit(solution)/shard_map/all_to_all | solution.py:401
  29.9 2.4 %first_columns.1 = (f32[2048,1024]{1,0:T(8,128)S(1)}, f32[2048,128]{1,0:T(8,128)S(1)}, f32[16,128]{1,0:T(8,128)S(1)}, f32[16,128]{1,0:T(8,128)S(1)}, f32[8,128]{1,0:T(8,128)S(1)}) custom-call(bf16[1024,128]{1,0:T(8,128)(2,1)S(1)} %get-tuple-element.46.sources_ref, bf16[2048,128]{1,0:T(8,128)(2,1)S(1)} %get-tuple-element.47.targets_ref, ...), custom_call_target="tpu_custom_call" | custom-call | tf_op jit(solution)/shard_map/first_columns/pallas_call | solution.py:304
  33.0 1.3 %collective-permute-start.7 = (f32[16,128]{1,0:T(8,128)S(1)}, f32[16,128]{1,0:T(8,128)S(1)}, u32[]{:S(2)}, u32[]{:S(2)}) collective-permute-start(f32[16,128]{1,0:T(8,128)S(1)} %get-tuple-element.49.refs_0_), channel_id=1, source_target_pairs={{0,1},{1,0},{16,17},{17,16},{2,3},{3,2},{18,19},{19,18},{4,5},{5,4... | collective-permute-start | bytes 24584 | tf_op jit(solution)/shard_map/ppermute | solution.py:388
  35.5 0.7 collective-permute-done.8.refs_2_
  36.1 0.7 %later_rows.2 = f32[8,128]{1,0:T(8,128)S(1)} custom-call(f32[2048,1024]{1,0:T(8,128)S(1)} %get-tuple-element.41.plan_ref, f32[2048,128]{1,0:T(8,128)S(1)} %get-tuple-element.42.reach_ref, f32[16,128]{1,0:T(8,128)S(1)} %get-tuple-element.43.top_ref, f32[16,128]{1,0:T(8,128)S(1)} %get-tuple-element.44.log_ref, f32[16,128]{1,0:T(8,128)S(1)} %get-tuple-element.49.refs_0_, ...), custom_call_target="tpu_custom_call" | custom-call | tf_op jit(solution)/shard_map/later_rows/pallas_call | solution.py:338
  36.9 9.1 %all_to_all.16.parts_ref = f32[8,8,128]{2,1,0:T(8,128)S(1)} all-to-all(f32[8,8,128]{2,1,0:T(8,128)S(1)} %broadcast_in_dim.7), channel_id=1, replica_groups=mesh['src'=2,'z'=4,'x'=2,'core'=2] {'z','x'}, dimensions={0} | all-to-all | bytes 65536 | tf_op jit(solution)/shard_map/all_to_all | solution.py:401
  45.9 0.7 %later_columns.2.refs_0_ = f32[16,128]{1,0:T(8,128)S(1)} custom-call(f32[2048,1024]{1,0:T(8,128)S(1)} %get-tuple-element.41.plan_ref, f32[2048,128]{1,0:T(8,128)S(1)} %get-tuple-element.42.reach_ref, f32[16,128]{1,0:T(8,128)S(1)} %get-tuple-element.43.top_ref, f32[8,8,128]{2,1,0:T(8,128)S(1)} %all_to_all.16.parts_ref, ...), custom_call_target="tpu_custom_call" | custom-call | tf_op jit(solution)/shard_map/later_columns/pallas_call | solution.py:367
  47.3 1.3 %collective-permute-start.10 = (f32[16,128]{1,0:T(8,128)S(1)}, f32[16,128]{1,0:T(8,128)S(1)}, u32[]{:S(2)}, u32[]{:S(2)}) collective-permute-start(f32[16,128]{1,0:T(8,128)S(1)} %later_columns.2.refs_0_), channel_id=1, source_target_pairs={{0,1},{1,0},{16,17},{17,16},{2,3},{3,2},{18,19},{19,18},{4,5},{5,4... | collective-permute-start | bytes 24584 | tf_op jit(solution)/shard_map/ppermute | solution.py:388
  48.6 1.2 %collective-permute-done.12.refs_3_ = f32[16,128]{1,0:T(8,128)S(1)} collective-permute-done((f32[16,128]{1,0:T(8,128)S(1)}, f32[16,128]{1,0:T(8,128)S(1)}, u32[]{:S(2)}, u32[]{:S(2)}) %collective-permute-start.12) | collective-permute-done | bytes 8224 | tf_op jit(solution)/shard_map/ppermute | solution.py:388
  50.5 0.7 %later_rows.3 = f32[8,128]{1,0:T(8,128)S(1)} custom-call(f32[2048,1024]{1,0:T(8,128)S(1)} %get-tuple-element.41.plan_ref, f32[2048,128]{1,0:T(8,128)S(1)} %get-tuple-element.42.reach_ref, f32[16,128]{1,0:T(8,128)S(1)} %get-tuple-element.43.top_ref, f32[16,128]{1,0:T(8,128)S(1)} %get-tuple-element.44.log_ref, f32[16,128]{1,0:T(8,128)S(1)} %later_columns.2.refs_0_, ...), custom_call_target="tpu_custom_call" | custom-call | tf_op jit(solution)/shard_map/later_rows/pallas_call | solution.py:338
  51.2 9.1 %all_to_all.17.parts_ref = f32[8,8,128]{2,1,0:T(8,128)S(1)} all-to-all(f32[8,8,128]{2,1,0:T(8,128)S(1)} %broadcast_in_dim.8), channel_id=1, replica_groups=mesh['src'=2,'z'=4,'x'=2,'core'=2] {'z','x'}, dimensions={0} | all-to-all | bytes 65536 | tf_op jit(solution)/shard_map/all_to_all | solution.py:401
  60.3 0.7 %later_columns.3 = (f32[16,128]{1,0:T(8,128)S(1)}, f32[8,128]{1,0:T(8,128)S(1)}) custom-call(f32[2048,1024]{1,0:T(8,128)S(1)} %get-tuple-element.41.plan_ref, f32[2048,128]{1,0:T(8,128)S(1)} %get-tuple-element.42.reach_ref, f32[16,128]{1,0:T(8,128)S(1)} %get-tuple-element.43.top_ref, f32[8,8,128]{2,1,0:T(8,128)S(1)} %all_to_all.17.parts_ref, ...), custom_call_target="tpu_custom_call" | custom-call | tf_op jit(solution)/shard_map/later_columns/pallas_call | solution.py:367
  61.8 1.5 %collective-permute-start.15 = (f32[16,128]{1,0:T(8,128)S(1)}, f32[16,128]{1,0:T(8,128)S(1)}, u32[]{:S(2)}, u32[]{:S(2)}) collective-permute-start(f32[16,128]{1,0:T(8,128)S(1)} %get-tuple-element.57), channel_id=1, source_target_pairs={{0,16},{1,17},{16,0},{17,1},{2,18},{3,19},{18,2},{19,3},{4,20},{5,... | collective-permute-start | bytes 24584 | tf_op jit(solution)/shard_map/ppermute | solution.py:388
  64.3 1.1 %collective-permute-done.15 = f32[16,128]{1,0:T(8,128)S(1)} collective-permute-done((f32[16,128]{1,0:T(8,128)S(1)}, f32[16,128]{1,0:T(8,128)S(1)}, u32[]{:S(2)}, u32[]{:S(2)}) %collective-permute-start.15) | collective-permute-done | bytes 8224 | tf_op jit(solution)/shard_map/ppermute | solution.py:388
  (41 shorter events, 6.3 us)
Async XLA Ops:
  0.6 7.2 %copy-start = (f32[2048]{0:T(1024)S(1)}, f32[2048]{0:T(1024)}, u32[]{:S(2)}) copy-start(f32[2048]{0:T(1024)} %param.6) | copy-start | bytes 24580
  0.6 8.3 %collective-permute-start.4 = (bf16[512,128]{1,0:T(8,128)(2,1)}, bf16[512,128]{1,0:T(8,128)(2,1)S(1)}, u32[]{:S(2)}, u32[]{:S(2)}) collective-permute-start(bf16[512,128]{1,0:T(8,128)(2,1)} %targets_ref.1), channel_id=1, source_target_pairs={{0,16},{16,0},{1,17},{17,1},{2,18},{18,2},{3,19},{19,3},{4,20},{20... | collective-permute-start | bytes 393224 | tf_op jit(solution)/shard_map/ppermute | solution.py:388
  3.7 7.7 %collective-permute-start = (bf16[128,128]{1,0:T(8,128)(2,1)}, bf16[128,128]{1,0:T(8,128)(2,1)S(1)}, u32[]{:S(2)}, u32[]{:S(2)}) collective-permute-start(bf16[128,128]{1,0:T(8,128)(2,1)} %sources_ref.1), channel_id=1, source_target_pairs={{0,4},{4,0},{8,12},{12,8},{1,5},{5,1},{9,13},{13,9},{2,6},{6,2},{1... | collective-permute-start | bytes 98312 | tf_op jit(solution)/shard_map/ppermute | solution.py:388
  5.3 6.1 %collective-permute-start.2 = (bf16[128,128]{1,0:T(8,128)(2,1)}, bf16[128,128]{1,0:T(8,128)(2,1)S(1)}, u32[]{:S(2)}, u32[]{:S(2)}) collective-permute-start(bf16[128,128]{1,0:T(8,128)(2,1)} %sources_ref.1), channel_id=1, source_target_pairs={{0,12},{4,8},{8,4},{12,0},{1,13},{5,9},{9,5},{13,1},{2,14},{6,10},... | collective-permute-start | bytes 98312 | tf_op jit(solution)/shard_map/ppermute | solution.py:388
  7.7 5.4 %collective-permute-start.1 = (bf16[128,128]{1,0:T(8,128)(2,1)}, bf16[128,128]{1,0:T(8,128)(2,1)S(1)}, u32[]{:S(2)}, u32[]{:S(2)}) collective-permute-start(bf16[128,128]{1,0:T(8,128)(2,1)} %sources_ref.1), channel_id=1, source_target_pairs={{0,8},{4,12},{8,0},{12,4},{1,9},{5,13},{9,1},{13,5},{2,10},{6,14},... | collective-permute-start | bytes 98312 | tf_op jit(solution)/shard_map/ppermute | solution.py:388
  8.8 5.9 %collective-permute-start.3 = (bf16[544,128]{1,0:T(8,128)(2,1)S(1)}, bf16[544,128]{1,0:T(8,128)(2,1)S(1)}, u32[]{:S(2)}, u32[]{:S(2)}) collective-permute-start(bf16[544,128]{1,0:T(8,128)(2,1)S(1)} %get-tuple-element.34.refs_0_), channel_id=1, source_target_pairs={{0,1},{1,0},{2,3},{3,2},{4,5},{5,4},{6,7},{7,6},{8,9},{9,8},{10,11... | collective-permute-start | bytes 417800 | tf_op jit(solution)/shard_map/ppermute | solution.py:388
  8.9 5.8 %collective-permute-start.5 = (bf16[512,128]{1,0:T(8,128)(2,1)S(1)}, bf16[512,128]{1,0:T(8,128)(2,1)S(1)}, u32[]{:S(2)}, u32[]{:S(2)}) collective-permute-start(bf16[512,128]{1,0:T(8,128)(2,1)S(1)} %collective-permute-done.4.refs_2_), channel_id=1, source_target_pairs={{0,1},{1,0},{2,3},{3,2},{4,5},{5,4},{6,7},{7,6},{8,9},{9,8},{10,11... | collective-permute-start | bytes 393224 | tf_op jit(solution)/shard_map/ppermute | solution.py:388
  13.1 5.0 %collective-permute-start.6 = (bf16[512,128]{1,0:T(8,128)(2,1)S(1)}, bf16[512,128]{1,0:T(8,128)(2,1)S(1)}, u32[]{:S(2)}, u32[]{:S(2)}) collective-permute-start(bf16[512,128]{1,0:T(8,128)(2,1)S(1)} %pack.1.sources_ref.mine_ref), channel_id=1, source_target_pairs={{0,2},{2,0},{1,3},{3,1},{4,6},{6,4},{5,7},{7,5},{8,10},{10,8},{9,1... | collective-permute-start | bytes 393224 | tf_op jit(solution)/shard_map/ppermute | solution.py:388
  32.3 3.1 %collective-permute-start.9 = (f32[16,128]{1,0:T(8,128)S(1)}, f32[16,128]{1,0:T(8,128)S(1)}, u32[]{:S(2)}, u32[]{:S(2)}) collective-permute-start(f32[16,128]{1,0:T(8,128)S(1)} %get-tuple-element.49.refs_0_), channel_id=1, source_target_pairs={{0,17},{1,16},{16,1},{17,0},{2,19},{3,18},{18,3},{19,2},{4,21},{5,... | collective-permute-start | bytes 24584 | tf_op jit(solution)/shard_map/ppermute | solution.py:388
  32.4 3.7 %collective-permute-start.8 = (f32[16,128]{1,0:T(8,128)S(1)}, f32[16,128]{1,0:T(8,128)S(1)}, u32[]{:S(2)}, u32[]{:S(2)}) collective-permute-start(f32[16,128]{1,0:T(8,128)S(1)} %get-tuple-element.49.refs_0_), channel_id=1, source_target_pairs={{0,16},{1,17},{16,0},{17,1},{2,18},{3,19},{18,2},{19,3},{4,20},{5,... | collective-permute-start | bytes 24584 | tf_op jit(solution)/shard_map/ppermute | solution.py:388
  33.0 3.1 %collective-permute-start.7 = (f32[16,128]{1,0:T(8,128)S(1)}, f32[16,128]{1,0:T(8,128)S(1)}, u32[]{:S(2)}, u32[]{:S(2)}) collective-permute-start(f32[16,128]{1,0:T(8,128)S(1)} %get-tuple-element.49.refs_0_), channel_id=1, source_target_pairs={{0,1},{1,0},{16,17},{17,16},{2,3},{3,2},{18,19},{19,18},{4,5},{5,4... | collective-permute-start | bytes 24584 | tf_op jit(solution)/shard_map/ppermute | solution.py:388
  46.7 3.1 %collective-permute-start.12 = (f32[16,128]{1,0:T(8,128)S(1)}, f32[16,128]{1,0:T(8,128)S(1)}, u32[]{:S(2)}, u32[]{:S(2)}) collective-permute-start(f32[16,128]{1,0:T(8,128)S(1)} %later_columns.2.refs_0_), channel_id=1, source_target_pairs={{0,17},{1,16},{16,1},{17,0},{2,19},{3,18},{18,3},{19,2},{4,21},{5,... | collective-permute-start | bytes 24584 | tf_op jit(solution)/shard_map/ppermute | solution.py:388
  46.8 3.7 %collective-permute-start.11 = (f32[16,128]{1,0:T(8,128)S(1)}, f32[16,128]{1,0:T(8,128)S(1)}, u32[]{:S(2)}, u32[]{:S(2)}) collective-permute-start(f32[16,128]{1,0:T(8,128)S(1)} %later_columns.2.refs_0_), channel_id=1, source_target_pairs={{0,16},{1,17},{16,0},{17,1},{2,18},{3,19},{18,2},{19,3},{4,20},{5,... | collective-permute-start | bytes 24584 | tf_op jit(solution)/shard_map/ppermute | solution.py:388
  47.3 3.1 %collective-permute-start.10 = (f32[16,128]{1,0:T(8,128)S(1)}, f32[16,128]{1,0:T(8,128)S(1)}, u32[]{:S(2)}, u32[]{:S(2)}) collective-permute-start(f32[16,128]{1,0:T(8,128)S(1)} %later_columns.2.refs_0_), channel_id=1, source_target_pairs={{0,1},{1,0},{16,17},{17,16},{2,3},{3,2},{18,19},{19,18},{4,5},{5,4... | collective-permute-start | bytes 24584 | tf_op jit(solution)/shard_map/ppermute | solution.py:388
  61.1 2.2 %collective-permute-start.13 = (f32[2,4,128]{2,0,1:T(2,128)S(1)}, f32[2,4,128]{2,0,1:T(2,128)S(1)}, u32[]{:S(2)}, u32[]{:S(2)}) collective-permute-start(f32[2,4,128]{2,0,1:T(2,128)S(1)} %copy.13), channel_id=1, source_target_pairs={{0,1},{1,0},{2,3},{3,2},{4,5},{5,4},{6,7},{7,6},{8,9},{9,8},{10,11... | collective-permute-start | bytes 12296 | tf_op jit(solution)/shard_map/ppermute | solution.py:388
  61.2 3.1 %collective-permute-start.16 = (f32[16,128]{1,0:T(8,128)S(1)}, f32[16,128]{1,0:T(8,128)S(1)}, u32[]{:S(2)}, u32[]{:S(2)}) collective-permute-start(f32[16,128]{1,0:T(8,128)S(1)} %get-tuple-element.57), channel_id=1, source_target_pairs={{0,17},{1,16},{16,1},{17,0},{2,19},{3,18},{18,3},{19,2},{4,21},{5,... | collective-permute-start | bytes 24584 | tf_op jit(solution)/shard_map/ppermute | solution.py:388
  61.8 3.7 %collective-permute-start.15 = (f32[16,128]{1,0:T(8,128)S(1)}, f32[16,128]{1,0:T(8,128)S(1)}, u32[]{:S(2)}, u32[]{:S(2)}) collective-permute-start(f32[16,128]{1,0:T(8,128)S(1)} %get-tuple-element.57), channel_id=1, source_target_pairs={{0,16},{1,17},{16,0},{17,1},{2,18},{3,19},{18,2},{19,3},{4,20},{5,... | collective-permute-start | bytes 24584 | tf_op jit(solution)/shard_map/ppermute | solution.py:388
  63.3 2.1 %collective-permute-start.14 = (f32[16,128]{1,0:T(8,128)S(1)}, f32[16,128]{1,0:T(8,128)S(1)}, u32[]{:S(2)}, u32[]{:S(2)}) collective-permute-start(f32[16,128]{1,0:T(8,128)S(1)} %get-tuple-element.57), channel_id=1, source_target_pairs={{0,1},{1,0},{16,17},{17,16},{2,3},{3,2},{18,19},{19,18},{4,5},{5,4... | collective-permute-start | bytes 24584 | tf_op jit(solution)/shard_map/ppermute | solution.py:388

commit v14 on v10

--- a/solution.py
+++ b/solution.py
@@ -396,9 +396,12 @@
     return values
 
 
-def share(value, size):
-    copies = jnp.broadcast_to(value[None], (size,) + value.shape)
-    return lax.all_to_all(copies, ("z", "x"), 0, 0, tiled=True)
+def share(value, n_z, n_x):
+    walk = [z * n_x + (x if z % 2 == 0 else n_x - 1 - x) for z in range(n_z) for x in range(n_x)]
+    if n_x == 2:
+        walk = [z * n_x for z in range(n_z)] + [z * n_x + 1 for z in reversed(range(n_z))]
+    copies = jnp.broadcast_to(value[None], (n_z * n_x,) + value.shape)
+    return lax.all_to_all(copies, "far", 0, 0, axis_index_groups=[walk], tiled=True)
 
 
 def half_norm(points):
@@ -410,31 +413,34 @@
     near, n_near = ("src", "core"), n_src * CORES
     n_far = n_z * n_x
 
+    def swap_x(value):
+        return [value] + [swap(value, "far", n_far, dx) for dx in range(1, n_x)]
+
     def local(source_points, target_points, source_mass, target_mass):
-        core, x = lax.axis_index("core"), lax.axis_index("x")
+        core, x = lax.axis_index("core"), (lax.axis_index("far") % n_x)
         place = jnp.stack([lax.axis_index("src"), core, x]).astype(jnp.int32)
-        along = lax.axis_index("z").astype(jnp.int32).reshape(1)
+        along = (lax.axis_index("far") // n_x).astype(jnp.int32).reshape(1)
         part = source_points.shape[0]
         a = source_mass.reshape(n_z, n_x, CORES, part)
         a = lax.dynamic_index_in_dim(a, core, axis=2, keepdims=False).swapaxes(0, 1).reshape(-1, LANES)
         blocks = swap_all(target_points, "src", n_src)[1:]
-        three, two, one = [swap(source_points, "z", n_z, d) for d in (3, 2, 1)]
+        three, two, one = [swap(source_points, "far", n_far, d * n_x) for d in (3, 2, 1)]
         mine, packed, b, a = ready(source_points, target_points, target_mass.reshape(-1, LANES), a)
         laid = lay(along, three, 3, n_z)
         packed = swap_all(packed, "core", CORES)
         blocks = blocks + [swap(block, "core", CORES, 1) for block in blocks]
-        groups = swap_all(pack(along, [mine, one, two], laid), "x", n_x)
+        groups = swap_x(pack(along, [mine, one, two], laid))
         place, a = lax.optimization_barrier((place, a))
         targets, offsets, b, first = first_rows(place, b, packed, blocks, groups[0])
         own, sources = other_rows(place, targets, offsets, first, groups)
-        plan, reach, top, own, row_lse = first_columns(sources, targets, share(own, n_far), a)
+        plan, reach, top, own, row_lse = first_columns(sources, targets, share(own, n_z, n_x), a)
         early_x, early_y, own = lax.optimization_barrier((sources, targets, own))
         half_x, half_y = half_norm(early_x).reshape(-1, LANES), half_norm(early_y).reshape(-1, LANES)
         parts = swap_all(own, near, n_near)
         half_x, half_y, *parts = lax.optimization_barrier((half_x, half_y, *parts))
         for step in range(1, ITERS):
             rows = later_rows(plan, reach, top, b, parts)
-            own, *potential = later_columns(plan, reach, top, share(rows, n_far), a, row_lse, half_x, step == ITERS - 1)
+            own, *potential = later_columns(plan, reach, top, share(rows, n_z, n_x), a, row_lse, half_x, step == ITERS - 1)
             parts = swap_all(own, near, n_near)
         mine, other = swap_all(potential[0].reshape(n_x, n_z, part), "core", CORES)
         first, second = jnp.where(core == 0, mine, other), jnp.where(core == 0, other, mine)
@@ -451,8 +457,8 @@
     n_src, n_tgt = mesh.shape["src"], mesh.shape["tgt"]
     n_z = 4
     n_x = n_tgt // (n_z * CORES)
-    split = Mesh(mesh.devices.reshape(n_src, n_z, n_x, CORES), ("src", "z", "x", "core"))
-    tgt = ("z", "x", "core")
+    split = Mesh(mesh.devices.reshape(n_src, n_z * n_x, CORES), ("src", "far", "core"))
+    tgt = ("far", "core")
     placed = (P(("src", *tgt), None), P((*tgt, "src"), None), P("src"), P(tgt))
     return jax.shard_map(
         make_local(n_src, n_z, n_x),

time: 66.3 us -> 66.4 us (level)
  no operation moved by 1% of the time
where the time goes in v14:
time: 66.4 us; the launch traced here: 66.2 us
  blocking collectives  28.2 us (42%)
  starting transfers between devices  15.4 us (23%)
  Pallas kernels  10.3 us (16%)
  waiting for transfers between devices  9.57 us (14%)
  other arithmetic  1.28 us (2%)
  between operations  0.83 us (1%)
    all_to_all x3, blocking collectives, share(): lax.all_to_all(copies, 'far', 0, 0, axis_index_groups=[walk], tiled=True)  28.2 us
    ppermute x17, starting transfers between devices, swap(): return lax.ppermute(value, axes, [(i, i ^ distance) for i in range(size)])  15.4 us
    ppermute x17, waiting for transfers between devices, swap(): return lax.ppermute(value, axes, [(i, i ^ distance) for i in range(size)])  9.57 us
    pallas_call x1, Pallas kernels, first_columns(): pl.pallas_call(kernel, out_shape=(pltpu.VMEM((width, count), F32), pltpu....  2.44 us
    pallas_call x1, Pallas kernels, first_rows(): pl.pallas_call(kernel, out_shape=(pltpu.VMEM((width, LANES), jnp.bfloat16...  2.18 us
    pallas_call x1, Pallas kernels, other_rows(): pl.pallas_call(kernel, out_shape=(rows_of(count + each * LANES), pltpu.VM...  1.77 us
    pallas_call x2, Pallas kernels, later_columns(): pl.pallas_call(kernel, out_shape=(rows_of(width),) + (rows_of(count),) *...  1.49 us
    pallas_call x2, Pallas kernels, later_rows(): pl.pallas_call(kernel, out_shape=rows_of(count), in_specs=[VMEM] * (4 + l...  1.47 us
  transfers between devices with their start and end apart: 17, of which 9 were waited for; matrix products, arithmetic and copies ran while one was open for 2% of the time, Pallas kernels for 5%

profile of v14, /device:TPU:0, one launch (start us, length us, event | category | flops | bytes accessed | tf_op | source)
XLA Modules:
  0.0 66.2 jit_solution(1438114411674973263)
XLA Ops:
  0.6 3.0 %collective-permute-start.4 = (bf16[512,128]{1,0:T(8,128)(2,1)}, bf16[512,128]{1,0:T(8,128)(2,1)S(1)}, u32[]{:S(2)}, u32[]{:S(2)}) collective-permute-start(bf16[512,128]{1,0:T(8,128)(2,1)} %targets_ref.1), channel_id=1, source_target_pairs={{0,16},{16,0},{1,17},{17,1},{2,18},{18,2},{3,19},{19,3},{4,20},{20... | collective-permute-start | bytes 393224 | tf_op jit(solution)/shard_map/ppermute | solution.py:388
  3.7 1.6 %collective-permute-start = (bf16[128,128]{1,0:T(8,128)(2,1)}, bf16[128,128]{1,0:T(8,128)(2,1)S(1)}, u32[]{:S(2)}, u32[]{:S(2)}) collective-permute-start(bf16[128,128]{1,0:T(8,128)(2,1)} %sources_ref.1), channel_id=1, source_target_pairs={{0,4},{2,6},{4,0},{6,2},{8,12},{10,14},{12,8},{14,10},{1,5},{3,7},... | collective-permute-start | bytes 98312 | tf_op jit(solution)/shard_map/ppermute | solution.py:388
  5.3 2.5 %collective-permute-start.2 = (bf16[128,128]{1,0:T(8,128)(2,1)}, bf16[128,128]{1,0:T(8,128)(2,1)S(1)}, u32[]{:S(2)}, u32[]{:S(2)}) collective-permute-start(bf16[128,128]{1,0:T(8,128)(2,1)} %sources_ref.1), channel_id=1, source_target_pairs={{0,12},{2,14},{4,8},{6,10},{8,4},{10,6},{12,0},{14,2},{1,13},{3,15... | collective-permute-start | bytes 98312 | tf_op jit(solution)/shard_map/ppermute | solution.py:388
  7.9 1.0 %ready.1 = (bf16[128,128]{1,0:T(8,128)(2,1)S(1)}, bf16[544,128]{1,0:T(8,128)(2,1)S(1)}, f32[8,128]{1,0:T(8,128)S(1)}, f32[8,128]{1,0:T(8,128)S(1)}) custom-call(bf16[128,128]{1,0:T(8,128)(2,1)} %sources_ref.1, bf16[512,128]{1,0:T(8,128)(2,1)} %targets_ref.1, f32[8,128]{1,0:T(8,128)} %bitcast.31, f32[8,128]{1,0:T(8,128)S(1)} %bitcast.24), custom_call_target="tpu_custom_call" | custom-call | flops 1048576 | bytes 1048576 | tf_op jit(solution)/shard_map/ready/pallas_call | solution.py:95
  9.4 1.9 %collective-permute-done.2.block_ref = bf16[128,128]{1,0:T(8,128)(2,1)S(1)} collective-permute-done((bf16[128,128]{1,0:T(8,128)(2,1)}, bf16[128,128]{1,0:T(8,128)(2,1)S(1)}, u32[]{:S(2)}, u32[]{:S(2)}) %collective-permute-start.2) | collective-permute-done | bytes 32800 | tf_op jit(solution)/shard_map/ppermute | solution.py:388
  11.4 1.8 %collective-permute-done.1.refs_2_ = bf16[128,128]{1,0:T(8,128)(2,1)S(1)} collective-permute-done((bf16[128,128]{1,0:T(8,128)(2,1)}, bf16[128,128]{1,0:T(8,128)(2,1)S(1)}, u32[]{:S(2)}, u32[]{:S(2)}) %collective-permute-start.1) | collective-permute-done | bytes 32800 | tf_op jit(solution)/shard_map/ppermute | solution.py:388
  13.1 1.6 %collective-permute-start.6 = (bf16[512,128]{1,0:T(8,128)(2,1)S(1)}, bf16[512,128]{1,0:T(8,128)(2,1)S(1)}, u32[]{:S(2)}, u32[]{:S(2)}) collective-permute-start(bf16[512,128]{1,0:T(8,128)(2,1)S(1)} %pack.1.sources_ref.mine_ref), channel_id=1, source_target_pairs={{0,2},{2,0},{4,6},{6,4},{8,10},{10,8},{12,14},{14,12},{1,3},{3,1},... | collective-permute-start | bytes 393224 | tf_op jit(solution)/shard_map/ppermute | solution.py:388
  14.8 2.2 %first_rows.1 = (bf16[2048,128]{1,0:T(8,128)(2,1)S(1)}, bf16[2048,128]{1,0:T(8,128)(2,1)S(1)}, f32[16,128]{1,0:T(8,128)S(1)}, f32[4,128]{1,0:T(4,128)S(1)}) custom-call(s32[3]{0:T(128)S(1)} %pad_add_fusion.place_ref, f32[8,128]{1,0:T(8,128)S(1)} %get-tuple-element.32.mass_ref, bf16[512,128]{1,0:T(8,128)(2,1)S(1)} %pack.1.sources_ref.mine_ref, ...), custom_call_target="tpu_custom_call" | custom-call | flops 536870912 | bytes 1048576 | tf_op jit(solution)/shard_map/first_rows/pallas_call | solution.py:221
  16.9 1.2 %collective-permute-done.6.refs_0_ = bf16[512,128]{1,0:T(8,128)(2,1)S(1)} collective-permute-done((bf16[512,128]{1,0:T(8,128)(2,1)S(1)}, bf16[512,128]{1,0:T(8,128)(2,1)S(1)}, u32[]{:S(2)}, u32[]{:S(2)}) %collective-permute-start.6) | collective-permute-done | bytes 131104 | tf_op jit(solution)/shard_map/ppermute | solution.py:388
  18.2 1.8 %other_rows.1 = (f32[8,128]{1,0:T(8,128)S(1)}, bf16[1024,128]{1,0:T(8,128)(2,1)S(1)}) custom-call(s32[3]{0:T(128)S(1)} %pad_add_fusion.place_ref, bf16[2048,128]{1,0:T(8,128)(2,1)S(1)} %get-tuple-element.47.targets_ref, bf16[2048,128]{1,0:T(8,128)(2,1)S(1)} %get-tuple-element.36.offset_ref, f32[4,128]{1,0:T(4,128)S(1)} %get-tuple-element.37.first_ref, ...), custom_call_target="tpu_custom_call" | custom-call | tf_op jit(solution)/shard_map/other_rows/pallas_call | solution.py:260
  19.9 10.0 %all_to_all.15.parts_ref = f32[8,8,128]{2,1,0:T(8,128)S(1)} all-to-all(f32[8,8,128]{2,1,0:T(8,128)S(1)} %broadcast_in_dim.6), channel_id=1, replica_groups={{0,4,8,12,14,10,6,2},{1,5,9,13,15,11,7,3},{16,20,24,28,30,26,22,18},{17..., dimensions={0} | all-to-all | bytes 65536 | tf_op jit(solution)/shard_map/all_to_all | solution.py:404
  29.9 2.4 %first_columns.1 = (f32[2048,1024]{1,0:T(8,128)S(1)}, f32[2048,128]{1,0:T(8,128)S(1)}, f32[16,128]{1,0:T(8,128)S(1)}, f32[16,128]{1,0:T(8,128)S(1)}, f32[8,128]{1,0:T(8,128)S(1)}) custom-call(bf16[1024,128]{1,0:T(8,128)(2,1)S(1)} %get-tuple-element.46.sources_ref, bf16[2048,128]{1,0:T(8,128)(2,1)S(1)} %get-tuple-element.47.targets_ref, ...), custom_call_target="tpu_custom_call" | custom-call | tf_op jit(solution)/shard_map/first_columns/pallas_call | solution.py:304
  33.0 1.3 %collective-permute-start.7 = (f32[16,128]{1,0:T(8,128)S(1)}, f32[16,128]{1,0:T(8,128)S(1)}, u32[]{:S(2)}, u32[]{:S(2)}) collective-permute-start(f32[16,128]{1,0:T(8,128)S(1)} %get-tuple-element.49.refs_0_), channel_id=1, source_target_pairs={{0,1},{1,0},{16,17},{17,16},{2,3},{3,2},{18,19},{19,18},{4,5},{5,4... | collective-permute-start | bytes 24584 | tf_op jit(solution)/shard_map/ppermute | solution.py:388
  35.5 0.7 collective-permute-done.8.refs_2_
  36.2 0.7 %later_rows.2 = f32[8,128]{1,0:T(8,128)S(1)} custom-call(f32[2048,1024]{1,0:T(8,128)S(1)} %get-tuple-element.41.plan_ref, f32[2048,128]{1,0:T(8,128)S(1)} %get-tuple-element.42.reach_ref, f32[16,128]{1,0:T(8,128)S(1)} %get-tuple-element.43.top_ref, f32[16,128]{1,0:T(8,128)S(1)} %get-tuple-element.44.log_ref, f32[16,128]{1,0:T(8,128)S(1)} %get-tuple-element.49.refs_0_, ...), custom_call_target="tpu_custom_call" | custom-call | tf_op jit(solution)/shard_map/later_rows/pallas_call | solution.py:338
  36.9 9.1 %all_to_all.16.parts_ref = f32[8,8,128]{2,1,0:T(8,128)S(1)} all-to-all(f32[8,8,128]{2,1,0:T(8,128)S(1)} %broadcast_in_dim.7), channel_id=1, replica_groups={{0,4,8,12,14,10,6,2},{1,5,9,13,15,11,7,3},{16,20,24,28,30,26,22,18},{17..., dimensions={0} | all-to-all | bytes 65536 | tf_op jit(solution)/shard_map/all_to_all | solution.py:404
  46.0 0.7 %later_columns.2.refs_0_ = f32[16,128]{1,0:T(8,128)S(1)} custom-call(f32[2048,1024]{1,0:T(8,128)S(1)} %get-tuple-element.41.plan_ref, f32[2048,128]{1,0:T(8,128)S(1)} %get-tuple-element.42.reach_ref, f32[16,128]{1,0:T(8,128)S(1)} %get-tuple-element.43.top_ref, f32[8,8,128]{2,1,0:T(8,128)S(1)} %all_to_all.16.parts_ref, ...), custom_call_target="tpu_custom_call" | custom-call | tf_op jit(solution)/shard_map/later_columns/pallas_call | solution.py:367
  47.4 1.3 %collective-permute-start.10 = (f32[16,128]{1,0:T(8,128)S(1)}, f32[16,128]{1,0:T(8,128)S(1)}, u32[]{:S(2)}, u32[]{:S(2)}) collective-permute-start(f32[16,128]{1,0:T(8,128)S(1)} %later_columns.2.refs_0_), channel_id=1, source_target_pairs={{0,1},{1,0},{16,17},{17,16},{2,3},{3,2},{18,19},{19,18},{4,5},{5,4... | collective-permute-start | bytes 24584 | tf_op jit(solution)/shard_map/ppermute | solution.py:388
  48.7 1.2 %collective-permute-done.12.refs_3_ = f32[16,128]{1,0:T(8,128)S(1)} collective-permute-done((f32[16,128]{1,0:T(8,128)S(1)}, f32[16,128]{1,0:T(8,128)S(1)}, u32[]{:S(2)}, u32[]{:S(2)}) %collective-permute-start.12) | collective-permute-done | bytes 8224 | tf_op jit(solution)/shard_map/ppermute | solution.py:388
  50.6 0.7 %later_rows.3 = f32[8,128]{1,0:T(8,128)S(1)} custom-call(f32[2048,1024]{1,0:T(8,128)S(1)} %get-tuple-element.41.plan_ref, f32[2048,128]{1,0:T(8,128)S(1)} %get-tuple-element.42.reach_ref, f32[16,128]{1,0:T(8,128)S(1)} %get-tuple-element.43.top_ref, f32[16,128]{1,0:T(8,128)S(1)} %get-tuple-element.44.log_ref, f32[16,128]{1,0:T(8,128)S(1)} %later_columns.2.refs_0_, ...), custom_call_target="tpu_custom_call" | custom-call | tf_op jit(solution)/shard_map/later_rows/pallas_call | solution.py:338
  51.3 9.1 %all_to_all.17.parts_ref = f32[8,8,128]{2,1,0:T(8,128)S(1)} all-to-all(f32[8,8,128]{2,1,0:T(8,128)S(1)} %broadcast_in_dim.8), channel_id=1, replica_groups={{0,4,8,12,14,10,6,2},{1,5,9,13,15,11,7,3},{16,20,24,28,30,26,22,18},{17..., dimensions={0} | all-to-all | bytes 65536 | tf_op jit(solution)/shard_map/all_to_all | solution.py:404
  60.4 0.7 %later_columns.3 = (f32[16,128]{1,0:T(8,128)S(1)}, f32[8,128]{1,0:T(8,128)S(1)}) custom-call(f32[2048,1024]{1,0:T(8,128)S(1)} %get-tuple-element.41.plan_ref, f32[2048,128]{1,0:T(8,128)S(1)} %get-tuple-element.42.reach_ref, f32[16,128]{1,0:T(8,128)S(1)} %get-tuple-element.43.top_ref, f32[8,8,128]{2,1,0:T(8,128)S(1)} %all_to_all.17.parts_ref, ...), custom_call_target="tpu_custom_call" | custom-call | tf_op jit(solution)/shard_map/later_columns/pallas_call | solution.py:367
  61.9 1.5 %collective-permute-start.15 = (f32[16,128]{1,0:T(8,128)S(1)}, f32[16,128]{1,0:T(8,128)S(1)}, u32[]{:S(2)}, u32[]{:S(2)}) collective-permute-start(f32[16,128]{1,0:T(8,128)S(1)} %get-tuple-element.57), channel_id=1, source_target_pairs={{0,16},{1,17},{16,0},{17,1},{2,18},{3,19},{18,2},{19,3},{4,20},{5,... | collective-permute-start | bytes 24584 | tf_op jit(solution)/shard_map/ppermute | solution.py:388
  64.4 1.1 %collective-permute-done.15 = f32[16,128]{1,0:T(8,128)S(1)} collective-permute-done((f32[16,128]{1,0:T(8,128)S(1)}, f32[16,128]{1,0:T(8,128)S(1)}, u32[]{:S(2)}, u32[]{:S(2)}) %collective-permute-start.15) | collective-permute-done | bytes 8224 | tf_op jit(solution)/shard_map/ppermute | solution.py:388
  (41 shorter events, 6.3 us)
Async XLA Ops:
  0.6 7.2 %copy-start = (f32[2048]{0:T(1024)S(1)}, f32[2048]{0:T(1024)}, u32[]{:S(2)}) copy-start(f32[2048]{0:T(1024)} %param.6) | copy-start | bytes 24580
  0.6 8.3 %collective-permute-start.4 = (bf16[512,128]{1,0:T(8,128)(2,1)}, bf16[512,128]{1,0:T(8,128)(2,1)S(1)}, u32[]{:S(2)}, u32[]{:S(2)}) collective-permute-start(bf16[512,128]{1,0:T(8,128)(2,1)} %targets_ref.1), channel_id=1, source_target_pairs={{0,16},{16,0},{1,17},{17,1},{2,18},{18,2},{3,19},{19,3},{4,20},{20... | collective-permute-start | bytes 393224 | tf_op jit(solution)/shard_map/ppermute | solution.py:388
  3.7 7.7 %collective-permute-start = (bf16[128,128]{1,0:T(8,128)(2,1)}, bf16[128,128]{1,0:T(8,128)(2,1)S(1)}, u32[]{:S(2)}, u32[]{:S(2)}) collective-permute-start(bf16[128,128]{1,0:T(8,128)(2,1)} %sources_ref.1), channel_id=1, source_target_pairs={{0,4},{2,6},{4,0},{6,2},{8,12},{10,14},{12,8},{14,10},{1,5},{3,7},... | collective-permute-start | bytes 98312 | tf_op jit(solution)/shard_map/ppermute | solution.py:388
  5.3 6.1 %collective-permute-start.2 = (bf16[128,128]{1,0:T(8,128)(2,1)}, bf16[128,128]{1,0:T(8,128)(2,1)S(1)}, u32[]{:S(2)}, u32[]{:S(2)}) collective-permute-start(bf16[128,128]{1,0:T(8,128)(2,1)} %sources_ref.1), channel_id=1, source_target_pairs={{0,12},{2,14},{4,8},{6,10},{8,4},{10,6},{12,0},{14,2},{1,13},{3,15... | collective-permute-start | bytes 98312 | tf_op jit(solution)/shard_map/ppermute | solution.py:388
  7.7 5.4 %collective-permute-start.1 = (bf16[128,128]{1,0:T(8,128)(2,1)}, bf16[128,128]{1,0:T(8,128)(2,1)S(1)}, u32[]{:S(2)}, u32[]{:S(2)}) collective-permute-start(bf16[128,128]{1,0:T(8,128)(2,1)} %sources_ref.1), channel_id=1, source_target_pairs={{0,8},{2,10},{4,12},{6,14},{8,0},{10,2},{12,4},{14,6},{1,9},{3,11}... | collective-permute-start | bytes 98312 | tf_op jit(solution)/shard_map/ppermute | solution.py:388
  8.8 5.9 %collective-permute-start.3 = (bf16[544,128]{1,0:T(8,128)(2,1)S(1)}, bf16[544,128]{1,0:T(8,128)(2,1)S(1)}, u32[]{:S(2)}, u32[]{:S(2)}) collective-permute-start(bf16[544,128]{1,0:T(8,128)(2,1)S(1)} %get-tuple-element.34.refs_0_), channel_id=1, source_target_pairs={{0,1},{1,0},{2,3},{3,2},{4,5},{5,4},{6,7},{7,6},{8,9},{9,8},{10,11... | collective-permute-start | bytes 417800 | tf_op jit(solution)/shard_map/ppermute | solution.py:388
  8.9 5.8 %collective-permute-start.5 = (bf16[512,128]{1,0:T(8,128)(2,1)S(1)}, bf16[512,128]{1,0:T(8,128)(2,1)S(1)}, u32[]{:S(2)}, u32[]{:S(2)}) collective-permute-start(bf16[512,128]{1,0:T(8,128)(2,1)S(1)} %collective-permute-done.4.refs_2_), channel_id=1, source_target_pairs={{0,1},{1,0},{2,3},{3,2},{4,5},{5,4},{6,7},{7,6},{8,9},{9,8},{10,11... | collective-permute-start | bytes 393224 | tf_op jit(solution)/shard_map/ppermute | solution.py:388
  13.1 5.0 %collective-permute-start.6 = (bf16[512,128]{1,0:T(8,128)(2,1)S(1)}, bf16[512,128]{1,0:T(8,128)(2,1)S(1)}, u32[]{:S(2)}, u32[]{:S(2)}) collective-permute-start(bf16[512,128]{1,0:T(8,128)(2,1)S(1)} %pack.1.sources_ref.mine_ref), channel_id=1, source_target_pairs={{0,2},{2,0},{4,6},{6,4},{8,10},{10,8},{12,14},{14,12},{1,3},{3,1},... | collective-permute-start | bytes 393224 | tf_op jit(solution)/shard_map/ppermute | solution.py:388
  32.4 3.1 %collective-permute-start.9 = (f32[16,128]{1,0:T(8,128)S(1)}, f32[16,128]{1,0:T(8,128)S(1)}, u32[]{:S(2)}, u32[]{:S(2)}) collective-permute-start(f32[16,128]{1,0:T(8,128)S(1)} %get-tuple-element.49.refs_0_), channel_id=1, source_target_pairs={{0,17},{1,16},{16,1},{17,0},{2,19},{3,18},{18,3},{19,2},{4,21},{5,... | collective-permute-start | bytes 24584 | tf_op jit(solution)/shard_map/ppermute | solution.py:388
  32.4 3.7 %collective-permute-start.8 = (f32[16,128]{1,0:T(8,128)S(1)}, f32[16,128]{1,0:T(8,128)S(1)}, u32[]{:S(2)}, u32[]{:S(2)}) collective-permute-start(f32[16,128]{1,0:T(8,128)S(1)} %get-tuple-element.49.refs_0_), channel_id=1, source_target_pairs={{0,16},{1,17},{16,0},{17,1},{2,18},{3,19},{18,2},{19,3},{4,20},{5,... | collective-permute-start | bytes 24584 | tf_op jit(solution)/shard_map/ppermute | solution.py:388
  33.0 3.1 %collective-permute-start.7 = (f32[16,128]{1,0:T(8,128)S(1)}, f32[16,128]{1,0:T(8,128)S(1)}, u32[]{:S(2)}, u32[]{:S(2)}) collective-permute-start(f32[16,128]{1,0:T(8,128)S(1)} %get-tuple-element.49.refs_0_), channel_id=1, source_target_pairs={{0,1},{1,0},{16,17},{17,16},{2,3},{3,2},{18,19},{19,18},{4,5},{5,4... | collective-permute-start | bytes 24584 | tf_op jit(solution)/shard_map/ppermute | solution.py:388
  46.8 3.1 %collective-permute-start.12 = (f32[16,128]{1,0:T(8,128)S(1)}, f32[16,128]{1,0:T(8,128)S(1)}, u32[]{:S(2)}, u32[]{:S(2)}) collective-permute-start(f32[16,128]{1,0:T(8,128)S(1)} %later_columns.2.refs_0_), channel_id=1, source_target_pairs={{0,17},{1,16},{16,1},{17,0},{2,19},{3,18},{18,3},{19,2},{4,21},{5,... | collective-permute-start | bytes 24584 | tf_op jit(solution)/shard_map/ppermute | solution.py:388
  46.8 3.7 %collective-permute-start.11 = (f32[16,128]{1,0:T(8,128)S(1)}, f32[16,128]{1,0:T(8,128)S(1)}, u32[]{:S(2)}, u32[]{:S(2)}) collective-permute-start(f32[16,128]{1,0:T(8,128)S(1)} %later_columns.2.refs_0_), channel_id=1, source_target_pairs={{0,16},{1,17},{16,0},{17,1},{2,18},{3,19},{18,2},{19,3},{4,20},{5,... | collective-permute-start | bytes 24584 | tf_op jit(solution)/shard_map/ppermute | solution.py:388
  47.4 3.1 %collective-permute-start.10 = (f32[16,128]{1,0:T(8,128)S(1)}, f32[16,128]{1,0:T(8,128)S(1)}, u32[]{:S(2)}, u32[]{:S(2)}) collective-permute-start(f32[16,128]{1,0:T(8,128)S(1)} %later_columns.2.refs_0_), channel_id=1, source_target_pairs={{0,1},{1,0},{16,17},{17,16},{2,3},{3,2},{18,19},{19,18},{4,5},{5,4... | collective-permute-start | bytes 24584 | tf_op jit(solution)/shard_map/ppermute | solution.py:388
  61.2 2.2 %collective-permute-start.13 = (f32[2,4,128]{2,0,1:T(2,128)S(1)}, f32[2,4,128]{2,0,1:T(2,128)S(1)}, u32[]{:S(2)}, u32[]{:S(2)}) collective-permute-start(f32[2,4,128]{2,0,1:T(2,128)S(1)} %copy.13), channel_id=1, source_target_pairs={{0,1},{1,0},{2,3},{3,2},{4,5},{5,4},{6,7},{7,6},{8,9},{9,8},{10,11... | collective-permute-start | bytes 12296 | tf_op jit(solution)/shard_map/ppermute | solution.py:388
  61.3 3.1 %collective-permute-start.16 = (f32[16,128]{1,0:T(8,128)S(1)}, f32[16,128]{1,0:T(8,128)S(1)}, u32[]{:S(2)}, u32[]{:S(2)}) collective-permute-start(f32[16,128]{1,0:T(8,128)S(1)} %get-tuple-element.57), channel_id=1, source_target_pairs={{0,17},{1,16},{16,1},{17,0},{2,19},{3,18},{18,3},{19,2},{4,21},{5,... | collective-permute-start | bytes 24584 | tf_op jit(solution)/shard_map/ppermute | solution.py:388
  61.9 3.7 %collective-permute-start.15 = (f32[16,128]{1,0:T(8,128)S(1)}, f32[16,128]{1,0:T(8,128)S(1)}, u32[]{:S(2)}, u32[]{:S(2)}) collective-permute-start(f32[16,128]{1,0:T(8,128)S(1)} %get-tuple-element.57), channel_id=1, source_target_pairs={{0,16},{1,17},{16,0},{17,1},{2,18},{3,19},{18,2},{19,3},{4,20},{5,... | collective-permute-start | bytes 24584 | tf_op jit(solution)/shard_map/ppermute | solution.py:388
  63.4 2.1 %collective-permute-start.14 = (f32[16,128]{1,0:T(8,128)S(1)}, f32[16,128]{1,0:T(8,128)S(1)}, u32[]{:S(2)}, u32[]{:S(2)}) collective-permute-start(f32[16,128]{1,0:T(8,128)S(1)} %get-tuple-element.57), channel_id=1, source_target_pairs={{0,1},{1,0},{16,17},{17,16},{2,3},{3,2},{18,19},{19,18},{4,5},{5,4... | collective-permute-start | bytes 24584 | tf_op jit(solution)/shard_map/ppermute | solution.py:388

commit v15 on v10

--- a/solution.py
+++ b/solution.py
@@ -351,7 +351,7 @@
     def kernel(plan_ref, reach_ref, top_ref, parts_ref, log_ref, lse_ref, half_ref, out_ref, *potential_refs):
         factor = log_ref[...] - jnp.log2(tree([parts_ref[i] for i in range(parts.shape[0])], jnp.add))
         for ref in potential_refs:
-            ref[...] = half_ref[...] + UNIT * (factor - lse_ref[...])
+            ref[width // LANES :, :] = half_ref[...] + UNIT * (factor - lse_ref[...])
         factor = unfold(jnp.exp2(factor))
         factors = [factor[:, lane : lane + LANES] for lane in range(0, count, LANES)]
         for at in range(0, width, LANES):
@@ -362,11 +362,12 @@
             total = jnp.concatenate(totals, axis=0) * reach_ref[at : at + LANES, :]
             index = at // LANES
             total = jnp.log2(jnp.sum(total.T, axis=0, keepdims=True))
-            out_ref[index : index + 1, :] = top_ref[index : index + 1, :] + total
-
-    return pl.pallas_call(
-        kernel,
-        out_shape=(rows_of(width),) + (rows_of(count),) * last,
+            for ref in (out_ref, *potential_refs):
+                ref[index : index + 1, :] = top_ref[index : index + 1, :] + total
+
+    return pl.pallas_call(
+        kernel,
+        out_shape=(rows_of(width),) + (rows_of(width + count),) * last,
         in_specs=[VMEM] * 7,
         out_specs=(VMEM,) * (1 + last),
         compiler_params=params(),
@@ -399,6 +400,14 @@
 def share(value, size):
     copies = jnp.broadcast_to(value[None], (size,) + value.shape)
     return lax.all_to_all(copies, ("z", "x"), 0, 0, tiled=True)
+
+
+def swap_far(value, pair, axes, size):
+    levels = levels_of(size)
+    if len(levels) == 1:
+        return pair + [swap(value, axes, size, d) for d in levels[0][1:]]
+    values = swap_all(value, axes, size)
+    return pair + values[2:]
 
 
 def half_norm(points):
@@ -434,11 +443,17 @@
         half_x, half_y, *parts = lax.optimization_barrier((half_x, half_y, *parts))
         for step in range(1, ITERS):
             rows = later_rows(plan, reach, top, b, parts)
-            own, *potential = later_columns(plan, reach, top, share(rows, n_far), a, row_lse, half_x, step == ITERS - 1)
-            parts = swap_all(own, near, n_near)
-        mine, other = swap_all(potential[0].reshape(n_x, n_z, part), "core", CORES)
+            own, *joint = later_columns(plan, reach, top, share(rows, n_far), a, row_lse, half_x, step == ITERS - 1)
+            if step < ITERS - 1:
+                parts = swap_all(own, near, n_near)
+        rows = own.shape[0]
+        joint = [joint[0], swap(joint[0], near, n_near, 1)]
+        mine, other = [value[rows:].reshape(n_x, n_z, part) for value in joint]
+        pair = [value[:rows] for value in joint]
+        parts = swap_far(own, pair, near, n_near)
         first, second = jnp.where(core == 0, mine, other), jnp.where(core == 0, other, mine)
         source_potential = jnp.stack([first, second], axis=2).swapaxes(0, 1).reshape(-1)
+        source_potential, *parts = lax.optimization_barrier((source_potential, *parts))
         target_potential = half_y - UNIT * log_sum(parts)
         target_potential = target_potential.reshape(CORES, -1)
         target_potential = lax.dynamic_index_in_dim(target_potential, core, axis=0, keepdims=False)

time: 66.3 us -> 66.3 us (level)
    ppermute x17 -> x16, waiting for transfers between devices: 9.57 us -> 9.55 us  [swap(): return lax.ppermute(value, axes, [(i, i ^ distance) for i in range(size)])]
    ppermute x17 -> x16, starting transfers between devices: 15.4 us -> 15.4 us  [swap(): return lax.ppermute(value, axes, [(i, i ^ distance) for i in range(size)])]
  transfers between devices with their start and end apart: 17 -> 16, of which waited for: 9 -> 9; matrix products, arithmetic and copies ran while one was open for 2% -> 2% of each run, Pallas kernels for 5% -> 5%
where the time goes in v15:
time: 66.3 us; the launch traced here: 66 us
  blocking collectives  28.1 us (42%)
  starting transfers between devices  15.4 us (23%)
  Pallas kernels  10.3 us (16%)
  waiting for transfers between devices  9.55 us (14%)
  other arithmetic  1.27 us (2%)
  between operations  0.83 us (1%)
  local copies, waits for them, and re-layouts  0.67 us (1%)
    all_to_all x3, blocking collectives, share(): return lax.all_to_all(copies, ('z', 'x'), 0, 0, tiled=True)  28.1 us
    ppermute x16, starting transfers between devices, swap(): return lax.ppermute(value, axes, [(i, i ^ distance) for i in range(size)])  15.4 us
    ppermute x16, waiting for transfers between devices, swap(): return lax.ppermute(value, axes, [(i, i ^ distance) for i in range(size)])  9.55 us
    pallas_call x1, Pallas kernels, first_columns(): pl.pallas_call(kernel, out_shape=(pltpu.VMEM((width, count), F32), pltpu....  2.44 us
    pallas_call x1, Pallas kernels, first_rows(): pl.pallas_call(kernel, out_shape=(pltpu.VMEM((width, LANES), jnp.bfloat16...  2.18 us
    pallas_call x1, Pallas kernels, other_rows(): pl.pallas_call(kernel, out_shape=(rows_of(count + each * LANES), pltpu.VM...  1.77 us
    pallas_call x2, Pallas kernels, later_rows(): pl.pallas_call(kernel, out_shape=rows_of(count), in_specs=[VMEM] * (4 + l...  1.47 us
    pallas_call x2, Pallas kernels, later_columns(): pl.pallas_call(kernel, out_shape=(rows_of(width),) + (rows_of(width + cou...  1.47 us
  transfers between devices with their start and end apart: 16, of which 9 were waited for; matrix products, arithmetic and copies ran while one was open for 2% of the time, Pallas kernels for 5%

profile of v15, /device:TPU:0, one launch (start us, length us, event | category | flops | bytes accessed | tf_op | source)
XLA Modules:
  0.0 66.0 jit_solution(5436262600912103896)
XLA Ops:
  0.6 3.0 %collective-permute-start.4 = (bf16[512,128]{1,0:T(8,128)(2,1)}, bf16[512,128]{1,0:T(8,128)(2,1)S(1)}, u32[]{:S(2)}, u32[]{:S(2)}) collective-permute-start(bf16[512,128]{1,0:T(8,128)(2,1)} %targets_ref.1), channel_id=1, source_target_pairs={{0,16},{16,0},{1,17},{17,1},{2,18},{18,2},{3,19},{19,3},{4,20},{20... | collective-permute-start | bytes 393224 | tf_op jit(solution)/shard_map/ppermute | solution.py:389
  3.7 1.6 %collective-permute-start = (bf16[128,128]{1,0:T(8,128)(2,1)}, bf16[128,128]{1,0:T(8,128)(2,1)S(1)}, u32[]{:S(2)}, u32[]{:S(2)}) collective-permute-start(bf16[128,128]{1,0:T(8,128)(2,1)} %sources_ref.1), channel_id=1, source_target_pairs={{0,4},{4,0},{8,12},{12,8},{1,5},{5,1},{9,13},{13,9},{2,6},{6,2},{1... | collective-permute-start | bytes 98312 | tf_op jit(solution)/shard_map/ppermute | solution.py:389
  5.3 2.5 %collective-permute-start.2 = (bf16[128,128]{1,0:T(8,128)(2,1)}, bf16[128,128]{1,0:T(8,128)(2,1)S(1)}, u32[]{:S(2)}, u32[]{:S(2)}) collective-permute-start(bf16[128,128]{1,0:T(8,128)(2,1)} %sources_ref.1), channel_id=1, source_target_pairs={{0,12},{4,8},{8,4},{12,0},{1,13},{5,9},{9,5},{13,1},{2,14},{6,10},... | collective-permute-start | bytes 98312 | tf_op jit(solution)/shard_map/ppermute | solution.py:389
  7.9 1.0 %ready.1 = (bf16[128,128]{1,0:T(8,128)(2,1)S(1)}, bf16[544,128]{1,0:T(8,128)(2,1)S(1)}, f32[8,128]{1,0:T(8,128)S(1)}, f32[8,128]{1,0:T(8,128)S(1)}) custom-call(bf16[128,128]{1,0:T(8,128)(2,1)} %sources_ref.1, bf16[512,128]{1,0:T(8,128)(2,1)} %targets_ref.1, f32[8,128]{1,0:T(8,128)} %bitcast.26, f32[8,128]{1,0:T(8,128)S(1)} %bitcast.21), custom_call_target="tpu_custom_call" | custom-call | flops 1048576 | bytes 1048576 | tf_op jit(solution)/shard_map/ready/pallas_call | solution.py:95
  9.4 1.9 %collective-permute-done.2.block_ref = bf16[128,128]{1,0:T(8,128)(2,1)S(1)} collective-permute-done((bf16[128,128]{1,0:T(8,128)(2,1)}, bf16[128,128]{1,0:T(8,128)(2,1)S(1)}, u32[]{:S(2)}, u32[]{:S(2)}) %collective-permute-start.2) | collective-permute-done | bytes 32800 | tf_op jit(solution)/shard_map/ppermute | solution.py:389
  11.4 1.8 %collective-permute-done.1.refs_2_ = bf16[128,128]{1,0:T(8,128)(2,1)S(1)} collective-permute-done((bf16[128,128]{1,0:T(8,128)(2,1)}, bf16[128,128]{1,0:T(8,128)(2,1)S(1)}, u32[]{:S(2)}, u32[]{:S(2)}) %collective-permute-start.1) | collective-permute-done | bytes 32800 | tf_op jit(solution)/shard_map/ppermute | solution.py:389
  13.1 1.6 %collective-permute-start.6 = (bf16[512,128]{1,0:T(8,128)(2,1)S(1)}, bf16[512,128]{1,0:T(8,128)(2,1)S(1)}, u32[]{:S(2)}, u32[]{:S(2)}) collective-permute-start(bf16[512,128]{1,0:T(8,128)(2,1)S(1)} %pack.1.sources_ref.mine_ref), channel_id=1, source_target_pairs={{0,2},{2,0},{1,3},{3,1},{4,6},{6,4},{5,7},{7,5},{8,10},{10,8},{9,1... | collective-permute-start | bytes 393224 | tf_op jit(solution)/shard_map/ppermute | solution.py:389
  14.8 2.2 %first_rows.1 = (bf16[2048,128]{1,0:T(8,128)(2,1)S(1)}, bf16[2048,128]{1,0:T(8,128)(2,1)S(1)}, f32[16,128]{1,0:T(8,128)S(1)}, f32[4,128]{1,0:T(4,128)S(1)}) custom-call(s32[3]{0:T(128)S(1)} %pad_add_fusion.place_ref, f32[8,128]{1,0:T(8,128)S(1)} %get-tuple-element.37.mass_ref, bf16[512,128]{1,0:T(8,128)(2,1)S(1)} %pack.1.sources_ref.mine_ref, ...), custom_call_target="tpu_custom_call" | custom-call | flops 536870912 | bytes 1048576 | tf_op jit(solution)/shard_map/first_rows/pallas_call | solution.py:221
  16.9 1.2 %collective-permute-done.6.refs_0_ = bf16[512,128]{1,0:T(8,128)(2,1)S(1)} collective-permute-done((bf16[512,128]{1,0:T(8,128)(2,1)S(1)}, bf16[512,128]{1,0:T(8,128)(2,1)S(1)}, u32[]{:S(2)}, u32[]{:S(2)}) %collective-permute-start.6) | collective-permute-done | bytes 131104 | tf_op jit(solution)/shard_map/ppermute | solution.py:389
  18.2 1.8 %other_rows.1 = (f32[8,128]{1,0:T(8,128)S(1)}, bf16[1024,128]{1,0:T(8,128)(2,1)S(1)}) custom-call(s32[3]{0:T(128)S(1)} %pad_add_fusion.place_ref, bf16[2048,128]{1,0:T(8,128)(2,1)S(1)} %get-tuple-element.52.targets_ref, bf16[2048,128]{1,0:T(8,128)(2,1)S(1)} %get-tuple-element.41.offset_ref, f32[4,128]{1,0:T(4,128)S(1)} %get-tuple-element.42.first_ref, ...), custom_call_target="tpu_custom_call" | custom-call | tf_op jit(solution)/shard_map/other_rows/pallas_call | solution.py:260
  19.9 9.9 %all_to_all.15.parts_ref = f32[8,8,128]{2,1,0:T(8,128)S(1)} all-to-all(f32[8,8,128]{2,1,0:T(8,128)S(1)} %broadcast_in_dim.6), channel_id=1, replica_groups=mesh['src'=2,'z'=4,'x'=2,'core'=2] {'z','x'}, dimensions={0} | all-to-all | bytes 65536 | tf_op jit(solution)/shard_map/all_to_all | solution.py:402
  29.9 2.4 %first_columns.1 = (f32[2048,1024]{1,0:T(8,128)S(1)}, f32[2048,128]{1,0:T(8,128)S(1)}, f32[16,128]{1,0:T(8,128)S(1)}, f32[16,128]{1,0:T(8,128)S(1)}, f32[8,128]{1,0:T(8,128)S(1)}) custom-call(bf16[1024,128]{1,0:T(8,128)(2,1)S(1)} %get-tuple-element.51.sources_ref, bf16[2048,128]{1,0:T(8,128)(2,1)S(1)} %get-tuple-element.52.targets_ref, ...), custom_call_target="tpu_custom_call" | custom-call | tf_op jit(solution)/shard_map/first_columns/pallas_call | solution.py:304
  33.0 1.3 %collective-permute-start.7 = (f32[16,128]{1,0:T(8,128)S(1)}, f32[16,128]{1,0:T(8,128)S(1)}, u32[]{:S(2)}, u32[]{:S(2)}) collective-permute-start(f32[16,128]{1,0:T(8,128)S(1)} %get-tuple-element.54.refs_0_), channel_id=1, source_target_pairs={{0,1},{1,0},{16,17},{17,16},{2,3},{3,2},{18,19},{19,18},{4,5},{5,4... | collective-permute-start | bytes 24584 | tf_op jit(solution)/shard_map/ppermute | solution.py:389
  35.5 0.7 collective-permute-done.8.refs_2_
  36.1 0.7 %later_rows.2 = f32[8,128]{1,0:T(8,128)S(1)} custom-call(f32[2048,1024]{1,0:T(8,128)S(1)} %get-tuple-element.46.plan_ref, f32[2048,128]{1,0:T(8,128)S(1)} %get-tuple-element.47.reach_ref, f32[16,128]{1,0:T(8,128)S(1)} %get-tuple-element.48.top_ref, f32[16,128]{1,0:T(8,128)S(1)} %get-tuple-element.49.log_ref, f32[16,128]{1,0:T(8,128)S(1)} %get-tuple-element.54.refs_0_, ...), custom_call_target="tpu_custom_call" | custom-call | tf_op jit(solution)/shard_map/later_rows/pallas_call | solution.py:338
  36.9 9.1 %all_to_all.16.parts_ref = f32[8,8,128]{2,1,0:T(8,128)S(1)} all-to-all(f32[8,8,128]{2,1,0:T(8,128)S(1)} %broadcast_in_dim.7), channel_id=1, replica_groups=mesh['src'=2,'z'=4,'x'=2,'core'=2] {'z','x'}, dimensions={0} | all-to-all | bytes 65536 | tf_op jit(solution)/shard_map/all_to_all | solution.py:402
  45.9 0.7 %later_columns.2.refs_0_ = f32[16,128]{1,0:T(8,128)S(1)} custom-call(f32[2048,1024]{1,0:T(8,128)S(1)} %get-tuple-element.46.plan_ref, f32[2048,128]{1,0:T(8,128)S(1)} %get-tuple-element.47.reach_ref, f32[16,128]{1,0:T(8,128)S(1)} %get-tuple-element.48.top_ref, f32[8,8,128]{2,1,0:T(8,128)S(1)} %all_to_all.16.parts_ref, ...), custom_call_target="tpu_custom_call" | custom-call | tf_op jit(solution)/shard_map/later_columns/pallas_call | solution.py:368
  47.3 1.3 %collective-permute-start.10 = (f32[16,128]{1,0:T(8,128)S(1)}, f32[16,128]{1,0:T(8,128)S(1)}, u32[]{:S(2)}, u32[]{:S(2)}) collective-permute-start(f32[16,128]{1,0:T(8,128)S(1)} %later_columns.2.refs_0_), channel_id=1, source_target_pairs={{0,1},{1,0},{16,17},{17,16},{2,3},{3,2},{18,19},{19,18},{4,5},{5,4... | collective-permute-start | bytes 24584 | tf_op jit(solution)/shard_map/ppermute | solution.py:389
  48.6 1.2 %collective-permute-done.12.refs_3_ = f32[16,128]{1,0:T(8,128)S(1)} collective-permute-done((f32[16,128]{1,0:T(8,128)S(1)}, f32[16,128]{1,0:T(8,128)S(1)}, u32[]{:S(2)}, u32[]{:S(2)}) %collective-permute-start.12) | collective-permute-done | bytes 8224 | tf_op jit(solution)/shard_map/ppermute | solution.py:389
  50.5 0.7 %later_rows.3 = f32[8,128]{1,0:T(8,128)S(1)} custom-call(f32[2048,1024]{1,0:T(8,128)S(1)} %get-tuple-element.46.plan_ref, f32[2048,128]{1,0:T(8,128)S(1)} %get-tuple-element.47.reach_ref, f32[16,128]{1,0:T(8,128)S(1)} %get-tuple-element.48.top_ref, f32[16,128]{1,0:T(8,128)S(1)} %get-tuple-element.49.log_ref, f32[16,128]{1,0:T(8,128)S(1)} %later_columns.2.refs_0_, ...), custom_call_target="tpu_custom_call" | custom-call | tf_op jit(solution)/shard_map/later_rows/pallas_call | solution.py:338
  51.2 9.1 %all_to_all.17.parts_ref = f32[8,8,128]{2,1,0:T(8,128)S(1)} all-to-all(f32[8,8,128]{2,1,0:T(8,128)S(1)} %broadcast_in_dim.8), channel_id=1, replica_groups=mesh['src'=2,'z'=4,'x'=2,'core'=2] {'z','x'}, dimensions={0} | all-to-all | bytes 65536 | tf_op jit(solution)/shard_map/all_to_all | solution.py:402
  60.3 0.7 %later_columns.3 = (f32[16,128]{1,0:T(8,128)S(1)}, f32[24,128]{1,0:T(8,128)S(1)}) custom-call(f32[2048,1024]{1,0:T(8,128)S(1)} %get-tuple-element.46.plan_ref, f32[2048,128]{1,0:T(8,128)S(1)} %get-tuple-element.47.reach_ref, f32[16,128]{1,0:T(8,128)S(1)} %get-tuple-element.48.top_ref, f32[8,8,128]{2,1,0:T(8,128)S(1)} %all_to_all.17.parts_ref, ...), custom_call_target="tpu_custom_call" | custom-call | tf_op jit(solution)/shard_map/later_columns/pallas_call | solution.py:368
  61.7 1.5 %collective-permute-start.14 = (f32[16,128]{1,0:T(8,128)S(1)}, f32[16,128]{1,0:T(8,128)S(1)}, u32[]{:S(2)}, u32[]{:S(2)}) collective-permute-start(f32[16,128]{1,0:T(8,128)S(1)} %get-tuple-element.61), channel_id=1, source_target_pairs={{0,16},{1,17},{16,0},{17,1},{2,18},{3,19},{18,2},{19,3},{4,20},{5,... | collective-permute-start | bytes 24584 | tf_op jit(solution)/shard_map/ppermute | solution.py:389
  64.3 1.1 %collective-permute-done.14 = f32[16,128]{1,0:T(8,128)S(1)} collective-permute-done((f32[16,128]{1,0:T(8,128)S(1)}, f32[16,128]{1,0:T(8,128)S(1)}, u32[]{:S(2)}, u32[]{:S(2)}) %collective-permute-start.14) | collective-permute-done | bytes 8224 | tf_op jit(solution)/shard_map/ppermute | solution.py:389
  (42 shorter events, 6.3 us)
Async XLA Ops:
  0.6 7.2 %copy-start = (f32[2048]{0:T(1024)S(1)}, f32[2048]{0:T(1024)}, u32[]{:S(2)}) copy-start(f32[2048]{0:T(1024)} %param.6) | copy-start | bytes 24580
  0.6 8.3 %collective-permute-start.4 = (bf16[512,128]{1,0:T(8,128)(2,1)}, bf16[512,128]{1,0:T(8,128)(2,1)S(1)}, u32[]{:S(2)}, u32[]{:S(2)}) collective-permute-start(bf16[512,128]{1,0:T(8,128)(2,1)} %targets_ref.1), channel_id=1, source_target_pairs={{0,16},{16,0},{1,17},{17,1},{2,18},{18,2},{3,19},{19,3},{4,20},{20... | collective-permute-start | bytes 393224 | tf_op jit(solution)/shard_map/ppermute | solution.py:389
  3.7 7.7 %collective-permute-start = (bf16[128,128]{1,0:T(8,128)(2,1)}, bf16[128,128]{1,0:T(8,128)(2,1)S(1)}, u32[]{:S(2)}, u32[]{:S(2)}) collective-permute-start(bf16[128,128]{1,0:T(8,128)(2,1)} %sources_ref.1), channel_id=1, source_target_pairs={{0,4},{4,0},{8,12},{12,8},{1,5},{5,1},{9,13},{13,9},{2,6},{6,2},{1... | collective-permute-start | bytes 98312 | tf_op jit(solution)/shard_map/ppermute | solution.py:389
  5.3 6.1 %collective-permute-start.2 = (bf16[128,128]{1,0:T(8,128)(2,1)}, bf16[128,128]{1,0:T(8,128)(2,1)S(1)}, u32[]{:S(2)}, u32[]{:S(2)}) collective-permute-start(bf16[128,128]{1,0:T(8,128)(2,1)} %sources_ref.1), channel_id=1, source_target_pairs={{0,12},{4,8},{8,4},{12,0},{1,13},{5,9},{9,5},{13,1},{2,14},{6,10},... | collective-permute-start | bytes 98312 | tf_op jit(solution)/shard_map/ppermute | solution.py:389
  7.7 5.4 %collective-permute-start.1 = (bf16[128,128]{1,0:T(8,128)(2,1)}, bf16[128,128]{1,0:T(8,128)(2,1)S(1)}, u32[]{:S(2)}, u32[]{:S(2)}) collective-permute-start(bf16[128,128]{1,0:T(8,128)(2,1)} %sources_ref.1), channel_id=1, source_target_pairs={{0,8},{4,12},{8,0},{12,4},{1,9},{5,13},{9,1},{13,5},{2,10},{6,14},... | collective-permute-start | bytes 98312 | tf_op jit(solution)/shard_map/ppermute | solution.py:389
  8.8 5.9 %collective-permute-start.3 = (bf16[544,128]{1,0:T(8,128)(2,1)S(1)}, bf16[544,128]{1,0:T(8,128)(2,1)S(1)}, u32[]{:S(2)}, u32[]{:S(2)}) collective-permute-start(bf16[544,128]{1,0:T(8,128)(2,1)S(1)} %get-tuple-element.39.refs_0_), channel_id=1, source_target_pairs={{0,1},{1,0},{2,3},{3,2},{4,5},{5,4},{6,7},{7,6},{8,9},{9,8},{10,11... | collective-permute-start | bytes 417800 | tf_op jit(solution)/shard_map/ppermute | solution.py:389
  8.9 5.8 %collective-permute-start.5 = (bf16[512,128]{1,0:T(8,128)(2,1)S(1)}, bf16[512,128]{1,0:T(8,128)(2,1)S(1)}, u32[]{:S(2)}, u32[]{:S(2)}) collective-permute-start(bf16[512,128]{1,0:T(8,128)(2,1)S(1)} %collective-permute-done.4.refs_2_), channel_id=1, source_target_pairs={{0,1},{1,0},{2,3},{3,2},{4,5},{5,4},{6,7},{7,6},{8,9},{9,8},{10,11... | collective-permute-start | bytes 393224 | tf_op jit(solution)/shard_map/ppermute | solution.py:389
  13.1 5.0 %collective-permute-start.6 = (bf16[512,128]{1,0:T(8,128)(2,1)S(1)}, bf16[512,128]{1,0:T(8,128)(2,1)S(1)}, u32[]{:S(2)}, u32[]{:S(2)}) collective-permute-start(bf16[512,128]{1,0:T(8,128)(2,1)S(1)} %pack.1.sources_ref.mine_ref), channel_id=1, source_target_pairs={{0,2},{2,0},{1,3},{3,1},{4,6},{6,4},{5,7},{7,5},{8,10},{10,8},{9,1... | collective-permute-start | bytes 393224 | tf_op jit(solution)/shard_map/ppermute | solution.py:389
  32.3 3.1 %collective-permute-start.9 = (f32[16,128]{1,0:T(8,128)S(1)}, f32[16,128]{1,0:T(8,128)S(1)}, u32[]{:S(2)}, u32[]{:S(2)}) collective-permute-start(f32[16,128]{1,0:T(8,128)S(1)} %get-tuple-element.54.refs_0_), channel_id=1, source_target_pairs={{0,17},{1,16},{16,1},{17,0},{2,19},{3,18},{18,3},{19,2},{4,21},{5,... | collective-permute-start | bytes 24584 | tf_op jit(solution)/shard_map/ppermute | solution.py:389
  32.4 3.7 %collective-permute-start.8 = (f32[16,128]{1,0:T(8,128)S(1)}, f32[16,128]{1,0:T(8,128)S(1)}, u32[]{:S(2)}, u32[]{:S(2)}) collective-permute-start(f32[16,128]{1,0:T(8,128)S(1)} %get-tuple-element.54.refs_0_), channel_id=1, source_target_pairs={{0,16},{1,17},{16,0},{17,1},{2,18},{3,19},{18,2},{19,3},{4,20},{5,... | collective-permute-start | bytes 24584 | tf_op jit(solution)/shard_map/ppermute | solution.py:389
  33.0 3.1 %collective-permute-start.7 = (f32[16,128]{1,0:T(8,128)S(1)}, f32[16,128]{1,0:T(8,128)S(1)}, u32[]{:S(2)}, u32[]{:S(2)}) collective-permute-start(f32[16,128]{1,0:T(8,128)S(1)} %get-tuple-element.54.refs_0_), channel_id=1, source_target_pairs={{0,1},{1,0},{16,17},{17,16},{2,3},{3,2},{18,19},{19,18},{4,5},{5,4... | collective-permute-start | bytes 24584 | tf_op jit(solution)/shard_map/ppermute | solution.py:389
  46.7 3.1 %collective-permute-start.12 = (f32[16,128]{1,0:T(8,128)S(1)}, f32[16,128]{1,0:T(8,128)S(1)}, u32[]{:S(2)}, u32[]{:S(2)}) collective-permute-start(f32[16,128]{1,0:T(8,128)S(1)} %later_columns.2.refs_0_), channel_id=1, source_target_pairs={{0,17},{1,16},{16,1},{17,0},{2,19},{3,18},{18,3},{19,2},{4,21},{5,... | collective-permute-start | bytes 24584 | tf_op jit(solution)/shard_map/ppermute | solution.py:389
  46.8 3.7 %collective-permute-start.11 = (f32[16,128]{1,0:T(8,128)S(1)}, f32[16,128]{1,0:T(8,128)S(1)}, u32[]{:S(2)}, u32[]{:S(2)}) collective-permute-start(f32[16,128]{1,0:T(8,128)S(1)} %later_columns.2.refs_0_), channel_id=1, source_target_pairs={{0,16},{1,17},{16,0},{17,1},{2,18},{3,19},{18,2},{19,3},{4,20},{5,... | collective-permute-start | bytes 24584 | tf_op jit(solution)/shard_map/ppermute | solution.py:389
  47.3 3.1 %collective-permute-start.10 = (f32[16,128]{1,0:T(8,128)S(1)}, f32[16,128]{1,0:T(8,128)S(1)}, u32[]{:S(2)}, u32[]{:S(2)}) collective-permute-start(f32[16,128]{1,0:T(8,128)S(1)} %later_columns.2.refs_0_), channel_id=1, source_target_pairs={{0,1},{1,0},{16,17},{17,16},{2,3},{3,2},{18,19},{19,18},{4,5},{5,4... | collective-permute-start | bytes 24584 | tf_op jit(solution)/shard_map/ppermute | solution.py:389
  61.0 2.2 %collective-permute-start.13 = (f32[24,128]{1,0:T(8,128)S(1)}, f32[24,128]{1,0:T(8,128)S(1)}, u32[]{:S(2)}, u32[]{:S(2)}) collective-permute-start(f32[24,128]{1,0:T(8,128)S(1)} %get-tuple-element.60), channel_id=1, source_target_pairs={{0,1},{1,0},{16,17},{17,16},{2,3},{3,2},{18,19},{19,18},{4,5},{5,4... | collective-permute-start | bytes 36872 | tf_op jit(solution)/shard_map/ppermute | solution.py:389
  61.1 3.1 %collective-permute-start.15 = (f32[16,128]{1,0:T(8,128)S(1)}, f32[16,128]{1,0:T(8,128)S(1)}, u32[]{:S(2)}, u32[]{:S(2)}) collective-permute-start(f32[16,128]{1,0:T(8,128)S(1)} %get-tuple-element.61), channel_id=1, source_target_pairs={{0,17},{1,16},{16,1},{17,0},{2,19},{3,18},{18,3},{19,2},{4,21},{5,... | collective-permute-start | bytes 24584 | tf_op jit(solution)/shard_map/ppermute | solution.py:389
  61.7 3.7 %collective-permute-start.14 = (f32[16,128]{1,0:T(8,128)S(1)}, f32[16,128]{1,0:T(8,128)S(1)}, u32[]{:S(2)}, u32[]{:S(2)}) collective-permute-start(f32[16,128]{1,0:T(8,128)S(1)} %get-tuple-element.61), channel_id=1, source_target_pairs={{0,16},{1,17},{16,0},{17,1},{2,18},{3,19},{18,2},{19,3},{4,20},{5,... | collective-permute-start | bytes 24584 | tf_op jit(solution)/shard_map/ppermute | solution.py:389

commit v16 on v10

--- a/solution.py
+++ b/solution.py
@@ -122,7 +122,7 @@
         in_specs=[SMEM, VMEM],
         out_specs=VMEM,
         compiler_params=params(),
-        cost_estimate=pl.CostEstimate(flops=1 << 20, bytes_accessed=1 << 20, transcendentals=0),
+        cost_estimate=pl.CostEstimate(flops=1 << 30, bytes_accessed=1 << 18, transcendentals=0),
         name="lay",
     )(place, block)
 
@@ -417,12 +417,12 @@
         part = source_points.shape[0]
         a = source_mass.reshape(n_z, n_x, CORES, part)
         a = lax.dynamic_index_in_dim(a, core, axis=2, keepdims=False).swapaxes(0, 1).reshape(-1, LANES)
-        blocks = swap_all(target_points, "src", n_src)[1:]
+        direct = swap_all(target_points, near, n_near)
+        blocks = direct[CORES::CORES] + direct[CORES + 1 :: CORES]
         three, two, one = [swap(source_points, "z", n_z, d) for d in (3, 2, 1)]
         mine, packed, b, a = ready(source_points, target_points, target_mass.reshape(-1, LANES), a)
         laid = lay(along, three, 3, n_z)
         packed = swap_all(packed, "core", CORES)
-        blocks = blocks + [swap(block, "core", CORES, 1) for block in blocks]
         groups = swap_all(pack(along, [mine, one, two], laid), "x", n_x)
         place, a = lax.optimization_barrier((place, a))
         targets, offsets, b, first = first_rows(place, b, packed, blocks, groups[0])

time: 66.3 us -> 66.9 us (level)
  blocking collectives: 28.1 us -> 29.7 us
    all_to_all x3, blocking collectives: 28.1 us -> 29.7 us  [share(): return lax.all_to_all(copies, ('z', 'x'), 0, 0, tiled=True)]
where the time goes in v16:
time: 66.9 us; the launch traced here: 66.6 us
  blocking collectives  29.7 us (44%)
  starting transfers between devices  14.8 us (22%)
  Pallas kernels  10.3 us (15%)
  waiting for transfers between devices  8.95 us (13%)
  other arithmetic  1.28 us (2%)
  between operations  0.84 us (1%)
    all_to_all x3, blocking collectives, share(): return lax.all_to_all(copies, ('z', 'x'), 0, 0, tiled=True)  29.7 us
    ppermute x17, starting transfers between devices, swap(): return lax.ppermute(value, axes, [(i, i ^ distance) for i in range(size)])  14.8 us
    ppermute x17, waiting for transfers between devices, swap(): return lax.ppermute(value, axes, [(i, i ^ distance) for i in range(size)])  8.95 us
    pallas_call x1, Pallas kernels, first_columns(): pl.pallas_call(kernel, out_shape=(pltpu.VMEM((width, count), F32), pltpu....  2.44 us
    pallas_call x1, Pallas kernels, first_rows(): pl.pallas_call(kernel, out_shape=(pltpu.VMEM((width, LANES), jnp.bfloat16...  2.17 us
    pallas_call x1, Pallas kernels, other_rows(): pl.pallas_call(kernel, out_shape=(rows_of(count + each * LANES), pltpu.VM...  1.79 us
    pallas_call x2, Pallas kernels, later_columns(): pl.pallas_call(kernel, out_shape=(rows_of(width),) + (rows_of(count),) *...  1.49 us
    pallas_call x2, Pallas kernels, later_rows(): pl.pallas_call(kernel, out_shape=rows_of(count), in_specs=[VMEM] * (4 + l...  1.47 us
  transfers between devices with their start and end apart: 17, of which 9 were waited for; matrix products, arithmetic and copies ran while one was open for 2% of the time, Pallas kernels for 5%

profile of v16, /device:TPU:0, one launch (start us, length us, event | category | flops | bytes accessed | tf_op | source)
XLA Modules:
  0.0 66.6 jit_solution(11494552112619415657)
XLA Ops:
  0.6 3.1 %collective-permute-start = (bf16[128,128]{1,0:T(8,128)(2,1)}, bf16[128,128]{1,0:T(8,128)(2,1)S(1)}, u32[]{:S(2)}, u32[]{:S(2)}) collective-permute-start(bf16[128,128]{1,0:T(8,128)(2,1)} %sources_ref.1), channel_id=1, source_target_pairs={{0,4},{4,0},{8,12},{12,8},{1,5},{5,1},{9,13},{13,9},{2,6},{6,2},{1... | collective-permute-start | bytes 98312 | tf_op jit(solution)/shard_map/ppermute | solution.py:388
  3.7 2.5 %collective-permute-start.2 = (bf16[128,128]{1,0:T(8,128)(2,1)}, bf16[128,128]{1,0:T(8,128)(2,1)S(1)}, u32[]{:S(2)}, u32[]{:S(2)}) collective-permute-start(bf16[128,128]{1,0:T(8,128)(2,1)} %sources_ref.1), channel_id=1, source_target_pairs={{0,12},{4,8},{8,4},{12,0},{1,13},{5,9},{9,5},{13,1},{2,14},{6,10},... | collective-permute-start | bytes 98312 | tf_op jit(solution)/shard_map/ppermute | solution.py:388
  6.7 1.2 %collective-permute-start.4 = (bf16[512,128]{1,0:T(8,128)(2,1)}, bf16[512,128]{1,0:T(8,128)(2,1)S(1)}, u32[]{:S(2)}, u32[]{:S(2)}) collective-permute-start(bf16[512,128]{1,0:T(8,128)(2,1)} %targets_ref.1), channel_id=1, source_target_pairs={{0,16},{1,17},{16,0},{17,1},{2,18},{3,19},{18,2},{19,3},{4,20},{5,... | collective-permute-start | bytes 393224 | tf_op jit(solution)/shard_map/ppermute | solution.py:388
  7.9 1.0 %ready.1 = (bf16[128,128]{1,0:T(8,128)(2,1)S(1)}, bf16[544,128]{1,0:T(8,128)(2,1)S(1)}, f32[8,128]{1,0:T(8,128)S(1)}, f32[8,128]{1,0:T(8,128)S(1)}) custom-call(bf16[128,128]{1,0:T(8,128)(2,1)} %sources_ref.1, bf16[512,128]{1,0:T(8,128)(2,1)} %targets_ref.1, f32[8,128]{1,0:T(8,128)} %bitcast.31, f32[8,128]{1,0:T(8,128)S(1)} %bitcast.24), custom_call_target="tpu_custom_call" | custom-call | flops 1048576 | bytes 1048576 | tf_op jit(solution)/shard_map/ready/pallas_call | solution.py:95
  8.9 1.2 %collective-permute-done.2.block_ref = bf16[128,128]{1,0:T(8,128)(2,1)S(1)} collective-permute-done((bf16[128,128]{1,0:T(8,128)(2,1)}, bf16[128,128]{1,0:T(8,128)(2,1)S(1)}, u32[]{:S(2)}, u32[]{:S(2)}) %collective-permute-start.2) | collective-permute-done | bytes 32800 | tf_op jit(solution)/shard_map/ppermute | solution.py:388
  10.1 1.5 %collective-permute-done.1.refs_2_ = bf16[128,128]{1,0:T(8,128)(2,1)S(1)} collective-permute-done((bf16[128,128]{1,0:T(8,128)(2,1)}, bf16[128,128]{1,0:T(8,128)(2,1)S(1)}, u32[]{:S(2)}, u32[]{:S(2)}) %collective-permute-start.1) | collective-permute-done | bytes 32800 | tf_op jit(solution)/shard_map/ppermute | solution.py:388
  11.6 1.6 %collective-permute-start.6 = (bf16[512,128]{1,0:T(8,128)(2,1)S(1)}, bf16[512,128]{1,0:T(8,128)(2,1)S(1)}, u32[]{:S(2)}, u32[]{:S(2)}) collective-permute-start(bf16[512,128]{1,0:T(8,128)(2,1)S(1)} %pack.1.sources_ref.mine_ref), channel_id=1, source_target_pairs={{0,2},{2,0},{1,3},{3,1},{4,6},{6,4},{5,7},{7,5},{8,10},{10,8},{9,1... | collective-permute-start | bytes 393224 | tf_op jit(solution)/shard_map/ppermute | solution.py:388
  13.2 1.9 %collective-permute-done.4.refs_2_ = bf16[512,128]{1,0:T(8,128)(2,1)S(1)} collective-permute-done((bf16[512,128]{1,0:T(8,128)(2,1)}, bf16[512,128]{1,0:T(8,128)(2,1)S(1)}, u32[]{:S(2)}, u32[]{:S(2)}) %collective-permute-start.4) | collective-permute-done | bytes 131104 | tf_op jit(solution)/shard_map/ppermute | solution.py:388
  15.1 2.2 %first_rows.1 = (bf16[2048,128]{1,0:T(8,128)(2,1)S(1)}, bf16[2048,128]{1,0:T(8,128)(2,1)S(1)}, f32[16,128]{1,0:T(8,128)S(1)}, f32[4,128]{1,0:T(4,128)S(1)}) custom-call(s32[3]{0:T(128)S(1)} %pad_add_fusion.place_ref, f32[8,128]{1,0:T(8,128)S(1)} %get-tuple-element.32.mass_ref, bf16[512,128]{1,0:T(8,128)(2,1)S(1)} %pack.1.sources_ref.mine_ref, ...), custom_call_target="tpu_custom_call" | custom-call | flops 536870912 | bytes 1048576 | tf_op jit(solution)/shard_map/first_rows/pallas_call | solution.py:221
  17.3 1.8 %other_rows.1 = (f32[8,128]{1,0:T(8,128)S(1)}, bf16[1024,128]{1,0:T(8,128)(2,1)S(1)}) custom-call(s32[3]{0:T(128)S(1)} %pad_add_fusion.place_ref, bf16[2048,128]{1,0:T(8,128)(2,1)S(1)} %get-tuple-element.47.targets_ref, bf16[2048,128]{1,0:T(8,128)(2,1)S(1)} %get-tuple-element.36.offset_ref, f32[4,128]{1,0:T(4,128)S(1)} %get-tuple-element.37.first_ref, ...), custom_call_target="tpu_custom_call" | custom-call | tf_op jit(solution)/shard_map/other_rows/pallas_call | solution.py:260
  19.1 11.6 %all_to_all.15.parts_ref = f32[8,8,128]{2,1,0:T(8,128)S(1)} all-to-all(f32[8,8,128]{2,1,0:T(8,128)S(1)} %broadcast_in_dim.6), channel_id=1, replica_groups=mesh['src'=2,'z'=4,'x'=2,'core'=2] {'z','x'}, dimensions={0} | all-to-all | bytes 65536 | tf_op jit(solution)/shard_map/all_to_all | solution.py:401
  30.7 2.4 %first_columns.1 = (f32[2048,1024]{1,0:T(8,128)S(1)}, f32[2048,128]{1,0:T(8,128)S(1)}, f32[16,128]{1,0:T(8,128)S(1)}, f32[16,128]{1,0:T(8,128)S(1)}, f32[8,128]{1,0:T(8,128)S(1)}) custom-call(bf16[1024,128]{1,0:T(8,128)(2,1)S(1)} %get-tuple-element.46.sources_ref, bf16[2048,128]{1,0:T(8,128)(2,1)S(1)} %get-tuple-element.47.targets_ref, ...), custom_call_target="tpu_custom_call" | custom-call | tf_op jit(solution)/shard_map/first_columns/pallas_call | solution.py:304
  33.5 1.6 %collective-permute-start.7 = (f32[16,128]{1,0:T(8,128)S(1)}, f32[16,128]{1,0:T(8,128)S(1)}, u32[]{:S(2)}, u32[]{:S(2)}) collective-permute-start(f32[16,128]{1,0:T(8,128)S(1)} %get-tuple-element.49.refs_0_), channel_id=1, source_target_pairs={{0,1},{1,0},{16,17},{17,16},{2,3},{3,2},{18,19},{19,18},{4,5},{5,4... | collective-permute-start | bytes 24584 | tf_op jit(solution)/shard_map/ppermute | solution.py:388
  36.3 0.7 collective-permute-done.8.refs_2_
  37.0 0.7 %later_rows.2 = f32[8,128]{1,0:T(8,128)S(1)} custom-call(f32[2048,1024]{1,0:T(8,128)S(1)} %get-tuple-element.41.plan_ref, f32[2048,128]{1,0:T(8,128)S(1)} %get-tuple-element.42.reach_ref, f32[16,128]{1,0:T(8,128)S(1)} %get-tuple-element.43.top_ref, f32[16,128]{1,0:T(8,128)S(1)} %get-tuple-element.44.log_ref, f32[16,128]{1,0:T(8,128)S(1)} %get-tuple-element.49.refs_0_, ...), custom_call_target="tpu_custom_call" | custom-call | tf_op jit(solution)/shard_map/later_rows/pallas_call | solution.py:338
  37.7 9.1 %all_to_all.16.parts_ref = f32[8,8,128]{2,1,0:T(8,128)S(1)} all-to-all(f32[8,8,128]{2,1,0:T(8,128)S(1)} %broadcast_in_dim.7), channel_id=1, replica_groups=mesh['src'=2,'z'=4,'x'=2,'core'=2] {'z','x'}, dimensions={0} | all-to-all | bytes 65536 | tf_op jit(solution)/shard_map/all_to_all | solution.py:401
  46.8 0.7 %later_columns.2.refs_0_ = f32[16,128]{1,0:T(8,128)S(1)} custom-call(f32[2048,1024]{1,0:T(8,128)S(1)} %get-tuple-element.41.plan_ref, f32[2048,128]{1,0:T(8,128)S(1)} %get-tuple-element.42.reach_ref, f32[16,128]{1,0:T(8,128)S(1)} %get-tuple-element.43.top_ref, f32[8,8,128]{2,1,0:T(8,128)S(1)} %all_to_all.16.parts_ref, ...), custom_call_target="tpu_custom_call" | custom-call | tf_op jit(solution)/shard_map/later_columns/pallas_call | solution.py:367
  47.9 1.6 %collective-permute-start.10 = (f32[16,128]{1,0:T(8,128)S(1)}, f32[16,128]{1,0:T(8,128)S(1)}, u32[]{:S(2)}, u32[]{:S(2)}) collective-permute-start(f32[16,128]{1,0:T(8,128)S(1)} %later_columns.2.refs_0_), channel_id=1, source_target_pairs={{0,1},{1,0},{16,17},{17,16},{2,3},{3,2},{18,19},{19,18},{4,5},{5,4... | collective-permute-start | bytes 24584 | tf_op jit(solution)/shard_map/ppermute | solution.py:388
  49.5 1.2 %collective-permute-done.12.refs_3_ = f32[16,128]{1,0:T(8,128)S(1)} collective-permute-done((f32[16,128]{1,0:T(8,128)S(1)}, f32[16,128]{1,0:T(8,128)S(1)}, u32[]{:S(2)}, u32[]{:S(2)}) %collective-permute-start.12) | collective-permute-done | bytes 8224 | tf_op jit(solution)/shard_map/ppermute | solution.py:388
  51.3 0.7 %later_rows.3 = f32[8,128]{1,0:T(8,128)S(1)} custom-call(f32[2048,1024]{1,0:T(8,128)S(1)} %get-tuple-element.41.plan_ref, f32[2048,128]{1,0:T(8,128)S(1)} %get-tuple-element.42.reach_ref, f32[16,128]{1,0:T(8,128)S(1)} %get-tuple-element.43.top_ref, f32[16,128]{1,0:T(8,128)S(1)} %get-tuple-element.44.log_ref, f32[16,128]{1,0:T(8,128)S(1)} %later_columns.2.refs_0_, ...), custom_call_target="tpu_custom_call" | custom-call | tf_op jit(solution)/shard_map/later_rows/pallas_call | solution.py:338
  52.1 9.1 %all_to_all.17.parts_ref = f32[8,8,128]{2,1,0:T(8,128)S(1)} all-to-all(f32[8,8,128]{2,1,0:T(8,128)S(1)} %broadcast_in_dim.8), channel_id=1, replica_groups=mesh['src'=2,'z'=4,'x'=2,'core'=2] {'z','x'}, dimensions={0} | all-to-all | bytes 65536 | tf_op jit(solution)/shard_map/all_to_all | solution.py:401
  61.2 0.7 %later_columns.3 = (f32[16,128]{1,0:T(8,128)S(1)}, f32[8,128]{1,0:T(8,128)S(1)}) custom-call(f32[2048,1024]{1,0:T(8,128)S(1)} %get-tuple-element.41.plan_ref, f32[2048,128]{1,0:T(8,128)S(1)} %get-tuple-element.42.reach_ref, f32[16,128]{1,0:T(8,128)S(1)} %get-tuple-element.43.top_ref, f32[8,8,128]{2,1,0:T(8,128)S(1)} %all_to_all.17.parts_ref, ...), custom_call_target="tpu_custom_call" | custom-call | tf_op jit(solution)/shard_map/later_columns/pallas_call | solution.py:367
  62.3 1.8 %collective-permute-start.15 = (f32[16,128]{1,0:T(8,128)S(1)}, f32[16,128]{1,0:T(8,128)S(1)}, u32[]{:S(2)}, u32[]{:S(2)}) collective-permute-start(f32[16,128]{1,0:T(8,128)S(1)} %get-tuple-element.57), channel_id=1, source_target_pairs={{0,16},{1,17},{16,0},{17,1},{2,18},{3,19},{18,2},{19,3},{4,20},{5,... | collective-permute-start | bytes 24584 | tf_op jit(solution)/shard_map/ppermute | solution.py:388
  65.2 0.8 %collective-permute-done.15 = f32[16,128]{1,0:T(8,128)S(1)} collective-permute-done((f32[16,128]{1,0:T(8,128)S(1)}, f32[16,128]{1,0:T(8,128)S(1)}, u32[]{:S(2)}, u32[]{:S(2)}) %collective-permute-start.15) | collective-permute-done | bytes 8224 | tf_op jit(solution)/shard_map/ppermute | solution.py:388
  (41 shorter events, 5.2 us)
Async XLA Ops:
  0.6 7.3 %copy-start = (f32[2048]{0:T(1024)S(1)}, f32[2048]{0:T(1024)}, u32[]{:S(2)}) copy-start(f32[2048]{0:T(1024)} %param.6) | copy-start | bytes 24580
  0.6 9.5 %collective-permute-start = (bf16[128,128]{1,0:T(8,128)(2,1)}, bf16[128,128]{1,0:T(8,128)(2,1)S(1)}, u32[]{:S(2)}, u32[]{:S(2)}) collective-permute-start(bf16[128,128]{1,0:T(8,128)(2,1)} %sources_ref.1), channel_id=1, source_target_pairs={{0,4},{4,0},{8,12},{12,8},{1,5},{5,1},{9,13},{13,9},{2,6},{6,2},{1... | collective-permute-start | bytes 98312 | tf_op jit(solution)/shard_map/ppermute | solution.py:388
  3.7 6.4 %collective-permute-start.2 = (bf16[128,128]{1,0:T(8,128)(2,1)}, bf16[128,128]{1,0:T(8,128)(2,1)S(1)}, u32[]{:S(2)}, u32[]{:S(2)}) collective-permute-start(bf16[128,128]{1,0:T(8,128)(2,1)} %sources_ref.1), channel_id=1, source_target_pairs={{0,12},{4,8},{8,4},{12,0},{1,13},{5,9},{9,5},{13,1},{2,14},{6,10},... | collective-permute-start | bytes 98312 | tf_op jit(solution)/shard_map/ppermute | solution.py:388
  6.2 5.4 %collective-permute-start.1 = (bf16[128,128]{1,0:T(8,128)(2,1)}, bf16[128,128]{1,0:T(8,128)(2,1)S(1)}, u32[]{:S(2)}, u32[]{:S(2)}) collective-permute-start(bf16[128,128]{1,0:T(8,128)(2,1)} %sources_ref.1), channel_id=1, source_target_pairs={{0,8},{4,12},{8,0},{12,4},{1,9},{5,13},{9,1},{13,5},{2,10},{6,14},... | collective-permute-start | bytes 98312 | tf_op jit(solution)/shard_map/ppermute | solution.py:388
  6.3 6.9 %collective-permute-start.5 = (bf16[512,128]{1,0:T(8,128)(2,1)}, bf16[512,128]{1,0:T(8,128)(2,1)S(1)}, u32[]{:S(2)}, u32[]{:S(2)}) collective-permute-start(bf16[512,128]{1,0:T(8,128)(2,1)} %targets_ref.1), channel_id=1, source_target_pairs={{0,17},{1,16},{16,1},{17,0},{2,19},{3,18},{18,3},{19,2},{4,21},{5,... | collective-permute-start | bytes 393224 | tf_op jit(solution)/shard_map/ppermute | solution.py:388
  6.7 8.4 %collective-permute-start.4 = (bf16[512,128]{1,0:T(8,128)(2,1)}, bf16[512,128]{1,0:T(8,128)(2,1)S(1)}, u32[]{:S(2)}, u32[]{:S(2)}) collective-permute-start(bf16[512,128]{1,0:T(8,128)(2,1)} %targets_ref.1), channel_id=1, source_target_pairs={{0,16},{1,17},{16,0},{17,1},{2,18},{3,19},{18,2},{19,3},{4,20},{5,... | collective-permute-start | bytes 393224 | tf_op jit(solution)/shard_map/ppermute | solution.py:388
  10.1 5.0 %collective-permute-start.3 = (bf16[544,128]{1,0:T(8,128)(2,1)S(1)}, bf16[544,128]{1,0:T(8,128)(2,1)S(1)}, u32[]{:S(2)}, u32[]{:S(2)}) collective-permute-start(bf16[544,128]{1,0:T(8,128)(2,1)S(1)} %get-tuple-element.34.refs_0_), channel_id=1, source_target_pairs={{0,1},{1,0},{2,3},{3,2},{4,5},{5,4},{6,7},{7,6},{8,9},{9,8},{10,11... | collective-permute-start | bytes 417800 | tf_op jit(solution)/shard_map/ppermute | solution.py:388
  11.6 5.7 %collective-permute-start.6 = (bf16[512,128]{1,0:T(8,128)(2,1)S(1)}, bf16[512,128]{1,0:T(8,128)(2,1)S(1)}, u32[]{:S(2)}, u32[]{:S(2)}) collective-permute-start(bf16[512,128]{1,0:T(8,128)(2,1)S(1)} %pack.1.sources_ref.mine_ref), channel_id=1, source_target_pairs={{0,2},{2,0},{1,3},{3,1},{4,6},{6,4},{5,7},{7,5},{8,10},{10,8},{9,1... | collective-permute-start | bytes 393224 | tf_op jit(solution)/shard_map/ppermute | solution.py:388
  33.2 3.1 %collective-permute-start.9 = (f32[16,128]{1,0:T(8,128)S(1)}, f32[16,128]{1,0:T(8,128)S(1)}, u32[]{:S(2)}, u32[]{:S(2)}) collective-permute-start(f32[16,128]{1,0:T(8,128)S(1)} %get-tuple-element.49.refs_0_), channel_id=1, source_target_pairs={{0,17},{1,16},{16,1},{17,0},{2,19},{3,18},{18,3},{19,2},{4,21},{5,... | collective-permute-start | bytes 24584 | tf_op jit(solution)/shard_map/ppermute | solution.py:388
  33.3 3.7 %collective-permute-start.8 = (f32[16,128]{1,0:T(8,128)S(1)}, f32[16,128]{1,0:T(8,128)S(1)}, u32[]{:S(2)}, u32[]{:S(2)}) collective-permute-start(f32[16,128]{1,0:T(8,128)S(1)} %get-tuple-element.49.refs_0_), channel_id=1, source_target_pairs={{0,16},{1,17},{16,0},{17,1},{2,18},{3,19},{18,2},{19,3},{4,20},{5,... | collective-permute-start | bytes 24584 | tf_op jit(solution)/shard_map/ppermute | solution.py:388
  33.5 3.5 %collective-permute-start.7 = (f32[16,128]{1,0:T(8,128)S(1)}, f32[16,128]{1,0:T(8,128)S(1)}, u32[]{:S(2)}, u32[]{:S(2)}) collective-permute-start(f32[16,128]{1,0:T(8,128)S(1)} %get-tuple-element.49.refs_0_), channel_id=1, source_target_pairs={{0,1},{1,0},{16,17},{17,16},{2,3},{3,2},{18,19},{19,18},{4,5},{5,4... | collective-permute-start | bytes 24584 | tf_op jit(solution)/shard_map/ppermute | solution.py:388
  47.5 3.1 %collective-permute-start.12 = (f32[16,128]{1,0:T(8,128)S(1)}, f32[16,128]{1,0:T(8,128)S(1)}, u32[]{:S(2)}, u32[]{:S(2)}) collective-permute-start(f32[16,128]{1,0:T(8,128)S(1)} %later_columns.2.refs_0_), channel_id=1, source_target_pairs={{0,17},{1,16},{16,1},{17,0},{2,19},{3,18},{18,3},{19,2},{4,21},{5,... | collective-permute-start | bytes 24584 | tf_op jit(solution)/shard_map/ppermute | solution.py:388
  47.6 3.7 %collective-permute-start.11 = (f32[16,128]{1,0:T(8,128)S(1)}, f32[16,128]{1,0:T(8,128)S(1)}, u32[]{:S(2)}, u32[]{:S(2)}) collective-permute-start(f32[16,128]{1,0:T(8,128)S(1)} %later_columns.2.refs_0_), channel_id=1, source_target_pairs={{0,16},{1,17},{16,0},{17,1},{2,18},{3,19},{18,2},{19,3},{4,20},{5,... | collective-permute-start | bytes 24584 | tf_op jit(solution)/shard_map/ppermute | solution.py:388
  47.9 3.4 %collective-permute-start.10 = (f32[16,128]{1,0:T(8,128)S(1)}, f32[16,128]{1,0:T(8,128)S(1)}, u32[]{:S(2)}, u32[]{:S(2)}) collective-permute-start(f32[16,128]{1,0:T(8,128)S(1)} %later_columns.2.refs_0_), channel_id=1, source_target_pairs={{0,1},{1,0},{16,17},{17,16},{2,3},{3,2},{18,19},{19,18},{4,5},{5,4... | collective-permute-start | bytes 24584 | tf_op jit(solution)/shard_map/ppermute | solution.py:388
  61.9 2.2 %collective-permute-start.13 = (f32[2,4,128]{2,0,1:T(2,128)S(1)}, f32[2,4,128]{2,0,1:T(2,128)S(1)}, u32[]{:S(2)}, u32[]{:S(2)}) collective-permute-start(f32[2,4,128]{2,0,1:T(2,128)S(1)} %copy.13), channel_id=1, source_target_pairs={{0,1},{1,0},{2,3},{3,2},{4,5},{5,4},{6,7},{7,6},{8,9},{9,8},{10,11... | collective-permute-start | bytes 12296 | tf_op jit(solution)/shard_map/ppermute | solution.py:388
  62.0 3.1 %collective-permute-start.16 = (f32[16,128]{1,0:T(8,128)S(1)}, f32[16,128]{1,0:T(8,128)S(1)}, u32[]{:S(2)}, u32[]{:S(2)}) collective-permute-start(f32[16,128]{1,0:T(8,128)S(1)} %get-tuple-element.57), channel_id=1, source_target_pairs={{0,17},{1,16},{16,1},{17,0},{2,19},{3,18},{18,3},{19,2},{4,21},{5,... | collective-permute-start | bytes 24584 | tf_op jit(solution)/shard_map/ppermute | solution.py:388
  62.3 3.7 %collective-permute-start.15 = (f32[16,128]{1,0:T(8,128)S(1)}, f32[16,128]{1,0:T(8,128)S(1)}, u32[]{:S(2)}, u32[]{:S(2)}) collective-permute-start(f32[16,128]{1,0:T(8,128)S(1)} %get-tuple-element.57), channel_id=1, source_target_pairs={{0,16},{1,17},{16,0},{17,1},{2,18},{3,19},{18,2},{19,3},{4,20},{5,... | collective-permute-start | bytes 24584 | tf_op jit(solution)/shard_map/ppermute | solution.py:388
  64.1 1.8 %collective-permute-start.14 = (f32[16,128]{1,0:T(8,128)S(1)}, f32[16,128]{1,0:T(8,128)S(1)}, u32[]{:S(2)}, u32[]{:S(2)}) collective-permute-start(f32[16,128]{1,0:T(8,128)S(1)} %get-tuple-element.57), channel_id=1, source_target_pairs={{0,1},{1,0},{16,17},{17,16},{2,3},{3,2},{18,19},{19,18},{4,5},{5,4... | collective-permute-start | bytes 24584 | tf_op jit(solution)/shard_map/ppermute | solution.py:388
